TPU v7x, 32 devices: a whole 2x2x4 slice. The times are simulated.
32 devices in a mesh: groups: 2 (over x), rows: 16 (over z, y, core).
Axes of the slice: x: 2, y: 2, z: 4, core: 2. Of those that a mesh axis runs over, the one named last changes fastest.
Arguments:
- dictionary: bfloat16 [8192, 32768], P('rows'), may hold values from -0.0625 to 0.0625
- patches: bfloat16 [8192, 2048], P('rows', 'groups'), parts along dimension 1, may hold values from -6 to 6
- initial_codes: bfloat16 [32, 16, 4096], P(('groups', 'rows')), parts along dimension 0, may hold values from -3 to 3
- support: int32 [32, 16], P('groups'), parts along dimension 0, may hold values from 0 to 511, as said below
- counts: int32 [32], P('groups'), parts along dimension 0, may hold values from 4 to 16, as said below
- group_order: int32 [32], P('groups'), parts along dimension 0, may hold values from 0 to 15, each once
- penalty: float32 [32, 64], P('groups'), parts along dimension 0, may hold values from 0.05 to 0.5
Outputs:
- codes: float32 [32, 16, 4096], P(('groups', 'rows')), parts along dimension 0
There are 2 independent parts, one for each index of `groups`. A program takes and returns all parts, laid end to end along the dimension named above; an argument that names none is the same for every part. Nothing has to cross between parts.
Inputs may be any that keep to these rules, and one draw needn't show every extreme that they name: `support`: in each group's list the first counts entries are distinct block ids; entries at positions counts and beyond are padding and are ignored. The counts of one part sum to exactly 160.
All inputs are finite; a program needn't handle non-finite values.
Results may differ from a plain program's by a relative error of at most 0.0055.
Values may be sent and summed in bfloat16 or wider, within the bound.
No kernel may reach another device: no remote copies, remote signals or barrier semaphores. Data moves between devices by JAX's collectives and lax.ppermute only.
A program may use at most 192 MiB of HBM per device.

v0:
```python
import jax
import jax.numpy as jnp
from jax import lax
from jax.sharding import PartitionSpec as P

BLOCK = 64
SLOTS = 16
PATCHES = 64
ITERS = 3


def momentum_list():
    values = []
    tvalue = 1.0
    for turn in range(ITERS):
        tnext = (1.0 + (1.0 + 4.0 * tvalue * tvalue) ** 0.5) / 2.0
        values.append((tvalue - 1.0) / tnext)
        tvalue = tnext
    return values


def local(dictionary, patches, initial_codes, support, counts, group_order, penalty):
    pixel_rows = dictionary.shape[0]
    groups = group_order.shape[0]
    nblocks = dictionary.shape[1] // BLOCK
    tile_size = PATCHES * BLOCK
    devices_axis = lax.axis_size("rows")
    position = lax.axis_index("rows")
    owned = groups // devices_axis
    momenta = momentum_list()
    blocks_all = dictionary.reshape(pixel_rows, nblocks, BLOCK)
    ordered_ids = jnp.take(support, group_order, axis=0)
    ordered_counts = jnp.take(counts, group_order, axis=0)
    live_grid = jnp.arange(SLOTS)[None, :] < ordered_counts[:, None]
    targets = jnp.take(patches.reshape(pixel_rows, groups, PATCHES), group_order, axis=1)
    thresh_all = 0.5 * jnp.repeat(jnp.take(penalty, group_order, axis=0), BLOCK, axis=1)
    first_owned = position * owned
    local_live = lax.dynamic_slice_in_dim(live_grid, first_owned, owned, 0)
    masked = initial_codes * local_live[:, :, None].astype(jnp.bfloat16)

    def group_terms(point_full, group_count):
        dict_blocks = jnp.take(blocks_all, ordered_ids, axis=1)
        code_block = point_full
        code_block = code_block.reshape(group_count, SLOTS, PATCHES, BLOCK)
        residual = jnp.einsum(
            "pgsa,gsna->pgn", dict_blocks, code_block, preferred_element_type=jnp.float32
        )
        residual = (residual - targets.astype(jnp.float32)).astype(jnp.bfloat16)
        gradient = jnp.einsum(
            "pgn,pgsa->gsna", residual, dict_blocks, preferred_element_type=jnp.float32
        )
        return gradient.reshape(group_count * SLOTS, tile_size)

    start_full = lax.all_gather(masked, "rows", axis=0, tiled=True)
    live_float = local_live[:, :, None].astype(jnp.float32)
    local_thresh = lax.dynamic_slice_in_dim(thresh_all, first_owned, owned, 0)[:, None, :]
    previous = masked.astype(jnp.float32)
    point_loc = previous
    point_full = start_full
    for turn in range(ITERS):

        def partial_term(row_start, row_count, current_full=point_full):
            return group_terms(current_full, row_count // SLOTS)

        gradient = lax.psum_scatter(
            partial_term(jnp.int32(0), lax.axis_size("rows") * (owned * SLOTS)),
            "rows",
            scatter_dimension=0,
            tiled=True,
        )
        gradient = gradient.reshape(owned, SLOTS, tile_size)
        stepped = point_loc - 0.5 * gradient
        current = (stepped - jnp.clip(stepped, -local_thresh, local_thresh)) * live_float
        point_loc = current + momenta[turn] * (current - previous)
        previous = current
        if turn + 1 < ITERS:
            point_full = lax.all_gather(point_loc.astype(jnp.bfloat16), "rows", axis=0, tiled=True)
    return previous


def solution(mesh):
    in_specs = (
        P("rows", None),
        P("rows", "groups"),
        P(("groups", "rows"), None, None),
        P("groups", None),
        P("groups"),
        P("groups"),
        P("groups", None),
    )
    out_specs = P(("groups", "rows"), None, None)
    return jax.shard_map(local, mesh=mesh, in_specs=in_specs, out_specs=out_specs, check_vma=False)
```

profile of v0, /device:TPU:0, one launch (start us, length us, event | category | flops | bytes accessed | tf_op | source)
XLA Modules:
  0.0 523.5 jit_solution(1216521591889111576)
XLA Ops:
  6.5 0.7 compare_select_fusion.1
  7.2 1.3 gather_fusion
  8.5 0.7 broadcast_select_fusion.8
  9.2 0.6 dynamic-slice
  9.8 0.6 fusion.48
  10.4 1.6 broadcast_multiply_fusion
  12.2 1.3 gather_fusion.1
  13.6 44.0 %copy.14 = bf16[512,32768]{0,1:T(8,128)(2,1)} copy(bf16[512,32768]{1,0:T(8,128)(2,1)} %param.9) | data formatting | bytes 67108864 | tf_op args[0]
  58.1 0.6 gather_fusion.2
  58.7 12.7 %gather_fusion.4 = bf16[256,512,64]{1,2,0:T(8,128)(2,1)} fusion(bf16[512,512,64]{0,2,1:T(8,128)(2,1)} %bitcast.149, s32[1024]{0:T(1024)S(1)} %pad_clamp_fusion), kind=kCustom, calls=%fused_computation.clone | custom fusion | bytes 33555456 | tf_op jit(solution)/shard_map/jit(_take)/gather | solution.py:42
  71.4 6.9 %reshape.81 = bf16[16,16,64,64]{3,2,1,0:T(8,128)(2,1)} reshape(bf16[16,16,4096]{2,1,0:T(8,128)(2,1)} %all-gather.4.cloned.1.call-done) | data formatting | bytes 4194304 | tf_op jit(solution)/shard_map/reshape | solution.py:44
  78.3 22.6 %fusion.12 = f32[16,16,64,64]{2,3,1,0:T(8,128)} fusion(bf16[16,16,512,64]{2,3,1,0:T(8,128)(2,1)} %bitcast.150, pred[16,16]{1,0:T(8,128)(4,1)S(1)} %get-tuple-element.10, bf16[16,16,64,64]{3,2,1,0:T(8,128)(2,1)} %reshape.81, bf16[16,512,64]{1,2,0:T(8,128)(2,1)S(1)} %gather_fusion.2, pred[16]{0:T(512)(128)(4,1)S(1)} %get-tuple-element.9), kind=kOutput, calls=%fused_computation.18 | convolution fusion | flops 2166358016 | bytes 24117520 | tf_op jit(solution)/shard_map/pgn,pgsa->gsna/dot_general | solution.py:49
  100.9 9.2 %copy.16 = f32[16,16,64,64]{3,2,1,0:T(8,128)} copy(f32[16,16,64,64]{2,3,1,0:T(8,128)} %fusion.12) | data formatting | bytes 8388608 | tf_op jit(solution)/shard_map/pgn,pgsa->gsna/transpose | solution.py:49
  110.2 8.0 %reshape.83 = f32[256,4096]{1,0:T(8,128)} reshape(f32[16,16,64,64]{3,2,1,0:T(8,128)} %copy.16) | data formatting | bytes 8388608 | tf_op jit(solution)/shard_map/reshape | solution.py:52
  118.2 0.6 gather_fusion.3
  119.3 0.6 fusion.49
  119.9 73.5 %reduce-scatter.4.cloned.1.call-done = f32[16,4096]{1,0:T(8,128)} async-done(((f32[256,4096]{1,0:T(8,128)}), f32[16,4096]{1,0:T(8,128)}) %reduce-scatter.4.cloned.1.call-update) | async-done | bytes 262160 | tf_op jit(solution)/shard_map/reduce_scatter | solution.py:65
  193.5 1.8 fusion.47
  195.5 40.8 %all-gather.6.cloned.1.call-done = bf16[16,16,4096]{2,1,0:T(8,128)(2,1)} async-done(((bf16[1,16,4096]{2,1,0:T(8,128)(2,1)}), bf16[16,16,4096]{2,1,0:T(8,128)(2,1)}) %all-gather.6.cloned.1.call-update) | async-done | bytes 2097168 | tf_op jit(solution)/shard_map/all_gather | solution.py:77
  236.3 6.9 %reshape.84 = bf16[16,16,64,64]{3,2,1,0:T(8,128)(2,1)} reshape(bf16[16,16,4096]{2,1,0:T(8,128)(2,1)} %all-gather.6.cloned.1.call-done) | data formatting | bytes 4194304 | tf_op jit(solution)/shard_map/reshape | solution.py:44
  243.2 22.6 %fusion.15 = f32[16,16,64,64]{2,3,1,0:T(8,128)} fusion(bf16[16,16,512,64]{2,3,1,0:T(8,128)(2,1)} %bitcast.151, pred[16,16]{1,0:T(8,128)(4,1)S(1)} %get-tuple-element.10, bf16[16,16,64,64]{3,2,1,0:T(8,128)(2,1)} %reshape.84, bf16[16,512,64]{1,2,0:T(8,128)(2,1)S(1)} %gather_fusion.2, pred[16]{0:T(512)(128)(4,1)S(1)} %get-tuple-element.9), kind=kOutput, calls=%fused_computation.19 | convolution fusion | flops 2166358016 | bytes 24117520 | tf_op jit(solution)/shard_map/pgn,pgsa->gsna/dot_general | solution.py:49
  265.8 9.2 %copy.17 = f32[16,16,64,64]{3,2,1,0:T(8,128)} copy(f32[16,16,64,64]{2,3,1,0:T(8,128)} %fusion.15) | data formatting | bytes 8388608 | tf_op jit(solution)/shard_map/pgn,pgsa->gsna/transpose | solution.py:49
  275.1 8.0 %reshape.85 = f32[256,4096]{1,0:T(8,128)} reshape(f32[16,16,64,64]{3,2,1,0:T(8,128)} %copy.17) | data formatting | bytes 8388608 | tf_op jit(solution)/shard_map/reshape | solution.py:52
  283.1 71.2 %reduce-scatter.6.cloned.1.call-done = f32[16,4096]{1,0:T(8,128)} async-done(((f32[256,4096]{1,0:T(8,128)}), f32[16,4096]{1,0:T(8,128)}) %reduce-scatter.6.cloned.1.call-update) | async-done | bytes 262160 | tf_op jit(solution)/shard_map/reduce_scatter | solution.py:65
  354.4 1.9 fusion.56
  356.3 40.6 %all-gather.8.cloned.1.call-done = bf16[16,16,4096]{2,1,0:T(8,128)(2,1)} async-done(((bf16[1,16,4096]{2,1,0:T(8,128)(2,1)}), bf16[16,16,4096]{2,1,0:T(8,128)(2,1)}) %all-gather.8.cloned.1.call-update) | async-done | bytes 2097168 | tf_op jit(solution)/shard_map/all_gather | solution.py:77
  396.9 6.9 %reshape.86 = bf16[16,16,64,64]{3,2,1,0:T(8,128)(2,1)} reshape(bf16[16,16,4096]{2,1,0:T(8,128)(2,1)} %all-gather.8.cloned.1.call-done) | data formatting | bytes 4194304 | tf_op jit(solution)/shard_map/reshape | solution.py:44
  403.8 22.6 %fusion.18 = f32[16,16,64,64]{2,3,1,0:T(8,128)} fusion(bf16[16,16,512,64]{2,3,1,0:T(8,128)(2,1)} %bitcast.152, pred[16,16]{1,0:T(8,128)(4,1)S(1)} %get-tuple-element.10, bf16[16,16,64,64]{3,2,1,0:T(8,128)(2,1)} %reshape.86, bf16[16,512,64]{1,2,0:T(8,128)(2,1)S(1)} %gather_fusion.2, pred[16]{0:T(512)(128)(4,1)S(1)} %get-tuple-element.9), kind=kOutput, calls=%fused_computation.20 | convolution fusion | flops 2166358016 | bytes 24117520 | tf_op jit(solution)/shard_map/pgn,pgsa->gsna/dot_general | solution.py:49
  426.5 9.3 %copy.18 = f32[16,16,64,64]{3,2,1,0:T(8,128)} copy(f32[16,16,64,64]{2,3,1,0:T(8,128)} %fusion.18) | data formatting | bytes 8388608 | tf_op jit(solution)/shard_map/pgn,pgsa->gsna/transpose | solution.py:49
  435.7 7.9 %reshape.87 = f32[256,4096]{1,0:T(8,128)} reshape(f32[16,16,64,64]{3,2,1,0:T(8,128)} %copy.18) | data formatting | bytes 8388608 | tf_op jit(solution)/shard_map/reshape | solution.py:52
  443.7 71.3 %reduce-scatter.8.cloned.1.call-done = f32[16,4096]{1,0:T(8,128)} async-done(((f32[256,4096]{1,0:T(8,128)}), f32[16,4096]{1,0:T(8,128)}) %reduce-scatter.8.cloned.1.call-update) | async-done | bytes 262160 | tf_op jit(solution)/shard_map/reduce_scatter | solution.py:65
  514.9 1.7 subtract_multiply_fusion
  (33 shorter events, 1.7 us)
Async XLA Ops:
  6.5 111.7 %copy-start = (f32[16,64]{1,0:T(8,128)S(1)}, f32[16,64]{1,0:T(8,128)}, u32[]{:S(2)}) copy-start(f32[16,64]{1,0:T(8,128)} %param.15) | copy-start | bytes 12292
  6.5 64.9 %all-gather.4.cloned.1.call-start = ((), (), s32[]{:S(2)}) async-start(), calls=%async_computation.3 | async-start | bytes 2228224 | tf_op jit(solution)/shard_map/all_gather | solution.py:54
  12.1 181.4 %reduce-scatter.4.cloned.1.call-start = ((), (), s32[]{:S(2)}) async-start(), calls=%async_computation.4 | async-start | bytes 4456448 | tf_op jit(solution)/shard_map/reduce_scatter | solution.py:65
  13.6 44.0 %copy-start.4 = (bf16[512,1024]{1,0:T(8,128)(2,1)S(1)}, bf16[512,1024]{1,0:T(8,128)(2,1)}, u32[]{:S(2)}) copy-start(bf16[512,1024]{1,0:T(8,128)(2,1)} %param.10) | copy-start | bytes 3145732
  110.2 83.3 %copy-start.2 = (bf16[1,16,4096]{2,1,0:T(8,128)(2,1)S(1)}, bf16[1,16,4096]{2,1,0:T(8,128)(2,1)}, u32[]{:S(2)}) copy-start(bf16[1,16,4096]{2,1,0:T(8,128)(2,1)} %param.11) | copy-start | bytes 393220
  118.2 118.1 %all-gather.6.cloned.1.call-start = ((), (), s32[]{:S(2)}) async-start(), calls=%async_computation.5 | async-start | bytes 2228224 | tf_op jit(solution)/shard_map/all_gather | solution.py:77
  195.3 159.1 %reduce-scatter.6.cloned.1.call-start = ((), (), s32[]{:S(2)}) async-start(), calls=%async_computation.6 | async-start | bytes 4456448 | tf_op jit(solution)/shard_map/reduce_scatter | solution.py:65
  275.1 79.3 %copy-start.3 = (f32[16,4096]{1,0:T(8,128)S(1)}, f32[16,4096]{1,0:T(8,128)}, u32[]{:S(2)}) copy-start(f32[16,4096]{1,0:T(8,128)} %reduce-scatter.4.cloned.1.call-done) | copy-start | bytes 786436
  283.1 113.8 %all-gather.8.cloned.1.call-start = ((), (), s32[]{:S(2)}) async-start(), calls=%async_computation.7 | async-start | bytes 2228224 | tf_op jit(solution)/shard_map/all_gather | solution.py:77
  356.2 158.7 %reduce-scatter.8.cloned.1.call-start = ((), (), s32[]{:S(2)}) async-start(), calls=%async_computation.8 | async-start | bytes 4456448 | tf_op jit(solution)/shard_map/reduce_scatter | solution.py:65
  426.5 90.2 %copy-start.1 = (f32[16,64]{1,0:T(8,128)S(1)}, f32[16,64]{1,0:T(8,128)}, u32[]{:S(2)}) copy-start(f32[16,64]{1,0:T(8,128)} %param.15) | copy-start | bytes 12292
Sparse Core Ops, SparseCore 0:
  12.2 44.0 all-gather.3
  118.3 75.1 reduce-scatter.3
  195.9 40.3 all-gather.5
  283.2 71.1 reduce-scatter.5
  356.4 40.4 all-gather.7
  443.8 71.1 reduce-scatter.7
where the time goes:
time: 526 us; the launch traced here: 524 us
  waiting for transfers between devices  298 us (57%)
  local copies, waits for them, and re-layouts  134 us (25%)
  matrix products  67.9 us (13%)
  between operations  13.6 us (3%)
  other arithmetic  9.8 us (2%)
    reduce_scatter x3, waiting for transfers between devices, local(): lax.psum_scatter(partial_term(jnp.int32(0), lax.axis_size('rows') * (owne...  216 us
    all_gather x2, waiting for transfers between devices, local(): lax.all_gather(point_loc.astype(jnp.bfloat16), 'rows', axis=0, tiled=True)  81.4 us
    dot_general x3, matrix products, group_terms(): jnp.einsum('pgn,pgsa->gsna', residual, dict_blocks, preferred_element_typ...  67.9 us
    unnamed x12, local copies, waits for them, and re-layouts  44.5 us
    transpose x3, local copies, waits for them, and re-layouts, group_terms(): jnp.einsum('pgn,pgsa->gsna', residual, dict_blocks, preferred_element_typ...  27.7 us
    reshape x3, local copies, waits for them, and re-layouts, group_terms(): return gradient.reshape(group_count * SLOTS, tile_size)  23.9 us
    reshape x3, local copies, waits for them, and re-layouts, group_terms(): code_block = code_block.reshape(group_count, SLOTS, PATCHES, BLOCK)  20.7 us
    gather x1, local copies, waits for them, and re-layouts, group_terms(): dict_blocks = jnp.take(blocks_all, ordered_ids, axis=1)  12.7 us
  transfers between devices with their start and end apart: 6, of which 5 were waited for; matrix products, arithmetic and copies ran while one was open for 12% of the time, Pallas kernels for 0%

commit v1 on v0

v1 whole, which is shorter than its diff:
```python
import functools

import jax
import jax.numpy as jnp
from jax import lax
from jax.experimental import pallas as pl
from jax.experimental.pallas import tpu as pltpu
from jax.sharding import PartitionSpec as P

BLOCK = 64
SLOTS = 16
PATCHES = 64
ITERS = 3
MEAN_LIVE = 10
LANES = 2 * BLOCK
SLOT_PAIRS = SLOTS // 2
VMEM_LIMIT = 56 * 1024 * 1024


def momentum_list():
    values = []
    tvalue = 1.0
    for turn in range(ITERS):
        tnext = (1.0 + (1.0 + 4.0 * tvalue * tvalue) ** 0.5) / 2.0
        values.append((tvalue - 1.0) / tnext)
        tvalue = tnext
    return values


def swap_halves(value):
    return jnp.concatenate([value[:, BLOCK:], value[:, :BLOCK]], axis=1)


def upper_half(shape):
    return lax.broadcasted_iota(jnp.int32, shape, 1) >= BLOCK


def support_kernel(order, support, counts, dictionary, out, held, sems):
    step = pl.program_id(0)

    def each_copy(index, act):
        group = order[index]
        half = index % 2
        for slot in range(SLOTS):

            @pl.when(slot < counts[group])
            def _():
                start = pl.multiple_of((support[group, slot] // 2) * LANES, LANES)
                act(pltpu.make_async_copy(dictionary.at[:, pl.ds(start, LANES)], held.at[half, slot], sems.at[half, slot]))

    @pl.when(step == 0)
    def _():
        each_copy(step, lambda copy: copy.start())

    @pl.when(step + 1 < pl.num_programs(0))
    def _():
        each_copy(step + 1, lambda copy: copy.start())

    each_copy(step, lambda copy: copy.wait())
    group = order[step]
    live = counts[group]
    half = step % 2
    upper = upper_half(held.shape[2:])
    for pair in range(SLOT_PAIRS):
        parts = []
        for side in range(2):
            slot = 2 * pair + side
            block = held[half, slot]
            swap = (support[group, slot] % 2) != side
            block = jnp.where(swap, swap_halves(block), block)
            parts.append(jnp.where(slot < live, block, jnp.zeros_like(block)))
        out[0, :, pair * LANES : (pair + 1) * LANES] = jnp.where(upper, parts[1], parts[0])


def collect_support(order, support, counts, dictionary):
    groups = order.shape[0]
    rows = dictionary.shape[0]
    return pl.pallas_call(
        support_kernel,
        grid_spec=pltpu.PrefetchScalarGridSpec(
            num_scalar_prefetch=3,
            grid=(groups,),
            in_specs=[pl.BlockSpec(memory_space=pl.ANY)],
            out_specs=pl.BlockSpec((1, rows, SLOTS * BLOCK), lambda j, *_: (j, 0, 0)),
            scratch_shapes=[
                pltpu.VMEM((2, SLOTS, rows, LANES), dictionary.dtype),
                pltpu.SemaphoreType.DMA((2, SLOTS)),
            ],
        ),
        out_shape=jax.ShapeDtypeStruct((groups, rows, SLOTS * BLOCK), dictionary.dtype),
        compiler_params=pltpu.CompilerParams(vmem_limit_bytes=VMEM_LIMIT),
        cost_estimate=pl.CostEstimate(
            flops=0, transcendentals=0, bytes_accessed=3 * groups * rows * SLOTS * BLOCK * 2
        ),
        name="collect_support",
    )(order, support, counts, dictionary)


def gradient_kernel(packed_in, packed_out, order, counts, own, blocks, codes, targets, *rest):
    if packed_out:
        (out, lhs, offset_ref) = rest
    else:
        (out, own_codes, lhs, offset_ref) = rest
    step = pl.program_id(0)
    live = counts[order[step]]

    @pl.when(step == 0)
    def _():
        offset_ref[0] = 0

    offset = offset_ref[0]
    first = offset // 2
    odd = (offset % 2) == 1
    shape = (PATCHES, LANES)
    upper = upper_half(shape)
    side = upper.astype(jnp.int32)
    if packed_in:
        last = codes.shape[0] - 1
        loads = [codes[jnp.minimum(first + pair, last)] for pair in range(SLOT_PAIRS + 1)]
        swapped = [swap_halves(value) for value in loads]
    for pair in range(SLOT_PAIRS):
        if packed_in:
            value = jnp.where(odd, jnp.where(upper, swapped[pair + 1], swapped[pair]), loads[pair])
        else:
            value = codes[0, pair]
        value = jnp.where(2 * pair + side < live, value, jnp.zeros_like(value))
        lhs[:, pair * LANES : (pair + 1) * LANES] = value
        if not packed_out:

            @pl.when(step == own[0])
            def _(pair=pair, value=value):
                own_codes[pair] = value

    matrix = blocks[0]
    residual = lax.dot_general(lhs[...], matrix, (((1,), (1,)), ((), ())), preferred_element_type=jnp.float32)
    residual = (residual - targets[...].astype(jnp.float32)).astype(jnp.bfloat16)
    gradient = jnp.dot(residual, matrix, preferred_element_type=jnp.float32)
    parts = [gradient[:, pair * LANES : (pair + 1) * LANES] for pair in range(SLOT_PAIRS)]
    if packed_out:
        turned = [swap_halves(part) for part in parts]
        final = out.shape[0] - 1
        for pair in range(SLOT_PAIRS + 1):
            straight = parts[min(pair, SLOT_PAIRS - 1)]
            before = turned[max(pair - 1, 0)]
            after = turned[min(pair, SLOT_PAIRS - 1)]
            value = jnp.where(odd, jnp.where(upper, after, before), straight)
            entry = 2 * (first + pair) + side
            mine = (entry >= offset) & (entry < offset + live)
            place = jnp.minimum(first + pair, final)
            out[place] = jnp.where(mine, value.astype(out.dtype), out[place])
    else:
        for pair in range(SLOT_PAIRS):
            out[0, pair] = parts[pair].astype(out.dtype)
    offset_ref[0] = offset + live


def gradient_call(order, counts, own, blocks, codes, targets, packed_in, packed_out, pairs):
    groups, rows, width = blocks.shape
    if packed_in:
        code_spec = pl.BlockSpec((pairs, PATCHES, LANES), lambda j, *_: (0, 0, 0))
    else:
        code_spec = pl.BlockSpec((1, SLOT_PAIRS, PATCHES, LANES), lambda j, *_: (j, 0, 0, 0))
    if packed_out:
        out_shape = [jax.ShapeDtypeStruct((pairs, PATCHES, LANES), jnp.float32)]
        out_specs = [pl.BlockSpec((pairs, PATCHES, LANES), lambda j, *_: (0, 0, 0))]
    else:
        out_shape = [
            jax.ShapeDtypeStruct((groups, SLOT_PAIRS, PATCHES, LANES), jnp.float32),
            jax.ShapeDtypeStruct((SLOT_PAIRS, PATCHES, LANES), jnp.bfloat16),
        ]
        out_specs = [
            pl.BlockSpec((1, SLOT_PAIRS, PATCHES, LANES), lambda j, *_: (j, 0, 0, 0)),
            pl.BlockSpec((SLOT_PAIRS, PATCHES, LANES), lambda j, *_: (0, 0, 0)),
        ]
    return pl.pallas_call(
        functools.partial(gradient_kernel, packed_in, packed_out),
        grid_spec=pltpu.PrefetchScalarGridSpec(
            num_scalar_prefetch=3,
            grid=(groups,),
            in_specs=[
                pl.BlockSpec((1, rows, width), lambda j, *_: (j, 0, 0)),
                code_spec,
                pl.BlockSpec((PATCHES, rows), lambda j, order, *_: (order[j], 0)),
            ],
            out_specs=out_specs,
            scratch_shapes=[pltpu.VMEM((PATCHES, width), jnp.bfloat16), pltpu.SMEM((1,), jnp.int32)],
        ),
        out_shape=out_shape,
        compiler_params=pltpu.CompilerParams(vmem_limit_bytes=VMEM_LIMIT),
        cost_estimate=pl.CostEstimate(
            flops=4 * groups * rows * width * PATCHES, transcendentals=0, bytes_accessed=groups * rows * width * 2
        ),
        name="gradient",
    )(order, counts, own, blocks, codes, targets)


def shrink(value, thresh):
    return value - jnp.clip(value, -thresh, thresh)


def local(dictionary, patches, initial_codes, support, counts, group_order, penalty):
    groups = group_order.shape[0]
    position = lax.axis_index("rows")
    devices = lax.axis_size("rows")
    momenta = momentum_list()
    owned_entries = MEAN_LIVE * groups // devices
    owned_pairs = owned_entries // 2
    pairs = owned_pairs * devices

    laid = initial_codes.reshape(SLOT_PAIRS, 2, PATCHES, BLOCK).transpose(0, 2, 1, 3)
    laid = laid.reshape(1, SLOT_PAIRS, PATCHES, LANES)
    start = lax.all_gather(laid, "rows", axis=0, tiled=True)

    own = position.astype(jnp.int32).reshape(1)
    blocks = collect_support(group_order, support, counts, dictionary)
    targets = patches.T

    half_penalty = 0.5 * penalty
    ends = jnp.cumsum(jnp.take(counts, group_order))
    entry = position * owned_entries + jnp.arange(owned_entries)
    holder = jnp.sum((entry[:, None] >= ends[None, :]).astype(jnp.int32), axis=1)
    thresh = jnp.take(half_penalty, jnp.take(group_order, holder), axis=0)
    thresh = jnp.repeat(thresh.reshape(owned_pairs, 2, PATCHES).transpose(0, 2, 1), BLOCK, axis=2)
    own_thresh = lax.dynamic_index_in_dim(half_penalty, group_order[position], 0, False)[None, :, None]

    def masked_start():
        begins = ends - jnp.take(counts, group_order)
        slot = entry - jnp.take(begins, holder)
        flat = start.reshape(groups * SLOT_PAIRS, PATCHES, 2, BLOCK)
        picked = [
            lax.dynamic_slice(
                flat,
                (holder[i] * SLOT_PAIRS + slot[i] // 2, 0, slot[i] % 2, 0),
                (1, PATCHES, 1, BLOCK),
            ).reshape(PATCHES, BLOCK)
            for i in range(owned_entries)
        ]
        return jnp.stack(
            [jnp.concatenate([picked[2 * i], picked[2 * i + 1]], axis=1) for i in range(owned_pairs)]
        )

    def run(codes, packed_in, packed_out):
        return gradient_call(group_order, counts, own, blocks, codes, targets, packed_in, packed_out, pairs)

    def scatter(value):
        return lax.psum_scatter(value, "rows", scatter_dimension=0, tiled=True)

    point = masked_start().astype(jnp.float32)
    previous = point
    codes = start
    for turn in range(ITERS - 1):
        (partial,) = run(codes, turn > 0, True)
        current = shrink(point - 0.5 * scatter(partial), thresh)
        point = current + momenta[turn] * (current - previous)
        previous = current
        codes = lax.all_gather(point.astype(jnp.bfloat16), "rows", axis=0, tiled=True)
    partial, sent = run(codes, True, False)
    gradient = scatter(partial)[0]
    result = shrink(sent.astype(jnp.float32) - 0.5 * gradient, own_thresh)
    result = result.reshape(SLOT_PAIRS, PATCHES, 2, BLOCK).transpose(0, 2, 1, 3)
    return result.reshape(1, SLOTS, PATCHES * BLOCK)


def solution(mesh):
    in_specs = (
        P("rows", None),
        P("rows", "groups"),
        P(("groups", "rows"), None, None),
        P("groups", None),
        P("groups"),
        P("groups"),
        P("groups", None),
    )
    out_specs = P(("groups", "rows"), None, None)
    return jax.shard_map(local, mesh=mesh, in_specs=in_specs, out_specs=out_specs, check_vma=False)
```

time: 526 us -> 404 us (0.77)
  local copies, waits for them, and re-layouts: 134 us -> 18 us
  Pallas kernels: 0 us -> 85 us
  matrix products: 67.9 us -> 0 us
  waiting for transfers between devices: 298 us -> 245 us
  between operations: 13.6 us -> 47.5 us
    pallas_call x0 -> x4, Pallas kernels: none -> 85 us  [the longest x3 61.4 us: gradient_call(): pl.pallas_call(functools.partial(gradient_kernel, packed_in, packed_out),...]
    dot_general x3 -> x0, matrix products: 67.9 us -> none  [group_terms(): jnp.einsum('pgn,pgsa->gsna', residual, dict_blocks, preferred_element_typ...]
    reduce_scatter x3, waiting for transfers between devices: 216 us -> 152 us  [scatter(): return lax.psum_scatter(value, 'rows', scatter_dimension=0, tiled=True)]
    unnamed x12 -> x18, local copies, waits for them, and re-layouts: 44.5 us -> 2.96 us
    reshape x6 -> x7, local copies, waits for them, and re-layouts: 44.6 us -> 7.01 us  [the longest x1 3.32 us: masked_start(): flat = start.reshape(groups * SLOT_PAIRS, PATCHES, 2, BLOCK)]
    transpose x3 -> x2, local copies, waits for them, and re-layouts: 27.7 us -> 0.17 us  [the longest x1 0.12 us: local(): thresh.reshape(owned_pairs, 2, PATCHES).transpose(0, 2, 1)]
    gather x5, local copies, waits for them, and re-layouts: 16.4 us -> 3.2 us  [the longest x1 1.31 us: local(): ends = jnp.cumsum(jnp.take(counts, group_order))]
    all_gather x3, waiting for transfers between devices: 81.4 us -> 92.6 us  [the longest x2 76.6 us: local(): lax.all_gather(point.astype(jnp.bfloat16), 'rows', axis=0, tiled=True)]
  transfers between devices with their start and end apart: 6 -> 6, of which waited for: 5 -> 6; matrix products, arithmetic and copies ran while one was open for 12% -> 4% of each run, Pallas kernels for 0% -> 6%
where the time goes in v1:
time: 404 us; the launch traced here: 402 us
  waiting for transfers between devices  245 us (61%)
  Pallas kernels  85 us (21%)
  between operations  47.5 us (12%)
  local copies, waits for them, and re-layouts  18 us (4%)
  other arithmetic  6.58 us (2%)
    reduce_scatter x3, waiting for transfers between devices, scatter(): return lax.psum_scatter(value, 'rows', scatter_dimension=0, tiled=True)  152 us
    all_gather x2, waiting for transfers between devices, local(): lax.all_gather(point.astype(jnp.bfloat16), 'rows', axis=0, tiled=True)  76.6 us
    pallas_call x3, Pallas kernels, gradient_call(): pl.pallas_call(functools.partial(gradient_kernel, packed_in, packed_out),...  61.4 us
    pallas_call x1, Pallas kernels, collect_support(): pl.pallas_call(support_kernel, grid_spec=pltpu.PrefetchScalarGridSpec(num...  23.6 us
    all_gather x1, waiting for transfers between devices, local(): start = lax.all_gather(laid, 'rows', axis=0, tiled=True)  16 us
  transfers between devices with their start and end apart: 6, of which 6 were waited for; matrix products, arithmetic and copies ran while one was open for 4% of the time, Pallas kernels for 6%

profile of v1, /device:TPU:0, one launch (start us, length us, event | category | flops | bytes accessed | tf_op | source)
XLA Modules:
  0.0 401.9 jit_solution(2658554412705902682)
XLA Ops:
  6.5 1.2 reshape.132
  8.0 0.8 reshape.133
  8.9 0.7 compare_select_fusion.1
  9.6 1.3 gather_fusion.1
  10.9 0.7 fusion.10
  11.8 2.3 copy.40
  14.1 23.6 %collect_support.1.blocks = bf16[16,512,1024]{2,1,0:T(8,128)(2,1)} custom-call(s32[16]{0:T(128)} %order.7, s32[16,16]{1,0:T(8,128)} %support.1, s32[16]{0:T(128)} %counts.7, bf16[512,32768]{1,0:T(8,128)(2,1)} %dictionary.1), custom_call_target="tpu_custom_call" | custom-call | bytes 50331648 | tf_op jit(solution)/shard_map/collect_support/pallas_call | solution.py:78
  37.7 16.0 %all-gather.4.cloned.1.call-done.codes = bf16[16,8,64,128]{3,2,1,0:T(8,128)(2,1)} async-done(((bf16[1,8,64,128]{3,2,1,0:T(8,128)(2,1)}), bf16[16,8,64,128]{3,2,1,0:T(8,128)(2,1)}) %all-gather.4.cloned.1.call-update) | async-done | bytes 2097168 | tf_op jit(solution)/shard_map/all_gather | solution.py:212
  53.7 20.3 %gradient.3 = f32[80,64,128]{2,1,0:T(8,128)} custom-call(s32[16]{0:T(128)} %order.7, s32[16]{0:T(128)} %counts.7, s32[1]{0:T(128)} %bitcast.own, bf16[16,512,1024]{2,1,0:T(8,128)(2,1)} %collect_support.1.blocks, bf16[16,8,64,128]{3,2,1,0:T(8,128)(2,1)} %all-gather.4.cloned.1.call-done.codes, bf16[1024,512]{1,0:T(8,128)(2,1)} %bitcast.82), custom_call_target="tpu_custom_call" | custom-call | flops 2147483648 | bytes 16777216 | tf_op jit(solution)/shard_map/gradient/pallas_call | solution.py:175
  74.3 0.7 gather_fusion.3
  75.0 0.7 gather_fusion.2
  75.6 0.7 fusion.13
  81.5 0.7 fusion.14
  108.9 0.6 gather_fusion
  109.7 0.4 broadcast_in_dim.30
  110.4 3.3 reshape.134
  113.8 0.8 constant_dynamic-slice_fusion.10
  114.6 1.3 constant_dynamic-slice_fusion.2
  116.4 20.5 %reduce-scatter.4.cloned.1.call-done = f32[5,64,128]{2,1,0:T(8,128)} async-done(((f32[80,64,128]{2,1,0:T(8,128)}), f32[5,64,128]{2,1,0:T(8,128)}) %reduce-scatter.4.cloned.1.call-update) | async-done | bytes 163856 | tf_op jit(solution)/shard_map/reduce_scatter | solution.py:246
  136.8 1.6 fusion.2
  138.5 38.4 %all-gather.6.cloned.1.call-done.codes = bf16[80,64,128]{2,1,0:T(8,128)(2,1)} async-done(((bf16[5,64,128]{2,1,0:T(8,128)(2,1)}), bf16[80,64,128]{2,1,0:T(8,128)(2,1)}) %all-gather.6.cloned.1.call-update) | async-done | bytes 1310736 | tf_op jit(solution)/shard_map/all_gather | solution.py:256
  177.0 20.4 %gradient.4 = f32[80,64,128]{2,1,0:T(8,128)} custom-call(s32[16]{0:T(128)} %order.7, s32[16]{0:T(128)} %counts.7, s32[1]{0:T(128)} %bitcast.own, bf16[16,512,1024]{2,1,0:T(8,128)(2,1)} %collect_support.1.blocks, bf16[80,64,128]{2,1,0:T(8,128)(2,1)} %all-gather.6.cloned.1.call-done.codes, bf16[1024,512]{1,0:T(8,128)(2,1)} %bitcast.83), custom_call_target="tpu_custom_call" | custom-call | flops 2147483648 | bytes 16777216 | tf_op jit(solution)/shard_map/gradient/pallas_call | solution.py:175
  197.4 62.8 %reduce-scatter.6.cloned.1.call-done = f32[5,64,128]{2,1,0:T(8,128)} async-done(((f32[80,64,128]{2,1,0:T(8,128)}), f32[5,64,128]{2,1,0:T(8,128)}) %reduce-scatter.6.cloned.1.call-update) | async-done | bytes 163856 | tf_op jit(solution)/shard_map/reduce_scatter | solution.py:246
  260.2 1.7 add_convert_fusion
  262.0 38.2 %all-gather.8.cloned.1.call-done.codes = bf16[80,64,128]{2,1,0:T(8,128)(2,1)} async-done(((bf16[5,64,128]{2,1,0:T(8,128)(2,1)}), bf16[80,64,128]{2,1,0:T(8,128)(2,1)}) %all-gather.8.cloned.1.call-update) | async-done | bytes 1310736 | tf_op jit(solution)/shard_map/all_gather | solution.py:256
  300.2 20.7 %gradient.5 = (f32[16,8,64,128]{3,2,1,0:T(8,128)}, bf16[8,64,128]{2,1,0:T(8,128)(2,1)}) custom-call(s32[16]{0:T(128)} %order.7, s32[16]{0:T(128)} %counts.7, s32[1]{0:T(128)} %bitcast.own, bf16[16,512,1024]{2,1,0:T(8,128)(2,1)} %collect_support.1.blocks, bf16[80,64,128]{2,1,0:T(8,128)(2,1)} %all-gather.8.cloned.1.call-done.codes, bf16[1024,512]{1,0:T(8,128)(2,1)} %bitcast.84), custom_call_target="tpu_custom_call" | custom-call | flops 2147483648 | bytes 16777216 | tf_op jit(solution)/shard_map/gradient/pallas_call | solution.py:175
  320.9 0.6 copy-done.1
  321.6 0.7 dynamic_slice.47
  324.1 68.5 %reduce-scatter.8.cloned.1.call-done = f32[1,8,64,128]{3,2,1,0:T(8,128)} async-done(((f32[16,8,64,128]{3,2,1,0:T(8,128)}), f32[1,8,64,128]{3,2,1,0:T(8,128)}) %reduce-scatter.8.cloned.1.call-update) | async-done | bytes 262160 | tf_op jit(solution)/shard_map/reduce_scatter | solution.py:246
  392.7 1.1 minimum_subtract_fusion
  393.7 0.3 reshape.148
  394.1 0.9 reshape.149
  (54 shorter events, 2.1 us)
Async XLA Ops:
  6.5 47.1 %all-gather.4.cloned.1.call-start = ((), (), s32[]{:S(2)}) async-start(), calls=%async_computation.3 | async-start | bytes 2228224 | tf_op jit(solution)/shard_map/all_gather | solution.py:212
  8.8 128.0 %reduce-scatter.4.cloned.1.call-start = ((), (), s32[]{:S(2)}) async-start(), calls=%async_computation.4 | async-start | bytes 2785280 | tf_op jit(solution)/shard_map/reduce_scatter | solution.py:246
  53.7 20.6 %copy-start = (s32[16]{0:T(128)S(1)}, s32[16]{0:T(128)}, u32[]{:S(2)}) copy-start(s32[16]{0:T(128)} %order.7) | copy-start | bytes 196
  74.0 34.9 %copy-start.5 = (f32[16,64]{1,0:T(8,128)S(1)}, f32[16,64]{1,0:T(8,128)}, u32[]{:S(2)}) copy-start(f32[16,64]{1,0:T(8,128)} %param.17) | copy-start | bytes 12292
  74.0 36.5 %copy-start.2 = (bf16[16,8,64,128]{3,2,1,0:T(8,128)(2,1)S(1)}, bf16[16,8,64,128]{3,2,1,0:T(8,128)(2,1)}, u32[]{:S(2)}) copy-start(bf16[16,8,64,128]{3,2,1,0:T(8,128)(2,1)} %all-gather.4.cloned.1.call-done.codes) | copy-start | bytes 6291460
  74.0 103.0 %all-gather.6.cloned.1.call-start = ((), (), s32[]{:S(2)}) async-start(), calls=%async_computation.5 | async-start | bytes 1392640 | tf_op jit(solution)/shard_map/all_gather | solution.py:256
  138.5 121.8 %copy-start.3 = (f32[5,64,128]{2,1,0:T(8,128)S(1)}, f32[5,64,128]{2,1,0:T(8,128)}, u32[]{:S(2)}) copy-start(f32[5,64,128]{2,1,0:T(8,128)} %reduce-scatter.4.cloned.1.call-done) | copy-start | bytes 491524
  138.5 121.8 %reduce-scatter.6.cloned.1.call-start = ((), (), s32[]{:S(2)}) async-start(), calls=%async_computation.6 | async-start | bytes 2785280 | tf_op jit(solution)/shard_map/reduce_scatter | solution.py:246
  197.4 102.8 %all-gather.8.cloned.1.call-start = ((), (), s32[]{:S(2)}) async-start(), calls=%async_computation.7 | async-start | bytes 1392640 | tf_op jit(solution)/shard_map/all_gather | solution.py:256
  261.9 130.7 %reduce-scatter.8.cloned.1.call-start = ((), (), s32[]{:S(2)}) async-start(), calls=%async_computation.8 | async-start | bytes 4456448 | tf_op jit(solution)/shard_map/reduce_scatter | solution.py:246
  320.9 0.7 copy-start.1
  320.9 71.8 %copy-start.4 = (bf16[8,64,128]{2,1,0:T(8,128)(2,1)S(1)}, bf16[8,64,128]{2,1,0:T(8,128)(2,1)}, u32[]{:S(2)}) copy-start(bf16[8,64,128]{2,1,0:T(8,128)(2,1)} %get-tuple-element.9) | copy-start | bytes 393220
Sparse Core Ops, SparseCore 0:
  9.5 44.0 all-gather.3
  74.1 62.6 reduce-scatter.3
  139.1 37.8 all-gather.5
  197.5 62.6 reduce-scatter.5
  262.4 37.7 all-gather.7
  321.1 71.5 reduce-scatter.7

commit v2 on v1

v2 whole, which is shorter than its diff:
```python
import functools

import jax
import jax.numpy as jnp
from jax import lax
from jax.experimental import pallas as pl
from jax.experimental.pallas import tpu as pltpu
from jax.sharding import PartitionSpec as P

BLOCK = 64
SLOTS = 16
PATCHES = 64
ITERS = 3
MEAN_LIVE = 10
LANES = 2 * BLOCK
SLOT_PAIRS = SLOTS // 2
VMEM_LIMIT = 56 * 1024 * 1024


def momentum_list():
    values = []
    tvalue = 1.0
    for turn in range(ITERS):
        tnext = (1.0 + (1.0 + 4.0 * tvalue * tvalue) ** 0.5) / 2.0
        values.append((tvalue - 1.0) / tnext)
        tvalue = tnext
    return values


def swap_halves(value):
    return jnp.concatenate([value[:, BLOCK:], value[:, :BLOCK]], axis=1)


def upper_half(shape):
    return lax.broadcasted_iota(jnp.int32, shape, 1) >= BLOCK


def support_kernel(order, support, counts, dictionary, out, held, sems):
    step = pl.program_id(0)

    def each_copy(index, act):
        group = order[index]
        half = index % 2
        for slot in range(SLOTS):

            @pl.when(slot < counts[group])
            def _():
                start = pl.multiple_of((support[group, slot] // 2) * LANES, LANES)
                act(pltpu.make_async_copy(dictionary.at[:, pl.ds(start, LANES)], held.at[half, slot], sems.at[half, slot]))

    @pl.when(step == 0)
    def _():
        each_copy(step, lambda copy: copy.start())

    @pl.when(step + 1 < pl.num_programs(0))
    def _():
        each_copy(step + 1, lambda copy: copy.start())

    each_copy(step, lambda copy: copy.wait())
    group = order[step]
    live = counts[group]
    half = step % 2
    upper = upper_half(held.shape[2:])
    for pair in range(SLOT_PAIRS):
        parts = []
        for side in range(2):
            slot = 2 * pair + side
            block = held[half, slot]
            swap = (support[group, slot] % 2) != side
            block = jnp.where(swap, swap_halves(block), block)
            parts.append(jnp.where(slot < live, block, jnp.zeros_like(block)))
        out[0, :, pair * LANES : (pair + 1) * LANES] = jnp.where(upper, parts[1], parts[0])


def collect_support(order, support, counts, dictionary):
    groups = order.shape[0]
    rows = dictionary.shape[0]
    return pl.pallas_call(
        support_kernel,
        grid_spec=pltpu.PrefetchScalarGridSpec(
            num_scalar_prefetch=3,
            grid=(groups,),
            in_specs=[pl.BlockSpec(memory_space=pl.ANY)],
            out_specs=pl.BlockSpec((1, rows, SLOTS * BLOCK), lambda j, *_: (j, 0, 0)),
            scratch_shapes=[
                pltpu.VMEM((2, SLOTS, rows, LANES), dictionary.dtype),
                pltpu.SemaphoreType.DMA((2, SLOTS)),
            ],
        ),
        out_shape=jax.ShapeDtypeStruct((groups, rows, SLOTS * BLOCK), dictionary.dtype),
        compiler_params=pltpu.CompilerParams(vmem_limit_bytes=VMEM_LIMIT),
        cost_estimate=pl.CostEstimate(
            flops=0, transcendentals=0, bytes_accessed=3 * groups * rows * SLOTS * BLOCK * 2
        ),
        name="collect_support",
    )(order, support, counts, dictionary)


def relative_slot(index, me, devices):
    apart = index ^ me
    return (apart % 2) * (devices // 2) + ((apart // 2) % 2) * (devices // 4) + apart // 4


def gradient_kernel(
    packed_in, packed_out, shards, order, counts, own, blocks, near, far, targets, keep, send, extra, codes, lhs, offset_ref
):
    step = pl.program_id(0)
    me = own[0]
    live = counts[order[step]]
    half_in = near.shape[0]
    shard_in = 2 * half_in // shards
    half_out = keep.shape[0]
    shard_out = 2 * half_out // shards

    @pl.when(step == 0)
    def _():
        offset_ref[0] = 0
        codes[:half_in] = near[...]
        codes[half_in:] = far[...]

    offset = offset_ref[0]
    first = offset // 2
    odd = (offset % 2) == 1
    upper = upper_half((PATCHES, LANES))
    side = upper.astype(jnp.int32)

    def place(pair, shard):
        holder = pair // shard
        return relative_slot(holder, me, shards) * shard + (pair - holder * shard)

    def packed(parts):
        turned = [swap_halves(part) for part in parts]
        for pair in range(SLOT_PAIRS + 1):
            straight = parts[min(pair, SLOT_PAIRS - 1)]
            before = turned[max(pair - 1, 0)]
            after = turned[min(pair, SLOT_PAIRS - 1)]
            value = jnp.where(odd, jnp.where(upper, after, before), straight)
            entry = 2 * (first + pair) + side
            yield first + pair, value, (entry >= offset) & (entry < offset + live)

    if packed_in:
        last = 2 * half_in - 1
        loads = [codes[place(jnp.minimum(first + pair, last), shard_in)] for pair in range(SLOT_PAIRS + 1)]
        swapped = [swap_halves(value) for value in loads]
    values = []
    for pair in range(SLOT_PAIRS):
        if packed_in:
            value = jnp.where(odd, jnp.where(upper, swapped[pair + 1], swapped[pair]), loads[pair])
        else:
            value = codes[place(step * SLOT_PAIRS + pair, shard_in)]
        value = jnp.where(2 * pair + side < live, value, jnp.zeros_like(value))
        lhs[:, pair * LANES : (pair + 1) * LANES] = value
        values.append(value)
    if packed_out and not packed_in:
        for pair, value, mine in packed(values):
            nearby = pair - me * shard_out

            @pl.when((nearby >= 0) & (nearby < shard_out))
            def _(value=value, mine=mine, nearby=nearby):
                extra[nearby] = jnp.where(mine, value, extra[nearby])

    if not packed_out:

        @pl.when(step == me)
        def _():
            for pair in range(SLOT_PAIRS):
                extra[pair] = values[pair]

    matrix = blocks[0]
    residual = lax.dot_general(lhs[...], matrix, (((1,), (1,)), ((), ())), preferred_element_type=jnp.float32)
    residual = (residual - targets[...].astype(jnp.float32)).astype(jnp.bfloat16)
    gradient = jnp.dot(residual, matrix, preferred_element_type=jnp.float32)
    parts = [gradient[:, pair * LANES : (pair + 1) * LANES] for pair in range(SLOT_PAIRS)]
    if packed_out:
        final = 2 * half_out - 1
        for pair, value, mine in packed(parts):
            spot = place(jnp.minimum(pair, final), shard_out)

            @pl.when(spot < half_out)
            def _(value=value, mine=mine, spot=spot):
                keep[spot] = jnp.where(mine, value, keep[spot])

            @pl.when(spot >= half_out)
            def _(value=value, mine=mine, spot=spot):
                send[spot - half_out] = jnp.where(mine, value.astype(send.dtype), send[spot - half_out])

    else:
        spot = place(step * SLOT_PAIRS, shard_out)

        @pl.when(spot < half_out)
        def _():
            for pair in range(SLOT_PAIRS):
                keep[spot + pair] = parts[pair]

        @pl.when(spot >= half_out)
        def _():
            for pair in range(SLOT_PAIRS):
                send[spot - half_out + pair] = parts[pair].astype(send.dtype)

    offset_ref[0] = offset + live


def gradient_call(order, counts, own, blocks, near, far, targets, packed_in, packed_out, shards, packed_pairs):
    groups, rows, width = blocks.shape
    half_in = near.shape[0]
    pairs = packed_pairs if packed_out else groups * SLOT_PAIRS
    half_out = pairs // 2
    extra = packed_pairs // shards if packed_out else SLOT_PAIRS
    whole = lambda j, *_: (0, 0, 0)
    shapes = [
        jax.ShapeDtypeStruct((half_out, PATCHES, LANES), jnp.float32),
        jax.ShapeDtypeStruct((half_out, PATCHES, LANES), jnp.bfloat16),
        jax.ShapeDtypeStruct((extra, PATCHES, LANES), jnp.bfloat16),
    ]
    return pl.pallas_call(
        functools.partial(gradient_kernel, packed_in, packed_out, shards),
        grid_spec=pltpu.PrefetchScalarGridSpec(
            num_scalar_prefetch=3,
            grid=(groups,),
            in_specs=[
                pl.BlockSpec((1, rows, width), lambda j, *_: (j, 0, 0)),
                pl.BlockSpec((half_in, PATCHES, LANES), whole),
                pl.BlockSpec((half_in, PATCHES, LANES), whole),
                pl.BlockSpec((PATCHES, rows), lambda j, order, *_: (order[j], 0)),
            ],
            out_specs=[pl.BlockSpec(shape.shape, whole) for shape in shapes],
            scratch_shapes=[
                pltpu.VMEM((2 * half_in, PATCHES, LANES), jnp.bfloat16),
                pltpu.VMEM((PATCHES, width), jnp.bfloat16),
                pltpu.SMEM((1,), jnp.int32),
            ],
        ),
        out_shape=shapes,
        compiler_params=pltpu.CompilerParams(vmem_limit_bytes=VMEM_LIMIT),
        cost_estimate=pl.CostEstimate(
            flops=4 * groups * rows * width * PATCHES, transcendentals=0, bytes_accessed=groups * rows * width * 2
        ),
        name="gradient",
    )(order, counts, own, blocks, near, far, targets)


def exchange(value, distance):
    devices = lax.axis_size("rows")
    return lax.ppermute(value, "rows", [(i, i ^ distance) for i in range(devices)])


def gather_shards(own):
    devices = lax.axis_size("rows")
    parts = [own] + [exchange(own, 4 * k) for k in range(1, devices // 4)]
    quarter = jnp.concatenate(parts, axis=0)
    near = jnp.concatenate([quarter, exchange(quarter, 2)], axis=0)
    return near, exchange(near, 1)


def reduce_shards(keep, send):
    devices = lax.axis_size("rows")
    half = keep + exchange(send, 1).astype(jnp.float32)
    middle = half.shape[0] // 2
    quarter = half[:middle] + exchange(half[middle:].astype(jnp.bfloat16), 2).astype(jnp.float32)
    size = quarter.shape[0] // (devices // 4)
    sent = quarter.astype(jnp.bfloat16)
    total = quarter[:size]
    for k in range(1, devices // 4):
        total = total + exchange(sent[k * size : (k + 1) * size], 4 * k).astype(jnp.float32)
    return total


def shrink(value, thresh):
    return value - jnp.clip(value, -thresh, thresh)


def local(dictionary, patches, initial_codes, support, counts, group_order, penalty):
    groups = group_order.shape[0]
    position = lax.axis_index("rows")
    devices = lax.axis_size("rows")
    momenta = momentum_list()
    owned_entries = MEAN_LIVE * groups // devices
    owned_pairs = owned_entries // 2
    pairs = owned_pairs * devices

    laid = initial_codes.reshape(SLOT_PAIRS, 2, PATCHES, BLOCK).transpose(0, 2, 1, 3)
    near, far = gather_shards(laid.reshape(SLOT_PAIRS, PATCHES, LANES))

    own = position.astype(jnp.int32).reshape(1)
    blocks = collect_support(group_order, support, counts, dictionary)
    targets = patches.T

    half_penalty = 0.5 * penalty
    ends = jnp.cumsum(jnp.take(counts, group_order))
    entry = position * owned_entries + jnp.arange(owned_entries)
    holder = jnp.sum((entry[:, None] >= ends[None, :]).astype(jnp.int32), axis=1)
    thresh = jnp.take(half_penalty, jnp.take(group_order, holder), axis=0)
    thresh = jnp.repeat(thresh.reshape(owned_pairs, 2, PATCHES).transpose(0, 2, 1), BLOCK, axis=2)
    own_thresh = lax.dynamic_index_in_dim(half_penalty, group_order[position], 0, False)[None, :, None]

    def run(near, far, packed_in, packed_out):
        return gradient_call(
            group_order, counts, own, blocks, near, far, targets, packed_in, packed_out, devices, pairs
        )

    point = previous = None
    for turn in range(ITERS - 1):
        keep, send, extra = run(near, far, turn > 0, True)
        if turn == 0:
            point = previous = extra.astype(jnp.float32)
        current = shrink(point - 0.5 * reduce_shards(keep, send), thresh)
        point = current + momenta[turn] * (current - previous)
        previous = current
        near, far = gather_shards(point.astype(jnp.bfloat16))
    keep, send, sent = run(near, far, True, False)
    result = shrink(sent.astype(jnp.float32) - 0.5 * reduce_shards(keep, send), own_thresh)
    result = result.reshape(SLOT_PAIRS, PATCHES, 2, BLOCK).transpose(0, 2, 1, 3)
    return result.reshape(1, SLOTS, PATCHES * BLOCK)


def solution(mesh):
    in_specs = (
        P("rows", None),
        P("rows", "groups"),
        P(("groups", "rows"), None, None),
        P("groups", None),
        P("groups"),
        P("groups"),
        P("groups", None),
    )
    out_specs = P(("groups", "rows"), None, None)
    return jax.shard_map(local, mesh=mesh, in_specs=in_specs, out_specs=out_specs, check_vma=False)
```

time: 404 us -> 257 us (0.64)
  waiting for transfers between devices: 245 us -> 106 us
  between operations: 47.5 us -> 2.4 us
  starting transfers between devices: 0.21 us -> 35.7 us
  Pallas kernels: 85 us -> 93 us
  local copies, waits for them, and re-layouts: 18 us -> 11 us
    reduce_scatter x3 -> x0, waiting for transfers between devices: 152 us -> none  [scatter(): return lax.psum_scatter(value, 'rows', scatter_dimension=0, tiled=True)]
    ppermute x0 -> x30, waiting for transfers between devices: none -> 106 us  [exchange(): lax.ppermute(value, 'rows', [(i, i ^ distance) for i in range(devices)])]
    all_gather x3 -> x0, waiting for transfers between devices: 92.6 us -> none  [the longest x2 76.6 us: local(): lax.all_gather(point.astype(jnp.bfloat16), 'rows', axis=0, tiled=True)]
    ppermute x0 -> x30, starting transfers between devices: none -> 35.7 us  [exchange(): lax.ppermute(value, 'rows', [(i, i ^ distance) for i in range(devices)])]
    pallas_call x3, Pallas kernels: 61.4 us -> 70.4 us  [gradient_call(): pl.pallas_call(functools.partial(gradient_kernel, packed_in, packed_out,...]
    add x0 -> x3, other arithmetic: none -> 4.86 us  [reduce_shards(): half = keep + exchange(send, 1).astype(jnp.float32)]
  transfers between devices with their start and end apart: 6 -> 30, of which waited for: 6 -> 26; matrix products, arithmetic and copies ran while one was open for 4% -> 2% of each run, Pallas kernels for 6% -> 9%
where the time goes in v2:
time: 257 us; the launch traced here: 255 us
  waiting for transfers between devices  106 us (41%)
  Pallas kernels  93 us (36%)
  starting transfers between devices  35.7 us (14%)
  local copies, waits for them, and re-layouts  11 us (4%)
  other arithmetic  6.36 us (2%)
    ppermute x30, waiting for transfers between devices, exchange(): lax.ppermute(value, 'rows', [(i, i ^ distance) for i in range(devices)])  106 us
    pallas_call x3, Pallas kernels, gradient_call(): pl.pallas_call(functools.partial(gradient_kernel, packed_in, packed_out,...  70.4 us
    ppermute x30, starting transfers between devices, exchange(): lax.ppermute(value, 'rows', [(i, i ^ distance) for i in range(devices)])  35.7 us
    pallas_call x1, Pallas kernels, collect_support(): pl.pallas_call(support_kernel, grid_spec=pltpu.PrefetchScalarGridSpec(num...  22.6 us
  transfers between devices with their start and end apart: 30, of which 26 were waited for; matrix products, arithmetic and copies ran while one was open for 2% of the time, Pallas kernels for 9%

profile of v2, /device:TPU:0, one launch (start us, length us, event | category | flops | bytes accessed | tf_op | source)
XLA Modules:
  0.0 254.7 jit_solution(11412670306972909934)
XLA Ops:
  1.6 5.1 %collective-permute-start.2 = (bf16[8,64,128]{2,1,0:T(8,128)(2,1)S(1)}, bf16[8,64,128]{2,1,0:T(8,128)(2,1)S(1)}, u32[]{:S(2)}, u32[]{:S(2)}) collective-permute-start(bf16[8,64,128]{2,1,0:T(8,128)(2,1)S(1)} %reshape.124), channel_id=1, source_target_pairs={{0,12},{1,13},{2,14},{3,15},{4,8},{5,9},{6,10},{7,11},{8,4},{9,5},... | collective-permute-start | bytes 393224 | tf_op jit(solution)/shard_map/ppermute | solution.py:244
  7.4 3.8 %collective-permute-done.2 = bf16[8,64,128]{2,1,0:T(8,128)(2,1)S(1)} collective-permute-done((bf16[8,64,128]{2,1,0:T(8,128)(2,1)S(1)}, bf16[8,64,128]{2,1,0:T(8,128)(2,1)S(1)}, u32[]{:S(2)}, u32[]{:S(2)}) %collective-permute-start.2) | collective-permute-done | bytes 131104 | tf_op jit(solution)/shard_map/ppermute | solution.py:244
  11.2 6.6 %collective-permute-done.1 = bf16[8,64,128]{2,1,0:T(8,128)(2,1)S(1)} collective-permute-done((bf16[8,64,128]{2,1,0:T(8,128)(2,1)S(1)}, bf16[8,64,128]{2,1,0:T(8,128)(2,1)S(1)}, u32[]{:S(2)}, u32[]{:S(2)}) %collective-permute-start.1) | collective-permute-done | bytes 131104 | tf_op jit(solution)/shard_map/ppermute | solution.py:244
  19.6 11.4 %collective-permute-done.3 = bf16[32,64,128]{2,1,0:T(8,128)(2,1)S(1)} collective-permute-done((bf16[32,64,128]{2,1,0:T(8,128)(2,1)S(1)}, bf16[32,64,128]{2,1,0:T(8,128)(2,1)S(1)}, u32[]{:S(2)}, u32[]{:S(2)}) %collective-permute-start.3) | collective-permute-done | bytes 524320 | tf_op jit(solution)/shard_map/ppermute | solution.py:244
  33.4 22.6 %collect_support.1.blocks = bf16[16,512,1024]{2,1,0:T(8,128)(2,1)} custom-call(s32[16]{0:T(128)} %order.7, s32[16,16]{1,0:T(8,128)} %support.1, s32[16]{0:T(128)} %counts.7, bf16[512,32768]{1,0:T(8,128)(2,1)} %dictionary.1), custom_call_target="tpu_custom_call" | custom-call | bytes 50331648 | tf_op jit(solution)/shard_map/collect_support/pallas_call | solution.py:78
  57.2 26.9 %gradient.3 = (f32[40,64,128]{2,1,0:T(8,128)}, bf16[40,64,128]{2,1,0:T(8,128)(2,1)}, bf16[5,64,128]{2,1,0:T(8,128)(2,1)}) custom-call(s32[16]{0:T(128)} %order.7, s32[16]{0:T(128)} %counts.7, s32[1]{0:T(128)} %bitcast.own, bf16[16,512,1024]{2,1,0:T(8,128)(2,1)} %collect_support.1.blocks, bf16[64,64,128]{2,1,0:T(8,128)(2,1)} %copy-done.4, ...), custom_call_target="tpu_custom_call" | custom-call | flops 2147483648 | bytes 16777216 | tf_op jit(solution)/shard_map/gradient/pallas_call | solution.py:215
  90.2 7.9 %collective-permute-done.6 = bf16[20,64,128]{2,1,0:T(8,128)(2,1)S(1)} collective-permute-done((bf16[20,64,128]{2,1,0:T(8,128)(2,1)S(1)}, bf16[20,64,128]{2,1,0:T(8,128)(2,1)S(1)}, u32[]{:S(2)}, u32[]{:S(2)}) %collective-permute-start.6) | collective-permute-done | bytes 327712 | tf_op jit(solution)/shard_map/ppermute | solution.py:244
  98.3 2.3 collective-permute-start.9
  103.2 2.5 collective-permute-done.9
  105.7 3.3 %collective-permute-done.8 = bf16[5,64,128]{2,1,0:T(8,128)(2,1)S(1)} collective-permute-done((bf16[5,64,128]{2,1,0:T(8,128)(2,1)S(1)}, bf16[5,64,128]{2,1,0:T(8,128)(2,1)S(1)}, u32[]{:S(2)}, u32[]{:S(2)}) %collective-permute-start.8) | collective-permute-done | bytes 81952 | tf_op jit(solution)/shard_map/ppermute | solution.py:244
  109.1 2.0 collective-permute-start.12
  111.1 2.4 collective-permute-start.10
  113.5 2.7 %collective-permute-done.12 = bf16[5,64,128]{2,1,0:T(8,128)(2,1)S(1)} collective-permute-done((bf16[5,64,128]{2,1,0:T(8,128)(2,1)S(1)}, bf16[5,64,128]{2,1,0:T(8,128)(2,1)S(1)}, u32[]{:S(2)}, u32[]{:S(2)}) %collective-permute-start.12) | collective-permute-done | bytes 81952 | tf_op jit(solution)/shard_map/ppermute | solution.py:244
  119.8 7.7 %collective-permute-done.13 = bf16[20,64,128]{2,1,0:T(8,128)(2,1)S(1)} collective-permute-done((bf16[20,64,128]{2,1,0:T(8,128)(2,1)S(1)}, bf16[20,64,128]{2,1,0:T(8,128)(2,1)S(1)}, u32[]{:S(2)}, u32[]{:S(2)}) %collective-permute-start.13) | collective-permute-done | bytes 327712 | tf_op jit(solution)/shard_map/ppermute | solution.py:244
  127.6 2.1 collective-permute-done.14.far
  130.5 21.8 %gradient.4 = (f32[40,64,128]{2,1,0:T(8,128)}, bf16[40,64,128]{2,1,0:T(8,128)(2,1)}, bf16[5,64,128]{2,1,0:T(8,128)(2,1)}) custom-call(s32[16]{0:T(128)} %order.7, s32[16]{0:T(128)} %counts.7, s32[1]{0:T(128)} %bitcast.own, bf16[16,512,1024]{2,1,0:T(8,128)(2,1)} %collect_support.1.blocks, bf16[40,64,128]{2,1,0:T(8,128)(2,1)} %copy-done.8, ...), custom_call_target="tpu_custom_call" | custom-call | flops 2147483648 | bytes 16777216 | tf_op jit(solution)/shard_map/gradient/pallas_call | solution.py:215
  152.5 2.2 collective-permute-done.15
  157.8 8.2 %collective-permute-done.16 = bf16[20,64,128]{2,1,0:T(8,128)(2,1)S(1)} collective-permute-done((bf16[20,64,128]{2,1,0:T(8,128)(2,1)S(1)}, bf16[20,64,128]{2,1,0:T(8,128)(2,1)S(1)}, u32[]{:S(2)}, u32[]{:S(2)}) %collective-permute-start.16) | collective-permute-done | bytes 327712 | tf_op jit(solution)/shard_map/ppermute | solution.py:244
  166.3 2.0 collective-permute-start.19
  169.8 2.1 collective-permute-done.17
  173.4 3.2 %collective-permute-done.18 = bf16[5,64,128]{2,1,0:T(8,128)(2,1)S(1)} collective-permute-done((bf16[5,64,128]{2,1,0:T(8,128)(2,1)S(1)}, bf16[5,64,128]{2,1,0:T(8,128)(2,1)S(1)}, u32[]{:S(2)}, u32[]{:S(2)}) %collective-permute-start.18) | collective-permute-done | bytes 81952 | tf_op jit(solution)/shard_map/ppermute | solution.py:244
  176.8 1.9 collective-permute-start.22
  178.7 2.5 collective-permute-start.20
  181.2 2.4 collective-permute-done.22
  183.6 2.0 collective-permute-done.21
  187.3 7.6 %collective-permute-done.23 = bf16[20,64,128]{2,1,0:T(8,128)(2,1)S(1)} collective-permute-done((bf16[20,64,128]{2,1,0:T(8,128)(2,1)S(1)}, bf16[20,64,128]{2,1,0:T(8,128)(2,1)S(1)}, u32[]{:S(2)}, u32[]{:S(2)}) %collective-permute-start.23) | collective-permute-done | bytes 327712 | tf_op jit(solution)/shard_map/ppermute | solution.py:244
  195.1 2.1 collective-permute-done.24.far
  198.0 21.7 %gradient.5 = (f32[64,64,128]{2,1,0:T(8,128)}, bf16[64,64,128]{2,1,0:T(8,128)(2,1)}, bf16[8,64,128]{2,1,0:T(8,128)(2,1)}) custom-call(s32[16]{0:T(128)} %order.7, s32[16]{0:T(128)} %counts.7, s32[1]{0:T(128)} %bitcast.own, bf16[16,512,1024]{2,1,0:T(8,128)(2,1)} %collect_support.1.blocks, bf16[40,64,128]{2,1,0:T(8,128)(2,1)} %copy-done.7, ...), custom_call_target="tpu_custom_call" | custom-call | flops 2147483648 | bytes 16777216 | tf_op jit(solution)/shard_map/gradient/pallas_call | solution.py:215
  219.9 2.7 %collective-permute-done.25 = bf16[64,64,128]{2,1,0:T(8,128)(2,1)S(1)} collective-permute-done((bf16[64,64,128]{2,1,0:T(8,128)(2,1)}, bf16[64,64,128]{2,1,0:T(8,128)(2,1)S(1)}, u32[]{:S(2)}, u32[]{:S(2)}) %collective-permute-start.25) | collective-permute-done | bytes 1048608 | tf_op jit(solution)/shard_map/ppermute | solution.py:244
  222.6 1.9 convert_add_fusion
  226.3 12.5 %collective-permute-done.26 = bf16[32,64,128]{2,1,0:T(8,128)(2,1)S(1)} collective-permute-done((bf16[32,64,128]{2,1,0:T(8,128)(2,1)S(1)}, bf16[32,64,128]{2,1,0:T(8,128)(2,1)S(1)}, u32[]{:S(2)}, u32[]{:S(2)}) %collective-permute-start.26) | collective-permute-done | bytes 524320 | tf_op jit(solution)/shard_map/ppermute | solution.py:244
  247.7 5.6 %collective-permute-done.28 = bf16[8,64,128]{2,1,0:T(8,128)(2,1)S(1)} collective-permute-done((bf16[8,64,128]{2,1,0:T(8,128)(2,1)S(1)}, bf16[8,64,128]{2,1,0:T(8,128)(2,1)S(1)}, u32[]{:S(2)}, u32[]{:S(2)}) %collective-permute-start.28) | collective-permute-done | bytes 131104 | tf_op jit(solution)/shard_map/ppermute | solution.py:244
  (124 shorter events, 40.4 us)
Async XLA Ops:
  1.6 9.5 %collective-permute-start.2 = (bf16[8,64,128]{2,1,0:T(8,128)(2,1)S(1)}, bf16[8,64,128]{2,1,0:T(8,128)(2,1)S(1)}, u32[]{:S(2)}, u32[]{:S(2)}) collective-permute-start(bf16[8,64,128]{2,1,0:T(8,128)(2,1)S(1)} %reshape.124), channel_id=1, source_target_pairs={{0,12},{1,13},{2,14},{3,15},{4,8},{5,9},{6,10},{7,11},{8,4},{9,5},... | collective-permute-start | bytes 393224 | tf_op jit(solution)/shard_map/ppermute | solution.py:244
  6.7 11.1 %collective-permute-start.1 = (bf16[8,64,128]{2,1,0:T(8,128)(2,1)S(1)}, bf16[8,64,128]{2,1,0:T(8,128)(2,1)S(1)}, u32[]{:S(2)}, u32[]{:S(2)}) collective-permute-start(bf16[8,64,128]{2,1,0:T(8,128)(2,1)S(1)} %reshape.124), channel_id=1, source_target_pairs={{0,8},{1,9},{2,10},{3,11},{4,12},{5,13},{6,14},{7,15},{8,0},{9,1},... | collective-permute-start | bytes 393224 | tf_op jit(solution)/shard_map/ppermute | solution.py:244
  6.7 11.1 %collective-permute-start = (bf16[8,64,128]{2,1,0:T(8,128)(2,1)S(1)}, bf16[8,64,128]{2,1,0:T(8,128)(2,1)S(1)}, u32[]{:S(2)}, u32[]{:S(2)}) collective-permute-start(bf16[8,64,128]{2,1,0:T(8,128)(2,1)S(1)} %reshape.124), channel_id=1, source_target_pairs={{0,4},{1,5},{2,6},{3,7},{4,0},{5,1},{6,2},{7,3},{8,12},{9,13},{10,... | collective-permute-start | bytes 393224 | tf_op jit(solution)/shard_map/ppermute | solution.py:244
  17.9 13.0 %collective-permute-start.3 = (bf16[32,64,128]{2,1,0:T(8,128)(2,1)S(1)}, bf16[32,64,128]{2,1,0:T(8,128)(2,1)S(1)}, u32[]{:S(2)}, u32[]{:S(2)}) collective-permute-start(bf16[32,64,128]{2,1,0:T(8,128)(2,1)S(1)} %pad_maximum_fusion), channel_id=1, source_target_pairs={{0,2},{1,3},{2,0},{3,1},{4,6},{5,7},{6,4},{7,5},{8,10},{9,11},{10,... | collective-permute-start | bytes 1572872 | tf_op jit(solution)/shard_map/ppermute | solution.py:244
  31.0 25.2 %collective-permute-start.4 = (bf16[64,64,128]{2,1,0:T(8,128)(2,1)S(1)}, bf16[64,64,128]{2,1,0:T(8,128)(2,1)S(1)}, u32[]{:S(2)}, u32[]{:S(2)}) collective-permute-start(bf16[64,64,128]{2,1,0:T(8,128)(2,1)S(1)} %constant_dynamic-update-slice_fusion.near), channel_id=1, source_target_pairs={{0,1},{1,0},{2,3},{3,2},{4,5},{5,4},{6,7},{7,6},{8,9},{9,8},{10,11... | collective-permute-start | bytes 3145736 | tf_op jit(solution)/shard_map/ppermute | solution.py:244
  57.2 28.2 %copy-start.13 = (f32[16,64]{1,0:T(8,128)S(1)}, f32[16,64]{1,0:T(8,128)}, u32[]{:S(2)}) copy-start(f32[16,64]{1,0:T(8,128)} %param.13) | copy-start | bytes 12292
  84.1 2.4 collective-permute-start.5
  88.0 10.1 %collective-permute-start.6 = (bf16[20,64,128]{2,1,0:T(8,128)(2,1)S(1)}, bf16[20,64,128]{2,1,0:T(8,128)(2,1)S(1)}, u32[]{:S(2)}, u32[]{:S(2)}) collective-permute-start(bf16[20,64,128]{2,1,0:T(8,128)(2,1)S(1)} %slice.144), channel_id=1, source_target_pairs={{0,2},{1,3},{2,0},{3,1},{4,6},{5,7},{6,4},{7,5},{8,10},{9,11},{10,... | collective-permute-start | bytes 983048 | tf_op jit(solution)/shard_map/ppermute | solution.py:244
  98.2 4.9 %collective-permute-start.7 = (bf16[5,64,128]{2,1,0:T(8,128)(2,1)S(1)}, bf16[5,64,128]{2,1,0:T(8,128)(2,1)S(1)}, u32[]{:S(2)}, u32[]{:S(2)}) collective-permute-start(bf16[5,64,128]{2,1,0:T(8,128)(2,1)S(1)} %get-tuple-element.39), channel_id=1, source_target_pairs={{0,4},{1,5},{2,6},{3,7},{4,0},{5,1},{6,2},{7,3},{8,12},{9,13},{10,... | collective-permute-start | bytes 245768 | tf_op jit(solution)/shard_map/ppermute | solution.py:244
  98.3 7.3 %collective-permute-start.9 = (bf16[5,64,128]{2,1,0:T(8,128)(2,1)S(1)}, bf16[5,64,128]{2,1,0:T(8,128)(2,1)S(1)}, u32[]{:S(2)}, u32[]{:S(2)}) collective-permute-start(bf16[5,64,128]{2,1,0:T(8,128)(2,1)S(1)} %get-tuple-element.40), channel_id=1, source_target_pairs={{0,12},{1,13},{2,14},{3,15},{4,8},{5,9},{6,10},{7,11},{8,4},{9,5},... | collective-permute-start | bytes 245768 | tf_op jit(solution)/shard_map/ppermute | solution.py:244
  100.7 8.3 %collective-permute-start.8 = (bf16[5,64,128]{2,1,0:T(8,128)(2,1)S(1)}, bf16[5,64,128]{2,1,0:T(8,128)(2,1)S(1)}, u32[]{:S(2)}, u32[]{:S(2)}) collective-permute-start(bf16[5,64,128]{2,1,0:T(8,128)(2,1)S(1)} %get-tuple-element.41), channel_id=1, source_target_pairs={{0,8},{1,9},{2,10},{3,11},{4,12},{5,13},{6,14},{7,15},{8,0},{9,1},... | collective-permute-start | bytes 245768 | tf_op jit(solution)/shard_map/ppermute | solution.py:244
  109.1 7.1 %collective-permute-start.12 = (bf16[5,64,128]{2,1,0:T(8,128)(2,1)S(1)}, bf16[5,64,128]{2,1,0:T(8,128)(2,1)S(1)}, u32[]{:S(2)}, u32[]{:S(2)}) collective-permute-start(bf16[5,64,128]{2,1,0:T(8,128)(2,1)S(1)} %get-tuple-element.30), channel_id=1, source_target_pairs={{0,12},{1,13},{2,14},{3,15},{4,8},{5,9},{6,10},{7,11},{8,4},{9,5},... | collective-permute-start | bytes 245768 | tf_op jit(solution)/shard_map/ppermute | solution.py:244
  111.1 7.0 %collective-permute-start.11 = (bf16[5,64,128]{2,1,0:T(8,128)(2,1)S(1)}, bf16[5,64,128]{2,1,0:T(8,128)(2,1)S(1)}, u32[]{:S(2)}, u32[]{:S(2)}) collective-permute-start(bf16[5,64,128]{2,1,0:T(8,128)(2,1)S(1)} %get-tuple-element.30), channel_id=1, source_target_pairs={{0,8},{1,9},{2,10},{3,11},{4,12},{5,13},{6,14},{7,15},{8,0},{9,1},... | collective-permute-start | bytes 245768 | tf_op jit(solution)/shard_map/ppermute | solution.py:244
  111.1 7.0 %collective-permute-start.10 = (bf16[5,64,128]{2,1,0:T(8,128)(2,1)S(1)}, bf16[5,64,128]{2,1,0:T(8,128)(2,1)S(1)}, u32[]{:S(2)}, u32[]{:S(2)}) collective-permute-start(bf16[5,64,128]{2,1,0:T(8,128)(2,1)S(1)} %get-tuple-element.30), channel_id=1, source_target_pairs={{0,4},{1,5},{2,6},{3,7},{4,0},{5,1},{6,2},{7,3},{8,12},{9,13},{10,... | collective-permute-start | bytes 245768 | tf_op jit(solution)/shard_map/ppermute | solution.py:244
  118.1 9.3 %collective-permute-start.13 = (bf16[20,64,128]{2,1,0:T(8,128)(2,1)S(1)}, bf16[20,64,128]{2,1,0:T(8,128)(2,1)S(1)}, u32[]{:S(2)}, u32[]{:S(2)}) collective-permute-start(bf16[20,64,128]{2,1,0:T(8,128)(2,1)S(1)} %pad_maximum_fusion.1), channel_id=1, source_target_pairs={{0,2},{1,3},{2,0},{3,1},{4,6},{5,7},{6,4},{7,5},{8,10},{9,11},{10,... | collective-permute-start | bytes 983048 | tf_op jit(solution)/shard_map/ppermute | solution.py:244
  127.5 2.2 collective-permute-start.14
  152.4 2.3 collective-permute-start.15
  156.2 9.8 %collective-permute-start.16 = (bf16[20,64,128]{2,1,0:T(8,128)(2,1)S(1)}, bf16[20,64,128]{2,1,0:T(8,128)(2,1)S(1)}, u32[]{:S(2)}, u32[]{:S(2)}) collective-permute-start(bf16[20,64,128]{2,1,0:T(8,128)(2,1)S(1)} %slice.143), channel_id=1, source_target_pairs={{0,2},{1,3},{2,0},{3,1},{4,6},{5,7},{6,4},{7,5},{8,10},{9,11},{10,... | collective-permute-start | bytes 983048 | tf_op jit(solution)/shard_map/ppermute | solution.py:244
  166.2 5.7 %collective-permute-start.17 = (bf16[5,64,128]{2,1,0:T(8,128)(2,1)S(1)}, bf16[5,64,128]{2,1,0:T(8,128)(2,1)S(1)}, u32[]{:S(2)}, u32[]{:S(2)}) collective-permute-start(bf16[5,64,128]{2,1,0:T(8,128)(2,1)S(1)} %get-tuple-element.36), channel_id=1, source_target_pairs={{0,4},{1,5},{2,6},{3,7},{4,0},{5,1},{6,2},{7,3},{8,12},{9,13},{10,... | collective-permute-start | bytes 245768 | tf_op jit(solution)/shard_map/ppermute | solution.py:244
  166.3 7.1 %collective-permute-start.19 = (bf16[5,64,128]{2,1,0:T(8,128)(2,1)S(1)}, bf16[5,64,128]{2,1,0:T(8,128)(2,1)S(1)}, u32[]{:S(2)}, u32[]{:S(2)}) collective-permute-start(bf16[5,64,128]{2,1,0:T(8,128)(2,1)S(1)} %get-tuple-element.37), channel_id=1, source_target_pairs={{0,12},{1,13},{2,14},{3,15},{4,8},{5,9},{6,10},{7,11},{8,4},{9,5},... | collective-permute-start | bytes 245768 | tf_op jit(solution)/shard_map/ppermute | solution.py:244
  168.3 8.3 %collective-permute-start.18 = (bf16[5,64,128]{2,1,0:T(8,128)(2,1)S(1)}, bf16[5,64,128]{2,1,0:T(8,128)(2,1)S(1)}, u32[]{:S(2)}, u32[]{:S(2)}) collective-permute-start(bf16[5,64,128]{2,1,0:T(8,128)(2,1)S(1)} %get-tuple-element.38), channel_id=1, source_target_pairs={{0,8},{1,9},{2,10},{3,11},{4,12},{5,13},{6,14},{7,15},{8,0},{9,1},... | collective-permute-start | bytes 245768 | tf_op jit(solution)/shard_map/ppermute | solution.py:244
  176.8 6.9 %collective-permute-start.22 = (bf16[5,64,128]{2,1,0:T(8,128)(2,1)S(1)}, bf16[5,64,128]{2,1,0:T(8,128)(2,1)S(1)}, u32[]{:S(2)}, u32[]{:S(2)}) collective-permute-start(bf16[5,64,128]{2,1,0:T(8,128)(2,1)S(1)} %get-tuple-element.26), channel_id=1, source_target_pairs={{0,12},{1,13},{2,14},{3,15},{4,8},{5,9},{6,10},{7,11},{8,4},{9,5},... | collective-permute-start | bytes 245768 | tf_op jit(solution)/shard_map/ppermute | solution.py:244
  178.7 7.0 %collective-permute-start.21 = (bf16[5,64,128]{2,1,0:T(8,128)(2,1)S(1)}, bf16[5,64,128]{2,1,0:T(8,128)(2,1)S(1)}, u32[]{:S(2)}, u32[]{:S(2)}) collective-permute-start(bf16[5,64,128]{2,1,0:T(8,128)(2,1)S(1)} %get-tuple-element.26), channel_id=1, source_target_pairs={{0,8},{1,9},{2,10},{3,11},{4,12},{5,13},{6,14},{7,15},{8,0},{9,1},... | collective-permute-start | bytes 245768 | tf_op jit(solution)/shard_map/ppermute | solution.py:244
  178.7 7.0 %collective-permute-start.20 = (bf16[5,64,128]{2,1,0:T(8,128)(2,1)S(1)}, bf16[5,64,128]{2,1,0:T(8,128)(2,1)S(1)}, u32[]{:S(2)}, u32[]{:S(2)}) collective-permute-start(bf16[5,64,128]{2,1,0:T(8,128)(2,1)S(1)} %get-tuple-element.26), channel_id=1, source_target_pairs={{0,4},{1,5},{2,6},{3,7},{4,0},{5,1},{6,2},{7,3},{8,12},{9,13},{10,... | collective-permute-start | bytes 245768 | tf_op jit(solution)/shard_map/ppermute | solution.py:244
  185.7 9.2 %collective-permute-start.23 = (bf16[20,64,128]{2,1,0:T(8,128)(2,1)S(1)}, bf16[20,64,128]{2,1,0:T(8,128)(2,1)S(1)}, u32[]{:S(2)}, u32[]{:S(2)}) collective-permute-start(bf16[20,64,128]{2,1,0:T(8,128)(2,1)S(1)} %pad_maximum_fusion.2), channel_id=1, source_target_pairs={{0,2},{1,3},{2,0},{3,1},{4,6},{5,7},{6,4},{7,5},{8,10},{9,11},{10,... | collective-permute-start | bytes 983048 | tf_op jit(solution)/shard_map/ppermute | solution.py:244
  195.0 2.2 collective-permute-start.24
  219.8 2.9 %collective-permute-start.25 = (bf16[64,64,128]{2,1,0:T(8,128)(2,1)}, bf16[64,64,128]{2,1,0:T(8,128)(2,1)S(1)}, u32[]{:S(2)}, u32[]{:S(2)}) collective-permute-start(bf16[64,64,128]{2,1,0:T(8,128)(2,1)} %get-tuple-element.20), channel_id=1, source_target_pairs={{0,1},{1,0},{2,3},{3,2},{4,5},{5,4},{6,7},{7,6},{8,9},{9,8},{10,11... | collective-permute-start | bytes 3145736 | tf_op jit(solution)/shard_map/ppermute | solution.py:244
  224.7 28.7 %copy-start.12 = (bf16[8,64,128]{2,1,0:T(8,128)(2,1)S(1)}, bf16[8,64,128]{2,1,0:T(8,128)(2,1)}, u32[]{:S(2)}) copy-start(bf16[8,64,128]{2,1,0:T(8,128)(2,1)} %get-tuple-element.18) | copy-start | bytes 393220
  224.7 14.0 %collective-permute-start.26 = (bf16[32,64,128]{2,1,0:T(8,128)(2,1)S(1)}, bf16[32,64,128]{2,1,0:T(8,128)(2,1)S(1)}, u32[]{:S(2)}, u32[]{:S(2)}) collective-permute-start(bf16[32,64,128]{2,1,0:T(8,128)(2,1)S(1)} %slice.142), channel_id=1, source_target_pairs={{0,2},{1,3},{2,0},{3,1},{4,6},{5,7},{6,4},{7,5},{8,10},{9,11},{10,... | collective-permute-start | bytes 1572872 | tf_op jit(solution)/shard_map/ppermute | solution.py:244
  238.9 7.2 %collective-permute-start.27 = (bf16[8,64,128]{2,1,0:T(8,128)(2,1)S(1)}, bf16[8,64,128]{2,1,0:T(8,128)(2,1)S(1)}, u32[]{:S(2)}, u32[]{:S(2)}) collective-permute-start(bf16[8,64,128]{2,1,0:T(8,128)(2,1)S(1)} %get-tuple-element.33), channel_id=1, source_target_pairs={{0,4},{1,5},{2,6},{3,7},{4,0},{5,1},{6,2},{7,3},{8,12},{9,13},{10,... | collective-permute-start | bytes 393224 | tf_op jit(solution)/shard_map/ppermute | solution.py:244
  239.0 8.7 %collective-permute-start.29 = (bf16[8,64,128]{2,1,0:T(8,128)(2,1)S(1)}, bf16[8,64,128]{2,1,0:T(8,128)(2,1)S(1)}, u32[]{:S(2)}, u32[]{:S(2)}) collective-permute-start(bf16[8,64,128]{2,1,0:T(8,128)(2,1)S(1)} %get-tuple-element.34), channel_id=1, source_target_pairs={{0,12},{1,13},{2,14},{3,15},{4,8},{5,9},{6,10},{7,11},{8,4},{9,5},... | collective-permute-start | bytes 393224 | tf_op jit(solution)/shard_map/ppermute | solution.py:244
  240.9 12.4 %collective-permute-start.28 = (bf16[8,64,128]{2,1,0:T(8,128)(2,1)S(1)}, bf16[8,64,128]{2,1,0:T(8,128)(2,1)S(1)}, u32[]{:S(2)}, u32[]{:S(2)}) collective-permute-start(bf16[8,64,128]{2,1,0:T(8,128)(2,1)S(1)} %get-tuple-element.35), channel_id=1, source_target_pairs={{0,8},{1,9},{2,10},{3,11},{4,12},{5,13},{6,14},{7,15},{8,0},{9,1},... | collective-permute-start | bytes 393224 | tf_op jit(solution)/shard_map/ppermute | solution.py:244
  (12 other events, 106.2 us)

commit v3 on v0

v3 whole, which is shorter than its diff:
```python
import functools
import math

import jax
import jax.numpy as jnp
from jax import lax
from jax.experimental import pallas as pl
from jax.experimental.pallas import tpu as pltpu
from jax.sharding import PartitionSpec as P

BLOCK = 64
SLOTS = 16
PATCHES = 64
ITERS = 3
MEAN_LIVE = 10
LEAST_LIVE = 4
LANES = 2 * BLOCK
SLOT_PAIRS = SLOTS // 2
SPARE = SLOT_PAIRS + 2
ROW_TILE = 16
PIECE = 4
MATRIX_UNIT = 256
VMEM_MARGIN = 3 * 1024 * 1024


def momentum_list():
    values = []
    tvalue = 1.0
    for turn in range(ITERS):
        tnext = (1.0 + (1.0 + 4.0 * tvalue * tvalue) ** 0.5) / 2.0
        values.append((tvalue - 1.0) / tnext)
        tvalue = tnext
    return values


def swap_halves(value):
    return jnp.concatenate([value[:, BLOCK:], value[:, :BLOCK]], axis=1)


def upper_half(shape):
    return lax.broadcasted_iota(jnp.int32, shape, 1) >= BLOCK


def group_at(index, seq, order, counts):
    position = seq[index]
    group = order[position]
    return position, group, counts[group]


def support_kernel(chain, seq, order, support, counts, dictionary, out, held, picks, ids, sems, out_sems):
    entries, rows, _ = held.shape
    pairs = entries // 2
    seats = order.shape[0] // 2

    def fetch(entry, block):
        start = pl.multiple_of((block // 2) * LANES, LANES)
        return pltpu.make_async_copy(dictionary.at[:, pl.ds(start, LANES)], held.at[entry], sems.at[entry])

    def start_group(index, offset):
        _, group, live = group_at(index, seq, order, counts)

        def start_slot(slot, carry):
            block = support[group, slot]
            ids[offset + slot] = block
            fetch(offset + slot, block).start()
            return carry

        lax.fori_loop(0, live, start_slot, 0)
        return offset + live

    used = lax.fori_loop(chain * seats, (chain + 1) * seats, start_group, jnp.int32(0))

    def clear(entry, carry):
        ids[entry] = 0
        held[entry] = jnp.zeros((rows, LANES), held.dtype)
        return carry

    lax.fori_loop(used, entries, clear, 0)
    shape = (2 * LANES, LANES)
    source = lax.broadcasted_iota(jnp.int32, shape, 0)
    target = lax.broadcasted_iota(jnp.int32, shape, 1)
    for choice in range(4):
        wanted = jnp.where(target < BLOCK, (choice % 2) * BLOCK + target, LANES + (choice // 2) * BLOCK + target - BLOCK)
        picks[choice] = (source == wanted).astype(jnp.float32).astype(jnp.bfloat16)

    def store(pair):
        return pltpu.make_async_copy(held.at[2 * pair], out.at[pair], out_sems.at[pair])

    def pack(step, carry):
        for entry in range(4):
            index = 4 * step + entry

            @pl.when(index < used)
            def _(index=index):
                fetch(index, ids[index]).wait()

        packed = []
        for pair in (2 * step, 2 * step + 1):
            choice = ids[2 * pair] % 2 + 2 * (ids[2 * pair + 1] % 2)
            both = jnp.concatenate([held[2 * pair], held[2 * pair + 1]], axis=1)
            packed.append(jnp.dot(both, picks[choice], preferred_element_type=jnp.float32).astype(jnp.bfloat16))
        for pair, value in zip((2 * step, 2 * step + 1), packed):
            held[2 * pair] = value
            store(pair).start()
        return carry

    lax.fori_loop(0, pairs // 2, pack, 0)

    def drain(pair, carry):
        store(pair).wait()
        return carry

    lax.fori_loop(0, pairs, drain, 0)


def collect_support(chain, seq, order, support, counts, dictionary, pairs):
    rows = dictionary.shape[0]
    entries = 2 * pairs
    return pl.pallas_call(
        functools.partial(support_kernel, chain),
        grid_spec=pltpu.PrefetchScalarGridSpec(
            num_scalar_prefetch=4,
            grid=(),
            in_specs=[pl.BlockSpec(memory_space=pltpu.HBM)],
            out_specs=pl.BlockSpec(memory_space=pltpu.HBM),
            scratch_shapes=[
                pltpu.VMEM((entries, rows, LANES), dictionary.dtype),
                pltpu.VMEM((4, 2 * LANES, LANES), jnp.bfloat16),
                pltpu.SMEM((entries,), jnp.int32),
                pltpu.SemaphoreType.DMA((entries,)),
                pltpu.SemaphoreType.DMA((pairs,)),
            ],
        ),
        out_shape=jax.ShapeDtypeStruct((pairs, rows, LANES), dictionary.dtype),
        compiler_params=pltpu.CompilerParams(vmem_limit_bytes=entries * rows * LANES * 2 + VMEM_MARGIN),
        cost_estimate=pl.CostEstimate(flops=0, transcendentals=0, bytes_accessed=6 * pairs * rows * LANES * 2),
        name="collect_support",
    )(seq, order, support, counts, dictionary)


def reversed_bits(index, size):
    result = 0
    while size > 1:
        result = 2 * result + index % 2
        index //= 2
        size //= 2
    return result


def gradient_kernel(chain, mode, shards, seq, order, counts, own, blocks, near, far, targets, *refs):
    refs = list(refs)
    take = lambda: refs.pop(0)
    if mode == "first":
        thresh = take()
    if mode == "final":
        other = take()
    if mode == "raw":
        total, sent = take(), take()
    else:
        keep, send = take(), take()
        if mode == "first":
            start_out, thresh_out = take(), take()
        if mode == "final":
            sent = take()
    held, codes = take(), take()
    if mode != "raw":
        total = take()
    if mode == "first":
        starts, limits = take(), take()
    offsets, sems = refs

    seats = order.shape[0] // 2
    pairs = blocks.shape[0]
    places = pairs + SPARE
    pieces = pairs // PIECE
    base = places if mode == "final" else 0
    me = own[0]

    def load(index):
        span = pl.ds(index * PIECE, PIECE)
        return pltpu.make_async_copy(blocks.at[span], held.at[span], sems.at[index])

    for index in range(pieces):
        load(index).start()
    held[pairs:] = jnp.zeros((SPARE,) + held.shape[1:], held.dtype)

    def shard_span(slot, size):
        return pl.ds(pl.multiple_of((reversed_bits(slot, shards) ^ me) * size, ROW_TILE), size)

    size_in = 2 * near.shape[0] // shards
    for slot in range(shards):
        source = near if slot < shards // 2 else far
        begin = slot % (shards // 2) * size_in
        codes[shard_span(slot, size_in), :] = source[begin : begin + size_in, :]

    for which in range(2):

        def seat(index, offset):
            position, _, live = group_at(index, seq, order, counts)
            offsets[position] = offset
            return offset + live

        lax.fori_loop(which * seats, (which + 1) * seats, seat, jnp.int32(which * 2 * places))

    upper = upper_half((PATCHES, LANES))
    side = upper.astype(jnp.int32)

    def tile(pair):
        return pl.ds(pl.multiple_of(pair * PATCHES, PATCHES), PATCHES)

    def shifted(parts, count, odd, ahead):
        turned = [swap_halves(part) for part in parts]
        last = len(parts) - 1
        moved = []
        for pair in range(count):
            low, high = (pair, pair + 1) if ahead else (pair - 1, pair)
            low, high = min(max(low, 0), last), min(max(high, 0), last)
            value = jnp.where(upper, turned[high], turned[low])
            moved.append(jnp.where(odd, value, parts[min(pair, last)]))
        return moved

    def read_codes(position, offset, live, count):
        first = offset // 2
        if mode == "first":
            parts = [codes[tile(position * SLOT_PAIRS + pair), :] for pair in range(min(count, SLOT_PAIRS))]
            parts = shifted(parts, count, offset % 2 == 1, False)
        else:
            parts = [codes[tile(first + pair), :] for pair in range(count)]
        masked = []
        for pair, part in enumerate(parts):
            entry = 2 * (first + pair) + side
            mine = (entry >= offset) & (entry < offset + live)
            masked.append(jnp.where(mine, part, jnp.zeros_like(part)))
        return masked

    def write_packed(ref, parts, offset, begin=0):
        first = offset // 2
        for pair, part in enumerate(parts):
            if pair == 0:
                part = jnp.where(upper | (offset % 2 == 0), part, ref[tile(begin + first), :])
            ref[tile(begin + first + pair), :] = part

    def one_group(position, group, offset, live, count):
        first = offset // 2
        parts = read_codes(position, offset, live, count)
        if mode == "first":
            write_packed(starts, parts, offset)
            write_packed(limits, [thresh[group]] * count, offset)
        matrix = jnp.concatenate([held[first + pair] for pair in range(count)], axis=1)
        point = jnp.concatenate(parts, axis=1)
        residual = lax.dot_general(point, matrix, (((1,), (1,)), ((), ())), preferred_element_type=jnp.float32)
        target = targets[tile(group), :].astype(jnp.float32)
        residual = (residual - target).astype(jnp.bfloat16)
        gradient = jnp.dot(residual, matrix, preferred_element_type=jnp.float32)
        write_packed(total, [gradient[:, pair * LANES : (pair + 1) * LANES] for pair in range(count)], offset, base)

    def wait_piece(index, carry):
        load(index).wait()
        return carry

    def two_groups(step, waited):
        picks = []
        chunks = 1
        for index in (2 * step, 2 * step + 1):
            position, group, live = group_at(chain * seats + index, seq, order, counts)
            offset = offsets[position] - chain * 2 * places
            picks.append((position, group, offset, live))
            chunks = jnp.maximum(chunks, (live + offset % 2 + 3) // 4)
        reach = jnp.minimum(picks[1][2] // 2 + 2 * chunks - 1, pairs - 1)
        needed = jnp.maximum(reach // PIECE + 1, waited)
        lax.fori_loop(waited, needed, wait_piece, 0)
        for count in range(1, SLOTS // 4 + 2):

            @pl.when(chunks == count)
            def _(count=count):
                for pick in picks:
                    one_group(*pick, 2 * count)

        return needed

    waited = lax.fori_loop(0, seats // 2, two_groups, jnp.int32(0))
    lax.fori_loop(waited, pieces, wait_piece, 0)

    if mode in ("first", "shards"):
        size = 2 * keep.shape[0] // shards
        for slot in range(shards):
            begin = slot % (shards // 2) * size
            value = total[shard_span(slot, size), :]
            if slot < shards // 2:
                keep[begin : begin + size, :] = value
            else:
                send[begin : begin + size, :] = value.astype(send.dtype)
    if mode == "first":
        size = start_out.shape[0]
        span = pl.ds(pl.multiple_of(me * size, ROW_TILE), size)
        start_out[...] = starts[span, :]
        thresh_out[...] = limits[span, :]
    if mode in ("raw", "final"):
        offset = offsets[me] - chain * 2 * places
        mine = (offset >= 0) & (offset < 2 * places)

        @pl.when(mine)
        def _():
            parts = read_codes(me, offset, counts[order[me]], SLOT_PAIRS + 1)
            for pair, part in enumerate(shifted(parts, SLOT_PAIRS, offset % 2 == 1, True)):
                sent[pair] = part

        @pl.when(jnp.logical_not(mine))
        def _():
            sent[...] = jnp.zeros(sent.shape, sent.dtype)

    if mode == "final":
        total[: places * PATCHES, :] = other[...]
        for slot in range(shards):
            position = reversed_bits(slot, shards) ^ me
            offset = offsets[position]
            live = counts[order[position]]
            parts = [total[tile(offset // 2 + pair), :] for pair in range(SLOT_PAIRS + 1)]
            begin = slot % (shards // 2) * SLOT_PAIRS * PATCHES
            for pair, part in enumerate(shifted(parts, SLOT_PAIRS, offset % 2 == 1, True)):
                value = jnp.where(2 * pair + side < live, part, 0.0)
                rows = slice(begin + pair * PATCHES, begin + (pair + 1) * PATCHES)
                if slot < shards // 2:
                    keep[rows, :] = value
                else:
                    send[rows, :] = value.astype(send.dtype)


def gradient_call(chain, mode, shards, scalars, blocks, near, far, targets, extra=()):
    pairs, rows, _ = blocks.shape
    places = pairs + SPARE
    groups = scalars[1].shape[0]
    half_in = near.shape[0]
    single, double = jnp.bfloat16, jnp.float32
    packed = (places * PATCHES, LANES)
    half_out = (groups * SLOT_PAIRS if mode == "final" else pairs) * PATCHES // 2
    shard = (2 * half_out // shards, LANES)
    slots = (SLOT_PAIRS, PATCHES, LANES)
    if mode == "raw":
        outs = [(packed, double), (slots, single)]
    else:
        outs = [((half_out, LANES), double), ((half_out, LANES), single)]
        if mode == "first":
            outs += [(shard, single), (shard, double)]
        if mode == "final":
            outs += [(slots, single)]
    codes = groups * SLOT_PAIRS * PATCHES if mode == "first" else packed[0]
    scratch = [((places, rows, LANES), single), ((codes, LANES), single)]
    if mode == "final":
        scratch += [((2 * packed[0], LANES), double)]
    elif mode != "raw":
        scratch += [(packed, double)]
    if mode == "first":
        scratch += [(packed, single), (packed, double)]
    room = sum(math.prod(shape) * jnp.dtype(kind).itemsize for shape, kind in scratch)
    return pl.pallas_call(
        functools.partial(gradient_kernel, chain, mode, shards),
        grid_spec=pltpu.PrefetchScalarGridSpec(
            num_scalar_prefetch=4,
            grid=(),
            in_specs=[pl.BlockSpec(memory_space=pltpu.HBM)]
            + [pl.BlockSpec(memory_space=pltpu.VMEM)] * (3 + len(extra)),
            out_specs=[pl.BlockSpec(memory_space=pltpu.VMEM)] * len(outs),
            scratch_shapes=[pltpu.VMEM(shape, kind) for shape, kind in scratch]
            + [pltpu.SMEM((groups,), jnp.int32), pltpu.SemaphoreType.DMA((pairs // PIECE,))],
        ),
        out_shape=[jax.ShapeDtypeStruct(shape, kind) for shape, kind in outs],
        compiler_params=pltpu.CompilerParams(vmem_limit_bytes=room + VMEM_MARGIN),
        cost_estimate=pl.CostEstimate(
            flops=4 * pairs * rows * LANES * MATRIX_UNIT, transcendentals=0, bytes_accessed=pairs * rows * LANES * 2
        ),
        name="gradient",
    )(*scalars, blocks, near, far, targets, *extra)


def exchange(value, distance):
    devices = lax.axis_size("rows")
    return lax.ppermute(value, "rows", [(i, i ^ distance) for i in range(devices)])


def double_up(value, distance):
    return jnp.concatenate([value, exchange(value, distance)], axis=0)


def gather_shards(own, beside=()):
    made = []
    value = own
    distance = lax.axis_size("rows") // 2
    while distance > 1:
        if beside and distance == 2:
            value, array = lax.optimization_barrier((value, beside[0]))
            made.append(array)
        value = double_up(value, distance)
        distance //= 2
    if beside:
        value, array = lax.optimization_barrier((value, beside[1]))
        made.append(array)
    return value, exchange(value, 1), made


def reduce_shards(keep, send):
    devices = lax.axis_size("rows")
    total = keep + exchange(send, 1).astype(jnp.float32)
    distance = 2
    while distance < devices:
        middle = total.shape[0] // 2
        total = total[:middle] + exchange(total[middle:].astype(jnp.bfloat16), distance).astype(jnp.float32)
        distance *= 2
    return total


def chain_seats(live):
    groups = live.shape[0]
    index = jnp.arange(groups)
    ahead = (live[None, :] > live[:, None]) | ((live[None, :] == live[:, None]) & (index[None, :] < index[:, None]))
    rank = jnp.sum(ahead.astype(jnp.int32), axis=1)
    spot = ((rank + 1) // 2 % 2) * (groups // 2) + rank // 2
    return jnp.sum(jnp.where(spot[:, None] == index[None, :], index[:, None], 0), axis=0).astype(jnp.int32)


def shrink(value, thresh):
    return value - jnp.clip(value, -thresh, thresh)


def local(dictionary, patches, initial_codes, support, counts, group_order, penalty):
    groups = group_order.shape[0]
    position = lax.axis_index("rows")
    devices = lax.axis_size("rows")
    momenta = momentum_list()
    most_entries = MEAN_LIVE * groups // 2 + (SLOTS - LEAST_LIVE) // 2
    shard_rows = -(-most_entries * PATCHES // (2 * devices * ROW_TILE)) * ROW_TILE
    pairs = shard_rows * devices // PATCHES

    laid = initial_codes.reshape(SLOT_PAIRS, 2, PATCHES, BLOCK).transpose(0, 2, 1, 3)
    laid = laid.reshape(SLOT_PAIRS * PATCHES, LANES)
    seq = chain_seats(jnp.take(counts, group_order))
    blocks = [collect_support(chain, seq, group_order, support, counts, dictionary, pairs) for chain in range(2)]
    near, far, blocks = gather_shards(laid, blocks)

    scalars = (seq, group_order, counts, position.astype(jnp.int32).reshape(1))
    targets = patches.T
    half_penalty = 0.5 * penalty
    thresh_tiles = jnp.broadcast_to(half_penalty[:, :, None], (groups, PATCHES, LANES))
    own_thresh = lax.dynamic_index_in_dim(half_penalty, group_order[position], 0, False)[None, :, None]

    chains = [dict(near=near, far=far) for _ in range(2)]
    for turn in range(ITERS - 1):
        for chain, state in enumerate(chains):
            mode, extra = ("first", (thresh_tiles,)) if turn == 0 else ("shards", ())
            keep, send, *more = gradient_call(
                chain, mode, devices, scalars, blocks[chain], state["near"], state["far"], targets, extra
            )
            if turn == 0:
                state["point"] = state["previous"] = more[0].astype(jnp.float32)
                state["thresh"] = more[1]
            current = shrink(state["point"] - 0.5 * reduce_shards(keep, send), state["thresh"])
            state["point"] = current + momenta[turn] * (current - state["previous"])
            state["previous"] = current
            state["near"], state["far"], _ = gather_shards(state["point"].astype(jnp.bfloat16))
    raw, sent = gradient_call(
        0, "raw", devices, scalars, blocks[0], chains[0]["near"], chains[0]["far"], targets
    )
    keep, send, more = gradient_call(
        1, "final", devices, scalars, blocks[1], chains[1]["near"], chains[1]["far"], targets, (raw,)
    )
    gradient = reduce_shards(keep, send).reshape(SLOT_PAIRS, PATCHES, LANES)
    sent = sent.astype(jnp.float32) + more.astype(jnp.float32)
    result = shrink(sent - 0.5 * gradient, own_thresh)
    result = result.reshape(SLOT_PAIRS, PATCHES, 2, BLOCK).transpose(0, 2, 1, 3)
    return result.reshape(1, SLOTS, PATCHES * BLOCK)


def solution(mesh):
    in_specs = (
        P("rows", None),
        P("rows", "groups"),
        P(("groups", "rows"), None, None),
        P("groups", None),
        P("groups"),
        P("groups"),
        P("groups", None),
    )
    out_specs = P(("groups", "rows"), None, None)
    return jax.shard_map(local, mesh=mesh, in_specs=in_specs, out_specs=out_specs, check_vma=False)
```

time: 526 us -> 227 us (0.43)
  waiting for transfers between devices: 298 us -> 78.4 us
  local copies, waits for them, and re-layouts: 134 us -> 24.9 us
  Pallas kernels: 0 us -> 80.4 us
  matrix products: 67.9 us -> 0 us
  starting transfers between devices: 0.39 us -> 37.5 us
  between operations: 13.6 us -> 2.52 us
  other arithmetic: 9.8 us -> 3.25 us
    reduce_scatter x3 -> x0, waiting for transfers between devices: 216 us -> none  [local(): lax.psum_scatter(partial_term(jnp.int32(0), lax.axis_size('rows') * (owne...]
    all_gather x3 -> x0, waiting for transfers between devices: 81.4 us -> none  [the longest x2 81.4 us: local(): lax.all_gather(point_loc.astype(jnp.bfloat16), 'rows', axis=0, tiled=True)]
    pallas_call x0 -> x8, Pallas kernels: none -> 80.4 us  [the longest x2 42.2 us: collect_support(): pl.pallas_call(functools.partial(support_kernel, chain), grid_spec=pltpu....]
    ppermute x0 -> x40, waiting for transfers between devices: none -> 78.4 us  [exchange(): lax.ppermute(value, 'rows', [(i, i ^ distance) for i in range(devices)])]
    dot_general x3 -> x0, matrix products: 67.9 us -> none  [group_terms(): jnp.einsum('pgn,pgsa->gsna', residual, dict_blocks, preferred_element_typ...]
    reshape x6 -> x5, local copies, waits for them, and re-layouts: 44.6 us -> 2.85 us  [the longest x2 1.49 us: local(): initial_codes.reshape(SLOT_PAIRS, 2, PATCHES, BLOCK).transpose(0, 2, 1, 3)]
    ppermute x0 -> x40, starting transfers between devices: none -> 37.5 us  [exchange(): lax.ppermute(value, 'rows', [(i, i ^ distance) for i in range(devices)])]
    transpose x3 -> x1, local copies, waits for them, and re-layouts: 27.7 us -> 0.04 us  [local(): result = result.reshape(SLOT_PAIRS, PATCHES, 2, BLOCK).transpose(0, 2, 1, 3)]
  transfers between devices with their start and end apart: 6 -> 40, of which waited for: 5 -> 29; matrix products, arithmetic and copies ran while one was open for 12% -> 3% of each run, Pallas kernels for 0% -> 29%
where the time goes in v3:
time: 227 us
  Pallas kernels  80.4 us (35%)
  waiting for transfers between devices  78.4 us (35%)
  starting transfers between devices  37.5 us (17%)
  local copies, waits for them, and re-layouts  24.9 us (11%)
  other arithmetic  3.25 us (1%)
  between operations  2.52 us (1%)
    ppermute x40, waiting for transfers between devices, exchange(): lax.ppermute(value, 'rows', [(i, i ^ distance) for i in range(devices)])  78.4 us
    pallas_call x2, Pallas kernels, collect_support(): pl.pallas_call(functools.partial(support_kernel, chain), grid_spec=pltpu....  42.2 us
    pallas_call x6, Pallas kernels, gradient_call(): pl.pallas_call(functools.partial(gradient_kernel, chain, mode, shards), g...  38.2 us
    ppermute x40, starting transfers between devices, exchange(): lax.ppermute(value, 'rows', [(i, i ^ distance) for i in range(devices)])  37.5 us
    unnamed x23, local copies, waits for them, and re-layouts  19.7 us
  transfers between devices with their start and end apart: 40, of which 29 were waited for; matrix products, arithmetic and copies ran while one was open for 3% of the time, Pallas kernels for 29%

profile of v3, /device:TPU:0, one launch (start us, length us, event | category | flops | bytes accessed | tf_op | source)
XLA Modules:
  0.0 227.0 jit_solution(10719877498310778926)
XLA Ops:
  1.7 4.1 %collective-permute-start = (bf16[512,128]{1,0:T(8,128)(2,1)S(1)}, bf16[512,128]{1,0:T(8,128)(2,1)S(1)}, u32[]{:S(2)}, u32[]{:S(2)}) collective-permute-start(bf16[512,128]{1,0:T(8,128)(2,1)S(1)} %reshape.88), channel_id=1, source_target_pairs={{0,8},{1,9},{2,10},{3,11},{4,12},{5,13},{6,14},{7,15},{8,0},{9,1},... | collective-permute-start | bytes 393224 | tf_op jit(solution)/shard_map/ppermute | solution.py:378
  8.6 3.5 %collective-permute-done = bf16[512,128]{1,0:T(8,128)(2,1)S(1)} collective-permute-done((bf16[512,128]{1,0:T(8,128)(2,1)S(1)}, bf16[512,128]{1,0:T(8,128)(2,1)S(1)}, u32[]{:S(2)}, u32[]{:S(2)}) %collective-permute-start) | collective-permute-done | bytes 131104 | tf_op jit(solution)/shard_map/ppermute | solution.py:378
  13.0 10.5 %copy-done.1 = bf16[512,32768]{1,0:T(8,128)(2,1)S(1)} copy-done((bf16[512,32768]{1,0:T(8,128)(2,1)S(1)}, bf16[512,32768]{1,0:T(8,128)(2,1)}, u32[]{:S(2)}) %copy-start.1) | copy-done | bytes 33554456
  23.6 21.1 %collect_support.2.blocks = bf16[44,512,128]{2,1,0:T(8,128)(2,1)S(1)} custom-call(s32[16]{0:T(128)S(1)} %select_reduce_fusion.seq, s32[16]{0:T(128)S(1)} %copy-done.7, s32[16,16]{1,0:T(8,128)S(1)} %copy-done.6, s32[16]{0:T(128)S(1)} %copy-done, bf16[512,32768]{1,0:T(8,128)(2,1)S(1)} %copy-done.1), custom_call_target="tpu_custom_call" | custom-call | bytes 34603008 | tf_op jit(solution)/shard_map/collect_support/pallas_call | solution.py:119
  44.7 2.5 %copy-done.2 = bf16[44,512,128]{2,1,0:T(8,128)(2,1)} copy-done((bf16[44,512,128]{2,1,0:T(8,128)(2,1)}, bf16[44,512,128]{2,1,0:T(8,128)(2,1)S(1)}, u32[]{:S(2)}) %copy-start.2) | copy-done | bytes 5767192
  48.8 21.1 %collect_support.3.blocks = bf16[44,512,128]{2,1,0:T(8,128)(2,1)S(1)} custom-call(s32[16]{0:T(128)S(1)} %select_reduce_fusion.seq, s32[16]{0:T(128)S(1)} %copy-done.7, s32[16,16]{1,0:T(8,128)S(1)} %copy-done.6, s32[16]{0:T(128)S(1)} %copy-done, bf16[512,32768]{1,0:T(8,128)(2,1)S(1)} %copy-done.1), custom_call_target="tpu_custom_call" | custom-call | bytes 34603008 | tf_op jit(solution)/shard_map/collect_support/pallas_call | solution.py:119
  69.9 2.5 %copy-done.4 = bf16[44,512,128]{2,1,0:T(8,128)(2,1)} copy-done((bf16[44,512,128]{2,1,0:T(8,128)(2,1)}, bf16[44,512,128]{2,1,0:T(8,128)(2,1)S(1)}, u32[]{:S(2)}) %copy-start.4) | copy-done | bytes 5767192
  75.4 2.6 %copy-done.3 = bf16[44,512,128]{2,1,0:T(8,128)(2,1)S(1)} copy-done((bf16[44,512,128]{2,1,0:T(8,128)(2,1)S(1)}, bf16[44,512,128]{2,1,0:T(8,128)(2,1)}, u32[]{:S(2)}) %copy-start.3) | copy-done | bytes 5767192
  78.0 6.3 %gradient.6 = (f32[1408,128]{1,0:T(8,128)S(1)}, bf16[1408,128]{1,0:T(8,128)(2,1)S(1)}, bf16[176,128]{1,0:T(8,128)(2,1)S(1)}, f32[176,128]{1,0:T(8,128)S(1)}) custom-call(s32[16]{0:T(128)S(1)} %select_reduce_fusion.seq, s32[16]{0:T(128)S(1)} %copy-done.7, s32[16]{0:T(128)S(1)} %copy-done, s32[1]{0:T(128)} %bitcast.own, bf16[44,512,128]{2,1,0:T(8,128)(2,1)S(1)} %copy-done.3, ...), custom_call_target="tpu_custom_call" | custom-call | flops 2952790016 | bytes 5767168 | tf_op jit(solution)/shard_map/gradient/pallas_call | solution.py:356
  84.5 6.3 %gradient.9 = (f32[1408,128]{1,0:T(8,128)S(1)}, bf16[1408,128]{1,0:T(8,128)(2,1)S(1)}, bf16[176,128]{1,0:T(8,128)(2,1)S(1)}, f32[176,128]{1,0:T(8,128)S(1)}) custom-call(s32[16]{0:T(128)S(1)} %select_reduce_fusion.seq, s32[16]{0:T(128)S(1)} %copy-done.7, s32[16]{0:T(128)S(1)} %copy-done, s32[1]{0:T(128)} %bitcast.own, bf16[44,512,128]{2,1,0:T(8,128)(2,1)S(1)} %copy-done.5, ...), custom_call_target="tpu_custom_call" | custom-call | flops 2952790016 | bytes 5767168 | tf_op jit(solution)/shard_map/gradient/pallas_call | solution.py:356
  93.7 5.2 %collective-permute-done.5 = bf16[704,128]{1,0:T(8,128)(2,1)S(1)} collective-permute-done((bf16[704,128]{1,0:T(8,128)(2,1)S(1)}, bf16[704,128]{1,0:T(8,128)(2,1)S(1)}, u32[]{:S(2)}, u32[]{:S(2)}) %collective-permute-start.5) | collective-permute-done | bytes 180256 | tf_op jit(solution)/shard_map/ppermute | solution.py:378
  103.5 3.4 %collective-permute-start.7 = (bf16[176,128]{1,0:T(8,128)(2,1)S(1)}, bf16[176,128]{1,0:T(8,128)(2,1)S(1)}, u32[]{:S(2)}, u32[]{:S(2)}) collective-permute-start(bf16[176,128]{1,0:T(8,128)(2,1)S(1)} %slice.245), channel_id=1, source_target_pairs={{0,8},{1,9},{2,10},{3,11},{4,12},{5,13},{6,14},{7,15},{8,0},{9,1},... | collective-permute-start | bytes 135176 | tf_op jit(solution)/shard_map/ppermute | solution.py:378
  107.1 3.0 %collective-permute-start.23 = (bf16[176,128]{1,0:T(8,128)(2,1)S(1)}, bf16[176,128]{1,0:T(8,128)(2,1)S(1)}, u32[]{:S(2)}, u32[]{:S(2)}) collective-permute-start(bf16[176,128]{1,0:T(8,128)(2,1)S(1)} %slice.243), channel_id=1, source_target_pairs={{0,8},{1,9},{2,10},{3,11},{4,12},{5,13},{6,14},{7,15},{8,0},{9,1},... | collective-permute-start | bytes 135176 | tf_op jit(solution)/shard_map/ppermute | solution.py:378
  110.2 2.1 collective-permute-start.8
  116.1 2.5 %collective-permute-done.24 = bf16[176,128]{1,0:T(8,128)(2,1)S(1)} collective-permute-done((bf16[176,128]{1,0:T(8,128)(2,1)S(1)}, bf16[176,128]{1,0:T(8,128)(2,1)S(1)}, u32[]{:S(2)}, u32[]{:S(2)}) %collective-permute-start.24) | collective-permute-done | bytes 45088 | tf_op jit(solution)/shard_map/ppermute | solution.py:378
  123.7 2.3 %collective-permute-done.10 = bf16[704,128]{1,0:T(8,128)(2,1)S(1)} collective-permute-done((bf16[704,128]{1,0:T(8,128)(2,1)S(1)}, bf16[704,128]{1,0:T(8,128)(2,1)S(1)}, u32[]{:S(2)}, u32[]{:S(2)}) %collective-permute-start.10) | collective-permute-done | bytes 180256 | tf_op jit(solution)/shard_map/ppermute | solution.py:378
  126.1 2.6 %collective-permute-done.26 = bf16[704,128]{1,0:T(8,128)(2,1)S(1)} collective-permute-done((bf16[704,128]{1,0:T(8,128)(2,1)S(1)}, bf16[704,128]{1,0:T(8,128)(2,1)S(1)}, u32[]{:S(2)}, u32[]{:S(2)}) %collective-permute-start.26) | collective-permute-done | bytes 180256 | tf_op jit(solution)/shard_map/ppermute | solution.py:378
  128.8 6.2 %gradient.7 = (f32[1408,128]{1,0:T(8,128)S(1)}, bf16[1408,128]{1,0:T(8,128)(2,1)S(1)}) custom-call(s32[16]{0:T(128)S(1)} %select_reduce_fusion.seq, s32[16]{0:T(128)S(1)} %copy-done.7, s32[16]{0:T(128)S(1)} %copy-done, s32[1]{0:T(128)} %bitcast.own, bf16[44,512,128]{2,1,0:T(8,128)(2,1)S(1)} %bitcast.14, bf16[1408,128]{1,0:T(8,128)(2,1)S(1)} %pad_maximum_fusion.2.near, ...), custom_call_target="tpu_custom_call" | custom-call | flops 2952790016 | bytes 5767168 | tf_op jit(solution)/shard_map/gradient/pallas_call | solution.py:356
  135.6 6.2 %gradient.10 = (f32[1408,128]{1,0:T(8,128)S(1)}, bf16[1408,128]{1,0:T(8,128)(2,1)S(1)}) custom-call(s32[16]{0:T(128)S(1)} %select_reduce_fusion.seq, s32[16]{0:T(128)S(1)} %copy-done.7, s32[16]{0:T(128)S(1)} %copy-done, s32[1]{0:T(128)} %bitcast.own, bf16[44,512,128]{2,1,0:T(8,128)(2,1)S(1)} %copy-done.5, bf16[1408,128]{1,0:T(8,128)(2,1)S(1)} %pad_maximum_fusion.4.near, ...), custom_call_target="tpu_custom_call" | custom-call | flops 2952790016 | bytes 5767168 | tf_op jit(solution)/shard_map/gradient/pallas_call | solution.py:356
  144.2 5.2 %collective-permute-done.13 = bf16[704,128]{1,0:T(8,128)(2,1)S(1)} collective-permute-done((bf16[704,128]{1,0:T(8,128)(2,1)S(1)}, bf16[704,128]{1,0:T(8,128)(2,1)S(1)}, u32[]{:S(2)}, u32[]{:S(2)}) %collective-permute-start.13) | collective-permute-done | bytes 180256 | tf_op jit(solution)/shard_map/ppermute | solution.py:378
  149.8 3.1 %collective-permute-done.29 = bf16[704,128]{1,0:T(8,128)(2,1)S(1)} collective-permute-done((bf16[704,128]{1,0:T(8,128)(2,1)S(1)}, bf16[704,128]{1,0:T(8,128)(2,1)S(1)}, u32[]{:S(2)}, u32[]{:S(2)}) %collective-permute-start.29) | collective-permute-done | bytes 180256 | tf_op jit(solution)/shard_map/ppermute | solution.py:378
  154.1 2.1 collective-permute-start.15
  165.8 2.9 %collective-permute-done.32 = bf16[176,128]{1,0:T(8,128)(2,1)S(1)} collective-permute-done((bf16[176,128]{1,0:T(8,128)(2,1)S(1)}, bf16[176,128]{1,0:T(8,128)(2,1)S(1)}, u32[]{:S(2)}, u32[]{:S(2)}) %collective-permute-start.32) | collective-permute-done | bytes 45088 | tf_op jit(solution)/shard_map/ppermute | solution.py:378
  171.1 2.2 collective-permute-done.33
  173.9 2.5 %collective-permute-done.18 = bf16[704,128]{1,0:T(8,128)(2,1)S(1)} collective-permute-done((bf16[704,128]{1,0:T(8,128)(2,1)S(1)}, bf16[704,128]{1,0:T(8,128)(2,1)S(1)}, u32[]{:S(2)}, u32[]{:S(2)}) %collective-permute-start.18) | collective-permute-done | bytes 180256 | tf_op jit(solution)/shard_map/ppermute | solution.py:378
  176.5 2.3 %collective-permute-done.34 = bf16[704,128]{1,0:T(8,128)(2,1)S(1)} collective-permute-done((bf16[704,128]{1,0:T(8,128)(2,1)S(1)}, bf16[704,128]{1,0:T(8,128)(2,1)S(1)}, u32[]{:S(2)}, u32[]{:S(2)}) %collective-permute-start.34) | collective-permute-done | bytes 180256 | tf_op jit(solution)/shard_map/ppermute | solution.py:378
  179.0 6.1 %gradient.8 = (f32[3456,128]{1,0:T(8,128)S(1)}, bf16[8,64,128]{2,1,0:T(8,128)(2,1)S(1)}) custom-call(s32[16]{0:T(128)S(1)} %select_reduce_fusion.seq, s32[16]{0:T(128)S(1)} %copy-done.7, s32[16]{0:T(128)S(1)} %copy-done, s32[1]{0:T(128)} %bitcast.own, bf16[44,512,128]{2,1,0:T(8,128)(2,1)S(1)} %bitcast.14, bf16[1408,128]{1,0:T(8,128)(2,1)S(1)} %pad_maximum_fusion.3.near, ...), custom_call_target="tpu_custom_call" | custom-call | flops 2952790016 | bytes 5767168 | tf_op jit(solution)/shard_map/gradient/pallas_call | solution.py:356
  185.1 7.2 %gradient.11 = (f32[4096,128]{1,0:T(8,128)S(1)}, bf16[4096,128]{1,0:T(8,128)(2,1)S(1)}, bf16[8,64,128]{2,1,0:T(8,128)(2,1)S(1)}) custom-call(s32[16]{0:T(128)S(1)} %select_reduce_fusion.seq, s32[16]{0:T(128)S(1)} %copy-done.7, s32[16]{0:T(128)S(1)} %copy-done, s32[1]{0:T(128)} %bitcast.own, bf16[44,512,128]{2,1,0:T(8,128)(2,1)S(1)} %copy-done.5, ...), custom_call_target="tpu_custom_call" | custom-call | flops 2952790016 | bytes 5767168 | tf_op jit(solution)/shard_map/gradient/pallas_call | solution.py:356
  192.8 2.3 %collective-permute-done.36 = bf16[4096,128]{1,0:T(8,128)(2,1)S(1)} collective-permute-done((bf16[4096,128]{1,0:T(8,128)(2,1)S(1)}, bf16[4096,128]{1,0:T(8,128)(2,1)S(1)}, u32[]{:S(2)}, u32[]{:S(2)}) %collective-permute-start.36) | collective-permute-done | bytes 1048608 | tf_op jit(solution)/shard_map/ppermute | solution.py:378
  196.0 13.7 %collective-permute-done.37 = bf16[2048,128]{1,0:T(8,128)(2,1)S(1)} collective-permute-done((bf16[2048,128]{1,0:T(8,128)(2,1)S(1)}, bf16[2048,128]{1,0:T(8,128)(2,1)S(1)}, u32[]{:S(2)}, u32[]{:S(2)}) %collective-permute-start.37) | collective-permute-done | bytes 524320 | tf_op jit(solution)/shard_map/ppermute | solution.py:378
  209.9 7.8 %collective-permute-done.38 = bf16[1024,128]{1,0:T(8,128)(2,1)S(1)} collective-permute-done((bf16[1024,128]{1,0:T(8,128)(2,1)S(1)}, bf16[1024,128]{1,0:T(8,128)(2,1)S(1)}, u32[]{:S(2)}, u32[]{:S(2)}) %collective-permute-start.38) | collective-permute-done | bytes 262176 | tf_op jit(solution)/shard_map/ppermute | solution.py:378
  222.0 3.6 %collective-permute-done.39 = bf16[512,128]{1,0:T(8,128)(2,1)S(1)} collective-permute-done((bf16[512,128]{1,0:T(8,128)(2,1)S(1)}, bf16[512,128]{1,0:T(8,128)(2,1)S(1)}, u32[]{:S(2)}, u32[]{:S(2)}) %collective-permute-start.39) | collective-permute-done | bytes 131104 | tf_op jit(solution)/shard_map/ppermute | solution.py:378
  (148 shorter events, 49.6 us)
Async XLA Ops:
  1.7 10.4 %collective-permute-start = (bf16[512,128]{1,0:T(8,128)(2,1)S(1)}, bf16[512,128]{1,0:T(8,128)(2,1)S(1)}, u32[]{:S(2)}, u32[]{:S(2)}) collective-permute-start(bf16[512,128]{1,0:T(8,128)(2,1)S(1)} %reshape.88), channel_id=1, source_target_pairs={{0,8},{1,9},{2,10},{3,11},{4,12},{5,13},{6,14},{7,15},{8,0},{9,1},... | collective-permute-start | bytes 393224 | tf_op jit(solution)/shard_map/ppermute | solution.py:378
  12.1 35.1 %collective-permute-start.1 = (bf16[1024,128]{1,0:T(8,128)(2,1)S(1)}, bf16[1024,128]{1,0:T(8,128)(2,1)S(1)}, u32[]{:S(2)}, u32[]{:S(2)}) collective-permute-start(bf16[1024,128]{1,0:T(8,128)(2,1)S(1)} %pad_maximum_fusion.6), channel_id=1, source_target_pairs={{0,4},{1,5},{2,6},{3,7},{4,0},{5,1},{6,2},{7,3},{8,12},{9,13},{10,... | collective-permute-start | bytes 786440 | tf_op jit(solution)/shard_map/ppermute | solution.py:378
  47.2 25.2 %collective-permute-start.2 = (bf16[2048,128]{1,0:T(8,128)(2,1)S(1)}, bf16[2048,128]{1,0:T(8,128)(2,1)S(1)}, u32[]{:S(2)}, u32[]{:S(2)}) collective-permute-start(bf16[2048,128]{1,0:T(8,128)(2,1)S(1)} %pad_maximum_fusion.1), channel_id=1, source_target_pairs={{0,2},{1,3},{2,0},{3,1},{4,6},{5,7},{6,4},{7,5},{8,10},{9,11},{10,... | collective-permute-start | bytes 1572872 | tf_op jit(solution)/shard_map/ppermute | solution.py:378
  84.3 6.9 %collective-permute-start.4 = (bf16[1408,128]{1,0:T(8,128)(2,1)S(1)}, bf16[1408,128]{1,0:T(8,128)(2,1)S(1)}, u32[]{:S(2)}, u32[]{:S(2)}) collective-permute-start(bf16[1408,128]{1,0:T(8,128)(2,1)S(1)} %get-tuple-element.31), channel_id=1, source_target_pairs={{0,1},{1,0},{2,3},{3,2},{4,5},{5,4},{6,7},{7,6},{8,9},{9,8},{10,11... | collective-permute-start | bytes 1081352 | tf_op jit(solution)/shard_map/ppermute | solution.py:378
  91.4 7.5 %collective-permute-start.5 = (bf16[704,128]{1,0:T(8,128)(2,1)S(1)}, bf16[704,128]{1,0:T(8,128)(2,1)S(1)}, u32[]{:S(2)}, u32[]{:S(2)}) collective-permute-start(bf16[704,128]{1,0:T(8,128)(2,1)S(1)} %slice.236), channel_id=1, source_target_pairs={{0,2},{1,3},{2,0},{3,1},{4,6},{5,7},{6,4},{7,5},{8,10},{9,11},{10,... | collective-permute-start | bytes 540680 | tf_op jit(solution)/shard_map/ppermute | solution.py:378
  92.7 9.2 %collective-permute-start.21 = (bf16[704,128]{1,0:T(8,128)(2,1)S(1)}, bf16[704,128]{1,0:T(8,128)(2,1)S(1)}, u32[]{:S(2)}, u32[]{:S(2)}) collective-permute-start(bf16[704,128]{1,0:T(8,128)(2,1)S(1)} %slice.234), channel_id=1, source_target_pairs={{0,2},{1,3},{2,0},{3,1},{4,6},{5,7},{6,4},{7,5},{8,10},{9,11},{10,... | collective-permute-start | bytes 540680 | tf_op jit(solution)/shard_map/ppermute | solution.py:378
  98.9 4.6 %collective-permute-start.6 = (bf16[352,128]{1,0:T(8,128)(2,1)S(1)}, bf16[352,128]{1,0:T(8,128)(2,1)S(1)}, u32[]{:S(2)}, u32[]{:S(2)}) collective-permute-start(bf16[352,128]{1,0:T(8,128)(2,1)S(1)} %slice.241), channel_id=1, source_target_pairs={{0,4},{1,5},{2,6},{3,7},{4,0},{5,1},{6,2},{7,3},{8,12},{9,13},{10,... | collective-permute-start | bytes 270344 | tf_op jit(solution)/shard_map/ppermute | solution.py:378
  102.0 5.1 %collective-permute-start.22 = (bf16[352,128]{1,0:T(8,128)(2,1)S(1)}, bf16[352,128]{1,0:T(8,128)(2,1)S(1)}, u32[]{:S(2)}, u32[]{:S(2)}) collective-permute-start(bf16[352,128]{1,0:T(8,128)(2,1)S(1)} %slice.239), channel_id=1, source_target_pairs={{0,4},{1,5},{2,6},{3,7},{4,0},{5,1},{6,2},{7,3},{8,12},{9,13},{10,... | collective-permute-start | bytes 270344 | tf_op jit(solution)/shard_map/ppermute | solution.py:378
  103.5 6.6 %collective-permute-start.7 = (bf16[176,128]{1,0:T(8,128)(2,1)S(1)}, bf16[176,128]{1,0:T(8,128)(2,1)S(1)}, u32[]{:S(2)}, u32[]{:S(2)}) collective-permute-start(bf16[176,128]{1,0:T(8,128)(2,1)S(1)} %slice.245), channel_id=1, source_target_pairs={{0,8},{1,9},{2,10},{3,11},{4,12},{5,13},{6,14},{7,15},{8,0},{9,1},... | collective-permute-start | bytes 135176 | tf_op jit(solution)/shard_map/ppermute | solution.py:378
  107.1 6.4 %collective-permute-start.23 = (bf16[176,128]{1,0:T(8,128)(2,1)S(1)}, bf16[176,128]{1,0:T(8,128)(2,1)S(1)}, u32[]{:S(2)}, u32[]{:S(2)}) collective-permute-start(bf16[176,128]{1,0:T(8,128)(2,1)S(1)} %slice.243), channel_id=1, source_target_pairs={{0,8},{1,9},{2,10},{3,11},{4,12},{5,13},{6,14},{7,15},{8,0},{9,1},... | collective-permute-start | bytes 135176 | tf_op jit(solution)/shard_map/ppermute | solution.py:378
  110.2 5.7 %collective-permute-start.8 = (bf16[176,128]{1,0:T(8,128)(2,1)S(1)}, bf16[176,128]{1,0:T(8,128)(2,1)S(1)}, u32[]{:S(2)}, u32[]{:S(2)}) collective-permute-start(bf16[176,128]{1,0:T(8,128)(2,1)S(1)} %fusion.12), channel_id=1, source_target_pairs={{0,8},{1,9},{2,10},{3,11},{4,12},{5,13},{6,14},{7,15},{8,0},{9,1},... | collective-permute-start | bytes 135176 | tf_op jit(solution)/shard_map/ppermute | solution.py:378
  113.5 5.0 %collective-permute-start.24 = (bf16[176,128]{1,0:T(8,128)(2,1)S(1)}, bf16[176,128]{1,0:T(8,128)(2,1)S(1)}, u32[]{:S(2)}, u32[]{:S(2)}) collective-permute-start(bf16[176,128]{1,0:T(8,128)(2,1)S(1)} %fusion.11), channel_id=1, source_target_pairs={{0,8},{1,9},{2,10},{3,11},{4,12},{5,13},{6,14},{7,15},{8,0},{9,1},... | collective-permute-start | bytes 135176 | tf_op jit(solution)/shard_map/ppermute | solution.py:378
  118.5 4.6 %collective-permute-start.25 = (bf16[352,128]{1,0:T(8,128)(2,1)S(1)}, bf16[352,128]{1,0:T(8,128)(2,1)S(1)}, u32[]{:S(2)}, u32[]{:S(2)}) collective-permute-start(bf16[352,128]{1,0:T(8,128)(2,1)S(1)} %pad_maximum_fusion.13), channel_id=1, source_target_pairs={{0,4},{1,5},{2,6},{3,7},{4,0},{5,1},{6,2},{7,3},{8,12},{9,13},{10,... | collective-permute-start | bytes 270344 | tf_op jit(solution)/shard_map/ppermute | solution.py:378
  120.5 5.6 %collective-permute-start.10 = (bf16[704,128]{1,0:T(8,128)(2,1)S(1)}, bf16[704,128]{1,0:T(8,128)(2,1)S(1)}, u32[]{:S(2)}, u32[]{:S(2)}) collective-permute-start(bf16[704,128]{1,0:T(8,128)(2,1)S(1)} %pad_maximum_fusion.7), channel_id=1, source_target_pairs={{0,2},{1,3},{2,0},{3,1},{4,6},{5,7},{6,4},{7,5},{8,10},{9,11},{10,... | collective-permute-start | bytes 540680 | tf_op jit(solution)/shard_map/ppermute | solution.py:378
  123.1 5.6 %collective-permute-start.26 = (bf16[704,128]{1,0:T(8,128)(2,1)S(1)}, bf16[704,128]{1,0:T(8,128)(2,1)S(1)}, u32[]{:S(2)}, u32[]{:S(2)}) collective-permute-start(bf16[704,128]{1,0:T(8,128)(2,1)S(1)} %pad_maximum_fusion.9), channel_id=1, source_target_pairs={{0,2},{1,3},{2,0},{3,1},{4,6},{5,7},{6,4},{7,5},{8,10},{9,11},{10,... | collective-permute-start | bytes 540680 | tf_op jit(solution)/shard_map/ppermute | solution.py:378
  128.7 6.8 %collective-permute-start.27 = (bf16[1408,128]{1,0:T(8,128)(2,1)S(1)}, bf16[1408,128]{1,0:T(8,128)(2,1)S(1)}, u32[]{:S(2)}, u32[]{:S(2)}) collective-permute-start(bf16[1408,128]{1,0:T(8,128)(2,1)S(1)} %pad_maximum_fusion.4.near), channel_id=1, source_target_pairs={{0,1},{1,0},{2,3},{3,2},{4,5},{5,4},{6,7},{7,6},{8,9},{9,8},{10,11... | collective-permute-start | bytes 1081352 | tf_op jit(solution)/shard_map/ppermute | solution.py:378
  135.0 6.8 %collective-permute-start.12 = (bf16[1408,128]{1,0:T(8,128)(2,1)S(1)}, bf16[1408,128]{1,0:T(8,128)(2,1)S(1)}, u32[]{:S(2)}, u32[]{:S(2)}) collective-permute-start(bf16[1408,128]{1,0:T(8,128)(2,1)S(1)} %get-tuple-element.34), channel_id=1, source_target_pairs={{0,1},{1,0},{2,3},{3,2},{4,5},{5,4},{6,7},{7,6},{8,9},{9,8},{10,11... | collective-permute-start | bytes 1081352 | tf_op jit(solution)/shard_map/ppermute | solution.py:378
  142.0 7.4 %collective-permute-start.13 = (bf16[704,128]{1,0:T(8,128)(2,1)S(1)}, bf16[704,128]{1,0:T(8,128)(2,1)S(1)}, u32[]{:S(2)}, u32[]{:S(2)}) collective-permute-start(bf16[704,128]{1,0:T(8,128)(2,1)S(1)} %slice.235), channel_id=1, source_target_pairs={{0,2},{1,3},{2,0},{3,1},{4,6},{5,7},{6,4},{7,5},{8,10},{9,11},{10,... | collective-permute-start | bytes 540680 | tf_op jit(solution)/shard_map/ppermute | solution.py:378
  143.6 9.2 %collective-permute-start.29 = (bf16[704,128]{1,0:T(8,128)(2,1)S(1)}, bf16[704,128]{1,0:T(8,128)(2,1)S(1)}, u32[]{:S(2)}, u32[]{:S(2)}) collective-permute-start(bf16[704,128]{1,0:T(8,128)(2,1)S(1)} %slice.233), channel_id=1, source_target_pairs={{0,2},{1,3},{2,0},{3,1},{4,6},{5,7},{6,4},{7,5},{8,10},{9,11},{10,... | collective-permute-start | bytes 540680 | tf_op jit(solution)/shard_map/ppermute | solution.py:378
  149.4 4.6 %collective-permute-start.14 = (bf16[352,128]{1,0:T(8,128)(2,1)S(1)}, bf16[352,128]{1,0:T(8,128)(2,1)S(1)}, u32[]{:S(2)}, u32[]{:S(2)}) collective-permute-start(bf16[352,128]{1,0:T(8,128)(2,1)S(1)} %slice.240), channel_id=1, source_target_pairs={{0,4},{1,5},{2,6},{3,7},{4,0},{5,1},{6,2},{7,3},{8,12},{9,13},{10,... | collective-permute-start | bytes 270344 | tf_op jit(solution)/shard_map/ppermute | solution.py:378
  152.9 4.8 %collective-permute-start.30 = (bf16[352,128]{1,0:T(8,128)(2,1)S(1)}, bf16[352,128]{1,0:T(8,128)(2,1)S(1)}, u32[]{:S(2)}, u32[]{:S(2)}) collective-permute-start(bf16[352,128]{1,0:T(8,128)(2,1)S(1)} %slice.238), channel_id=1, source_target_pairs={{0,4},{1,5},{2,6},{3,7},{4,0},{5,1},{6,2},{7,3},{8,12},{9,13},{10,... | collective-permute-start | bytes 270344 | tf_op jit(solution)/shard_map/ppermute | solution.py:378
  154.1 5.8 %collective-permute-start.15 = (bf16[176,128]{1,0:T(8,128)(2,1)S(1)}, bf16[176,128]{1,0:T(8,128)(2,1)S(1)}, u32[]{:S(2)}, u32[]{:S(2)}) collective-permute-start(bf16[176,128]{1,0:T(8,128)(2,1)S(1)} %slice.244), channel_id=1, source_target_pairs={{0,8},{1,9},{2,10},{3,11},{4,12},{5,13},{6,14},{7,15},{8,0},{9,1},... | collective-permute-start | bytes 135176 | tf_op jit(solution)/shard_map/ppermute | solution.py:378
  157.8 5.7 %collective-permute-start.31 = (bf16[176,128]{1,0:T(8,128)(2,1)S(1)}, bf16[176,128]{1,0:T(8,128)(2,1)S(1)}, u32[]{:S(2)}, u32[]{:S(2)}) collective-permute-start(bf16[176,128]{1,0:T(8,128)(2,1)S(1)} %slice.242), channel_id=1, source_target_pairs={{0,8},{1,9},{2,10},{3,11},{4,12},{5,13},{6,14},{7,15},{8,0},{9,1},... | collective-permute-start | bytes 135176 | tf_op jit(solution)/shard_map/ppermute | solution.py:378
  159.9 5.7 %collective-permute-start.16 = (bf16[176,128]{1,0:T(8,128)(2,1)S(1)}, bf16[176,128]{1,0:T(8,128)(2,1)S(1)}, u32[]{:S(2)}, u32[]{:S(2)}) collective-permute-start(bf16[176,128]{1,0:T(8,128)(2,1)S(1)} %add_convert_fusion.1), channel_id=1, source_target_pairs={{0,8},{1,9},{2,10},{3,11},{4,12},{5,13},{6,14},{7,15},{8,0},{9,1},... | collective-permute-start | bytes 135176 | tf_op jit(solution)/shard_map/ppermute | solution.py:378
  163.6 5.1 %collective-permute-start.32 = (bf16[176,128]{1,0:T(8,128)(2,1)S(1)}, bf16[176,128]{1,0:T(8,128)(2,1)S(1)}, u32[]{:S(2)}, u32[]{:S(2)}) collective-permute-start(bf16[176,128]{1,0:T(8,128)(2,1)S(1)} %add_convert_fusion), channel_id=1, source_target_pairs={{0,8},{1,9},{2,10},{3,11},{4,12},{5,13},{6,14},{7,15},{8,0},{9,1},... | collective-permute-start | bytes 135176 | tf_op jit(solution)/shard_map/ppermute | solution.py:378
  165.6 4.9 %collective-permute-start.17 = (bf16[352,128]{1,0:T(8,128)(2,1)S(1)}, bf16[352,128]{1,0:T(8,128)(2,1)S(1)}, u32[]{:S(2)}, u32[]{:S(2)}) collective-permute-start(bf16[352,128]{1,0:T(8,128)(2,1)S(1)} %pad_maximum_fusion.12), channel_id=1, source_target_pairs={{0,4},{1,5},{2,6},{3,7},{4,0},{5,1},{6,2},{7,3},{8,12},{9,13},{10,... | collective-permute-start | bytes 270344 | tf_op jit(solution)/shard_map/ppermute | solution.py:378
  170.5 5.9 %collective-permute-start.18 = (bf16[704,128]{1,0:T(8,128)(2,1)S(1)}, bf16[704,128]{1,0:T(8,128)(2,1)S(1)}, u32[]{:S(2)}, u32[]{:S(2)}) collective-permute-start(bf16[704,128]{1,0:T(8,128)(2,1)S(1)} %pad_maximum_fusion.8), channel_id=1, source_target_pairs={{0,2},{1,3},{2,0},{3,1},{4,6},{5,7},{6,4},{7,5},{8,10},{9,11},{10,... | collective-permute-start | bytes 540680 | tf_op jit(solution)/shard_map/ppermute | solution.py:378
  173.3 5.6 %collective-permute-start.34 = (bf16[704,128]{1,0:T(8,128)(2,1)S(1)}, bf16[704,128]{1,0:T(8,128)(2,1)S(1)}, u32[]{:S(2)}, u32[]{:S(2)}) collective-permute-start(bf16[704,128]{1,0:T(8,128)(2,1)S(1)} %pad_maximum_fusion.10), channel_id=1, source_target_pairs={{0,2},{1,3},{2,0},{3,1},{4,6},{5,7},{6,4},{7,5},{8,10},{9,11},{10,... | collective-permute-start | bytes 540680 | tf_op jit(solution)/shard_map/ppermute | solution.py:378
  178.9 6.2 %collective-permute-start.35 = (bf16[1408,128]{1,0:T(8,128)(2,1)S(1)}, bf16[1408,128]{1,0:T(8,128)(2,1)S(1)}, u32[]{:S(2)}, u32[]{:S(2)}) collective-permute-start(bf16[1408,128]{1,0:T(8,128)(2,1)S(1)} %pad_maximum_fusion.5.near), channel_id=1, source_target_pairs={{0,1},{1,0},{2,3},{3,2},{4,5},{5,4},{6,7},{7,6},{8,9},{9,8},{10,11... | collective-permute-start | bytes 1081352 | tf_op jit(solution)/shard_map/ppermute | solution.py:378
  195.4 14.3 %collective-permute-start.37 = (bf16[2048,128]{1,0:T(8,128)(2,1)S(1)}, bf16[2048,128]{1,0:T(8,128)(2,1)S(1)}, u32[]{:S(2)}, u32[]{:S(2)}) collective-permute-start(bf16[2048,128]{1,0:T(8,128)(2,1)S(1)} %slice.231), channel_id=1, source_target_pairs={{0,2},{1,3},{2,0},{3,1},{4,6},{5,7},{6,4},{7,5},{8,10},{9,11},{10,... | collective-permute-start | bytes 1572872 | tf_op jit(solution)/shard_map/ppermute | solution.py:378
  209.8 7.8 %collective-permute-start.38 = (bf16[1024,128]{1,0:T(8,128)(2,1)S(1)}, bf16[1024,128]{1,0:T(8,128)(2,1)S(1)}, u32[]{:S(2)}, u32[]{:S(2)}) collective-permute-start(bf16[1024,128]{1,0:T(8,128)(2,1)S(1)} %slice.232), channel_id=1, source_target_pairs={{0,4},{1,5},{2,6},{3,7},{4,0},{5,1},{6,2},{7,3},{8,12},{9,13},{10,... | collective-permute-start | bytes 786440 | tf_op jit(solution)/shard_map/ppermute | solution.py:378
  217.7 7.8 %collective-permute-start.39 = (bf16[512,128]{1,0:T(8,128)(2,1)S(1)}, bf16[512,128]{1,0:T(8,128)(2,1)S(1)}, u32[]{:S(2)}, u32[]{:S(2)}) collective-permute-start(bf16[512,128]{1,0:T(8,128)(2,1)S(1)} %slice.237), channel_id=1, source_target_pairs={{0,8},{1,9},{2,10},{3,11},{4,12},{5,13},{6,14},{7,15},{8,0},{9,1},... | collective-permute-start | bytes 393224 | tf_op jit(solution)/shard_map/ppermute | solution.py:378
  (19 other events, 177.9 us)

commit v4 on v3

--- a/solution.py
+++ b/solution.py
@@ -21,6 +21,8 @@
 PIECE = 4
 MATRIX_UNIT = 256
 VMEM_MARGIN = 3 * 1024 * 1024
+SUPPORT_VMEM = 40 * 1024 * 1024
+HELD_BYTES = 65 * 1024 * 1024
 
 
 def momentum_list():
@@ -131,8 +133,8 @@
                 pltpu.SemaphoreType.DMA((pairs,)),
             ],
         ),
-        out_shape=jax.ShapeDtypeStruct((pairs, rows, LANES), dictionary.dtype),
-        compiler_params=pltpu.CompilerParams(vmem_limit_bytes=entries * rows * LANES * 2 + VMEM_MARGIN),
+        out_shape=jax.ShapeDtypeStruct((HELD_BYTES // (rows * LANES * 2), rows, LANES), dictionary.dtype),
+        compiler_params=pltpu.CompilerParams(vmem_limit_bytes=SUPPORT_VMEM),
         cost_estimate=pl.CostEstimate(flops=0, transcendentals=0, bytes_accessed=6 * pairs * rows * LANES * 2),
         name="collect_support",
     )(seq, order, support, counts, dictionary)
@@ -147,9 +149,10 @@
     return result
 
 
-def gradient_kernel(chain, mode, shards, seq, order, counts, own, blocks, near, far, targets, *refs):
+def gradient_kernel(chain, mode, shards, pairs, seq, order, counts, own, blocks, near, far, targets, *refs):
     refs = list(refs)
     take = lambda: refs.pop(0)
+    take()
     if mode == "first":
         thresh = take()
     if mode == "final":
@@ -170,7 +173,6 @@
     offsets, sems = refs
 
     seats = order.shape[0] // 2
-    pairs = blocks.shape[0]
     places = pairs + SPARE
     pieces = pairs // PIECE
     base = places if mode == "final" else 0
@@ -326,8 +328,8 @@
                     send[rows, :] = value.astype(send.dtype)
 
 
-def gradient_call(chain, mode, shards, scalars, blocks, near, far, targets, extra=()):
-    pairs, rows, _ = blocks.shape
+def gradient_call(chain, mode, shards, pairs, scalars, blocks, near, far, targets, after, extra=()):
+    rows = blocks.shape[1]
     places = pairs + SPARE
     groups = scalars[1].shape[0]
     half_in = near.shape[0]
@@ -354,12 +356,14 @@
         scratch += [(packed, single), (packed, double)]
     room = sum(math.prod(shape) * jnp.dtype(kind).itemsize for shape, kind in scratch)
     return pl.pallas_call(
-        functools.partial(gradient_kernel, chain, mode, shards),
+        functools.partial(gradient_kernel, chain, mode, shards, pairs),
         grid_spec=pltpu.PrefetchScalarGridSpec(
             num_scalar_prefetch=4,
             grid=(),
             in_specs=[pl.BlockSpec(memory_space=pltpu.HBM)]
-            + [pl.BlockSpec(memory_space=pltpu.VMEM)] * (3 + len(extra)),
+            + [pl.BlockSpec(memory_space=pltpu.VMEM)] * 3
+            + [pl.BlockSpec(memory_space=pl.ANY)]
+            + [pl.BlockSpec(memory_space=pltpu.VMEM)] * len(extra),
             out_specs=[pl.BlockSpec(memory_space=pltpu.VMEM)] * len(outs),
             scratch_shapes=[pltpu.VMEM(shape, kind) for shape, kind in scratch]
             + [pltpu.SMEM((groups,), jnp.int32), pltpu.SemaphoreType.DMA((pairs // PIECE,))],
@@ -370,7 +374,7 @@
             flops=4 * pairs * rows * LANES * MATRIX_UNIT, transcendentals=0, bytes_accessed=pairs * rows * LANES * 2
         ),
         name="gradient",
-    )(*scalars, blocks, near, far, targets, *extra)
+    )(*scalars, blocks, near, far, targets, after, *extra)
 
 
 def exchange(value, distance):
@@ -384,29 +388,32 @@
 
 def gather_shards(own, beside=()):
     made = []
+    early = own
     value = own
     distance = lax.axis_size("rows") // 2
     while distance > 1:
         if beside and distance == 2:
             value, array = lax.optimization_barrier((value, beside[0]))
             made.append(array)
+        early = value
         value = double_up(value, distance)
         distance //= 2
     if beside:
         value, array = lax.optimization_barrier((value, beside[1]))
         made.append(array)
-    return value, exchange(value, 1), made
+    return value, exchange(value, 1), made or early[:ROW_TILE]
 
 
 def reduce_shards(keep, send):
     devices = lax.axis_size("rows")
     total = keep + exchange(send, 1).astype(jnp.float32)
+    early = total[:ROW_TILE]
     distance = 2
     while distance < devices:
         middle = total.shape[0] // 2
         total = total[:middle] + exchange(total[middle:].astype(jnp.bfloat16), distance).astype(jnp.float32)
         distance *= 2
-    return total
+    return total, early
 
 
 def chain_seats(live):
@@ -444,26 +451,28 @@
     own_thresh = lax.dynamic_index_in_dim(half_penalty, group_order[position], 0, False)[None, :, None]
 
     chains = [dict(near=near, far=far) for _ in range(2)]
+    after = targets[:ROW_TILE]
+    run = functools.partial(gradient_call, shards=devices, pairs=pairs, scalars=scalars, targets=targets)
     for turn in range(ITERS - 1):
         for chain, state in enumerate(chains):
             mode, extra = ("first", (thresh_tiles,)) if turn == 0 else ("shards", ())
-            keep, send, *more = gradient_call(
-                chain, mode, devices, scalars, blocks[chain], state["near"], state["far"], targets, extra
+            keep, send, *more = run(
+                chain, mode, blocks=blocks[chain], near=state["near"], far=state["far"], after=after, extra=extra
             )
             if turn == 0:
                 state["point"] = state["previous"] = more[0].astype(jnp.float32)
                 state["thresh"] = more[1]
-            current = shrink(state["point"] - 0.5 * reduce_shards(keep, send), state["thresh"])
+            gradient, after = reduce_shards(keep, send)
+            current = shrink(state["point"] - 0.5 * gradient, state["thresh"])
             state["point"] = current + momenta[turn] * (current - state["previous"])
             state["previous"] = current
-            state["near"], state["far"], _ = gather_shards(state["point"].astype(jnp.bfloat16))
-    raw, sent = gradient_call(
-        0, "raw", devices, scalars, blocks[0], chains[0]["near"], chains[0]["far"], targets
+            state["near"], state["far"], early = gather_shards(state["point"].astype(jnp.bfloat16))
+        after = early
+    raw, sent = run(0, "raw", blocks=blocks[0], near=chains[0]["near"], far=chains[0]["far"], after=after)
+    keep, send, more = run(
+        1, "final", blocks=blocks[1], near=chains[1]["near"], far=chains[1]["far"], after=after, extra=(raw,)
     )
-    keep, send, more = gradient_call(
-        1, "final", devices, scalars, blocks[1], chains[1]["near"], chains[1]["far"], targets, (raw,)
-    )
-    gradient = reduce_shards(keep, send).reshape(SLOT_PAIRS, PATCHES, LANES)
+    gradient = reduce_shards(keep, send)[0].reshape(SLOT_PAIRS, PATCHES, LANES)
     sent = sent.astype(jnp.float32) + more.astype(jnp.float32)
     result = shrink(sent - 0.5 * gradient, own_thresh)
     result = result.reshape(SLOT_PAIRS, PATCHES, 2, BLOCK).transpose(0, 2, 1, 3)

time: 227 us -> 195 us (0.86)
  local copies, waits for them, and re-layouts: 24.9 us -> 6.76 us
  Pallas kernels: 80.4 us -> 64 us
  waiting for transfers between devices: 78.4 us -> 87 us
  starting transfers between devices: 37.5 us -> 31.8 us
    pallas_call x2, Pallas kernels: 42.2 us -> 22 us  [collect_support(): pl.pallas_call(functools.partial(support_kernel, chain), grid_spec=pltpu....]
    unnamed x23 -> x9, local copies, waits for them, and re-layouts: 19.7 us -> 1.52 us
    ppermute x40, waiting for transfers between devices: 78.4 us -> 87 us  [exchange(): lax.ppermute(value, 'rows', [(i, i ^ distance) for i in range(devices)])]
    ppermute x40, starting transfers between devices: 37.5 us -> 31.8 us  [exchange(): lax.ppermute(value, 'rows', [(i, i ^ distance) for i in range(devices)])]
    pallas_call x6, Pallas kernels: 38.2 us -> 42 us  [gradient_call(): pl.pallas_call(functools.partial(gradient_kernel, chain, mode, shards, pa...]
  transfers between devices with their start and end apart: 40 -> 40, of which waited for: 29 -> 32; matrix products, arithmetic and copies ran while one was open for 3% -> 3% of each run, Pallas kernels for 29% -> 22%
where the time goes in v4:
time: 195 us
  waiting for transfers between devices  87 us (45%)
  Pallas kernels  64 us (33%)
  starting transfers between devices  31.8 us (16%)
  local copies, waits for them, and re-layouts  6.76 us (3%)
  other arithmetic  3.21 us (2%)
  between operations  2.52 us (1%)
    ppermute x40, waiting for transfers between devices, exchange(): lax.ppermute(value, 'rows', [(i, i ^ distance) for i in range(devices)])  87 us
    pallas_call x6, Pallas kernels, gradient_call(): pl.pallas_call(functools.partial(gradient_kernel, chain, mode, shards, pa...  42 us
    ppermute x40, starting transfers between devices, exchange(): lax.ppermute(value, 'rows', [(i, i ^ distance) for i in range(devices)])  31.8 us
    pallas_call x2, Pallas kernels, collect_support(): pl.pallas_call(functools.partial(support_kernel, chain), grid_spec=pltpu....  22 us
  transfers between devices with their start and end apart: 40, of which 32 were waited for; matrix products, arithmetic and copies ran while one was open for 3% of the time, Pallas kernels for 22%

profile of v4, /device:TPU:0, one launch (start us, length us, event | category | flops | bytes accessed | tf_op | source)
XLA Modules:
  0.0 195.3 jit_solution(7799188338137838682)
XLA Ops:
  1.7 4.1 %collective-permute-start = (bf16[512,128]{1,0:T(8,128)(2,1)S(1)}, bf16[512,128]{1,0:T(8,128)(2,1)S(1)}, u32[]{:S(2)}, u32[]{:S(2)}) collective-permute-start(bf16[512,128]{1,0:T(8,128)(2,1)S(1)} %reshape.88), channel_id=1, source_target_pairs={{0,8},{1,9},{2,10},{3,11},{4,12},{5,13},{6,14},{7,15},{8,0},{9,1},... | collective-permute-start | bytes 393224 | tf_op jit(solution)/shard_map/ppermute | solution.py:382
  8.6 3.5 %collective-permute-done = bf16[512,128]{1,0:T(8,128)(2,1)S(1)} collective-permute-done((bf16[512,128]{1,0:T(8,128)(2,1)S(1)}, bf16[512,128]{1,0:T(8,128)(2,1)S(1)}, u32[]{:S(2)}, u32[]{:S(2)}) %collective-permute-start) | collective-permute-done | bytes 131104 | tf_op jit(solution)/shard_map/ppermute | solution.py:382
  13.0 11.0 %collect_support.2.blocks = bf16[520,512,128]{2,1,0:T(8,128)(2,1)} custom-call(s32[16]{0:T(128)S(1)} %select_reduce_fusion.seq, s32[16]{0:T(128)S(1)} %copy-done.2, s32[16,16]{1,0:T(8,128)S(1)} %copy-done.1, s32[16]{0:T(128)S(1)} %copy-done, bf16[512,32768]{1,0:T(8,128)(2,1)} %dictionary.3), custom_call_target="tpu_custom_call" | custom-call | bytes 34603008 | tf_op jit(solution)/shard_map/collect_support/pallas_call | solution.py:121
  25.7 11.0 %collect_support.3.blocks = bf16[520,512,128]{2,1,0:T(8,128)(2,1)} custom-call(s32[16]{0:T(128)S(1)} %select_reduce_fusion.seq, s32[16]{0:T(128)S(1)} %copy-done.2, s32[16,16]{1,0:T(8,128)S(1)} %copy-done.1, s32[16]{0:T(128)S(1)} %copy-done, bf16[512,32768]{1,0:T(8,128)(2,1)} %dictionary.3), custom_call_target="tpu_custom_call" | custom-call | bytes 34603008 | tf_op jit(solution)/shard_map/collect_support/pallas_call | solution.py:121
  40.7 6.9 %gradient.6 = (f32[1408,128]{1,0:T(8,128)S(1)}, bf16[1408,128]{1,0:T(8,128)(2,1)S(1)}, bf16[176,128]{1,0:T(8,128)(2,1)S(1)}, f32[176,128]{1,0:T(8,128)S(1)}) custom-call(s32[16]{0:T(128)S(1)} %select_reduce_fusion.seq, s32[16]{0:T(128)S(1)} %copy-done.2, s32[16]{0:T(128)S(1)} %copy-done, s32[1]{0:T(128)} %bitcast.own, ...), custom_call_target="tpu_custom_call" | custom-call | flops 2952790016 | bytes 5767168 | tf_op jit(solution)/shard_map/gradient/pallas_call | solution.py:358
  49.5 1.6 collective-permute-start.5
  51.1 6.8 %gradient.7 = (f32[1408,128]{1,0:T(8,128)S(1)}, bf16[1408,128]{1,0:T(8,128)(2,1)S(1)}, bf16[176,128]{1,0:T(8,128)(2,1)S(1)}, f32[176,128]{1,0:T(8,128)S(1)}) custom-call(s32[16]{0:T(128)S(1)} %select_reduce_fusion.seq, s32[16]{0:T(128)S(1)} %copy-done.2, s32[16]{0:T(128)S(1)} %copy-done, s32[1]{0:T(128)} %bitcast.own, ...), custom_call_target="tpu_custom_call" | custom-call | flops 2952790016 | bytes 5767168 | tf_op jit(solution)/shard_map/gradient/pallas_call | solution.py:358
  58.5 4.7 %collective-permute-done.6 = bf16[352,128]{1,0:T(8,128)(2,1)S(1)} collective-permute-done((bf16[352,128]{1,0:T(8,128)(2,1)S(1)}, bf16[352,128]{1,0:T(8,128)(2,1)S(1)}, u32[]{:S(2)}, u32[]{:S(2)}) %collective-permute-start.6) | collective-permute-done | bytes 90144 | tf_op jit(solution)/shard_map/ppermute | solution.py:382
  63.2 3.4 %collective-permute-start.7 = (bf16[176,128]{1,0:T(8,128)(2,1)S(1)}, bf16[176,128]{1,0:T(8,128)(2,1)S(1)}, u32[]{:S(2)}, u32[]{:S(2)}) collective-permute-start(bf16[176,128]{1,0:T(8,128)(2,1)S(1)} %slice.270), channel_id=1, source_target_pairs={{0,8},{1,9},{2,10},{3,11},{4,12},{5,13},{6,14},{7,15},{8,0},{9,1},... | collective-permute-start | bytes 135176 | tf_op jit(solution)/shard_map/ppermute | solution.py:382
  68.9 2.8 %collective-permute-start.8 = (bf16[176,128]{1,0:T(8,128)(2,1)S(1)}, bf16[176,128]{1,0:T(8,128)(2,1)S(1)}, u32[]{:S(2)}, u32[]{:S(2)}) collective-permute-start(bf16[176,128]{1,0:T(8,128)(2,1)S(1)} %fusion.12), channel_id=1, source_target_pairs={{0,8},{1,9},{2,10},{3,11},{4,12},{5,13},{6,14},{7,15},{8,0},{9,1},... | collective-permute-start | bytes 135176 | tf_op jit(solution)/shard_map/ppermute | solution.py:382
  74.9 2.4 %collective-permute-done.14 = bf16[352,128]{1,0:T(8,128)(2,1)S(1)} collective-permute-done((bf16[352,128]{1,0:T(8,128)(2,1)S(1)}, bf16[352,128]{1,0:T(8,128)(2,1)S(1)}, u32[]{:S(2)}, u32[]{:S(2)}) %collective-permute-start.14) | collective-permute-done | bytes 90144 | tf_op jit(solution)/shard_map/ppermute | solution.py:382
  80.1 3.5 %collective-permute-done.15 = bf16[176,128]{1,0:T(8,128)(2,1)S(1)} collective-permute-done((bf16[176,128]{1,0:T(8,128)(2,1)S(1)}, bf16[176,128]{1,0:T(8,128)(2,1)S(1)}, u32[]{:S(2)}, u32[]{:S(2)}) %collective-permute-start.15) | collective-permute-done | bytes 45088 | tf_op jit(solution)/shard_map/ppermute | solution.py:382
  85.1 3.5 %collective-permute-done.24 = bf16[176,128]{1,0:T(8,128)(2,1)S(1)} collective-permute-done((bf16[176,128]{1,0:T(8,128)(2,1)S(1)}, bf16[176,128]{1,0:T(8,128)(2,1)S(1)}, u32[]{:S(2)}, u32[]{:S(2)}) %collective-permute-start.24) | collective-permute-done | bytes 45088 | tf_op jit(solution)/shard_map/ppermute | solution.py:382
  88.7 4.5 %collective-permute-done.25 = bf16[352,128]{1,0:T(8,128)(2,1)S(1)} collective-permute-done((bf16[352,128]{1,0:T(8,128)(2,1)S(1)}, bf16[352,128]{1,0:T(8,128)(2,1)S(1)}, u32[]{:S(2)}, u32[]{:S(2)}) %collective-permute-start.25) | collective-permute-done | bytes 90144 | tf_op jit(solution)/shard_map/ppermute | solution.py:382
  93.8 6.8 %gradient.8 = (f32[1408,128]{1,0:T(8,128)S(1)}, bf16[1408,128]{1,0:T(8,128)(2,1)S(1)}) custom-call(s32[16]{0:T(128)S(1)} %select_reduce_fusion.seq, s32[16]{0:T(128)S(1)} %copy-done.2, s32[16]{0:T(128)S(1)} %copy-done, s32[1]{0:T(128)} %bitcast.own, bf16[520,512,128]{2,1,0:T(8,128)(2,1)} %collect_support.2.blocks, ...), custom_call_target="tpu_custom_call" | custom-call | flops 2952790016 | bytes 5767168 | tf_op jit(solution)/shard_map/gradient/pallas_call | solution.py:358
  102.9 6.6 %gradient.9 = (f32[1408,128]{1,0:T(8,128)S(1)}, bf16[1408,128]{1,0:T(8,128)(2,1)S(1)}) custom-call(s32[16]{0:T(128)S(1)} %select_reduce_fusion.seq, s32[16]{0:T(128)S(1)} %copy-done.2, s32[16]{0:T(128)S(1)} %copy-done, s32[1]{0:T(128)} %bitcast.own, bf16[520,512,128]{2,1,0:T(8,128)(2,1)} %collect_support.3.blocks, ...), custom_call_target="tpu_custom_call" | custom-call | flops 2952790016 | bytes 5767168 | tf_op jit(solution)/shard_map/gradient/pallas_call | solution.py:358
  113.0 4.3 %collective-permute-done.17 = bf16[704,128]{1,0:T(8,128)(2,1)S(1)} collective-permute-done((bf16[704,128]{1,0:T(8,128)(2,1)S(1)}, bf16[704,128]{1,0:T(8,128)(2,1)S(1)}, u32[]{:S(2)}, u32[]{:S(2)}) %collective-permute-start.17) | collective-permute-done | bytes 180256 | tf_op jit(solution)/shard_map/ppermute | solution.py:382
  117.4 3.2 %collective-permute-done.29 = bf16[704,128]{1,0:T(8,128)(2,1)S(1)} collective-permute-done((bf16[704,128]{1,0:T(8,128)(2,1)S(1)}, bf16[704,128]{1,0:T(8,128)(2,1)S(1)}, u32[]{:S(2)}, u32[]{:S(2)}) %collective-permute-start.29) | collective-permute-done | bytes 180256 | tf_op jit(solution)/shard_map/ppermute | solution.py:382
  122.2 3.1 %collective-permute-done.30 = bf16[352,128]{1,0:T(8,128)(2,1)S(1)} collective-permute-done((bf16[352,128]{1,0:T(8,128)(2,1)S(1)}, bf16[352,128]{1,0:T(8,128)(2,1)S(1)}, u32[]{:S(2)}, u32[]{:S(2)}) %collective-permute-start.30) | collective-permute-done | bytes 90144 | tf_op jit(solution)/shard_map/ppermute | solution.py:382
  125.5 2.5 %collective-permute-done.19 = bf16[176,128]{1,0:T(8,128)(2,1)S(1)} collective-permute-done((bf16[176,128]{1,0:T(8,128)(2,1)S(1)}, bf16[176,128]{1,0:T(8,128)(2,1)S(1)}, u32[]{:S(2)}, u32[]{:S(2)}) %collective-permute-start.19) | collective-permute-done | bytes 45088 | tf_op jit(solution)/shard_map/ppermute | solution.py:382
  128.5 2.0 %collective-permute-done.31 = bf16[176,128]{1,0:T(8,128)(2,1)S(1)} collective-permute-done((bf16[176,128]{1,0:T(8,128)(2,1)S(1)}, bf16[176,128]{1,0:T(8,128)(2,1)S(1)}, u32[]{:S(2)}, u32[]{:S(2)}) %collective-permute-start.31) | collective-permute-done | bytes 45088 | tf_op jit(solution)/shard_map/ppermute | solution.py:382
  131.3 2.0 %collective-permute-done.20 = bf16[176,128]{1,0:T(8,128)(2,1)S(1)} collective-permute-done((bf16[176,128]{1,0:T(8,128)(2,1)S(1)}, bf16[176,128]{1,0:T(8,128)(2,1)S(1)}, u32[]{:S(2)}, u32[]{:S(2)}) %collective-permute-start.20) | collective-permute-done | bytes 45088 | tf_op jit(solution)/shard_map/ppermute | solution.py:382
  133.4 2.4 %collective-permute-done.32 = bf16[176,128]{1,0:T(8,128)(2,1)S(1)} collective-permute-done((bf16[176,128]{1,0:T(8,128)(2,1)S(1)}, bf16[176,128]{1,0:T(8,128)(2,1)S(1)}, u32[]{:S(2)}, u32[]{:S(2)}) %collective-permute-start.32) | collective-permute-done | bytes 45088 | tf_op jit(solution)/shard_map/ppermute | solution.py:382
  136.0 1.9 collective-permute-done.21
  141.8 1.7 collective-permute-done.22
  143.6 2.3 %collective-permute-done.34 = bf16[704,128]{1,0:T(8,128)(2,1)S(1)} collective-permute-done((bf16[704,128]{1,0:T(8,128)(2,1)S(1)}, bf16[704,128]{1,0:T(8,128)(2,1)S(1)}, u32[]{:S(2)}, u32[]{:S(2)}) %collective-permute-start.34) | collective-permute-done | bytes 180256 | tf_op jit(solution)/shard_map/ppermute | solution.py:382
  146.0 7.1 %gradient.10 = (f32[3456,128]{1,0:T(8,128)S(1)}, bf16[8,64,128]{2,1,0:T(8,128)(2,1)S(1)}) custom-call(s32[16]{0:T(128)S(1)} %select_reduce_fusion.seq, s32[16]{0:T(128)S(1)} %copy-done.2, s32[16]{0:T(128)S(1)} %copy-done, s32[1]{0:T(128)} %bitcast.own, bf16[520,512,128]{2,1,0:T(8,128)(2,1)} %collect_support.2.blocks, ...), custom_call_target="tpu_custom_call" | custom-call | flops 2952790016 | bytes 5767168 | tf_op jit(solution)/shard_map/gradient/pallas_call | solution.py:358
  153.1 7.7 %gradient.11 = (f32[4096,128]{1,0:T(8,128)S(1)}, bf16[4096,128]{1,0:T(8,128)(2,1)S(1)}, bf16[8,64,128]{2,1,0:T(8,128)(2,1)S(1)}) custom-call(s32[16]{0:T(128)S(1)} %select_reduce_fusion.seq, s32[16]{0:T(128)S(1)} %copy-done.2, s32[16]{0:T(128)S(1)} %copy-done, s32[1]{0:T(128)} %bitcast.own, bf16[520,512,128]{2,1,0:T(8,128)(2,1)} %collect_support.3.blocks, ...), custom_call_target="tpu_custom_call" | custom-call | flops 2952790016 | bytes 5767168 | tf_op jit(solution)/shard_map/gradient/pallas_call | solution.py:358
  161.4 2.3 %collective-permute-done.36 = bf16[4096,128]{1,0:T(8,128)(2,1)S(1)} collective-permute-done((bf16[4096,128]{1,0:T(8,128)(2,1)S(1)}, bf16[4096,128]{1,0:T(8,128)(2,1)S(1)}, u32[]{:S(2)}, u32[]{:S(2)}) %collective-permute-start.36) | collective-permute-done | bytes 1048608 | tf_op jit(solution)/shard_map/ppermute | solution.py:382
  165.4 12.8 %collective-permute-done.37 = bf16[2048,128]{1,0:T(8,128)(2,1)S(1)} collective-permute-done((bf16[2048,128]{1,0:T(8,128)(2,1)S(1)}, bf16[2048,128]{1,0:T(8,128)(2,1)S(1)}, u32[]{:S(2)}, u32[]{:S(2)}) %collective-permute-start.37) | collective-permute-done | bytes 524320 | tf_op jit(solution)/shard_map/ppermute | solution.py:382
  178.6 7.5 %collective-permute-done.38 = bf16[1024,128]{1,0:T(8,128)(2,1)S(1)} collective-permute-done((bf16[1024,128]{1,0:T(8,128)(2,1)S(1)}, bf16[1024,128]{1,0:T(8,128)(2,1)S(1)}, u32[]{:S(2)}, u32[]{:S(2)}) %collective-permute-start.38) | collective-permute-done | bytes 262176 | tf_op jit(solution)/shard_map/ppermute | solution.py:382
  189.5 4.3 %collective-permute-done.39 = bf16[512,128]{1,0:T(8,128)(2,1)S(1)} collective-permute-done((bf16[512,128]{1,0:T(8,128)(2,1)S(1)}, bf16[512,128]{1,0:T(8,128)(2,1)S(1)}, u32[]{:S(2)}, u32[]{:S(2)}) %collective-permute-start.39) | collective-permute-done | bytes 131104 | tf_op jit(solution)/shard_map/ppermute | solution.py:382
  (138 shorter events, 42.6 us)
Async XLA Ops:
  1.7 10.4 %collective-permute-start = (bf16[512,128]{1,0:T(8,128)(2,1)S(1)}, bf16[512,128]{1,0:T(8,128)(2,1)S(1)}, u32[]{:S(2)}, u32[]{:S(2)}) collective-permute-start(bf16[512,128]{1,0:T(8,128)(2,1)S(1)} %reshape.88), channel_id=1, source_target_pairs={{0,8},{1,9},{2,10},{3,11},{4,12},{5,13},{6,14},{7,15},{8,0},{9,1},... | collective-permute-start | bytes 393224 | tf_op jit(solution)/shard_map/ppermute | solution.py:382
  12.1 11.9 %collective-permute-start.1 = (bf16[1024,128]{1,0:T(8,128)(2,1)S(1)}, bf16[1024,128]{1,0:T(8,128)(2,1)S(1)}, u32[]{:S(2)}, u32[]{:S(2)}) collective-permute-start(bf16[1024,128]{1,0:T(8,128)(2,1)S(1)} %pad_maximum_fusion.6), channel_id=1, source_target_pairs={{0,4},{1,5},{2,6},{3,7},{4,0},{5,1},{6,2},{7,3},{8,12},{9,13},{10,... | collective-permute-start | bytes 786440 | tf_op jit(solution)/shard_map/ppermute | solution.py:382
  24.1 13.6 %collective-permute-start.2 = (bf16[2048,128]{1,0:T(8,128)(2,1)S(1)}, bf16[2048,128]{1,0:T(8,128)(2,1)S(1)}, u32[]{:S(2)}, u32[]{:S(2)}) collective-permute-start(bf16[2048,128]{1,0:T(8,128)(2,1)S(1)} %pad_maximum_fusion.1), channel_id=1, source_target_pairs={{0,2},{1,3},{2,0},{3,1},{4,6},{5,7},{6,4},{7,5},{8,10},{9,11},{10,... | collective-permute-start | bytes 1572872 | tf_op jit(solution)/shard_map/ppermute | solution.py:382
  49.5 8.5 %collective-permute-start.5 = (bf16[704,128]{1,0:T(8,128)(2,1)S(1)}, bf16[704,128]{1,0:T(8,128)(2,1)S(1)}, u32[]{:S(2)}, u32[]{:S(2)}) collective-permute-start(bf16[704,128]{1,0:T(8,128)(2,1)S(1)} %slice.261), channel_id=1, source_target_pairs={{0,2},{1,3},{2,0},{3,1},{4,6},{5,7},{6,4},{7,5},{8,10},{9,11},{10,... | collective-permute-start | bytes 540680 | tf_op jit(solution)/shard_map/ppermute | solution.py:382
  57.9 8.7 %collective-permute-start.12 = (bf16[1408,128]{1,0:T(8,128)(2,1)S(1)}, bf16[1408,128]{1,0:T(8,128)(2,1)S(1)}, u32[]{:S(2)}, u32[]{:S(2)}) collective-permute-start(bf16[1408,128]{1,0:T(8,128)(2,1)S(1)} %get-tuple-element.36), channel_id=1, source_target_pairs={{0,1},{1,0},{2,3},{3,2},{4,5},{5,4},{6,7},{7,6},{8,9},{9,8},{10,11... | collective-permute-start | bytes 1081352 | tf_op jit(solution)/shard_map/ppermute | solution.py:382
  58.1 5.1 %collective-permute-start.6 = (bf16[352,128]{1,0:T(8,128)(2,1)S(1)}, bf16[352,128]{1,0:T(8,128)(2,1)S(1)}, u32[]{:S(2)}, u32[]{:S(2)}) collective-permute-start(bf16[352,128]{1,0:T(8,128)(2,1)S(1)} %slice.266), channel_id=1, source_target_pairs={{0,4},{1,5},{2,6},{3,7},{4,0},{5,1},{6,2},{7,3},{8,12},{9,13},{10,... | collective-permute-start | bytes 270344 | tf_op jit(solution)/shard_map/ppermute | solution.py:382
  63.2 5.7 %collective-permute-start.7 = (bf16[176,128]{1,0:T(8,128)(2,1)S(1)}, bf16[176,128]{1,0:T(8,128)(2,1)S(1)}, u32[]{:S(2)}, u32[]{:S(2)}) collective-permute-start(bf16[176,128]{1,0:T(8,128)(2,1)S(1)} %slice.270), channel_id=1, source_target_pairs={{0,8},{1,9},{2,10},{3,11},{4,12},{5,13},{6,14},{7,15},{8,0},{9,1},... | collective-permute-start | bytes 135176 | tf_op jit(solution)/shard_map/ppermute | solution.py:382
  66.7 6.0 %collective-permute-start.13 = (bf16[704,128]{1,0:T(8,128)(2,1)S(1)}, bf16[704,128]{1,0:T(8,128)(2,1)S(1)}, u32[]{:S(2)}, u32[]{:S(2)}) collective-permute-start(bf16[704,128]{1,0:T(8,128)(2,1)S(1)} %slice.260), channel_id=1, source_target_pairs={{0,2},{1,3},{2,0},{3,1},{4,6},{5,7},{6,4},{7,5},{8,10},{9,11},{10,... | collective-permute-start | bytes 540680 | tf_op jit(solution)/shard_map/ppermute | solution.py:382
  68.9 5.4 %collective-permute-start.8 = (bf16[176,128]{1,0:T(8,128)(2,1)S(1)}, bf16[176,128]{1,0:T(8,128)(2,1)S(1)}, u32[]{:S(2)}, u32[]{:S(2)}) collective-permute-start(bf16[176,128]{1,0:T(8,128)(2,1)S(1)} %fusion.12), channel_id=1, source_target_pairs={{0,8},{1,9},{2,10},{3,11},{4,12},{5,13},{6,14},{7,15},{8,0},{9,1},... | collective-permute-start | bytes 135176 | tf_op jit(solution)/shard_map/ppermute | solution.py:382
  72.7 4.6 %collective-permute-start.14 = (bf16[352,128]{1,0:T(8,128)(2,1)S(1)}, bf16[352,128]{1,0:T(8,128)(2,1)S(1)}, u32[]{:S(2)}, u32[]{:S(2)}) collective-permute-start(bf16[352,128]{1,0:T(8,128)(2,1)S(1)} %slice.265), channel_id=1, source_target_pairs={{0,4},{1,5},{2,6},{3,7},{4,0},{5,1},{6,2},{7,3},{8,12},{9,13},{10,... | collective-permute-start | bytes 270344 | tf_op jit(solution)/shard_map/ppermute | solution.py:382
  74.4 5.1 %collective-permute-start.9 = (bf16[352,128]{1,0:T(8,128)(2,1)S(1)}, bf16[352,128]{1,0:T(8,128)(2,1)S(1)}, u32[]{:S(2)}, u32[]{:S(2)}) collective-permute-start(bf16[352,128]{1,0:T(8,128)(2,1)S(1)} %pad_maximum_fusion.11), channel_id=1, source_target_pairs={{0,4},{1,5},{2,6},{3,7},{4,0},{5,1},{6,2},{7,3},{8,12},{9,13},{10,... | collective-permute-start | bytes 270344 | tf_op jit(solution)/shard_map/ppermute | solution.py:382
  77.4 6.2 %collective-permute-start.15 = (bf16[176,128]{1,0:T(8,128)(2,1)S(1)}, bf16[176,128]{1,0:T(8,128)(2,1)S(1)}, u32[]{:S(2)}, u32[]{:S(2)}) collective-permute-start(bf16[176,128]{1,0:T(8,128)(2,1)S(1)} %slice.269), channel_id=1, source_target_pairs={{0,8},{1,9},{2,10},{3,11},{4,12},{5,13},{6,14},{7,15},{8,0},{9,1},... | collective-permute-start | bytes 135176 | tf_op jit(solution)/shard_map/ppermute | solution.py:382
  79.5 5.6 %collective-permute-start.10 = (bf16[704,128]{1,0:T(8,128)(2,1)S(1)}, bf16[704,128]{1,0:T(8,128)(2,1)S(1)}, u32[]{:S(2)}, u32[]{:S(2)}) collective-permute-start(bf16[704,128]{1,0:T(8,128)(2,1)S(1)} %pad_maximum_fusion.7), channel_id=1, source_target_pairs={{0,2},{1,3},{2,0},{3,1},{4,6},{5,7},{6,4},{7,5},{8,10},{9,11},{10,... | collective-permute-start | bytes 540680 | tf_op jit(solution)/shard_map/ppermute | solution.py:382
  83.6 5.0 %collective-permute-start.24 = (bf16[176,128]{1,0:T(8,128)(2,1)S(1)}, bf16[176,128]{1,0:T(8,128)(2,1)S(1)}, u32[]{:S(2)}, u32[]{:S(2)}) collective-permute-start(bf16[176,128]{1,0:T(8,128)(2,1)S(1)} %fusion.11), channel_id=1, source_target_pairs={{0,8},{1,9},{2,10},{3,11},{4,12},{5,13},{6,14},{7,15},{8,0},{9,1},... | collective-permute-start | bytes 135176 | tf_op jit(solution)/shard_map/ppermute | solution.py:382
  85.1 8.8 %collective-permute-start.11 = (bf16[1408,128]{1,0:T(8,128)(2,1)S(1)}, bf16[1408,128]{1,0:T(8,128)(2,1)S(1)}, u32[]{:S(2)}, u32[]{:S(2)}) collective-permute-start(bf16[1408,128]{1,0:T(8,128)(2,1)S(1)} %pad_maximum_fusion.2.near), channel_id=1, source_target_pairs={{0,1},{1,0},{2,3},{3,2},{4,5},{5,4},{6,7},{7,6},{8,9},{9,8},{10,11... | collective-permute-start | bytes 1081352 | tf_op jit(solution)/shard_map/ppermute | solution.py:382
  88.6 4.6 %collective-permute-start.25 = (bf16[352,128]{1,0:T(8,128)(2,1)S(1)}, bf16[352,128]{1,0:T(8,128)(2,1)S(1)}, u32[]{:S(2)}, u32[]{:S(2)}) collective-permute-start(bf16[352,128]{1,0:T(8,128)(2,1)S(1)} %pad_maximum_fusion.13), channel_id=1, source_target_pairs={{0,4},{1,5},{2,6},{3,7},{4,0},{5,1},{6,2},{7,3},{8,12},{9,13},{10,... | collective-permute-start | bytes 270344 | tf_op jit(solution)/shard_map/ppermute | solution.py:382
  93.2 7.5 %collective-permute-start.26 = (bf16[704,128]{1,0:T(8,128)(2,1)S(1)}, bf16[704,128]{1,0:T(8,128)(2,1)S(1)}, u32[]{:S(2)}, u32[]{:S(2)}) collective-permute-start(bf16[704,128]{1,0:T(8,128)(2,1)S(1)} %pad_maximum_fusion.9), channel_id=1, source_target_pairs={{0,2},{1,3},{2,0},{3,1},{4,6},{5,7},{6,4},{7,5},{8,10},{9,11},{10,... | collective-permute-start | bytes 540680 | tf_op jit(solution)/shard_map/ppermute | solution.py:382
  109.8 7.4 %collective-permute-start.17 = (bf16[704,128]{1,0:T(8,128)(2,1)S(1)}, bf16[704,128]{1,0:T(8,128)(2,1)S(1)}, u32[]{:S(2)}, u32[]{:S(2)}) collective-permute-start(bf16[704,128]{1,0:T(8,128)(2,1)S(1)} %slice.259), channel_id=1, source_target_pairs={{0,2},{1,3},{2,0},{3,1},{4,6},{5,7},{6,4},{7,5},{8,10},{9,11},{10,... | collective-permute-start | bytes 540680 | tf_op jit(solution)/shard_map/ppermute | solution.py:382
  111.5 9.1 %collective-permute-start.29 = (bf16[704,128]{1,0:T(8,128)(2,1)S(1)}, bf16[704,128]{1,0:T(8,128)(2,1)S(1)}, u32[]{:S(2)}, u32[]{:S(2)}) collective-permute-start(bf16[704,128]{1,0:T(8,128)(2,1)S(1)} %slice.258), channel_id=1, source_target_pairs={{0,2},{1,3},{2,0},{3,1},{4,6},{5,7},{6,4},{7,5},{8,10},{9,11},{10,... | collective-permute-start | bytes 540680 | tf_op jit(solution)/shard_map/ppermute | solution.py:382
  117.3 4.6 %collective-permute-start.18 = (bf16[352,128]{1,0:T(8,128)(2,1)S(1)}, bf16[352,128]{1,0:T(8,128)(2,1)S(1)}, u32[]{:S(2)}, u32[]{:S(2)}) collective-permute-start(bf16[352,128]{1,0:T(8,128)(2,1)S(1)} %slice.264), channel_id=1, source_target_pairs={{0,4},{1,5},{2,6},{3,7},{4,0},{5,1},{6,2},{7,3},{8,12},{9,13},{10,... | collective-permute-start | bytes 270344 | tf_op jit(solution)/shard_map/ppermute | solution.py:382
  120.6 4.7 %collective-permute-start.30 = (bf16[352,128]{1,0:T(8,128)(2,1)S(1)}, bf16[352,128]{1,0:T(8,128)(2,1)S(1)}, u32[]{:S(2)}, u32[]{:S(2)}) collective-permute-start(bf16[352,128]{1,0:T(8,128)(2,1)S(1)} %slice.263), channel_id=1, source_target_pairs={{0,4},{1,5},{2,6},{3,7},{4,0},{5,1},{6,2},{7,3},{8,12},{9,13},{10,... | collective-permute-start | bytes 270344 | tf_op jit(solution)/shard_map/ppermute | solution.py:382
  121.9 6.1 %collective-permute-start.19 = (bf16[176,128]{1,0:T(8,128)(2,1)S(1)}, bf16[176,128]{1,0:T(8,128)(2,1)S(1)}, u32[]{:S(2)}, u32[]{:S(2)}) collective-permute-start(bf16[176,128]{1,0:T(8,128)(2,1)S(1)} %slice.268), channel_id=1, source_target_pairs={{0,8},{1,9},{2,10},{3,11},{4,12},{5,13},{6,14},{7,15},{8,0},{9,1},... | collective-permute-start | bytes 135176 | tf_op jit(solution)/shard_map/ppermute | solution.py:382
  125.3 5.2 %collective-permute-start.31 = (bf16[176,128]{1,0:T(8,128)(2,1)S(1)}, bf16[176,128]{1,0:T(8,128)(2,1)S(1)}, u32[]{:S(2)}, u32[]{:S(2)}) collective-permute-start(bf16[176,128]{1,0:T(8,128)(2,1)S(1)} %slice.267), channel_id=1, source_target_pairs={{0,8},{1,9},{2,10},{3,11},{4,12},{5,13},{6,14},{7,15},{8,0},{9,1},... | collective-permute-start | bytes 135176 | tf_op jit(solution)/shard_map/ppermute | solution.py:382
  128.1 5.2 %collective-permute-start.20 = (bf16[176,128]{1,0:T(8,128)(2,1)S(1)}, bf16[176,128]{1,0:T(8,128)(2,1)S(1)}, u32[]{:S(2)}, u32[]{:S(2)}) collective-permute-start(bf16[176,128]{1,0:T(8,128)(2,1)S(1)} %add_convert_fusion.1), channel_id=1, source_target_pairs={{0,8},{1,9},{2,10},{3,11},{4,12},{5,13},{6,14},{7,15},{8,0},{9,1},... | collective-permute-start | bytes 135176 | tf_op jit(solution)/shard_map/ppermute | solution.py:382
  130.6 5.2 %collective-permute-start.32 = (bf16[176,128]{1,0:T(8,128)(2,1)S(1)}, bf16[176,128]{1,0:T(8,128)(2,1)S(1)}, u32[]{:S(2)}, u32[]{:S(2)}) collective-permute-start(bf16[176,128]{1,0:T(8,128)(2,1)S(1)} %add_convert_fusion), channel_id=1, source_target_pairs={{0,8},{1,9},{2,10},{3,11},{4,12},{5,13},{6,14},{7,15},{8,0},{9,1},... | collective-permute-start | bytes 135176 | tf_op jit(solution)/shard_map/ppermute | solution.py:382
  133.3 4.6 %collective-permute-start.21 = (bf16[352,128]{1,0:T(8,128)(2,1)S(1)}, bf16[352,128]{1,0:T(8,128)(2,1)S(1)}, u32[]{:S(2)}, u32[]{:S(2)}) collective-permute-start(bf16[352,128]{1,0:T(8,128)(2,1)S(1)} %pad_maximum_fusion.12), channel_id=1, source_target_pairs={{0,4},{1,5},{2,6},{3,7},{4,0},{5,1},{6,2},{7,3},{8,12},{9,13},{10,... | collective-permute-start | bytes 270344 | tf_op jit(solution)/shard_map/ppermute | solution.py:382
  137.9 5.6 %collective-permute-start.22 = (bf16[704,128]{1,0:T(8,128)(2,1)S(1)}, bf16[704,128]{1,0:T(8,128)(2,1)S(1)}, u32[]{:S(2)}, u32[]{:S(2)}) collective-permute-start(bf16[704,128]{1,0:T(8,128)(2,1)S(1)} %pad_maximum_fusion.8), channel_id=1, source_target_pairs={{0,2},{1,3},{2,0},{3,1},{4,6},{5,7},{6,4},{7,5},{8,10},{9,11},{10,... | collective-permute-start | bytes 540680 | tf_op jit(solution)/shard_map/ppermute | solution.py:382
  140.3 5.6 %collective-permute-start.34 = (bf16[704,128]{1,0:T(8,128)(2,1)S(1)}, bf16[704,128]{1,0:T(8,128)(2,1)S(1)}, u32[]{:S(2)}, u32[]{:S(2)}) collective-permute-start(bf16[704,128]{1,0:T(8,128)(2,1)S(1)} %pad_maximum_fusion.10), channel_id=1, source_target_pairs={{0,2},{1,3},{2,0},{3,1},{4,6},{5,7},{6,4},{7,5},{8,10},{9,11},{10,... | collective-permute-start | bytes 540680 | tf_op jit(solution)/shard_map/ppermute | solution.py:382
  145.9 7.2 %collective-permute-start.35 = (bf16[1408,128]{1,0:T(8,128)(2,1)S(1)}, bf16[1408,128]{1,0:T(8,128)(2,1)S(1)}, u32[]{:S(2)}, u32[]{:S(2)}) collective-permute-start(bf16[1408,128]{1,0:T(8,128)(2,1)S(1)} %pad_maximum_fusion.5.near), channel_id=1, source_target_pairs={{0,1},{1,0},{2,3},{3,2},{4,5},{5,4},{6,7},{7,6},{8,9},{9,8},{10,11... | collective-permute-start | bytes 1081352 | tf_op jit(solution)/shard_map/ppermute | solution.py:382
  164.0 14.3 %collective-permute-start.37 = (bf16[2048,128]{1,0:T(8,128)(2,1)S(1)}, bf16[2048,128]{1,0:T(8,128)(2,1)S(1)}, u32[]{:S(2)}, u32[]{:S(2)}) collective-permute-start(bf16[2048,128]{1,0:T(8,128)(2,1)S(1)} %slice.256), channel_id=1, source_target_pairs={{0,2},{1,3},{2,0},{3,1},{4,6},{5,7},{6,4},{7,5},{8,10},{9,11},{10,... | collective-permute-start | bytes 1572872 | tf_op jit(solution)/shard_map/ppermute | solution.py:382
  178.3 7.8 %collective-permute-start.38 = (bf16[1024,128]{1,0:T(8,128)(2,1)S(1)}, bf16[1024,128]{1,0:T(8,128)(2,1)S(1)}, u32[]{:S(2)}, u32[]{:S(2)}) collective-permute-start(bf16[1024,128]{1,0:T(8,128)(2,1)S(1)} %slice.257), channel_id=1, source_target_pairs={{0,4},{1,5},{2,6},{3,7},{4,0},{5,1},{6,2},{7,3},{8,12},{9,13},{10,... | collective-permute-start | bytes 786440 | tf_op jit(solution)/shard_map/ppermute | solution.py:382
  186.3 7.6 %collective-permute-start.39 = (bf16[512,128]{1,0:T(8,128)(2,1)S(1)}, bf16[512,128]{1,0:T(8,128)(2,1)S(1)}, u32[]{:S(2)}, u32[]{:S(2)}) collective-permute-start(bf16[512,128]{1,0:T(8,128)(2,1)S(1)} %slice.262), channel_id=1, source_target_pairs={{0,8},{1,9},{2,10},{3,11},{4,12},{5,13},{6,14},{7,15},{8,0},{9,1},... | collective-permute-start | bytes 393224 | tf_op jit(solution)/shard_map/ppermute | solution.py:382
  (12 other events, 61.8 us)

commit v5 on v3

v5 whole, which is shorter than its diff:
```python
import functools
import math

import jax
import jax.numpy as jnp
from jax import lax
from jax.experimental import pallas as pl
from jax.experimental.pallas import tpu as pltpu
from jax.sharding import PartitionSpec as P

BLOCK = 64
SLOTS = 16
PATCHES = 64
ITERS = 3
MEAN_LIVE = 10
LANES = 2 * BLOCK
SLOT_PAIRS = SLOTS // 2
SPARE = SLOT_PAIRS + 2
ROW_TILE = 16
SUPPORT_PARTS = 4
PIECE = 5
MATRIX_UNIT = 256
VMEM_MARGIN = 3 * 1024 * 1024
SUPPORT_VMEM = 40 * 1024 * 1024
HELD_BYTES = 65 * 1024 * 1024


def momentum_list():
    values = []
    tvalue = 1.0
    for turn in range(ITERS):
        tnext = (1.0 + (1.0 + 4.0 * tvalue * tvalue) ** 0.5) / 2.0
        values.append((tvalue - 1.0) / tnext)
        tvalue = tnext
    return values


def swap_halves(value):
    return jnp.concatenate([value[:, BLOCK:], value[:, :BLOCK]], axis=1)


def upper_half(shape):
    return lax.broadcasted_iota(jnp.int32, shape, 1) >= BLOCK


def group_at(index, seq, order, counts):
    position = seq[index]
    group = order[position]
    return position, group, counts[group]


def support_kernel(begin, seq, order, support, counts, dictionary, *refs):
    out, held, picks, ids, sems, out_sems = refs[-6:]
    entries, rows, _ = held.shape
    pairs = entries // 2

    def fetch(entry, block):
        start = pl.multiple_of((block // 2) * LANES, LANES)
        return pltpu.make_async_copy(dictionary.at[:, pl.ds(start, LANES)], held.at[entry], sems.at[entry])

    def start_group(index, offset):
        _, group, live = group_at(index, seq, order, counts)

        def start_slot(slot, carry):
            block = support[group, slot]
            ids[offset + slot] = block
            fetch(offset + slot, block).start()
            return carry

        lax.fori_loop(jnp.clip(-offset, 0, live), jnp.clip(entries - offset, 0, live), start_slot, 0)
        return offset + live

    lax.fori_loop(0, order.shape[0], start_group, jnp.int32(-begin))
    shape = (2 * LANES, LANES)
    source = lax.broadcasted_iota(jnp.int32, shape, 0)
    target = lax.broadcasted_iota(jnp.int32, shape, 1)
    for choice in range(4):
        wanted = jnp.where(target < BLOCK, (choice % 2) * BLOCK + target, LANES + (choice // 2) * BLOCK + target - BLOCK)
        picks[choice] = (source == wanted).astype(jnp.float32).astype(jnp.bfloat16)

    def store(pair):
        return pltpu.make_async_copy(held.at[2 * pair], out.at[begin // 2 + pair], out_sems.at[pair])

    def pack(step, carry):
        for entry in range(4):
            index = 4 * step + entry
            fetch(index, ids[index]).wait()
        packed = []
        for pair in (2 * step, 2 * step + 1):
            choice = ids[2 * pair] % 2 + 2 * (ids[2 * pair + 1] % 2)
            both = jnp.concatenate([held[2 * pair], held[2 * pair + 1]], axis=1)
            packed.append(jnp.dot(both, picks[choice], preferred_element_type=jnp.float32).astype(jnp.bfloat16))
        for pair, value in zip((2 * step, 2 * step + 1), packed):
            held[2 * pair] = value
            store(pair).start()
        return carry

    lax.fori_loop(0, pairs // 2, pack, 0)

    def drain(pair, carry):
        store(pair).wait()
        return carry

    lax.fori_loop(0, pairs, drain, 0)


def collect_support(seq, order, support, counts, dictionary, pairs, part, *before):
    rows = dictionary.shape[0]
    pairs = pairs // SUPPORT_PARTS
    entries = 2 * pairs
    return pl.pallas_call(
        functools.partial(support_kernel, part * entries),
        grid_spec=pltpu.PrefetchScalarGridSpec(
            num_scalar_prefetch=4,
            grid=(),
            in_specs=[pl.BlockSpec(memory_space=pltpu.HBM)] * (1 + len(before)),
            out_specs=pl.BlockSpec(memory_space=pltpu.HBM),
            scratch_shapes=[
                pltpu.VMEM((entries, rows, LANES), dictionary.dtype),
                pltpu.VMEM((4, 2 * LANES, LANES), jnp.bfloat16),
                pltpu.SMEM((entries,), jnp.int32),
                pltpu.SemaphoreType.DMA((entries,)),
                pltpu.SemaphoreType.DMA((pairs,)),
            ],
        ),
        out_shape=jax.ShapeDtypeStruct((HELD_BYTES // (rows * LANES * 2), rows, LANES), dictionary.dtype),
        compiler_params=pltpu.CompilerParams(vmem_limit_bytes=SUPPORT_VMEM),
        cost_estimate=pl.CostEstimate(flops=0, transcendentals=0, bytes_accessed=6 * pairs * rows * LANES * 2),
        input_output_aliases={5: 0} if before else {},
        name="collect_support",
    )(seq, order, support, counts, dictionary, *before)


def stage_orders(devices):
    distances = [2**bit for bit in range(devices.bit_length() - 1)]
    return distances, distances[:1] + distances[2:] + distances[1:2]


def slot_distance(slot, distances):
    bits = reversed(range(len(distances)))
    return sum(distance for bit, distance in zip(bits, distances) if slot >> bit & 1)


def gradient_kernel(mode, shards, pairs, seq, order, counts, own, blocks, near, far, targets, *refs):
    refs = list(refs)
    take = lambda: refs.pop(0)
    if mode == "first":
        thresh = take()
    keep, send = take(), take()
    if mode == "first":
        start_out, thresh_out = take(), take()
    if mode == "final":
        sent = take()
    held, codes, total = take(), take(), take()
    if mode == "first":
        starts, limits = take(), take()
    offsets, sems = refs

    groups = order.shape[0]
    pieces = pairs // PIECE
    me = own[0]

    def load(index):
        span = pl.ds(index * PIECE, PIECE)
        return pltpu.make_async_copy(blocks.at[span], held.at[span], sems.at[index])

    for index in range(pieces):
        load(index).start()
    held[pairs:] = jnp.zeros((SPARE,) + held.shape[1:], held.dtype)

    orders = stage_orders(shards)

    def holder(slot):
        far_half = slot >= shards // 2
        even = slot_distance(slot, orders[1 if far_half else 0])
        odd = slot_distance(slot, orders[0 if far_half else 1])
        return jnp.where(me % 2 == 0, even, odd) ^ me

    def shard_span(slot, size):
        return pl.ds(pl.multiple_of(holder(slot) * size, ROW_TILE), size)

    size_in = 2 * near.shape[0] // shards
    for slot in range(shards):
        source = near if slot < shards // 2 else far
        begin = slot % (shards // 2) * size_in
        codes[shard_span(slot, size_in), :] = source[begin : begin + size_in, :]

    def seat(index, offset):
        position, _, live = group_at(index, seq, order, counts)
        offsets[position] = offset
        return offset + live

    lax.fori_loop(0, groups, seat, jnp.int32(0))

    upper = upper_half((PATCHES, LANES))
    side = upper.astype(jnp.int32)

    def tile(pair):
        return pl.ds(pl.multiple_of(pair * PATCHES, PATCHES), PATCHES)

    def shifted(parts, count, odd, ahead):
        turned = [swap_halves(part) for part in parts]
        last = len(parts) - 1
        moved = []
        for pair in range(count):
            low, high = (pair, pair + 1) if ahead else (pair - 1, pair)
            low, high = min(max(low, 0), last), min(max(high, 0), last)
            value = jnp.where(upper[: turned[low].shape[0]], turned[high], turned[low])
            moved.append(jnp.where(odd, value, parts[min(pair, last)]))
        return moved

    def read_codes(position, offset, live, count):
        first = offset // 2
        if mode == "first":
            parts = [codes[tile(position * SLOT_PAIRS + pair), :] for pair in range(min(count, SLOT_PAIRS))]
            parts = shifted(parts, count, offset % 2 == 1, False)
        else:
            parts = [codes[tile(first + pair), :] for pair in range(count)]
        masked = []
        for pair, part in enumerate(parts):
            entry = 2 * (first + pair) + side
            mine = (entry >= offset) & (entry < offset + live)
            masked.append(jnp.where(mine, part, jnp.zeros_like(part)))
        return masked

    def write_packed(ref, parts, offset):
        first = offset // 2
        for pair, part in enumerate(parts):
            if pair == 0:
                part = jnp.where(upper | (offset % 2 == 0), part, ref[tile(first), :])
            ref[tile(first + pair), :] = part

    def one_group(position, group, offset, live, count):
        first = offset // 2
        parts = read_codes(position, offset, live, count)
        if mode == "first":
            write_packed(starts, parts, offset)
            write_packed(limits, [thresh[group]] * count, offset)
        matrix = jnp.concatenate([held[first + pair] for pair in range(count)], axis=1)
        point = jnp.concatenate(parts, axis=1)
        residual = lax.dot_general(point, matrix, (((1,), (1,)), ((), ())), preferred_element_type=jnp.float32)
        target = targets[tile(group), :].astype(jnp.float32)
        residual = (residual - target).astype(jnp.bfloat16)
        gradient = jnp.dot(residual, matrix, preferred_element_type=jnp.float32)
        write_packed(total, [gradient[:, pair * LANES : (pair + 1) * LANES] for pair in range(count)], offset)

    def wait_piece(index, carry):
        load(index).wait()
        return carry

    def two_groups(step, waited):
        picks = []
        chunks = 1
        for index in (2 * step, 2 * step + 1):
            position, group, live = group_at(index, seq, order, counts)
            offset = offsets[position]
            picks.append((position, group, offset, live))
            chunks = jnp.maximum(chunks, (live + offset % 2 + 3) // 4)
        reach = jnp.minimum(picks[1][2] // 2 + 2 * chunks - 1, pairs - 1)
        needed = jnp.maximum(reach // PIECE + 1, waited)
        lax.fori_loop(waited, needed, wait_piece, 0)
        for count in range(1, SLOTS // 4 + 2):

            @pl.when(chunks == count)
            def _(count=count):
                for pick in picks:
                    one_group(*pick, 2 * count)

        return needed

    waited = lax.fori_loop(0, groups // 2, two_groups, jnp.int32(0))
    lax.fori_loop(waited, pieces, wait_piece, 0)

    if mode != "final":
        size = 2 * keep.shape[0] // shards
        for slot in range(shards):
            begin = slot % (shards // 2) * size
            value = total[shard_span(slot, size), :]
            if slot < shards // 2:
                keep[begin : begin + size, :] = value
            else:
                send[begin : begin + size, :] = value.astype(send.dtype)
    if mode == "first":
        size = start_out.shape[0]
        span = pl.ds(pl.multiple_of(me * size, ROW_TILE), size)
        start_out[...] = starts[span, :]
        thresh_out[...] = limits[span, :]
    if mode == "final":
        offset = offsets[me]
        parts = read_codes(me, offset, counts[order[me]], SLOT_PAIRS + 1)
        for pair, part in enumerate(shifted(parts, SLOT_PAIRS, offset % 2 == 1, True)):
            sent[pair] = part
        for slot in range(shards):
            position = holder(slot)
            offset = offsets[position]
            live = counts[order[position]]
            parts = [total[tile(offset // 2 + pair), :] for pair in range(SLOT_PAIRS + 1)]
            begin = slot % (shards // 2) * SLOT_PAIRS * PATCHES
            for pair, part in enumerate(shifted(parts, SLOT_PAIRS, offset % 2 == 1, True)):
                value = jnp.where(2 * pair + side < live, part, 0.0)
                rows = slice(begin + pair * PATCHES, begin + (pair + 1) * PATCHES)
                if slot < shards // 2:
                    keep[rows, :] = value
                else:
                    send[rows, :] = value.astype(send.dtype)


def gradient_call(mode, shards, pairs, scalars, blocks, near, far, targets, extra=()):
    rows = blocks.shape[1]
    places = pairs + SPARE
    groups = scalars[1].shape[0]
    single, double = jnp.bfloat16, jnp.float32
    packed = (places * PATCHES, LANES)
    half_out = (groups * SLOT_PAIRS if mode == "final" else pairs) * PATCHES // 2
    shard = (2 * half_out // shards, LANES)
    outs = [((half_out, LANES), double), ((half_out, LANES), single)]
    if mode == "first":
        outs += [(shard, single), (shard, double)]
    if mode == "final":
        outs += [((SLOT_PAIRS, PATCHES, LANES), single)]
    codes = groups * SLOT_PAIRS * PATCHES if mode == "first" else packed[0]
    scratch = [((places, rows, LANES), single), ((codes, LANES), single), (packed, double)]
    if mode == "first":
        scratch += [(packed, single), (packed, double)]
    room = sum(math.prod(shape) * jnp.dtype(kind).itemsize for shape, kind in scratch)
    return pl.pallas_call(
        functools.partial(gradient_kernel, mode, shards, pairs),
        grid_spec=pltpu.PrefetchScalarGridSpec(
            num_scalar_prefetch=4,
            grid=(),
            in_specs=[pl.BlockSpec(memory_space=pltpu.HBM)]
            + [pl.BlockSpec(memory_space=pltpu.VMEM)] * (3 + len(extra)),
            out_specs=[pl.BlockSpec(memory_space=pltpu.VMEM)] * len(outs),
            scratch_shapes=[pltpu.VMEM(shape, kind) for shape, kind in scratch]
            + [pltpu.SMEM((groups,), jnp.int32), pltpu.SemaphoreType.DMA((pairs // PIECE,))],
        ),
        out_shape=[jax.ShapeDtypeStruct(shape, kind) for shape, kind in outs],
        compiler_params=pltpu.CompilerParams(vmem_limit_bytes=room + VMEM_MARGIN),
        cost_estimate=pl.CostEstimate(
            flops=4 * pairs * rows * LANES * MATRIX_UNIT, transcendentals=0, bytes_accessed=pairs * rows * LANES * 2
        ),
        name="gradient",
    )(*scalars, blocks, near, far, targets, *extra)


def exchange(value, stage):
    devices = lax.axis_size("rows")
    orders = stage_orders(devices)
    return lax.ppermute(value, "rows", [(i, i ^ orders[i % 2][stage]) for i in range(devices)])


def gather_shards(own, beside=()):
    value, made = own, ()
    stages = len(stage_orders(lax.axis_size("rows"))[0])
    steps = list(beside)
    for stage in reversed(range(1, stages)):
        value = jnp.concatenate([value, exchange(value, stage)], axis=0)
        if steps:
            value, *made = lax.optimization_barrier((value, steps.pop(0)(*made)))
    for step in steps:
        value, *made = lax.optimization_barrier((value, step(*made)))
    return value, exchange(value, 0), made


def reduce_shards(keep, send):
    total = keep + exchange(send, 0).astype(jnp.float32)
    for stage in range(1, len(stage_orders(lax.axis_size("rows"))[0])):
        middle = total.shape[0] // 2
        total = total[:middle] + exchange(total[middle:].astype(jnp.bfloat16), stage).astype(jnp.float32)
    return total


def packed_order(live):
    index = jnp.arange(live.shape[0])
    ahead = (live[None, :] > live[:, None]) | ((live[None, :] == live[:, None]) & (index[None, :] < index[:, None]))
    rank = jnp.sum(ahead.astype(jnp.int32), axis=1)
    return jnp.sum(jnp.where(rank[:, None] == index[None, :], index[:, None], 0), axis=0).astype(jnp.int32)


def shrink(value, thresh):
    return value - jnp.clip(value, -thresh, thresh)


def local(dictionary, patches, initial_codes, support, counts, group_order, penalty):
    groups = group_order.shape[0]
    position = lax.axis_index("rows")
    devices = lax.axis_size("rows")
    momenta = momentum_list()
    pairs = MEAN_LIVE * groups // 2

    laid = initial_codes.reshape(SLOT_PAIRS, 2, PATCHES, BLOCK).transpose(0, 2, 1, 3)
    laid = laid.reshape(SLOT_PAIRS * PATCHES, LANES)
    seq = packed_order(jnp.take(counts, group_order))
    collect = functools.partial(collect_support, seq, group_order, support, counts, dictionary, pairs)
    near, far, (blocks,) = gather_shards(laid, [functools.partial(collect, part) for part in range(SUPPORT_PARTS)])

    scalars = (seq, group_order, counts, position.astype(jnp.int32).reshape(1))
    targets = patches.T
    half_penalty = 0.5 * penalty
    thresh_tiles = jnp.broadcast_to(half_penalty[:, :, None], (groups, PATCHES, LANES))
    own_thresh = lax.dynamic_index_in_dim(half_penalty, group_order[position], 0, False)[None, :, None]

    run = functools.partial(gradient_call, shards=devices, pairs=pairs, scalars=scalars, blocks=blocks, targets=targets)
    keep, send, start, thresh = run("first", near=near, far=far, extra=(thresh_tiles,))
    point = previous = start.astype(jnp.float32)
    for turn in range(ITERS - 1):
        if turn:
            keep, send = run("packed", near=near, far=far)
        current = shrink(point - 0.5 * reduce_shards(keep, send), thresh)
        point = current + momenta[turn] * (current - previous)
        previous = current
        near, far, _ = gather_shards(point.astype(jnp.bfloat16))
    keep, send, sent = run("final", near=near, far=far)
    gradient = reduce_shards(keep, send).reshape(SLOT_PAIRS, PATCHES, LANES)
    sent = sent.astype(jnp.float32)
    result = shrink(sent - 0.5 * gradient, own_thresh)
    result = result.reshape(SLOT_PAIRS, PATCHES, 2, BLOCK).transpose(0, 2, 1, 3)
    return result.reshape(1, SLOTS, PATCHES * BLOCK)


def solution(mesh):
    in_specs = (
        P("rows", None),
        P("rows", "groups"),
        P(("groups", "rows"), None, None),
        P("groups", None),
        P("groups"),
        P("groups"),
        P("groups", None),
    )
    out_specs = P(("groups", "rows"), None, None)
    return jax.shard_map(local, mesh=mesh, in_specs=in_specs, out_specs=out_specs, check_vma=False)
```

time: 227 us -> 198 us (0.87)
  waiting for transfers between devices: 78.4 us -> 108 us
  Pallas kernels: 80.4 us -> 60.9 us
  local copies, waits for them, and re-layouts: 24.9 us -> 6.07 us
  starting transfers between devices: 37.5 us -> 19 us
    ppermute x40 -> x24, waiting for transfers between devices: 78.4 us -> 108 us  [exchange(): lax.ppermute(value, 'rows', [(i, i ^ orders[i % 2][stage]) for i in range...]
    pallas_call x8 -> x7, Pallas kernels: 80.4 us -> 60.9 us  [the longest x3 35.8 us: gradient_call(): pl.pallas_call(functools.partial(gradient_kernel, mode, shards, pairs), g...]
    ppermute x40 -> x24, starting transfers between devices: 37.5 us -> 19 us  [exchange(): lax.ppermute(value, 'rows', [(i, i ^ orders[i % 2][stage]) for i in range...]
    unnamed x23 -> x9, local copies, waits for them, and re-layouts: 19.7 us -> 1.52 us
  transfers between devices with their start and end apart: 40 -> 24, of which waited for: 29 -> 23; matrix products, arithmetic and copies ran while one was open for 3% -> 2% of each run, Pallas kernels for 29% -> 9%
where the time goes in v5:
time: 198 us
  waiting for transfers between devices  108 us (55%)
  Pallas kernels  60.9 us (31%)
  starting transfers between devices  19 us (10%)
  local copies, waits for them, and re-layouts  6.07 us (3%)
  between operations  2.35 us (1%)
    ppermute x24, waiting for transfers between devices, exchange(): lax.ppermute(value, 'rows', [(i, i ^ orders[i % 2][stage]) for i in range...  108 us
    pallas_call x3, Pallas kernels, gradient_call(): pl.pallas_call(functools.partial(gradient_kernel, mode, shards, pairs), g...  35.8 us
    pallas_call x4, Pallas kernels, collect_support(): pl.pallas_call(functools.partial(support_kernel, part * entries), grid_sp...  25.1 us
    ppermute x24, starting transfers between devices, exchange(): lax.ppermute(value, 'rows', [(i, i ^ orders[i % 2][stage]) for i in range...  19 us
  transfers between devices with their start and end apart: 24, of which 23 were waited for; matrix products, arithmetic and copies ran while one was open for 2% of the time, Pallas kernels for 9%

profile of v5, /device:TPU:0, one launch (start us, length us, event | category | flops | bytes accessed | tf_op | source)
XLA Modules:
  0.0 198.4 jit_solution(12323833069573822207)
XLA Ops:
  1.7 4.1 %collective-permute-start = (bf16[512,128]{1,0:T(8,128)(2,1)S(1)}, bf16[512,128]{1,0:T(8,128)(2,1)S(1)}, u32[]{:S(2)}, u32[]{:S(2)}) collective-permute-start(bf16[512,128]{1,0:T(8,128)(2,1)S(1)} %reshape.43), channel_id=1, source_target_pairs={{0,8},{1,3},{2,10},{3,1},{4,12},{5,7},{6,14},{7,5},{8,0},{9,11},{1... | collective-permute-start | bytes 393224 | tf_op jit(solution)/shard_map/ppermute | solution.py:349
  6.8 6.2 %collect_support.4.refs_0_ = bf16[520,512,128]{2,1,0:T(8,128)(2,1)} custom-call(s32[16]{0:T(128)S(1)} %select_reduce_fusion.seq, s32[16]{0:T(128)S(1)} %copy-done.2, s32[16,16]{1,0:T(8,128)S(1)} %copy-done.1, s32[16]{0:T(128)S(1)} %copy-done, bf16[512,32768]{1,0:T(8,128)(2,1)} %dictionary.7), custom_call_target="tpu_custom_call" | custom-call | bytes 15728640 | tf_op jit(solution)/shard_map/collect_support/pallas_call | solution.py:111
  13.0 1.7 collective-permute-start.1
  14.6 6.3 %collect_support.5.refs_0_ = bf16[520,512,128]{2,1,0:T(8,128)(2,1)} custom-call(s32[16]{0:T(128)S(1)} %select_reduce_fusion.seq, s32[16]{0:T(128)S(1)} %copy-done.2, s32[16,16]{1,0:T(8,128)S(1)} %copy-done.1, s32[16]{0:T(128)S(1)} %copy-done, bf16[512,32768]{1,0:T(8,128)(2,1)} %dictionary.7, ...), custom_call_target="tpu_custom_call", output_to_operand_aliasing={{}: (5, {})} | custom-call | bytes 15728640 | tf_op jit(solution)/shard_map/collect_support/pallas_call | solution.py:111
  21.0 1.7 collective-permute-start.2
  22.7 6.3 %collect_support.6.refs_0_ = bf16[520,512,128]{2,1,0:T(8,128)(2,1)} custom-call(s32[16]{0:T(128)S(1)} %select_reduce_fusion.seq, s32[16]{0:T(128)S(1)} %copy-done.2, s32[16,16]{1,0:T(8,128)S(1)} %copy-done.1, s32[16]{0:T(128)S(1)} %copy-done, bf16[512,32768]{1,0:T(8,128)(2,1)} %dictionary.7, ...), custom_call_target="tpu_custom_call", output_to_operand_aliasing={{}: (5, {})} | custom-call | bytes 15728640 | tf_op jit(solution)/shard_map/collect_support/pallas_call | solution.py:111
  30.3 6.4 %collect_support.7.blocks = bf16[520,512,128]{2,1,0:T(8,128)(2,1)} custom-call(s32[16]{0:T(128)S(1)} %select_reduce_fusion.seq, s32[16]{0:T(128)S(1)} %copy-done.2, s32[16,16]{1,0:T(8,128)S(1)} %copy-done.1, s32[16]{0:T(128)S(1)} %copy-done, bf16[512,32768]{1,0:T(8,128)(2,1)} %dictionary.7, ...), custom_call_target="tpu_custom_call", output_to_operand_aliasing={{}: (5, {})} | custom-call | bytes 15728640 | tf_op jit(solution)/shard_map/collect_support/pallas_call | solution.py:111
  36.8 1.5 copy.18
  39.6 11.6 %gradient.3 = (f32[2560,128]{1,0:T(8,128)S(1)}, bf16[2560,128]{1,0:T(8,128)(2,1)S(1)}, bf16[320,128]{1,0:T(8,128)(2,1)S(1)}, f32[320,128]{1,0:T(8,128)S(1)}) custom-call(s32[16]{0:T(128)S(1)} %select_reduce_fusion.seq, s32[16]{0:T(128)S(1)} %copy-done.2, s32[16]{0:T(128)S(1)} %copy-done, s32[1]{0:T(128)} %bitcast.own, ...), custom_call_target="tpu_custom_call" | custom-call | flops 5368709120 | bytes 10485760 | tf_op jit(solution)/shard_map/gradient/pallas_call | solution.py:326
  51.4 2.0 collective-permute-done.4
  53.6 1.7 collective-permute-start.5
  55.3 5.5 %collective-permute-done.5 = bf16[1280,128]{1,0:T(8,128)(2,1)S(1)} collective-permute-done((bf16[1280,128]{1,0:T(8,128)(2,1)S(1)}, bf16[1280,128]{1,0:T(8,128)(2,1)S(1)}, u32[]{:S(2)}, u32[]{:S(2)}) %collective-permute-start.5) | collective-permute-done | bytes 327712 | tf_op jit(solution)/shard_map/ppermute | solution.py:349
  62.3 4.9 %collective-permute-done.6 = bf16[640,128]{1,0:T(8,128)(2,1)S(1)} collective-permute-done((bf16[640,128]{1,0:T(8,128)(2,1)S(1)}, bf16[640,128]{1,0:T(8,128)(2,1)S(1)}, u32[]{:S(2)}, u32[]{:S(2)}) %collective-permute-start.6) | collective-permute-done | bytes 163872 | tf_op jit(solution)/shard_map/ppermute | solution.py:349
  68.7 4.7 %collective-permute-done.7 = bf16[320,128]{1,0:T(8,128)(2,1)S(1)} collective-permute-done((bf16[320,128]{1,0:T(8,128)(2,1)S(1)}, bf16[320,128]{1,0:T(8,128)(2,1)S(1)}, u32[]{:S(2)}, u32[]{:S(2)}) %collective-permute-start.7) | collective-permute-done | bytes 81952 | tf_op jit(solution)/shard_map/ppermute | solution.py:349
  74.3 7.8 %collective-permute-done.8 = bf16[320,128]{1,0:T(8,128)(2,1)S(1)} collective-permute-done((bf16[320,128]{1,0:T(8,128)(2,1)S(1)}, bf16[320,128]{1,0:T(8,128)(2,1)S(1)}, u32[]{:S(2)}, u32[]{:S(2)}) %collective-permute-start.8) | collective-permute-done | bytes 81952 | tf_op jit(solution)/shard_map/ppermute | solution.py:349
  82.1 7.0 %collective-permute-done.9 = bf16[640,128]{1,0:T(8,128)(2,1)S(1)} collective-permute-done((bf16[640,128]{1,0:T(8,128)(2,1)S(1)}, bf16[640,128]{1,0:T(8,128)(2,1)S(1)}, u32[]{:S(2)}, u32[]{:S(2)}) %collective-permute-start.9) | collective-permute-done | bytes 163872 | tf_op jit(solution)/shard_map/ppermute | solution.py:349
  90.5 5.8 %collective-permute-done.10 = bf16[1280,128]{1,0:T(8,128)(2,1)S(1)} collective-permute-done((bf16[1280,128]{1,0:T(8,128)(2,1)S(1)}, bf16[1280,128]{1,0:T(8,128)(2,1)S(1)}, u32[]{:S(2)}, u32[]{:S(2)}) %collective-permute-start.10) | collective-permute-done | bytes 327712 | tf_op jit(solution)/shard_map/ppermute | solution.py:349
  96.4 2.1 %collective-permute-done.11.far = bf16[2560,128]{1,0:T(8,128)(2,1)S(1)} collective-permute-done((bf16[2560,128]{1,0:T(8,128)(2,1)S(1)}, bf16[2560,128]{1,0:T(8,128)(2,1)S(1)}, u32[]{:S(2)}, u32[]{:S(2)}) %collective-permute-start.11) | collective-permute-done | bytes 655392 | tf_op jit(solution)/shard_map/ppermute | solution.py:349
  98.5 11.7 %gradient.4 = (f32[2560,128]{1,0:T(8,128)S(1)}, bf16[2560,128]{1,0:T(8,128)(2,1)S(1)}) custom-call(s32[16]{0:T(128)S(1)} %select_reduce_fusion.seq, s32[16]{0:T(128)S(1)} %copy-done.2, s32[16]{0:T(128)S(1)} %copy-done, s32[1]{0:T(128)} %bitcast.own, bf16[520,512,128]{2,1,0:T(8,128)(2,1)} %collect_support.7.blocks, ...), custom_call_target="tpu_custom_call" | custom-call | flops 5368709120 | bytes 10485760 | tf_op jit(solution)/shard_map/gradient/pallas_call | solution.py:326
  110.4 2.0 collective-permute-done.12
  113.8 5.8 %collective-permute-done.13 = bf16[1280,128]{1,0:T(8,128)(2,1)S(1)} collective-permute-done((bf16[1280,128]{1,0:T(8,128)(2,1)S(1)}, bf16[1280,128]{1,0:T(8,128)(2,1)S(1)}, u32[]{:S(2)}, u32[]{:S(2)}) %collective-permute-start.13) | collective-permute-done | bytes 327712 | tf_op jit(solution)/shard_map/ppermute | solution.py:349
  119.9 6.7 %collective-permute-done.14 = bf16[640,128]{1,0:T(8,128)(2,1)S(1)} collective-permute-done((bf16[640,128]{1,0:T(8,128)(2,1)S(1)}, bf16[640,128]{1,0:T(8,128)(2,1)S(1)}, u32[]{:S(2)}, u32[]{:S(2)}) %collective-permute-start.14) | collective-permute-done | bytes 163872 | tf_op jit(solution)/shard_map/ppermute | solution.py:349
  126.7 5.3 %collective-permute-done.15 = bf16[320,128]{1,0:T(8,128)(2,1)S(1)} collective-permute-done((bf16[320,128]{1,0:T(8,128)(2,1)S(1)}, bf16[320,128]{1,0:T(8,128)(2,1)S(1)}, u32[]{:S(2)}, u32[]{:S(2)}) %collective-permute-start.15) | collective-permute-done | bytes 81952 | tf_op jit(solution)/shard_map/ppermute | solution.py:349
  132.2 7.9 %collective-permute-done.16 = bf16[320,128]{1,0:T(8,128)(2,1)S(1)} collective-permute-done((bf16[320,128]{1,0:T(8,128)(2,1)S(1)}, bf16[320,128]{1,0:T(8,128)(2,1)S(1)}, u32[]{:S(2)}, u32[]{:S(2)}) %collective-permute-start.16) | collective-permute-done | bytes 81952 | tf_op jit(solution)/shard_map/ppermute | solution.py:349
  140.2 7.1 %collective-permute-done.17 = bf16[640,128]{1,0:T(8,128)(2,1)S(1)} collective-permute-done((bf16[640,128]{1,0:T(8,128)(2,1)S(1)}, bf16[640,128]{1,0:T(8,128)(2,1)S(1)}, u32[]{:S(2)}, u32[]{:S(2)}) %collective-permute-start.17) | collective-permute-done | bytes 163872 | tf_op jit(solution)/shard_map/ppermute | solution.py:349
  148.4 6.0 %collective-permute-done.18 = bf16[1280,128]{1,0:T(8,128)(2,1)S(1)} collective-permute-done((bf16[1280,128]{1,0:T(8,128)(2,1)S(1)}, bf16[1280,128]{1,0:T(8,128)(2,1)S(1)}, u32[]{:S(2)}, u32[]{:S(2)}) %collective-permute-start.18) | collective-permute-done | bytes 327712 | tf_op jit(solution)/shard_map/ppermute | solution.py:349
  154.6 2.1 %collective-permute-done.19.far = bf16[2560,128]{1,0:T(8,128)(2,1)S(1)} collective-permute-done((bf16[2560,128]{1,0:T(8,128)(2,1)S(1)}, bf16[2560,128]{1,0:T(8,128)(2,1)S(1)}, u32[]{:S(2)}, u32[]{:S(2)}) %collective-permute-start.19) | collective-permute-done | bytes 655392 | tf_op jit(solution)/shard_map/ppermute | solution.py:349
  156.7 12.5 %gradient.5 = (f32[4096,128]{1,0:T(8,128)S(1)}, bf16[4096,128]{1,0:T(8,128)(2,1)S(1)}, bf16[8,64,128]{2,1,0:T(8,128)(2,1)S(1)}) custom-call(s32[16]{0:T(128)S(1)} %select_reduce_fusion.seq, s32[16]{0:T(128)S(1)} %copy-done.2, s32[16]{0:T(128)S(1)} %copy-done, s32[1]{0:T(128)} %bitcast.own, bf16[520,512,128]{2,1,0:T(8,128)(2,1)} %collect_support.7.blocks, ...), custom_call_target="tpu_custom_call" | custom-call | flops 5368709120 | bytes 10485760 | tf_op jit(solution)/shard_map/gradient/pallas_call | solution.py:326
  169.3 2.5 %collective-permute-done.20 = bf16[4096,128]{1,0:T(8,128)(2,1)S(1)} collective-permute-done((bf16[4096,128]{1,0:T(8,128)(2,1)S(1)}, bf16[4096,128]{1,0:T(8,128)(2,1)S(1)}, u32[]{:S(2)}, u32[]{:S(2)}) %collective-permute-start.20) | collective-permute-done | bytes 1048608 | tf_op jit(solution)/shard_map/ppermute | solution.py:349
  173.2 8.1 %collective-permute-done.21 = bf16[2048,128]{1,0:T(8,128)(2,1)S(1)} collective-permute-done((bf16[2048,128]{1,0:T(8,128)(2,1)S(1)}, bf16[2048,128]{1,0:T(8,128)(2,1)S(1)}, u32[]{:S(2)}, u32[]{:S(2)}) %collective-permute-start.21) | collective-permute-done | bytes 524320 | tf_op jit(solution)/shard_map/ppermute | solution.py:349
  181.6 9.0 %collective-permute-done.22 = bf16[1024,128]{1,0:T(8,128)(2,1)S(1)} collective-permute-done((bf16[1024,128]{1,0:T(8,128)(2,1)S(1)}, bf16[1024,128]{1,0:T(8,128)(2,1)S(1)}, u32[]{:S(2)}, u32[]{:S(2)}) %collective-permute-start.22) | collective-permute-done | bytes 262176 | tf_op jit(solution)/shard_map/ppermute | solution.py:349
  193.3 3.7 %collective-permute-done.23 = bf16[512,128]{1,0:T(8,128)(2,1)S(1)} collective-permute-done((bf16[512,128]{1,0:T(8,128)(2,1)S(1)}, bf16[512,128]{1,0:T(8,128)(2,1)S(1)}, u32[]{:S(2)}, u32[]{:S(2)}) %collective-permute-start.23) | collective-permute-done | bytes 131104 | tf_op jit(solution)/shard_map/ppermute | solution.py:349
  (79 shorter events, 18.7 us)
Async XLA Ops:
  0.0 5.8 %copy-start.2 = (s32[16]{0:T(128)S(1)}, s32[16]{0:T(128)}, u32[]{:S(2)}) copy-start(s32[16]{0:T(128)} %order.13) | copy-start | bytes 196
  0.0 5.8 %copy-start = (s32[16]{0:T(128)S(1)}, s32[16]{0:T(128)}, u32[]{:S(2)}) copy-start(s32[16]{0:T(128)} %counts.13) | copy-start | bytes 196
  0.0 6.7 %copy-start.1 = (s32[16,16]{1,0:T(8,128)S(1)}, s32[16,16]{1,0:T(8,128)}, u32[]{:S(2)}) copy-start(s32[16,16]{1,0:T(8,128)} %support.7) | copy-start | bytes 3076
  1.7 11.3 %collective-permute-start = (bf16[512,128]{1,0:T(8,128)(2,1)S(1)}, bf16[512,128]{1,0:T(8,128)(2,1)S(1)}, u32[]{:S(2)}, u32[]{:S(2)}) collective-permute-start(bf16[512,128]{1,0:T(8,128)(2,1)S(1)} %reshape.43), channel_id=1, source_target_pairs={{0,8},{1,3},{2,10},{3,1},{4,12},{5,7},{6,14},{7,5},{8,0},{9,11},{1... | collective-permute-start | bytes 393224 | tf_op jit(solution)/shard_map/ppermute | solution.py:349
  13.0 8.0 %collective-permute-start.1 = (bf16[1024,128]{1,0:T(8,128)(2,1)S(1)}, bf16[1024,128]{1,0:T(8,128)(2,1)S(1)}, u32[]{:S(2)}, u32[]{:S(2)}) collective-permute-start(bf16[1024,128]{1,0:T(8,128)(2,1)S(1)} %pad_maximum_fusion.6), channel_id=1, source_target_pairs={{0,4},{1,9},{2,6},{3,11},{4,0},{5,13},{6,2},{7,15},{8,12},{9,1},{1... | collective-permute-start | bytes 786440 | tf_op jit(solution)/shard_map/ppermute | solution.py:349
  21.0 9.2 %collective-permute-start.2 = (bf16[2048,128]{1,0:T(8,128)(2,1)S(1)}, bf16[2048,128]{1,0:T(8,128)(2,1)S(1)}, u32[]{:S(2)}, u32[]{:S(2)}) collective-permute-start(bf16[2048,128]{1,0:T(8,128)(2,1)S(1)} %pad_maximum_fusion.3), channel_id=1, source_target_pairs={{0,2},{1,5},{2,0},{3,7},{4,6},{5,1},{6,4},{7,3},{8,10},{9,13},{10,... | collective-permute-start | bytes 1572872 | tf_op jit(solution)/shard_map/ppermute | solution.py:349
  36.7 1.6 copy-start.3
  36.7 2.7 %collective-permute-start.3 = (bf16[4096,128]{1,0:T(8,128)(2,1)S(1)}, bf16[4096,128]{1,0:T(8,128)(2,1)S(1)}, u32[]{:S(2)}, u32[]{:S(2)}) collective-permute-start(bf16[4096,128]{1,0:T(8,128)(2,1)S(1)} %pad_maximum_fusion.near), channel_id=1, source_target_pairs={{0,1},{1,0},{2,3},{3,2},{4,5},{5,4},{6,7},{7,6},{8,9},{9,8},{10,11... | collective-permute-start | bytes 3145736 | tf_op jit(solution)/shard_map/ppermute | solution.py:349
  51.3 2.2 %collective-permute-start.4 = (bf16[2560,128]{1,0:T(8,128)(2,1)S(1)}, bf16[2560,128]{1,0:T(8,128)(2,1)S(1)}, u32[]{:S(2)}, u32[]{:S(2)}) collective-permute-start(bf16[2560,128]{1,0:T(8,128)(2,1)S(1)} %get-tuple-element.32), channel_id=1, source_target_pairs={{0,1},{1,0},{2,3},{3,2},{4,5},{5,4},{6,7},{7,6},{8,9},{9,8},{10,11... | collective-permute-start | bytes 1966088 | tf_op jit(solution)/shard_map/ppermute | solution.py:349
  53.6 7.1 %collective-permute-start.5 = (bf16[1280,128]{1,0:T(8,128)(2,1)S(1)}, bf16[1280,128]{1,0:T(8,128)(2,1)S(1)}, u32[]{:S(2)}, u32[]{:S(2)}) collective-permute-start(bf16[1280,128]{1,0:T(8,128)(2,1)S(1)} %slice.139), channel_id=1, source_target_pairs={{0,2},{1,5},{2,0},{3,7},{4,6},{5,1},{6,4},{7,3},{8,10},{9,13},{10,... | collective-permute-start | bytes 983048 | tf_op jit(solution)/shard_map/ppermute | solution.py:349
  60.9 6.4 %collective-permute-start.6 = (bf16[640,128]{1,0:T(8,128)(2,1)S(1)}, bf16[640,128]{1,0:T(8,128)(2,1)S(1)}, u32[]{:S(2)}, u32[]{:S(2)}) collective-permute-start(bf16[640,128]{1,0:T(8,128)(2,1)S(1)} %slice.142), channel_id=1, source_target_pairs={{0,4},{1,9},{2,6},{3,11},{4,0},{5,13},{6,2},{7,15},{8,12},{9,1},{1... | collective-permute-start | bytes 491528 | tf_op jit(solution)/shard_map/ppermute | solution.py:349
  67.3 6.1 %collective-permute-start.7 = (bf16[320,128]{1,0:T(8,128)(2,1)S(1)}, bf16[320,128]{1,0:T(8,128)(2,1)S(1)}, u32[]{:S(2)}, u32[]{:S(2)}) collective-permute-start(bf16[320,128]{1,0:T(8,128)(2,1)S(1)} %slice.145), channel_id=1, source_target_pairs={{0,8},{1,3},{2,10},{3,1},{4,12},{5,7},{6,14},{7,5},{8,0},{9,11},{1... | collective-permute-start | bytes 245768 | tf_op jit(solution)/shard_map/ppermute | solution.py:349
  73.5 8.5 %collective-permute-start.8 = (bf16[320,128]{1,0:T(8,128)(2,1)S(1)}, bf16[320,128]{1,0:T(8,128)(2,1)S(1)}, u32[]{:S(2)}, u32[]{:S(2)}) collective-permute-start(bf16[320,128]{1,0:T(8,128)(2,1)S(1)} %fusion.6), channel_id=1, source_target_pairs={{0,8},{1,3},{2,10},{3,1},{4,12},{5,7},{6,14},{7,5},{8,0},{9,11},{1... | collective-permute-start | bytes 245768 | tf_op jit(solution)/shard_map/ppermute | solution.py:349
  82.0 7.1 %collective-permute-start.9 = (bf16[640,128]{1,0:T(8,128)(2,1)S(1)}, bf16[640,128]{1,0:T(8,128)(2,1)S(1)}, u32[]{:S(2)}, u32[]{:S(2)}) collective-permute-start(bf16[640,128]{1,0:T(8,128)(2,1)S(1)} %pad_maximum_fusion.7), channel_id=1, source_target_pairs={{0,4},{1,9},{2,6},{3,11},{4,0},{5,13},{6,2},{7,15},{8,12},{9,1},{1... | collective-permute-start | bytes 491528 | tf_op jit(solution)/shard_map/ppermute | solution.py:349
  89.2 7.1 %collective-permute-start.10 = (bf16[1280,128]{1,0:T(8,128)(2,1)S(1)}, bf16[1280,128]{1,0:T(8,128)(2,1)S(1)}, u32[]{:S(2)}, u32[]{:S(2)}) collective-permute-start(bf16[1280,128]{1,0:T(8,128)(2,1)S(1)} %pad_maximum_fusion.4), channel_id=1, source_target_pairs={{0,2},{1,5},{2,0},{3,7},{4,6},{5,1},{6,4},{7,3},{8,10},{9,13},{10,... | collective-permute-start | bytes 983048 | tf_op jit(solution)/shard_map/ppermute | solution.py:349
  96.3 2.2 %collective-permute-start.11 = (bf16[2560,128]{1,0:T(8,128)(2,1)S(1)}, bf16[2560,128]{1,0:T(8,128)(2,1)S(1)}, u32[]{:S(2)}, u32[]{:S(2)}) collective-permute-start(bf16[2560,128]{1,0:T(8,128)(2,1)S(1)} %pad_maximum_fusion.1.near), channel_id=1, source_target_pairs={{0,1},{1,0},{2,3},{3,2},{4,5},{5,4},{6,7},{7,6},{8,9},{9,8},{10,11... | collective-permute-start | bytes 1966088 | tf_op jit(solution)/shard_map/ppermute | solution.py:349
  110.2 2.2 %collective-permute-start.12 = (bf16[2560,128]{1,0:T(8,128)(2,1)S(1)}, bf16[2560,128]{1,0:T(8,128)(2,1)S(1)}, u32[]{:S(2)}, u32[]{:S(2)}) collective-permute-start(bf16[2560,128]{1,0:T(8,128)(2,1)S(1)} %get-tuple-element.35), channel_id=1, source_target_pairs={{0,1},{1,0},{2,3},{3,2},{4,5},{5,4},{6,7},{7,6},{8,9},{9,8},{10,11... | collective-permute-start | bytes 1966088 | tf_op jit(solution)/shard_map/ppermute | solution.py:349
  112.5 7.1 %collective-permute-start.13 = (bf16[1280,128]{1,0:T(8,128)(2,1)S(1)}, bf16[1280,128]{1,0:T(8,128)(2,1)S(1)}, u32[]{:S(2)}, u32[]{:S(2)}) collective-permute-start(bf16[1280,128]{1,0:T(8,128)(2,1)S(1)} %slice.138), channel_id=1, source_target_pairs={{0,2},{1,5},{2,0},{3,7},{4,6},{5,1},{6,4},{7,3},{8,10},{9,13},{10,... | collective-permute-start | bytes 983048 | tf_op jit(solution)/shard_map/ppermute | solution.py:349
  119.8 6.8 %collective-permute-start.14 = (bf16[640,128]{1,0:T(8,128)(2,1)S(1)}, bf16[640,128]{1,0:T(8,128)(2,1)S(1)}, u32[]{:S(2)}, u32[]{:S(2)}) collective-permute-start(bf16[640,128]{1,0:T(8,128)(2,1)S(1)} %slice.141), channel_id=1, source_target_pairs={{0,4},{1,9},{2,6},{3,11},{4,0},{5,13},{6,2},{7,15},{8,12},{9,1},{1... | collective-permute-start | bytes 491528 | tf_op jit(solution)/shard_map/ppermute | solution.py:349
  126.6 5.4 %collective-permute-start.15 = (bf16[320,128]{1,0:T(8,128)(2,1)S(1)}, bf16[320,128]{1,0:T(8,128)(2,1)S(1)}, u32[]{:S(2)}, u32[]{:S(2)}) collective-permute-start(bf16[320,128]{1,0:T(8,128)(2,1)S(1)} %slice.144), channel_id=1, source_target_pairs={{0,8},{1,3},{2,10},{3,1},{4,12},{5,7},{6,14},{7,5},{8,0},{9,11},{1... | collective-permute-start | bytes 245768 | tf_op jit(solution)/shard_map/ppermute | solution.py:349
  132.2 8.0 %collective-permute-start.16 = (bf16[320,128]{1,0:T(8,128)(2,1)S(1)}, bf16[320,128]{1,0:T(8,128)(2,1)S(1)}, u32[]{:S(2)}, u32[]{:S(2)}) collective-permute-start(bf16[320,128]{1,0:T(8,128)(2,1)S(1)} %add_convert_fusion), channel_id=1, source_target_pairs={{0,8},{1,3},{2,10},{3,1},{4,12},{5,7},{6,14},{7,5},{8,0},{9,11},{1... | collective-permute-start | bytes 245768 | tf_op jit(solution)/shard_map/ppermute | solution.py:349
  140.1 7.1 %collective-permute-start.17 = (bf16[640,128]{1,0:T(8,128)(2,1)S(1)}, bf16[640,128]{1,0:T(8,128)(2,1)S(1)}, u32[]{:S(2)}, u32[]{:S(2)}) collective-permute-start(bf16[640,128]{1,0:T(8,128)(2,1)S(1)} %pad_maximum_fusion.8), channel_id=1, source_target_pairs={{0,4},{1,9},{2,6},{3,11},{4,0},{5,13},{6,2},{7,15},{8,12},{9,1},{1... | collective-permute-start | bytes 491528 | tf_op jit(solution)/shard_map/ppermute | solution.py:349
  147.3 7.1 %collective-permute-start.18 = (bf16[1280,128]{1,0:T(8,128)(2,1)S(1)}, bf16[1280,128]{1,0:T(8,128)(2,1)S(1)}, u32[]{:S(2)}, u32[]{:S(2)}) collective-permute-start(bf16[1280,128]{1,0:T(8,128)(2,1)S(1)} %pad_maximum_fusion.5), channel_id=1, source_target_pairs={{0,2},{1,5},{2,0},{3,7},{4,6},{5,1},{6,4},{7,3},{8,10},{9,13},{10,... | collective-permute-start | bytes 983048 | tf_op jit(solution)/shard_map/ppermute | solution.py:349
  154.5 2.2 %collective-permute-start.19 = (bf16[2560,128]{1,0:T(8,128)(2,1)S(1)}, bf16[2560,128]{1,0:T(8,128)(2,1)S(1)}, u32[]{:S(2)}, u32[]{:S(2)}) collective-permute-start(bf16[2560,128]{1,0:T(8,128)(2,1)S(1)} %pad_maximum_fusion.2.near), channel_id=1, source_target_pairs={{0,1},{1,0},{2,3},{3,2},{4,5},{5,4},{6,7},{7,6},{8,9},{9,8},{10,11... | collective-permute-start | bytes 1966088 | tf_op jit(solution)/shard_map/ppermute | solution.py:349
  169.1 2.7 %collective-permute-start.20 = (bf16[4096,128]{1,0:T(8,128)(2,1)S(1)}, bf16[4096,128]{1,0:T(8,128)(2,1)S(1)}, u32[]{:S(2)}, u32[]{:S(2)}) collective-permute-start(bf16[4096,128]{1,0:T(8,128)(2,1)S(1)} %get-tuple-element.38), channel_id=1, source_target_pairs={{0,1},{1,0},{2,3},{3,2},{4,5},{5,4},{6,7},{7,6},{8,9},{9,8},{10,11... | collective-permute-start | bytes 3145736 | tf_op jit(solution)/shard_map/ppermute | solution.py:349
  172.1 9.2 %collective-permute-start.21 = (bf16[2048,128]{1,0:T(8,128)(2,1)S(1)}, bf16[2048,128]{1,0:T(8,128)(2,1)S(1)}, u32[]{:S(2)}, u32[]{:S(2)}) collective-permute-start(bf16[2048,128]{1,0:T(8,128)(2,1)S(1)} %slice.137), channel_id=1, source_target_pairs={{0,2},{1,5},{2,0},{3,7},{4,6},{5,1},{6,4},{7,3},{8,10},{9,13},{10,... | collective-permute-start | bytes 1572872 | tf_op jit(solution)/shard_map/ppermute | solution.py:349
  181.5 9.1 %collective-permute-start.22 = (bf16[1024,128]{1,0:T(8,128)(2,1)S(1)}, bf16[1024,128]{1,0:T(8,128)(2,1)S(1)}, u32[]{:S(2)}, u32[]{:S(2)}) collective-permute-start(bf16[1024,128]{1,0:T(8,128)(2,1)S(1)} %slice.140), channel_id=1, source_target_pairs={{0,4},{1,9},{2,6},{3,11},{4,0},{5,13},{6,2},{7,15},{8,12},{9,1},{1... | collective-permute-start | bytes 786440 | tf_op jit(solution)/shard_map/ppermute | solution.py:349
  190.7 6.3 %collective-permute-start.23 = (bf16[512,128]{1,0:T(8,128)(2,1)S(1)}, bf16[512,128]{1,0:T(8,128)(2,1)S(1)}, u32[]{:S(2)}, u32[]{:S(2)}) collective-permute-start(bf16[512,128]{1,0:T(8,128)(2,1)S(1)} %slice.143), channel_id=1, source_target_pairs={{0,8},{1,3},{2,10},{3,1},{4,12},{5,7},{6,14},{7,5},{8,0},{9,11},{1... | collective-permute-start | bytes 393224 | tf_op jit(solution)/shard_map/ppermute | solution.py:349

commit v6 on v5

--- a/solution.py
+++ b/solution.py
@@ -17,7 +17,8 @@
 SLOT_PAIRS = SLOTS // 2
 SPARE = SLOT_PAIRS + 2
 ROW_TILE = 16
-SUPPORT_PARTS = 4
+SUPPORT_PARTS = 2
+SUPPORT_STEP = 4
 PIECE = 5
 MATRIX_UNIT = 256
 VMEM_MARGIN = 3 * 1024 * 1024
@@ -82,20 +83,21 @@
         return pltpu.make_async_copy(held.at[2 * pair], out.at[begin // 2 + pair], out_sems.at[pair])
 
     def pack(step, carry):
-        for entry in range(4):
-            index = 4 * step + entry
-            fetch(index, ids[index]).wait()
+        span = [SUPPORT_STEP * step + pair for pair in range(SUPPORT_STEP)]
+        for pair in span:
+            fetch(2 * pair, ids[2 * pair]).wait()
+            fetch(2 * pair + 1, ids[2 * pair + 1]).wait()
         packed = []
-        for pair in (2 * step, 2 * step + 1):
+        for pair in span:
             choice = ids[2 * pair] % 2 + 2 * (ids[2 * pair + 1] % 2)
             both = jnp.concatenate([held[2 * pair], held[2 * pair + 1]], axis=1)
             packed.append(jnp.dot(both, picks[choice], preferred_element_type=jnp.float32).astype(jnp.bfloat16))
-        for pair, value in zip((2 * step, 2 * step + 1), packed):
+        for pair, value in zip(span, packed):
             held[2 * pair] = value
             store(pair).start()
         return carry
 
-    lax.fori_loop(0, pairs // 2, pack, 0)
+    lax.fori_loop(0, pairs // SUPPORT_STEP, pack, 0)
 
     def drain(pair, carry):
         store(pair).wait()
@@ -144,13 +146,13 @@
 def gradient_kernel(mode, shards, pairs, seq, order, counts, own, blocks, near, far, targets, *refs):
     refs = list(refs)
     take = lambda: refs.pop(0)
-    if mode == "first":
+    if mode in ("first", "final"):
         thresh = take()
     keep, send = take(), take()
     if mode == "first":
         start_out, thresh_out = take(), take()
     if mode == "final":
-        sent = take()
+        sent, thresh_out = take(), take()
     held, codes, total = take(), take(), take()
     if mode == "first":
         starts, limits = take(), take()
@@ -290,6 +292,7 @@
         parts = read_codes(me, offset, counts[order[me]], SLOT_PAIRS + 1)
         for pair, part in enumerate(shifted(parts, SLOT_PAIRS, offset % 2 == 1, True)):
             sent[pair] = part
+        thresh_out[...] = thresh[order[me]]
         for slot in range(shards):
             position = holder(slot)
             offset = offsets[position]
@@ -317,7 +320,7 @@
     if mode == "first":
         outs += [(shard, single), (shard, double)]
     if mode == "final":
-        outs += [((SLOT_PAIRS, PATCHES, LANES), single)]
+        outs += [((SLOT_PAIRS, PATCHES, LANES), single), ((PATCHES, LANES), double)]
     codes = groups * SLOT_PAIRS * PATCHES if mode == "first" else packed[0]
     scratch = [((places, rows, LANES), single), ((codes, LANES), single), (packed, double)]
     if mode == "first":
@@ -343,31 +346,53 @@
     )(*scalars, blocks, near, far, targets, *extra)
 
 
-def exchange(value, stage):
+def exchange(value, distance, cores=(0, 1)):
     devices = lax.axis_size("rows")
-    orders = stage_orders(devices)
-    return lax.ppermute(value, "rows", [(i, i ^ orders[i % 2][stage]) for i in range(devices)])
+    return lax.ppermute(value, "rows", [(i, i ^ distance) for i in range(devices) if i % 2 in cores])
+
+
+def column_distances(devices):
+    distances = stage_orders(devices)[0][2:]
+    return [slot_distance(slot, distances) for slot in range(devices // 4)]
+
+
+def by_core(even, odd):
+    return jnp.where(lax.axis_index("rows") % 2 == 0, even, odd)
 
 
 def gather_shards(own, beside=()):
-    value, made = own, ()
-    stages = len(stage_orders(lax.axis_size("rows"))[0])
-    steps = list(beside)
-    for stage in reversed(range(1, stages)):
-        value = jnp.concatenate([value, exchange(value, stage)], axis=0)
-        if steps:
-            value, *made = lax.optimization_barrier((value, steps.pop(0)(*made)))
-    for step in steps:
-        value, *made = lax.optimization_barrier((value, step(*made)))
-    return value, exchange(value, 0), made
+    apart = column_distances(lax.axis_size("rows"))[1:]
+    made = ()
+    quarter = jnp.concatenate([own] + [exchange(own, distance, (0,)) for distance in apart], axis=0)
+    couple = jnp.concatenate([own, exchange(own, 2, (1,))], axis=0)
+    if beside:
+        quarter, couple, *made = lax.optimization_barrier((quarter, couple, beside[0]()))
+    even = jnp.concatenate([quarter, exchange(quarter, 2, (0,))], axis=0)
+    odd = jnp.concatenate([couple] + [exchange(couple, distance, (1,)) for distance in apart], axis=0)
+    near = by_core(even, odd)
+    if beside:
+        near, *made = lax.optimization_barrier((near, beside[1](*made)))
+    return near, exchange(near, 1), made
 
 
 def reduce_shards(keep, send):
-    total = keep + exchange(send, 0).astype(jnp.float32)
-    for stage in range(1, len(stage_orders(lax.axis_size("rows"))[0])):
-        middle = total.shape[0] // 2
-        total = total[:middle] + exchange(total[middle:].astype(jnp.bfloat16), stage).astype(jnp.float32)
-    return total
+    devices = lax.axis_size("rows")
+    apart = column_distances(devices)
+    size = 2 * keep.shape[0] // devices
+
+    def arrived(value, distance, cores):
+        return exchange(value.astype(jnp.bfloat16), distance, cores).astype(jnp.float32)
+
+    total = keep + exchange(send, 1).astype(jnp.float32)
+    middle = total.shape[0] // 2
+    even = total[:middle] + arrived(total[middle:], 2, (0,))
+    odd = total[: 2 * size]
+    for place in range(1, len(apart)):
+        odd = odd + arrived(total[2 * place * size : 2 * (place + 1) * size], apart[place], (1,))
+    sums = even[:size]
+    for place in range(1, len(apart)):
+        sums = sums + arrived(even[place * size : (place + 1) * size], apart[place], (0,))
+    return by_core(sums, odd[:size] + arrived(odd[size:], 2, (1,)))
 
 
 def packed_order(live):
@@ -398,7 +423,6 @@
     targets = patches.T
     half_penalty = 0.5 * penalty
     thresh_tiles = jnp.broadcast_to(half_penalty[:, :, None], (groups, PATCHES, LANES))
-    own_thresh = lax.dynamic_index_in_dim(half_penalty, group_order[position], 0, False)[None, :, None]
 
     run = functools.partial(gradient_call, shards=devices, pairs=pairs, scalars=scalars, blocks=blocks, targets=targets)
     keep, send, start, thresh = run("first", near=near, far=far, extra=(thresh_tiles,))
@@ -410,10 +434,10 @@
         point = current + momenta[turn] * (current - previous)
         previous = current
         near, far, _ = gather_shards(point.astype(jnp.bfloat16))
-    keep, send, sent = run("final", near=near, far=far)
+    keep, send, sent, thresh = run("final", near=near, far=far, extra=(thresh_tiles,))
     gradient = reduce_shards(keep, send).reshape(SLOT_PAIRS, PATCHES, LANES)
     sent = sent.astype(jnp.float32)
-    result = shrink(sent - 0.5 * gradient, own_thresh)
+    result = shrink(sent - 0.5 * gradient, thresh[None])
     result = result.reshape(SLOT_PAIRS, PATCHES, 2, BLOCK).transpose(0, 2, 1, 3)
     return result.reshape(1, SLOTS, PATCHES * BLOCK)
 

time: 198 us -> 224 us (1.13)
  starting transfers between devices: 19 us -> 94.2 us
  waiting for transfers between devices: 108 us -> 63.6 us
  Pallas kernels: 60.9 us -> 51.7 us
  local copies, waits for them, and re-layouts: 6.07 us -> 8.63 us
    ppermute x24 -> x54, starting transfers between devices: 19 us -> 94.2 us  [exchange(): lax.ppermute(value, 'rows', [(i, i ^ distance) for i in range(devices) if...]
    ppermute x24 -> x54, waiting for transfers between devices: 108 us -> 63.6 us  [exchange(): lax.ppermute(value, 'rows', [(i, i ^ distance) for i in range(devices) if...]
    pallas_call x4 -> x2, Pallas kernels: 25.1 us -> 17.5 us  [collect_support(): pl.pallas_call(functools.partial(support_kernel, part * entries), grid_sp...]
    unnamed x9 -> x29, local copies, waits for them, and re-layouts: 1.52 us -> 3.83 us
  transfers between devices with their start and end apart: 24 -> 54, of which waited for: 23 -> 19; matrix products, arithmetic and copies ran while one was open for 2% -> 3% of each run, Pallas kernels for 9% -> 8%
where the time goes in v6:
time: 224 us; the launch traced here: 223 us
  starting transfers between devices  94.2 us (42%)
  waiting for transfers between devices  63.6 us (28%)
  Pallas kernels  51.7 us (23%)
  local copies, waits for them, and re-layouts  8.63 us (4%)
  other arithmetic  3.82 us (2%)
    ppermute x54, starting transfers between devices, exchange(): lax.ppermute(value, 'rows', [(i, i ^ distance) for i in range(devices) if...  94.2 us
    ppermute x54, waiting for transfers between devices, exchange(): lax.ppermute(value, 'rows', [(i, i ^ distance) for i in range(devices) if...  63.6 us
    pallas_call x3, Pallas kernels, gradient_call(): pl.pallas_call(functools.partial(gradient_kernel, mode, shards, pairs), g...  34.2 us
    pallas_call x2, Pallas kernels, collect_support(): pl.pallas_call(functools.partial(support_kernel, part * entries), grid_sp...  17.5 us
  transfers between devices with their start and end apart: 54, of which 19 were waited for; matrix products, arithmetic and copies ran while one was open for 3% of the time, Pallas kernels for 8%

profile of v6, /device:TPU:0, one launch (start us, length us, event | category | flops | bytes accessed | tf_op | source)
XLA Modules:
  0.0 223.0 jit_solution(1251170402784939445)
XLA Ops:
  1.6 5.9 %collective-permute-start = (bf16[512,128]{1,0:T(8,128)(2,1)S(1)}, bf16[512,128]{1,0:T(8,128)(2,1)S(1)}, u32[]{:S(2)}, u32[]{:S(2)}) collective-permute-start(bf16[512,128]{1,0:T(8,128)(2,1)S(1)} %reshape.37), channel_id=1, source_target_pairs={{0,8},{2,10},{4,12},{6,14},{8,0},{10,2},{12,4},{14,6},{16,24},{18,... | collective-permute-start | bytes 393224 | tf_op jit(solution)/shard_map/ppermute | solution.py:351
  7.6 3.5 %collective-permute-start.1 = (bf16[512,128]{1,0:T(8,128)(2,1)S(1)}, bf16[512,128]{1,0:T(8,128)(2,1)S(1)}, u32[]{:S(2)}, u32[]{:S(2)}) collective-permute-start(bf16[512,128]{1,0:T(8,128)(2,1)S(1)} %reshape.37), channel_id=1, source_target_pairs={{0,4},{2,6},{4,0},{6,2},{8,12},{10,14},{12,8},{14,10},{16,20},{18,... | collective-permute-start | bytes 393224 | tf_op jit(solution)/shard_map/ppermute | solution.py:351
  18.6 8.6 %collect_support.2.refs_0_ = bf16[520,512,128]{2,1,0:T(8,128)(2,1)} custom-call(s32[16]{0:T(128)S(1)} %select_reduce_fusion.seq, s32[16]{0:T(128)S(1)} %copy-done.4, s32[16,16]{1,0:T(8,128)S(1)} %copy-done.2, s32[16]{0:T(128)S(1)} %copy-done, bf16[512,32768]{1,0:T(8,128)(2,1)} %dictionary.3), custom_call_target="tpu_custom_call" | custom-call | bytes 31457280 | tf_op jit(solution)/shard_map/collect_support/pallas_call | solution.py:113
  27.3 3.6 %collective-permute-start.4 = (bf16[2048,128]{1,0:T(8,128)(2,1)S(1)}, bf16[2048,128]{1,0:T(8,128)(2,1)S(1)}, u32[]{:S(2)}, u32[]{:S(2)}) collective-permute-start(bf16[2048,128]{1,0:T(8,128)(2,1)S(1)} %pad_maximum_fusion), channel_id=1, source_target_pairs={{0,2},{2,0},{4,6},{6,4},{8,10},{10,8},{12,14},{14,12},{16,18},{18,... | collective-permute-start | bytes 1572872 | tf_op jit(solution)/shard_map/ppermute | solution.py:351
  33.1 8.9 %collect_support.3.blocks = bf16[520,512,128]{2,1,0:T(8,128)(2,1)} custom-call(s32[16]{0:T(128)S(1)} %select_reduce_fusion.seq, s32[16]{0:T(128)S(1)} %copy-done.5, s32[16,16]{1,0:T(8,128)S(1)} %copy-done.3, s32[16]{0:T(128)S(1)} %copy-done.1, bf16[512,32768]{1,0:T(8,128)(2,1)} %dictionary.3, ...), custom_call_target="tpu_custom_call", output_to_operand_aliasing={{}: (5, {})} | custom-call | bytes 31457280 | tf_op jit(solution)/shard_map/collect_support/pallas_call | solution.py:113
  45.2 11.1 %gradient.3 = (f32[2560,128]{1,0:T(8,128)S(1)}, bf16[2560,128]{1,0:T(8,128)(2,1)S(1)}, bf16[320,128]{1,0:T(8,128)(2,1)S(1)}, f32[320,128]{1,0:T(8,128)S(1)}) custom-call(s32[16]{0:T(128)S(1)} %select_reduce_fusion.seq, s32[16]{0:T(128)S(1)} %copy-done.5, s32[16]{0:T(128)S(1)} %copy-done.1, s32[1]{0:T(128)} %bitcast.own, ...), custom_call_target="tpu_custom_call" | custom-call | flops 5368709120 | bytes 10485760 | tf_op jit(solution)/shard_map/gradient/pallas_call | solution.py:329
  63.9 5.9 %collective-permute-done.10 = bf16[1280,128]{1,0:T(8,128)(2,1)S(1)} collective-permute-done((bf16[1280,128]{1,0:T(8,128)(2,1)S(1)}, bf16[1280,128]{1,0:T(8,128)(2,1)S(1)}, u32[]{:S(2)}, u32[]{:S(2)}) %collective-permute-start.10) | collective-permute-done | bytes 327712 | tf_op jit(solution)/shard_map/ppermute | solution.py:351
  69.9 3.6 %collective-permute-start.11 = (bf16[320,128]{1,0:T(8,128)(2,1)S(1)}, bf16[320,128]{1,0:T(8,128)(2,1)S(1)}, u32[]{:S(2)}, u32[]{:S(2)}) collective-permute-start(bf16[320,128]{1,0:T(8,128)(2,1)S(1)} %get-tuple-element.67), channel_id=1, source_target_pairs={{0,8},{2,10},{4,12},{6,14},{8,0},{10,2},{12,4},{14,6},{16,24},{18,... | collective-permute-start | bytes 245768 | tf_op jit(solution)/shard_map/ppermute | solution.py:351
  73.6 4.4 %collective-permute-start.12 = (bf16[320,128]{1,0:T(8,128)(2,1)S(1)}, bf16[320,128]{1,0:T(8,128)(2,1)S(1)}, u32[]{:S(2)}, u32[]{:S(2)}) collective-permute-start(bf16[320,128]{1,0:T(8,128)(2,1)S(1)} %get-tuple-element.69), channel_id=1, source_target_pairs={{0,4},{2,6},{4,0},{6,2},{8,12},{10,14},{12,8},{14,10},{16,20},{18,... | collective-permute-start | bytes 245768 | tf_op jit(solution)/shard_map/ppermute | solution.py:351
  80.4 5.7 %collective-permute-done.13 = bf16[320,128]{1,0:T(8,128)(2,1)S(1)} collective-permute-done((bf16[320,128]{1,0:T(8,128)(2,1)S(1)}, bf16[320,128]{1,0:T(8,128)(2,1)S(1)}, u32[]{:S(2)}, u32[]{:S(2)}) %collective-permute-start.13) | collective-permute-done | bytes 81952 | tf_op jit(solution)/shard_map/ppermute | solution.py:351
  88.8 2.7 %collective-permute-start.19 = (bf16[320,128]{1,0:T(8,128)(2,1)S(1)}, bf16[320,128]{1,0:T(8,128)(2,1)S(1)}, u32[]{:S(2)}, u32[]{:S(2)}) collective-permute-start(bf16[320,128]{1,0:T(8,128)(2,1)S(1)} %get-tuple-element.46), channel_id=1, source_target_pairs={{0,4},{2,6},{4,0},{6,2},{8,12},{10,14},{12,8},{14,10},{16,20},{18,... | collective-permute-start | bytes 245768 | tf_op jit(solution)/shard_map/ppermute | solution.py:351
  91.5 5.5 %collective-permute-start.20 = (bf16[320,128]{1,0:T(8,128)(2,1)S(1)}, bf16[320,128]{1,0:T(8,128)(2,1)S(1)}, u32[]{:S(2)}, u32[]{:S(2)}) collective-permute-start(bf16[320,128]{1,0:T(8,128)(2,1)S(1)} %get-tuple-element.46), channel_id=1, source_target_pairs={{0,12},{2,14},{4,8},{6,10},{8,4},{10,6},{12,0},{14,2},{16,28},{18,... | collective-permute-start | bytes 245768 | tf_op jit(solution)/shard_map/ppermute | solution.py:351
  99.7 2.5 %collective-permute-start.21 = (bf16[1280,128]{1,0:T(8,128)(2,1)S(1)}, bf16[1280,128]{1,0:T(8,128)(2,1)S(1)}, u32[]{:S(2)}, u32[]{:S(2)}) collective-permute-start(bf16[1280,128]{1,0:T(8,128)(2,1)S(1)} %pad_maximum_fusion.1), channel_id=1, source_target_pairs={{0,2},{2,0},{4,6},{6,4},{8,10},{10,8},{12,14},{14,12},{16,18},{18,... | collective-permute-start | bytes 983048 | tf_op jit(solution)/shard_map/ppermute | solution.py:351
  102.4 6.2 %collective-permute-done.21 = bf16[1280,128]{1,0:T(8,128)(2,1)S(1)} collective-permute-done((bf16[1280,128]{1,0:T(8,128)(2,1)S(1)}, bf16[1280,128]{1,0:T(8,128)(2,1)S(1)}, u32[]{:S(2)}, u32[]{:S(2)}) %collective-permute-start.21) | collective-permute-done | bytes 327712 | tf_op jit(solution)/shard_map/ppermute | solution.py:351
  111.0 11.0 %gradient.4 = (f32[2560,128]{1,0:T(8,128)S(1)}, bf16[2560,128]{1,0:T(8,128)(2,1)S(1)}) custom-call(s32[16]{0:T(128)S(1)} %select_reduce_fusion.seq, s32[16]{0:T(128)S(1)} %copy-done.5, s32[16]{0:T(128)S(1)} %copy-done.1, s32[1]{0:T(128)} %bitcast.own, bf16[520,512,128]{2,1,0:T(8,128)(2,1)} %collect_support.3.blocks, ...), custom_call_target="tpu_custom_call" | custom-call | flops 5368709120 | bytes 10485760 | tf_op jit(solution)/shard_map/gradient/pallas_call | solution.py:329
  126.5 2.3 %collective-permute-start.28 = (bf16[1280,128]{1,0:T(8,128)(2,1)S(1)}, bf16[1280,128]{1,0:T(8,128)(2,1)S(1)}, u32[]{:S(2)}, u32[]{:S(2)}) collective-permute-start(bf16[1280,128]{1,0:T(8,128)(2,1)S(1)} %slice.183), channel_id=1, source_target_pairs={{0,2},{2,0},{4,6},{6,4},{8,10},{10,8},{12,14},{14,12},{16,18},{18,... | collective-permute-start | bytes 983048 | tf_op jit(solution)/shard_map/ppermute | solution.py:351
  129.6 5.8 %collective-permute-done.28 = bf16[1280,128]{1,0:T(8,128)(2,1)S(1)} collective-permute-done((bf16[1280,128]{1,0:T(8,128)(2,1)S(1)}, bf16[1280,128]{1,0:T(8,128)(2,1)S(1)}, u32[]{:S(2)}, u32[]{:S(2)}) %collective-permute-start.28) | collective-permute-done | bytes 327712 | tf_op jit(solution)/shard_map/ppermute | solution.py:351
  135.6 3.4 %collective-permute-start.29 = (bf16[320,128]{1,0:T(8,128)(2,1)S(1)}, bf16[320,128]{1,0:T(8,128)(2,1)S(1)}, u32[]{:S(2)}, u32[]{:S(2)}) collective-permute-start(bf16[320,128]{1,0:T(8,128)(2,1)S(1)} %get-tuple-element.64), channel_id=1, source_target_pairs={{0,8},{2,10},{4,12},{6,14},{8,0},{10,2},{12,4},{14,6},{16,24},{18,... | collective-permute-start | bytes 245768 | tf_op jit(solution)/shard_map/ppermute | solution.py:351
  138.9 4.6 %collective-permute-start.30 = (bf16[320,128]{1,0:T(8,128)(2,1)S(1)}, bf16[320,128]{1,0:T(8,128)(2,1)S(1)}, u32[]{:S(2)}, u32[]{:S(2)}) collective-permute-start(bf16[320,128]{1,0:T(8,128)(2,1)S(1)} %get-tuple-element.66), channel_id=1, source_target_pairs={{0,4},{2,6},{4,0},{6,2},{8,12},{10,14},{12,8},{14,10},{16,20},{18,... | collective-permute-start | bytes 245768 | tf_op jit(solution)/shard_map/ppermute | solution.py:351
  145.9 5.7 %collective-permute-done.31 = bf16[320,128]{1,0:T(8,128)(2,1)S(1)} collective-permute-done((bf16[320,128]{1,0:T(8,128)(2,1)S(1)}, bf16[320,128]{1,0:T(8,128)(2,1)S(1)}, u32[]{:S(2)}, u32[]{:S(2)}) %collective-permute-start.31) | collective-permute-done | bytes 81952 | tf_op jit(solution)/shard_map/ppermute | solution.py:351
  154.4 2.7 %collective-permute-start.37 = (bf16[320,128]{1,0:T(8,128)(2,1)S(1)}, bf16[320,128]{1,0:T(8,128)(2,1)S(1)}, u32[]{:S(2)}, u32[]{:S(2)}) collective-permute-start(bf16[320,128]{1,0:T(8,128)(2,1)S(1)} %get-tuple-element.40), channel_id=1, source_target_pairs={{0,4},{2,6},{4,0},{6,2},{8,12},{10,14},{12,8},{14,10},{16,20},{18,... | collective-permute-start | bytes 245768 | tf_op jit(solution)/shard_map/ppermute | solution.py:351
  157.1 5.5 %collective-permute-start.38 = (bf16[320,128]{1,0:T(8,128)(2,1)S(1)}, bf16[320,128]{1,0:T(8,128)(2,1)S(1)}, u32[]{:S(2)}, u32[]{:S(2)}) collective-permute-start(bf16[320,128]{1,0:T(8,128)(2,1)S(1)} %get-tuple-element.40), channel_id=1, source_target_pairs={{0,12},{2,14},{4,8},{6,10},{8,4},{10,6},{12,0},{14,2},{16,28},{18,... | collective-permute-start | bytes 245768 | tf_op jit(solution)/shard_map/ppermute | solution.py:351
  165.3 2.3 %collective-permute-start.39 = (bf16[1280,128]{1,0:T(8,128)(2,1)S(1)}, bf16[1280,128]{1,0:T(8,128)(2,1)S(1)}, u32[]{:S(2)}, u32[]{:S(2)}) collective-permute-start(bf16[1280,128]{1,0:T(8,128)(2,1)S(1)} %pad_maximum_fusion.2), channel_id=1, source_target_pairs={{0,2},{2,0},{4,6},{6,4},{8,10},{10,8},{12,14},{14,12},{16,18},{18,... | collective-permute-start | bytes 983048 | tf_op jit(solution)/shard_map/ppermute | solution.py:351
  167.9 6.4 %collective-permute-done.39 = bf16[1280,128]{1,0:T(8,128)(2,1)S(1)} collective-permute-done((bf16[1280,128]{1,0:T(8,128)(2,1)S(1)}, bf16[1280,128]{1,0:T(8,128)(2,1)S(1)}, u32[]{:S(2)}, u32[]{:S(2)}) %collective-permute-start.39) | collective-permute-done | bytes 327712 | tf_op jit(solution)/shard_map/ppermute | solution.py:351
  176.6 12.0 %gradient.5 = (f32[4096,128]{1,0:T(8,128)S(1)}, bf16[4096,128]{1,0:T(8,128)(2,1)S(1)}, bf16[8,64,128]{2,1,0:T(8,128)(2,1)S(1)}, f32[64,128]{1,0:T(8,128)S(1)}) custom-call(s32[16]{0:T(128)S(1)} %select_reduce_fusion.seq, s32[16]{0:T(128)S(1)} %copy-done.5, s32[16]{0:T(128)S(1)} %copy-done.1, s32[1]{0:T(128)} %bitcast.own, ...), custom_call_target="tpu_custom_call" | custom-call | flops 5368709120 | bytes 10485760 | tf_op jit(solution)/shard_map/gradient/pallas_call | solution.py:329
  188.8 2.5 %collective-permute-done.45 = bf16[4096,128]{1,0:T(8,128)(2,1)S(1)} collective-permute-done((bf16[4096,128]{1,0:T(8,128)(2,1)S(1)}, bf16[4096,128]{1,0:T(8,128)(2,1)S(1)}, u32[]{:S(2)}, u32[]{:S(2)}) %collective-permute-start.45) | collective-permute-done | bytes 1048608 | tf_op jit(solution)/shard_map/ppermute | solution.py:351
  193.8 2.3 %collective-permute-start.46 = (bf16[2048,128]{1,0:T(8,128)(2,1)S(1)}, bf16[2048,128]{1,0:T(8,128)(2,1)S(1)}, u32[]{:S(2)}, u32[]{:S(2)}) collective-permute-start(bf16[2048,128]{1,0:T(8,128)(2,1)S(1)} %slice.195), channel_id=1, source_target_pairs={{0,2},{2,0},{4,6},{6,4},{8,10},{10,8},{12,14},{14,12},{16,18},{18,... | collective-permute-start | bytes 1572872 | tf_op jit(solution)/shard_map/ppermute | solution.py:351
  197.0 7.9 %collective-permute-done.46 = bf16[2048,128]{1,0:T(8,128)(2,1)S(1)} collective-permute-done((bf16[2048,128]{1,0:T(8,128)(2,1)S(1)}, bf16[2048,128]{1,0:T(8,128)(2,1)S(1)}, u32[]{:S(2)}, u32[]{:S(2)}) %collective-permute-start.46) | collective-permute-done | bytes 524320 | tf_op jit(solution)/shard_map/ppermute | solution.py:351
  205.0 3.3 %collective-permute-start.47 = (bf16[512,128]{1,0:T(8,128)(2,1)S(1)}, bf16[512,128]{1,0:T(8,128)(2,1)S(1)}, u32[]{:S(2)}, u32[]{:S(2)}) collective-permute-start(bf16[512,128]{1,0:T(8,128)(2,1)S(1)} %get-tuple-element.61), channel_id=1, source_target_pairs={{0,8},{2,10},{4,12},{6,14},{8,0},{10,2},{12,4},{14,6},{16,24},{18,... | collective-permute-start | bytes 393224 | tf_op jit(solution)/shard_map/ppermute | solution.py:351
  208.4 4.6 %collective-permute-start.48 = (bf16[512,128]{1,0:T(8,128)(2,1)S(1)}, bf16[512,128]{1,0:T(8,128)(2,1)S(1)}, u32[]{:S(2)}, u32[]{:S(2)}) collective-permute-start(bf16[512,128]{1,0:T(8,128)(2,1)S(1)} %get-tuple-element.63), channel_id=1, source_target_pairs={{0,4},{2,6},{4,0},{6,2},{8,12},{10,14},{12,8},{14,10},{16,20},{18,... | collective-permute-start | bytes 393224 | tf_op jit(solution)/shard_map/ppermute | solution.py:351
  212.9 2.2 %collective-permute-start.49 = (bf16[512,128]{1,0:T(8,128)(2,1)S(1)}, bf16[512,128]{1,0:T(8,128)(2,1)S(1)}, u32[]{:S(2)}, u32[]{:S(2)}) collective-permute-start(bf16[512,128]{1,0:T(8,128)(2,1)S(1)} %get-tuple-element.62), channel_id=1, source_target_pairs={{0,12},{2,14},{4,8},{6,10},{8,4},{10,6},{12,0},{14,2},{16,28},{18,... | collective-permute-start | bytes 393224 | tf_op jit(solution)/shard_map/ppermute | solution.py:351
  215.9 5.7 %collective-permute-done.49 = bf16[512,128]{1,0:T(8,128)(2,1)S(1)} collective-permute-done((bf16[512,128]{1,0:T(8,128)(2,1)S(1)}, bf16[512,128]{1,0:T(8,128)(2,1)S(1)}, u32[]{:S(2)}, u32[]{:S(2)}) %collective-permute-start.49) | collective-permute-done | bytes 131104 | tf_op jit(solution)/shard_map/ppermute | solution.py:351
  (163 shorter events, 53.2 us)
Async XLA Ops:
  1.6 25.7 %collective-permute-start = (bf16[512,128]{1,0:T(8,128)(2,1)S(1)}, bf16[512,128]{1,0:T(8,128)(2,1)S(1)}, u32[]{:S(2)}, u32[]{:S(2)}) collective-permute-start(bf16[512,128]{1,0:T(8,128)(2,1)S(1)} %reshape.37), channel_id=1, source_target_pairs={{0,8},{2,10},{4,12},{6,14},{8,0},{10,2},{12,4},{14,6},{16,24},{18,... | collective-permute-start | bytes 393224 | tf_op jit(solution)/shard_map/ppermute | solution.py:351
  7.6 19.7 %collective-permute-start.1 = (bf16[512,128]{1,0:T(8,128)(2,1)S(1)}, bf16[512,128]{1,0:T(8,128)(2,1)S(1)}, u32[]{:S(2)}, u32[]{:S(2)}) collective-permute-start(bf16[512,128]{1,0:T(8,128)(2,1)S(1)} %reshape.37), channel_id=1, source_target_pairs={{0,4},{2,6},{4,0},{6,2},{8,12},{10,14},{12,8},{14,10},{16,20},{18,... | collective-permute-start | bytes 393224 | tf_op jit(solution)/shard_map/ppermute | solution.py:351
  11.1 16.2 %collective-permute-start.2 = (bf16[512,128]{1,0:T(8,128)(2,1)S(1)}, bf16[512,128]{1,0:T(8,128)(2,1)S(1)}, u32[]{:S(2)}, u32[]{:S(2)}) collective-permute-start(bf16[512,128]{1,0:T(8,128)(2,1)S(1)} %reshape.37), channel_id=1, source_target_pairs={{0,12},{2,14},{4,8},{6,10},{8,4},{10,6},{12,0},{14,2},{16,28},{18,... | collective-permute-start | bytes 393224 | tf_op jit(solution)/shard_map/ppermute | solution.py:351
  13.0 14.2 %collective-permute-start.3 = (bf16[512,128]{1,0:T(8,128)(2,1)S(1)}, bf16[512,128]{1,0:T(8,128)(2,1)S(1)}, u32[]{:S(2)}, u32[]{:S(2)}) collective-permute-start(bf16[512,128]{1,0:T(8,128)(2,1)S(1)} %reshape.37), channel_id=1, source_target_pairs={{1,3},{3,1},{5,7},{7,5},{9,11},{11,9},{13,15},{15,13},{17,19},{19,... | collective-permute-start | bytes 393224 | tf_op jit(solution)/shard_map/ppermute | solution.py:351
  27.3 14.7 %collective-permute-start.4 = (bf16[2048,128]{1,0:T(8,128)(2,1)S(1)}, bf16[2048,128]{1,0:T(8,128)(2,1)S(1)}, u32[]{:S(2)}, u32[]{:S(2)}) collective-permute-start(bf16[2048,128]{1,0:T(8,128)(2,1)S(1)} %pad_maximum_fusion), channel_id=1, source_target_pairs={{0,2},{2,0},{4,6},{6,4},{8,10},{10,8},{12,14},{14,12},{16,18},{18,... | collective-permute-start | bytes 1572872 | tf_op jit(solution)/shard_map/ppermute | solution.py:351
  31.0 11.0 %collective-permute-start.5 = (bf16[1024,128]{1,0:T(8,128)(2,1)S(1)}, bf16[1024,128]{1,0:T(8,128)(2,1)S(1)}, u32[]{:S(2)}, u32[]{:S(2)}) collective-permute-start(bf16[1024,128]{1,0:T(8,128)(2,1)S(1)} %pad_maximum_fusion.3), channel_id=1, source_target_pairs={{1,9},{3,11},{5,13},{7,15},{9,1},{11,3},{13,5},{15,7},{17,25},{19,... | collective-permute-start | bytes 786440 | tf_op jit(solution)/shard_map/ppermute | solution.py:351
  31.7 10.3 %collective-permute-start.6 = (bf16[1024,128]{1,0:T(8,128)(2,1)S(1)}, bf16[1024,128]{1,0:T(8,128)(2,1)S(1)}, u32[]{:S(2)}, u32[]{:S(2)}) collective-permute-start(bf16[1024,128]{1,0:T(8,128)(2,1)S(1)} %pad_maximum_fusion.3), channel_id=1, source_target_pairs={{1,5},{3,7},{5,1},{7,3},{9,13},{11,15},{13,9},{15,11},{17,21},{19,... | collective-permute-start | bytes 786440 | tf_op jit(solution)/shard_map/ppermute | solution.py:351
  32.4 9.6 %collective-permute-start.7 = (bf16[1024,128]{1,0:T(8,128)(2,1)S(1)}, bf16[1024,128]{1,0:T(8,128)(2,1)S(1)}, u32[]{:S(2)}, u32[]{:S(2)}) collective-permute-start(bf16[1024,128]{1,0:T(8,128)(2,1)S(1)} %pad_maximum_fusion.3), channel_id=1, source_target_pairs={{1,13},{3,15},{5,9},{7,11},{9,5},{11,7},{13,1},{15,3},{17,29},{19,... | collective-permute-start | bytes 786440 | tf_op jit(solution)/shard_map/ppermute | solution.py:351
  60.8 9.0 %collective-permute-start.10 = (bf16[1280,128]{1,0:T(8,128)(2,1)S(1)}, bf16[1280,128]{1,0:T(8,128)(2,1)S(1)}, u32[]{:S(2)}, u32[]{:S(2)}) collective-permute-start(bf16[1280,128]{1,0:T(8,128)(2,1)S(1)} %slice.171), channel_id=1, source_target_pairs={{0,2},{2,0},{4,6},{6,4},{8,10},{10,8},{12,14},{14,12},{16,18},{18,... | collective-permute-start | bytes 983048 | tf_op jit(solution)/shard_map/ppermute | solution.py:351
  63.2 16.9 %collective-permute-start.17 = (bf16[320,128]{1,0:T(8,128)(2,1)S(1)}, bf16[320,128]{1,0:T(8,128)(2,1)S(1)}, u32[]{:S(2)}, u32[]{:S(2)}) collective-permute-start(bf16[320,128]{1,0:T(8,128)(2,1)S(1)} %slice.277), channel_id=1, source_target_pairs={{1,3},{3,1},{5,7},{7,5},{9,11},{11,9},{13,15},{15,13},{17,19},{19,... | collective-permute-start | bytes 245768 | tf_op jit(solution)/shard_map/ppermute | solution.py:351
  69.9 10.1 %collective-permute-start.11 = (bf16[320,128]{1,0:T(8,128)(2,1)S(1)}, bf16[320,128]{1,0:T(8,128)(2,1)S(1)}, u32[]{:S(2)}, u32[]{:S(2)}) collective-permute-start(bf16[320,128]{1,0:T(8,128)(2,1)S(1)} %get-tuple-element.67), channel_id=1, source_target_pairs={{0,8},{2,10},{4,12},{6,14},{8,0},{10,2},{12,4},{14,6},{16,24},{18,... | collective-permute-start | bytes 245768 | tf_op jit(solution)/shard_map/ppermute | solution.py:351
  77.9 8.1 %collective-permute-start.13 = (bf16[320,128]{1,0:T(8,128)(2,1)S(1)}, bf16[320,128]{1,0:T(8,128)(2,1)S(1)}, u32[]{:S(2)}, u32[]{:S(2)}) collective-permute-start(bf16[320,128]{1,0:T(8,128)(2,1)S(1)} %get-tuple-element.68), channel_id=1, source_target_pairs={{0,12},{2,14},{4,8},{6,10},{8,4},{10,6},{12,0},{14,2},{16,28},{18,... | collective-permute-start | bytes 245768 | tf_op jit(solution)/shard_map/ppermute | solution.py:351
  86.2 10.9 %collective-permute-start.22 = (bf16[320,128]{1,0:T(8,128)(2,1)S(1)}, bf16[320,128]{1,0:T(8,128)(2,1)S(1)}, u32[]{:S(2)}, u32[]{:S(2)}) collective-permute-start(bf16[320,128]{1,0:T(8,128)(2,1)S(1)} %get-tuple-element.46), channel_id=1, source_target_pairs={{1,3},{3,1},{5,7},{7,5},{9,11},{11,9},{13,15},{15,13},{17,19},{19,... | collective-permute-start | bytes 245768 | tf_op jit(solution)/shard_map/ppermute | solution.py:351
  86.9 11.6 %collective-permute-start.18 = (bf16[320,128]{1,0:T(8,128)(2,1)S(1)}, bf16[320,128]{1,0:T(8,128)(2,1)S(1)}, u32[]{:S(2)}, u32[]{:S(2)}) collective-permute-start(bf16[320,128]{1,0:T(8,128)(2,1)S(1)} %get-tuple-element.46), channel_id=1, source_target_pairs={{0,8},{2,10},{4,12},{6,14},{8,0},{10,2},{12,4},{14,6},{16,24},{18,... | collective-permute-start | bytes 245768 | tf_op jit(solution)/shard_map/ppermute | solution.py:351
  88.8 10.3 %collective-permute-start.19 = (bf16[320,128]{1,0:T(8,128)(2,1)S(1)}, bf16[320,128]{1,0:T(8,128)(2,1)S(1)}, u32[]{:S(2)}, u32[]{:S(2)}) collective-permute-start(bf16[320,128]{1,0:T(8,128)(2,1)S(1)} %get-tuple-element.46), channel_id=1, source_target_pairs={{0,4},{2,6},{4,0},{6,2},{8,12},{10,14},{12,8},{14,10},{16,20},{18,... | collective-permute-start | bytes 245768 | tf_op jit(solution)/shard_map/ppermute | solution.py:351
  91.5 8.2 %collective-permute-start.20 = (bf16[320,128]{1,0:T(8,128)(2,1)S(1)}, bf16[320,128]{1,0:T(8,128)(2,1)S(1)}, u32[]{:S(2)}, u32[]{:S(2)}) collective-permute-start(bf16[320,128]{1,0:T(8,128)(2,1)S(1)} %get-tuple-element.46), channel_id=1, source_target_pairs={{0,12},{2,14},{4,8},{6,10},{8,4},{10,6},{12,0},{14,2},{16,28},{18,... | collective-permute-start | bytes 245768 | tf_op jit(solution)/shard_map/ppermute | solution.py:351
  99.7 9.0 %collective-permute-start.21 = (bf16[1280,128]{1,0:T(8,128)(2,1)S(1)}, bf16[1280,128]{1,0:T(8,128)(2,1)S(1)}, u32[]{:S(2)}, u32[]{:S(2)}) collective-permute-start(bf16[1280,128]{1,0:T(8,128)(2,1)S(1)} %pad_maximum_fusion.1), channel_id=1, source_target_pairs={{0,2},{2,0},{4,6},{6,4},{8,10},{10,8},{12,14},{14,12},{16,18},{18,... | collective-permute-start | bytes 983048 | tf_op jit(solution)/shard_map/ppermute | solution.py:351
  126.5 9.0 %collective-permute-start.28 = (bf16[1280,128]{1,0:T(8,128)(2,1)S(1)}, bf16[1280,128]{1,0:T(8,128)(2,1)S(1)}, u32[]{:S(2)}, u32[]{:S(2)}) collective-permute-start(bf16[1280,128]{1,0:T(8,128)(2,1)S(1)} %slice.183), channel_id=1, source_target_pairs={{0,2},{2,0},{4,6},{6,4},{8,10},{10,8},{12,14},{14,12},{16,18},{18,... | collective-permute-start | bytes 983048 | tf_op jit(solution)/shard_map/ppermute | solution.py:351
  128.9 16.8 %collective-permute-start.35 = (bf16[320,128]{1,0:T(8,128)(2,1)S(1)}, bf16[320,128]{1,0:T(8,128)(2,1)S(1)}, u32[]{:S(2)}, u32[]{:S(2)}) collective-permute-start(bf16[320,128]{1,0:T(8,128)(2,1)S(1)} %slice.276), channel_id=1, source_target_pairs={{1,3},{3,1},{5,7},{7,5},{9,11},{11,9},{13,15},{15,13},{17,19},{19,... | collective-permute-start | bytes 245768 | tf_op jit(solution)/shard_map/ppermute | solution.py:351
  135.6 10.1 %collective-permute-start.29 = (bf16[320,128]{1,0:T(8,128)(2,1)S(1)}, bf16[320,128]{1,0:T(8,128)(2,1)S(1)}, u32[]{:S(2)}, u32[]{:S(2)}) collective-permute-start(bf16[320,128]{1,0:T(8,128)(2,1)S(1)} %get-tuple-element.64), channel_id=1, source_target_pairs={{0,8},{2,10},{4,12},{6,14},{8,0},{10,2},{12,4},{14,6},{16,24},{18,... | collective-permute-start | bytes 245768 | tf_op jit(solution)/shard_map/ppermute | solution.py:351
  138.9 7.0 %collective-permute-start.30 = (bf16[320,128]{1,0:T(8,128)(2,1)S(1)}, bf16[320,128]{1,0:T(8,128)(2,1)S(1)}, u32[]{:S(2)}, u32[]{:S(2)}) collective-permute-start(bf16[320,128]{1,0:T(8,128)(2,1)S(1)} %get-tuple-element.66), channel_id=1, source_target_pairs={{0,4},{2,6},{4,0},{6,2},{8,12},{10,14},{12,8},{14,10},{16,20},{18,... | collective-permute-start | bytes 245768 | tf_op jit(solution)/shard_map/ppermute | solution.py:351
  143.5 8.1 %collective-permute-start.31 = (bf16[320,128]{1,0:T(8,128)(2,1)S(1)}, bf16[320,128]{1,0:T(8,128)(2,1)S(1)}, u32[]{:S(2)}, u32[]{:S(2)}) collective-permute-start(bf16[320,128]{1,0:T(8,128)(2,1)S(1)} %get-tuple-element.65), channel_id=1, source_target_pairs={{0,12},{2,14},{4,8},{6,10},{8,4},{10,6},{12,0},{14,2},{16,28},{18,... | collective-permute-start | bytes 245768 | tf_op jit(solution)/shard_map/ppermute | solution.py:351
  151.8 10.9 %collective-permute-start.40 = (bf16[320,128]{1,0:T(8,128)(2,1)S(1)}, bf16[320,128]{1,0:T(8,128)(2,1)S(1)}, u32[]{:S(2)}, u32[]{:S(2)}) collective-permute-start(bf16[320,128]{1,0:T(8,128)(2,1)S(1)} %get-tuple-element.40), channel_id=1, source_target_pairs={{1,3},{3,1},{5,7},{7,5},{9,11},{11,9},{13,15},{15,13},{17,19},{19,... | collective-permute-start | bytes 245768 | tf_op jit(solution)/shard_map/ppermute | solution.py:351
  152.5 11.6 %collective-permute-start.36 = (bf16[320,128]{1,0:T(8,128)(2,1)S(1)}, bf16[320,128]{1,0:T(8,128)(2,1)S(1)}, u32[]{:S(2)}, u32[]{:S(2)}) collective-permute-start(bf16[320,128]{1,0:T(8,128)(2,1)S(1)} %get-tuple-element.40), channel_id=1, source_target_pairs={{0,8},{2,10},{4,12},{6,14},{8,0},{10,2},{12,4},{14,6},{16,24},{18,... | collective-permute-start | bytes 245768 | tf_op jit(solution)/shard_map/ppermute | solution.py:351
  154.4 10.3 %collective-permute-start.37 = (bf16[320,128]{1,0:T(8,128)(2,1)S(1)}, bf16[320,128]{1,0:T(8,128)(2,1)S(1)}, u32[]{:S(2)}, u32[]{:S(2)}) collective-permute-start(bf16[320,128]{1,0:T(8,128)(2,1)S(1)} %get-tuple-element.40), channel_id=1, source_target_pairs={{0,4},{2,6},{4,0},{6,2},{8,12},{10,14},{12,8},{14,10},{16,20},{18,... | collective-permute-start | bytes 245768 | tf_op jit(solution)/shard_map/ppermute | solution.py:351
  157.1 8.2 %collective-permute-start.38 = (bf16[320,128]{1,0:T(8,128)(2,1)S(1)}, bf16[320,128]{1,0:T(8,128)(2,1)S(1)}, u32[]{:S(2)}, u32[]{:S(2)}) collective-permute-start(bf16[320,128]{1,0:T(8,128)(2,1)S(1)} %get-tuple-element.40), channel_id=1, source_target_pairs={{0,12},{2,14},{4,8},{6,10},{8,4},{10,6},{12,0},{14,2},{16,28},{18,... | collective-permute-start | bytes 245768 | tf_op jit(solution)/shard_map/ppermute | solution.py:351
  165.3 9.0 %collective-permute-start.39 = (bf16[1280,128]{1,0:T(8,128)(2,1)S(1)}, bf16[1280,128]{1,0:T(8,128)(2,1)S(1)}, u32[]{:S(2)}, u32[]{:S(2)}) collective-permute-start(bf16[1280,128]{1,0:T(8,128)(2,1)S(1)} %pad_maximum_fusion.2), channel_id=1, source_target_pairs={{0,2},{2,0},{4,6},{6,4},{8,10},{10,8},{12,14},{14,12},{16,18},{18,... | collective-permute-start | bytes 983048 | tf_op jit(solution)/shard_map/ppermute | solution.py:351
  193.8 11.1 %collective-permute-start.46 = (bf16[2048,128]{1,0:T(8,128)(2,1)S(1)}, bf16[2048,128]{1,0:T(8,128)(2,1)S(1)}, u32[]{:S(2)}, u32[]{:S(2)}) collective-permute-start(bf16[2048,128]{1,0:T(8,128)(2,1)S(1)} %slice.195), channel_id=1, source_target_pairs={{0,2},{2,0},{4,6},{6,4},{8,10},{10,8},{12,14},{14,12},{16,18},{18,... | collective-permute-start | bytes 1572872 | tf_op jit(solution)/shard_map/ppermute | solution.py:351
  196.3 18.9 %collective-permute-start.53 = (bf16[512,128]{1,0:T(8,128)(2,1)S(1)}, bf16[512,128]{1,0:T(8,128)(2,1)S(1)}, u32[]{:S(2)}, u32[]{:S(2)}) collective-permute-start(bf16[512,128]{1,0:T(8,128)(2,1)S(1)} %slice.275), channel_id=1, source_target_pairs={{1,3},{3,1},{5,7},{7,5},{9,11},{11,9},{13,15},{15,13},{17,19},{19,... | collective-permute-start | bytes 393224 | tf_op jit(solution)/shard_map/ppermute | solution.py:351
  205.0 10.2 %collective-permute-start.47 = (bf16[512,128]{1,0:T(8,128)(2,1)S(1)}, bf16[512,128]{1,0:T(8,128)(2,1)S(1)}, u32[]{:S(2)}, u32[]{:S(2)}) collective-permute-start(bf16[512,128]{1,0:T(8,128)(2,1)S(1)} %get-tuple-element.61), channel_id=1, source_target_pairs={{0,8},{2,10},{4,12},{6,14},{8,0},{10,2},{12,4},{14,6},{16,24},{18,... | collective-permute-start | bytes 393224 | tf_op jit(solution)/shard_map/ppermute | solution.py:351
  208.4 7.5 %collective-permute-start.48 = (bf16[512,128]{1,0:T(8,128)(2,1)S(1)}, bf16[512,128]{1,0:T(8,128)(2,1)S(1)}, u32[]{:S(2)}, u32[]{:S(2)}) collective-permute-start(bf16[512,128]{1,0:T(8,128)(2,1)S(1)} %get-tuple-element.63), channel_id=1, source_target_pairs={{0,4},{2,6},{4,0},{6,2},{8,12},{10,14},{12,8},{14,10},{16,20},{18,... | collective-permute-start | bytes 393224 | tf_op jit(solution)/shard_map/ppermute | solution.py:351
  212.9 8.7 %collective-permute-start.49 = (bf16[512,128]{1,0:T(8,128)(2,1)S(1)}, bf16[512,128]{1,0:T(8,128)(2,1)S(1)}, u32[]{:S(2)}, u32[]{:S(2)}) collective-permute-start(bf16[512,128]{1,0:T(8,128)(2,1)S(1)} %get-tuple-element.62), channel_id=1, source_target_pairs={{0,12},{2,14},{4,8},{6,10},{8,4},{10,6},{12,0},{14,2},{16,28},{18,... | collective-permute-start | bytes 393224 | tf_op jit(solution)/shard_map/ppermute | solution.py:351
  (29 other events, 128.6 us)

commit v7 on v6

--- a/solution.py
+++ b/solution.py
@@ -133,8 +133,12 @@
     )(seq, order, support, counts, dictionary, *before)
 
 
-def stage_orders(devices):
-    distances = [2**bit for bit in range(devices.bit_length() - 1)]
+def stage_distances(devices):
+    return [2**bit for bit in range(devices.bit_length() - 1)]
+
+
+def last_orders(devices):
+    distances = stage_distances(devices)
     return distances, distances[:1] + distances[2:] + distances[1:2]
 
 
@@ -170,16 +174,16 @@
         load(index).start()
     held[pairs:] = jnp.zeros((SPARE,) + held.shape[1:], held.dtype)
 
-    orders = stage_orders(shards)
-
-    def holder(slot):
-        far_half = slot >= shards // 2
-        even = slot_distance(slot, orders[1 if far_half else 0])
-        odd = slot_distance(slot, orders[0 if far_half else 1])
+    distances = stage_distances(shards)
+
+    def shard_span(slot, size):
+        return pl.ds(pl.multiple_of((slot_distance(slot, distances) ^ me) * size, ROW_TILE), size)
+
+    def last_holder(slot):
+        even, odd = (slot_distance(slot, order) for order in last_orders(shards))
+        if slot >= shards // 2:
+            even, odd = odd, even
         return jnp.where(me % 2 == 0, even, odd) ^ me
-
-    def shard_span(slot, size):
-        return pl.ds(pl.multiple_of(holder(slot) * size, ROW_TILE), size)
 
     size_in = 2 * near.shape[0] // shards
     for slot in range(shards):
@@ -294,7 +298,7 @@
             sent[pair] = part
         thresh_out[...] = thresh[order[me]]
         for slot in range(shards):
-            position = holder(slot)
+            position = last_holder(slot)
             offset = offsets[position]
             live = counts[order[position]]
             parts = [total[tile(offset // 2 + pair), :] for pair in range(SLOT_PAIRS + 1)]
@@ -346,53 +350,44 @@
     )(*scalars, blocks, near, far, targets, *extra)
 
 
-def exchange(value, distance, cores=(0, 1)):
+def exchange(value, even, odd=None):
     devices = lax.axis_size("rows")
-    return lax.ppermute(value, "rows", [(i, i ^ distance) for i in range(devices) if i % 2 in cores])
-
-
-def column_distances(devices):
-    distances = stage_orders(devices)[0][2:]
-    return [slot_distance(slot, distances) for slot in range(devices // 4)]
-
-
-def by_core(even, odd):
-    return jnp.where(lax.axis_index("rows") % 2 == 0, even, odd)
+    apart = (even, even if odd is None else odd)
+    return lax.ppermute(value, "rows", [(i, i ^ apart[i % 2]) for i in range(devices)])
 
 
 def gather_shards(own, beside=()):
-    apart = column_distances(lax.axis_size("rows"))[1:]
+    distances = stage_distances(lax.axis_size("rows"))
+    apart = [slot_distance(slot, distances[2:]) for slot in range(lax.axis_size("rows") // 4)]
     made = ()
-    quarter = jnp.concatenate([own] + [exchange(own, distance, (0,)) for distance in apart], axis=0)
-    couple = jnp.concatenate([own, exchange(own, 2, (1,))], axis=0)
+    value = jnp.concatenate([own] + [exchange(own, distance) for distance in apart[1:]], axis=0)
     if beside:
-        quarter, couple, *made = lax.optimization_barrier((quarter, couple, beside[0]()))
-    even = jnp.concatenate([quarter, exchange(quarter, 2, (0,))], axis=0)
-    odd = jnp.concatenate([couple] + [exchange(couple, distance, (1,)) for distance in apart], axis=0)
-    near = by_core(even, odd)
+        value, *made = lax.optimization_barrier((value, beside[0]()))
+    value = jnp.concatenate([value, exchange(value, distances[1])], axis=0)
     if beside:
-        near, *made = lax.optimization_barrier((near, beside[1](*made)))
-    return near, exchange(near, 1), made
+        value, *made = lax.optimization_barrier((value, beside[1](*made)))
+    return value, exchange(value, distances[0]), made
 
 
 def reduce_shards(keep, send):
     devices = lax.axis_size("rows")
-    apart = column_distances(devices)
+    distances = stage_distances(devices)
+    half = keep + exchange(send, distances[0]).astype(jnp.float32)
     size = 2 * keep.shape[0] // devices
-
-    def arrived(value, distance, cores):
-        return exchange(value.astype(jnp.bfloat16), distance, cores).astype(jnp.float32)
-
+    sent = half.astype(jnp.bfloat16)
+    total = half[:size]
+    for slot in range(1, devices // 2):
+        share = exchange(sent[slot * size : (slot + 1) * size], slot_distance(slot, distances[1:]))
+        total = total + share.astype(jnp.float32)
+    return total
+
+
+def last_reduce(keep, send):
     total = keep + exchange(send, 1).astype(jnp.float32)
-    middle = total.shape[0] // 2
-    even = total[:middle] + arrived(total[middle:], 2, (0,))
-    odd = total[: 2 * size]
-    for place in range(1, len(apart)):
-        odd = odd + arrived(total[2 * place * size : 2 * (place + 1) * size], apart[place], (1,))
-    sums = even[:size]
-    for place in range(1, len(apart)):
-        sums = sums + arrived(even[place * size : (place + 1) * size], apart[place], (0,))
-    return by_core(sums, odd[:size] + arrived(odd[size:], 2, (1,)))
+    for even, odd in list(zip(*last_orders(lax.axis_size("rows"))))[1:]:
+        middle = total.shape[0] // 2
+        total = total[:middle] + exchange(total[middle:].astype(jnp.bfloat16), even, odd).astype(jnp.float32)
+    return total
 
 
 def packed_order(live):
@@ -435,7 +430,7 @@
         previous = current
         near, far, _ = gather_shards(point.astype(jnp.bfloat16))
     keep, send, sent, thresh = run("final", near=near, far=far, extra=(thresh_tiles,))
-    gradient = reduce_shards(keep, send).reshape(SLOT_PAIRS, PATCHES, LANES)
+    gradient = last_reduce(keep, send).reshape(SLOT_PAIRS, PATCHES, LANES)
     sent = sent.astype(jnp.float32)
     result = shrink(sent - 0.5 * gradient, thresh[None])
     result = result.reshape(SLOT_PAIRS, PATCHES, 2, BLOCK).transpose(0, 2, 1, 3)

time: 224 us -> 183 us (0.82)
  starting transfers between devices: 94.2 us -> 52.8 us
  waiting for transfers between devices: 63.6 us -> 65.9 us
    ppermute x54 -> x35, starting transfers between devices: 94.2 us -> 52.8 us  [exchange(): lax.ppermute(value, 'rows', [(i, i ^ apart[i % 2]) for i in range(devices)])]
    ppermute x54 -> x35, waiting for transfers between devices: 63.6 us -> 65.9 us  [exchange(): lax.ppermute(value, 'rows', [(i, i ^ apart[i % 2]) for i in range(devices)])]
  transfers between devices with their start and end apart: 54 -> 35, of which waited for: 19 -> 21; matrix products, arithmetic and copies ran while one was open for 3% -> 2% of each run, Pallas kernels for 8% -> 10%
where the time goes in v7:
time: 183 us; the launch traced here: 182 us
  waiting for transfers between devices  65.9 us (36%)
  starting transfers between devices  52.8 us (29%)
  Pallas kernels  51.9 us (28%)
  local copies, waits for them, and re-layouts  8.23 us (4%)
  other arithmetic  2.82 us (2%)
    ppermute x35, waiting for transfers between devices, exchange(): lax.ppermute(value, 'rows', [(i, i ^ apart[i % 2]) for i in range(devices)])  65.9 us
    ppermute x35, starting transfers between devices, exchange(): lax.ppermute(value, 'rows', [(i, i ^ apart[i % 2]) for i in range(devices)])  52.8 us
    pallas_call x3, Pallas kernels, gradient_call(): pl.pallas_call(functools.partial(gradient_kernel, mode, shards, pairs), g...  34.4 us
    pallas_call x2, Pallas kernels, collect_support(): pl.pallas_call(functools.partial(support_kernel, part * entries), grid_sp...  17.5 us
  transfers between devices with their start and end apart: 35, of which 21 were waited for; matrix products, arithmetic and copies ran while one was open for 2% of the time, Pallas kernels for 10%

profile of v7, /device:TPU:0, one launch (start us, length us, event | category | flops | bytes accessed | tf_op | source)
XLA Modules:
  0.0 182.1 jit_solution(5272404311954577395)
XLA Ops:
  1.6 4.1 %collective-permute-start = (bf16[512,128]{1,0:T(8,128)(2,1)S(1)}, bf16[512,128]{1,0:T(8,128)(2,1)S(1)}, u32[]{:S(2)}, u32[]{:S(2)}) collective-permute-start(bf16[512,128]{1,0:T(8,128)(2,1)S(1)} %reshape.37), channel_id=1, source_target_pairs={{0,8},{1,9},{2,10},{3,11},{4,12},{5,13},{6,14},{7,15},{8,0},{9,1},... | collective-permute-start | bytes 393224 | tf_op jit(solution)/shard_map/ppermute | solution.py:356
  12.2 8.7 %collect_support.2.refs_0_ = bf16[520,512,128]{2,1,0:T(8,128)(2,1)} custom-call(s32[16]{0:T(128)S(1)} %select_reduce_fusion.seq, s32[16]{0:T(128)S(1)} %copy-done.3, s32[16,16]{1,0:T(8,128)S(1)} %copy-done.2, s32[16]{0:T(128)S(1)} %copy-done, bf16[512,32768]{1,0:T(8,128)(2,1)} %dictionary.3), custom_call_target="tpu_custom_call" | custom-call | bytes 31457280 | tf_op jit(solution)/shard_map/collect_support/pallas_call | solution.py:113
  22.8 8.9 %collect_support.3.blocks = bf16[520,512,128]{2,1,0:T(8,128)(2,1)} custom-call(s32[16]{0:T(128)S(1)} %select_reduce_fusion.seq, s32[16]{0:T(128)S(1)} %copy-done.3, s32[16,16]{1,0:T(8,128)S(1)} %copy-done.2, s32[16]{0:T(128)S(1)} %copy-done, bf16[512,32768]{1,0:T(8,128)(2,1)} %dictionary.3, ...), custom_call_target="tpu_custom_call", output_to_operand_aliasing={{}: (5, {})} | custom-call | bytes 31457280 | tf_op jit(solution)/shard_map/collect_support/pallas_call | solution.py:113
  31.7 2.4 %collective-permute-done.3 = bf16[2048,128]{1,0:T(8,128)(2,1)S(1)} collective-permute-done((bf16[2048,128]{1,0:T(8,128)(2,1)S(1)}, bf16[2048,128]{1,0:T(8,128)(2,1)S(1)}, u32[]{:S(2)}, u32[]{:S(2)}) %collective-permute-start.3) | collective-permute-done | bytes 524320 | tf_op jit(solution)/shard_map/ppermute | solution.py:356
  37.1 11.2 %gradient.3 = (f32[2560,128]{1,0:T(8,128)S(1)}, bf16[2560,128]{1,0:T(8,128)(2,1)S(1)}, bf16[320,128]{1,0:T(8,128)(2,1)S(1)}, f32[320,128]{1,0:T(8,128)S(1)}) custom-call(s32[16]{0:T(128)S(1)} %select_reduce_fusion.seq, s32[16]{0:T(128)S(1)} %copy-done.4, s32[16]{0:T(128)S(1)} %copy-done.1, s32[1]{0:T(128)} %bitcast.own, ...), custom_call_target="tpu_custom_call" | custom-call | flops 5368709120 | bytes 10485760 | tf_op jit(solution)/shard_map/gradient/pallas_call | solution.py:333
  48.5 2.0 %collective-permute-done.5 = bf16[2560,128]{1,0:T(8,128)(2,1)S(1)} collective-permute-done((bf16[2560,128]{1,0:T(8,128)(2,1)S(1)}, bf16[2560,128]{1,0:T(8,128)(2,1)S(1)}, u32[]{:S(2)}, u32[]{:S(2)}) %collective-permute-start.5) | collective-permute-done | bytes 655392 | tf_op jit(solution)/shard_map/ppermute | solution.py:356
  50.7 2.7 %collective-permute-start.10 = (bf16[320,128]{1,0:T(8,128)(2,1)S(1)}, bf16[320,128]{1,0:T(8,128)(2,1)S(1)}, u32[]{:S(2)}, u32[]{:S(2)}) collective-permute-start(bf16[320,128]{1,0:T(8,128)(2,1)S(1)} %get-tuple-element.52), channel_id=1, source_target_pairs={{0,10},{1,11},{2,8},{3,9},{4,14},{5,15},{6,12},{7,13},{8,2},{9,3},... | collective-permute-start | bytes 245768 | tf_op jit(solution)/shard_map/ppermute | solution.py:356
  53.3 2.4 %collective-permute-start.11 = (bf16[320,128]{1,0:T(8,128)(2,1)S(1)}, bf16[320,128]{1,0:T(8,128)(2,1)S(1)}, u32[]{:S(2)}, u32[]{:S(2)}) collective-permute-start(bf16[320,128]{1,0:T(8,128)(2,1)S(1)} %get-tuple-element.51), channel_id=1, source_target_pairs={{0,6},{1,7},{2,4},{3,5},{4,2},{5,3},{6,0},{7,1},{8,14},{9,15},{10,... | collective-permute-start | bytes 245768 | tf_op jit(solution)/shard_map/ppermute | solution.py:356
  57.7 3.4 %collective-permute-start.7 = (bf16[320,128]{1,0:T(8,128)(2,1)S(1)}, bf16[320,128]{1,0:T(8,128)(2,1)S(1)}, u32[]{:S(2)}, u32[]{:S(2)}) collective-permute-start(bf16[320,128]{1,0:T(8,128)(2,1)S(1)} %get-tuple-element.55), channel_id=1, source_target_pairs={{0,4},{1,5},{2,6},{3,7},{4,0},{5,1},{6,2},{7,3},{8,12},{9,13},{10,... | collective-permute-start | bytes 245768 | tf_op jit(solution)/shard_map/ppermute | solution.py:356
  61.5 2.5 %collective-permute-start.9 = (bf16[320,128]{1,0:T(8,128)(2,1)S(1)}, bf16[320,128]{1,0:T(8,128)(2,1)S(1)}, u32[]{:S(2)}, u32[]{:S(2)}) collective-permute-start(bf16[320,128]{1,0:T(8,128)(2,1)S(1)} %get-tuple-element.53), channel_id=1, source_target_pairs={{0,2},{1,3},{2,0},{3,1},{4,6},{5,7},{6,4},{7,5},{8,10},{9,11},{10,... | collective-permute-start | bytes 245768 | tf_op jit(solution)/shard_map/ppermute | solution.py:356
  64.0 4.2 %collective-permute-done.6 = bf16[320,128]{1,0:T(8,128)(2,1)S(1)} collective-permute-done((bf16[320,128]{1,0:T(8,128)(2,1)S(1)}, bf16[320,128]{1,0:T(8,128)(2,1)S(1)}, u32[]{:S(2)}, u32[]{:S(2)}) %collective-permute-start.6) | collective-permute-done | bytes 81952 | tf_op jit(solution)/shard_map/ppermute | solution.py:356
  68.3 3.0 %collective-permute-start.13 = (bf16[320,128]{1,0:T(8,128)(2,1)S(1)}, bf16[320,128]{1,0:T(8,128)(2,1)S(1)}, u32[]{:S(2)}, u32[]{:S(2)}) collective-permute-start(bf16[320,128]{1,0:T(8,128)(2,1)S(1)} %get-tuple-element.38), channel_id=1, source_target_pairs={{0,8},{1,9},{2,10},{3,11},{4,12},{5,13},{6,14},{7,15},{8,0},{9,1},... | collective-permute-start | bytes 245768 | tf_op jit(solution)/shard_map/ppermute | solution.py:356
  72.8 3.3 %collective-permute-done.13 = bf16[320,128]{1,0:T(8,128)(2,1)S(1)} collective-permute-done((bf16[320,128]{1,0:T(8,128)(2,1)S(1)}, bf16[320,128]{1,0:T(8,128)(2,1)S(1)}, u32[]{:S(2)}, u32[]{:S(2)}) %collective-permute-start.13) | collective-permute-done | bytes 81952 | tf_op jit(solution)/shard_map/ppermute | solution.py:356
  79.0 7.6 %collective-permute-done.16 = bf16[1280,128]{1,0:T(8,128)(2,1)S(1)} collective-permute-done((bf16[1280,128]{1,0:T(8,128)(2,1)S(1)}, bf16[1280,128]{1,0:T(8,128)(2,1)S(1)}, u32[]{:S(2)}, u32[]{:S(2)}) %collective-permute-start.16) | collective-permute-done | bytes 327712 | tf_op jit(solution)/shard_map/ppermute | solution.py:356
  86.7 2.1 %collective-permute-done.17.far = bf16[2560,128]{1,0:T(8,128)(2,1)S(1)} collective-permute-done((bf16[2560,128]{1,0:T(8,128)(2,1)S(1)}, bf16[2560,128]{1,0:T(8,128)(2,1)S(1)}, u32[]{:S(2)}, u32[]{:S(2)}) %collective-permute-start.17) | collective-permute-done | bytes 655392 | tf_op jit(solution)/shard_map/ppermute | solution.py:356
  88.8 11.2 %gradient.4 = (f32[2560,128]{1,0:T(8,128)S(1)}, bf16[2560,128]{1,0:T(8,128)(2,1)S(1)}) custom-call(s32[16]{0:T(128)S(1)} %select_reduce_fusion.seq, s32[16]{0:T(128)S(1)} %copy-done.4, s32[16]{0:T(128)S(1)} %copy-done.1, s32[1]{0:T(128)} %bitcast.own, bf16[520,512,128]{2,1,0:T(8,128)(2,1)} %collect_support.3.blocks, ...), custom_call_target="tpu_custom_call" | custom-call | flops 5368709120 | bytes 10485760 | tf_op jit(solution)/shard_map/gradient/pallas_call | solution.py:333
  100.2 2.0 %collective-permute-done.18 = bf16[2560,128]{1,0:T(8,128)(2,1)S(1)} collective-permute-done((bf16[2560,128]{1,0:T(8,128)(2,1)S(1)}, bf16[2560,128]{1,0:T(8,128)(2,1)S(1)}, u32[]{:S(2)}, u32[]{:S(2)}) %collective-permute-start.18) | collective-permute-done | bytes 655392 | tf_op jit(solution)/shard_map/ppermute | solution.py:356
  102.4 2.9 %collective-permute-start.19 = (bf16[320,128]{1,0:T(8,128)(2,1)S(1)}, bf16[320,128]{1,0:T(8,128)(2,1)S(1)}, u32[]{:S(2)}, u32[]{:S(2)}) collective-permute-start(bf16[320,128]{1,0:T(8,128)(2,1)S(1)} %get-tuple-element.42), channel_id=1, source_target_pairs={{0,8},{1,9},{2,10},{3,11},{4,12},{5,13},{6,14},{7,15},{8,0},{9,1},... | collective-permute-start | bytes 245768 | tf_op jit(solution)/shard_map/ppermute | solution.py:356
  108.0 2.2 %collective-permute-start.23 = (bf16[320,128]{1,0:T(8,128)(2,1)S(1)}, bf16[320,128]{1,0:T(8,128)(2,1)S(1)}, u32[]{:S(2)}, u32[]{:S(2)}) collective-permute-start(bf16[320,128]{1,0:T(8,128)(2,1)S(1)} %get-tuple-element.45), channel_id=1, source_target_pairs={{0,10},{1,11},{2,8},{3,9},{4,14},{5,15},{6,12},{7,13},{8,2},{9,3},... | collective-permute-start | bytes 245768 | tf_op jit(solution)/shard_map/ppermute | solution.py:356
  111.8 4.0 %collective-permute-start.25 = (bf16[320,128]{1,0:T(8,128)(2,1)S(1)}, bf16[320,128]{1,0:T(8,128)(2,1)S(1)}, u32[]{:S(2)}, u32[]{:S(2)}) collective-permute-start(bf16[320,128]{1,0:T(8,128)(2,1)S(1)} %get-tuple-element.43), channel_id=1, source_target_pairs={{0,14},{1,15},{2,12},{3,13},{4,10},{5,11},{6,8},{7,9},{8,6},{9,7},... | collective-permute-start | bytes 245768 | tf_op jit(solution)/shard_map/ppermute | solution.py:356
  115.9 2.5 %collective-permute-done.23 = bf16[320,128]{1,0:T(8,128)(2,1)S(1)} collective-permute-done((bf16[320,128]{1,0:T(8,128)(2,1)S(1)}, bf16[320,128]{1,0:T(8,128)(2,1)S(1)}, u32[]{:S(2)}, u32[]{:S(2)}) %collective-permute-start.23) | collective-permute-done | bytes 81952 | tf_op jit(solution)/shard_map/ppermute | solution.py:356
  119.4 3.0 %collective-permute-start.26 = (bf16[320,128]{1,0:T(8,128)(2,1)S(1)}, bf16[320,128]{1,0:T(8,128)(2,1)S(1)}, u32[]{:S(2)}, u32[]{:S(2)}) collective-permute-start(bf16[320,128]{1,0:T(8,128)(2,1)S(1)} %get-tuple-element.34), channel_id=1, source_target_pairs={{0,8},{1,9},{2,10},{3,11},{4,12},{5,13},{6,14},{7,15},{8,0},{9,1},... | collective-permute-start | bytes 245768 | tf_op jit(solution)/shard_map/ppermute | solution.py:356
  124.0 3.6 %collective-permute-done.26 = bf16[320,128]{1,0:T(8,128)(2,1)S(1)} collective-permute-done((bf16[320,128]{1,0:T(8,128)(2,1)S(1)}, bf16[320,128]{1,0:T(8,128)(2,1)S(1)}, u32[]{:S(2)}, u32[]{:S(2)}) %collective-permute-start.26) | collective-permute-done | bytes 81952 | tf_op jit(solution)/shard_map/ppermute | solution.py:356
  130.9 6.6 %collective-permute-done.29 = bf16[1280,128]{1,0:T(8,128)(2,1)S(1)} collective-permute-done((bf16[1280,128]{1,0:T(8,128)(2,1)S(1)}, bf16[1280,128]{1,0:T(8,128)(2,1)S(1)}, u32[]{:S(2)}, u32[]{:S(2)}) %collective-permute-start.29) | collective-permute-done | bytes 327712 | tf_op jit(solution)/shard_map/ppermute | solution.py:356
  137.6 2.1 %collective-permute-done.30.far = bf16[2560,128]{1,0:T(8,128)(2,1)S(1)} collective-permute-done((bf16[2560,128]{1,0:T(8,128)(2,1)S(1)}, bf16[2560,128]{1,0:T(8,128)(2,1)S(1)}, u32[]{:S(2)}, u32[]{:S(2)}) %collective-permute-start.30) | collective-permute-done | bytes 655392 | tf_op jit(solution)/shard_map/ppermute | solution.py:356
  139.7 12.0 %gradient.5 = (f32[4096,128]{1,0:T(8,128)S(1)}, bf16[4096,128]{1,0:T(8,128)(2,1)S(1)}, bf16[8,64,128]{2,1,0:T(8,128)(2,1)S(1)}, f32[64,128]{1,0:T(8,128)S(1)}) custom-call(s32[16]{0:T(128)S(1)} %select_reduce_fusion.seq, s32[16]{0:T(128)S(1)} %copy-done.4, s32[16]{0:T(128)S(1)} %copy-done.1, s32[1]{0:T(128)} %bitcast.own, ...), custom_call_target="tpu_custom_call" | custom-call | flops 5368709120 | bytes 10485760 | tf_op jit(solution)/shard_map/gradient/pallas_call | solution.py:333
  151.9 2.5 %collective-permute-done.31 = bf16[4096,128]{1,0:T(8,128)(2,1)S(1)} collective-permute-done((bf16[4096,128]{1,0:T(8,128)(2,1)S(1)}, bf16[4096,128]{1,0:T(8,128)(2,1)S(1)}, u32[]{:S(2)}, u32[]{:S(2)}) %collective-permute-start.31) | collective-permute-done | bytes 1048608 | tf_op jit(solution)/shard_map/ppermute | solution.py:356
  156.2 7.7 %collective-permute-done.32 = bf16[2048,128]{1,0:T(8,128)(2,1)S(1)} collective-permute-done((bf16[2048,128]{1,0:T(8,128)(2,1)S(1)}, bf16[2048,128]{1,0:T(8,128)(2,1)S(1)}, u32[]{:S(2)}, u32[]{:S(2)}) %collective-permute-start.32) | collective-permute-done | bytes 524320 | tf_op jit(solution)/shard_map/ppermute | solution.py:356
  164.0 2.8 %collective-permute-start.33 = (bf16[1024,128]{1,0:T(8,128)(2,1)S(1)}, bf16[1024,128]{1,0:T(8,128)(2,1)S(1)}, u32[]{:S(2)}, u32[]{:S(2)}) collective-permute-start(bf16[1024,128]{1,0:T(8,128)(2,1)S(1)} %slice.162), channel_id=1, source_target_pairs={{0,4},{1,9},{2,6},{3,11},{4,0},{5,13},{6,2},{7,15},{8,12},{9,1},{1... | collective-permute-start | bytes 786440 | tf_op jit(solution)/shard_map/ppermute | solution.py:356
  166.8 6.5 %collective-permute-done.33 = bf16[1024,128]{1,0:T(8,128)(2,1)S(1)} collective-permute-done((bf16[1024,128]{1,0:T(8,128)(2,1)S(1)}, bf16[1024,128]{1,0:T(8,128)(2,1)S(1)}, u32[]{:S(2)}, u32[]{:S(2)}) %collective-permute-start.33) | collective-permute-done | bytes 262176 | tf_op jit(solution)/shard_map/ppermute | solution.py:356
  173.4 2.0 %collective-permute-start.34 = (bf16[512,128]{1,0:T(8,128)(2,1)S(1)}, bf16[512,128]{1,0:T(8,128)(2,1)S(1)}, u32[]{:S(2)}, u32[]{:S(2)}) collective-permute-start(bf16[512,128]{1,0:T(8,128)(2,1)S(1)} %slice.163), channel_id=1, source_target_pairs={{0,8},{1,3},{2,10},{3,1},{4,12},{5,7},{6,14},{7,5},{8,0},{9,11},{1... | collective-permute-start | bytes 393224 | tf_op jit(solution)/shard_map/ppermute | solution.py:356
  175.4 5.3 %collective-permute-done.34 = bf16[512,128]{1,0:T(8,128)(2,1)S(1)} collective-permute-done((bf16[512,128]{1,0:T(8,128)(2,1)S(1)}, bf16[512,128]{1,0:T(8,128)(2,1)S(1)}, u32[]{:S(2)}, u32[]{:S(2)}) %collective-permute-start.34) | collective-permute-done | bytes 131104 | tf_op jit(solution)/shard_map/ppermute | solution.py:356
  (97 shorter events, 34.6 us)
Async XLA Ops:
  1.6 19.3 %collective-permute-start = (bf16[512,128]{1,0:T(8,128)(2,1)S(1)}, bf16[512,128]{1,0:T(8,128)(2,1)S(1)}, u32[]{:S(2)}, u32[]{:S(2)}) collective-permute-start(bf16[512,128]{1,0:T(8,128)(2,1)S(1)} %reshape.37), channel_id=1, source_target_pairs={{0,8},{1,9},{2,10},{3,11},{4,12},{5,13},{6,14},{7,15},{8,0},{9,1},... | collective-permute-start | bytes 393224 | tf_op jit(solution)/shard_map/ppermute | solution.py:356
  5.7 15.2 %collective-permute-start.1 = (bf16[512,128]{1,0:T(8,128)(2,1)S(1)}, bf16[512,128]{1,0:T(8,128)(2,1)S(1)}, u32[]{:S(2)}, u32[]{:S(2)}) collective-permute-start(bf16[512,128]{1,0:T(8,128)(2,1)S(1)} %reshape.37), channel_id=1, source_target_pairs={{0,4},{1,5},{2,6},{3,7},{4,0},{5,1},{6,2},{7,3},{8,12},{9,13},{10,... | collective-permute-start | bytes 393224 | tf_op jit(solution)/shard_map/ppermute | solution.py:356
  7.3 13.6 %collective-permute-start.2 = (bf16[512,128]{1,0:T(8,128)(2,1)S(1)}, bf16[512,128]{1,0:T(8,128)(2,1)S(1)}, u32[]{:S(2)}, u32[]{:S(2)}) collective-permute-start(bf16[512,128]{1,0:T(8,128)(2,1)S(1)} %reshape.37), channel_id=1, source_target_pairs={{0,12},{1,13},{2,14},{3,15},{4,8},{5,9},{6,10},{7,11},{8,4},{9,5},... | collective-permute-start | bytes 393224 | tf_op jit(solution)/shard_map/ppermute | solution.py:356
  21.0 13.2 %collective-permute-start.3 = (bf16[2048,128]{1,0:T(8,128)(2,1)S(1)}, bf16[2048,128]{1,0:T(8,128)(2,1)S(1)}, u32[]{:S(2)}, u32[]{:S(2)}) collective-permute-start(bf16[2048,128]{1,0:T(8,128)(2,1)S(1)} %pad_maximum_fusion.1), channel_id=1, source_target_pairs={{0,2},{1,3},{2,0},{3,1},{4,6},{5,7},{6,4},{7,5},{8,10},{9,11},{10,... | collective-permute-start | bytes 1572872 | tf_op jit(solution)/shard_map/ppermute | solution.py:356
  34.2 2.7 %collective-permute-start.4 = (bf16[4096,128]{1,0:T(8,128)(2,1)S(1)}, bf16[4096,128]{1,0:T(8,128)(2,1)S(1)}, u32[]{:S(2)}, u32[]{:S(2)}) collective-permute-start(bf16[4096,128]{1,0:T(8,128)(2,1)S(1)} %pad_maximum_fusion.near), channel_id=1, source_target_pairs={{0,1},{1,0},{2,3},{3,2},{4,5},{5,4},{6,7},{7,6},{8,9},{9,8},{10,11... | collective-permute-start | bytes 3145736 | tf_op jit(solution)/shard_map/ppermute | solution.py:356
  48.3 2.2 %collective-permute-start.5 = (bf16[2560,128]{1,0:T(8,128)(2,1)S(1)}, bf16[2560,128]{1,0:T(8,128)(2,1)S(1)}, u32[]{:S(2)}, u32[]{:S(2)}) collective-permute-start(bf16[2560,128]{1,0:T(8,128)(2,1)S(1)} %get-tuple-element.25), channel_id=1, source_target_pairs={{0,1},{1,0},{2,3},{3,2},{4,5},{5,4},{6,7},{7,6},{8,9},{9,8},{10,11... | collective-permute-start | bytes 1966088 | tf_op jit(solution)/shard_map/ppermute | solution.py:356
  50.7 10.4 %collective-permute-start.10 = (bf16[320,128]{1,0:T(8,128)(2,1)S(1)}, bf16[320,128]{1,0:T(8,128)(2,1)S(1)}, u32[]{:S(2)}, u32[]{:S(2)}) collective-permute-start(bf16[320,128]{1,0:T(8,128)(2,1)S(1)} %get-tuple-element.52), channel_id=1, source_target_pairs={{0,10},{1,11},{2,8},{3,9},{4,14},{5,15},{6,12},{7,13},{8,2},{9,3},... | collective-permute-start | bytes 245768 | tf_op jit(solution)/shard_map/ppermute | solution.py:356
  53.3 8.1 %collective-permute-start.11 = (bf16[320,128]{1,0:T(8,128)(2,1)S(1)}, bf16[320,128]{1,0:T(8,128)(2,1)S(1)}, u32[]{:S(2)}, u32[]{:S(2)}) collective-permute-start(bf16[320,128]{1,0:T(8,128)(2,1)S(1)} %get-tuple-element.51), channel_id=1, source_target_pairs={{0,6},{1,7},{2,4},{3,5},{4,2},{5,3},{6,0},{7,1},{8,14},{9,15},{10,... | collective-permute-start | bytes 245768 | tf_op jit(solution)/shard_map/ppermute | solution.py:356
  55.8 8.2 %collective-permute-start.12 = (bf16[320,128]{1,0:T(8,128)(2,1)S(1)}, bf16[320,128]{1,0:T(8,128)(2,1)S(1)}, u32[]{:S(2)}, u32[]{:S(2)}) collective-permute-start(bf16[320,128]{1,0:T(8,128)(2,1)S(1)} %get-tuple-element.50), channel_id=1, source_target_pairs={{0,14},{1,15},{2,12},{3,13},{4,10},{5,11},{6,8},{7,9},{8,6},{9,7},... | collective-permute-start | bytes 245768 | tf_op jit(solution)/shard_map/ppermute | solution.py:356
  57.0 11.1 %collective-permute-start.6 = (bf16[320,128]{1,0:T(8,128)(2,1)S(1)}, bf16[320,128]{1,0:T(8,128)(2,1)S(1)}, u32[]{:S(2)}, u32[]{:S(2)}) collective-permute-start(bf16[320,128]{1,0:T(8,128)(2,1)S(1)} %get-tuple-element.49), channel_id=1, source_target_pairs={{0,8},{1,9},{2,10},{3,11},{4,12},{5,13},{6,14},{7,15},{8,0},{9,1},... | collective-permute-start | bytes 245768 | tf_op jit(solution)/shard_map/ppermute | solution.py:356
  57.7 10.4 %collective-permute-start.7 = (bf16[320,128]{1,0:T(8,128)(2,1)S(1)}, bf16[320,128]{1,0:T(8,128)(2,1)S(1)}, u32[]{:S(2)}, u32[]{:S(2)}) collective-permute-start(bf16[320,128]{1,0:T(8,128)(2,1)S(1)} %get-tuple-element.55), channel_id=1, source_target_pairs={{0,4},{1,5},{2,6},{3,7},{4,0},{5,1},{6,2},{7,3},{8,12},{9,13},{10,... | collective-permute-start | bytes 245768 | tf_op jit(solution)/shard_map/ppermute | solution.py:356
  61.1 7.0 %collective-permute-start.8 = (bf16[320,128]{1,0:T(8,128)(2,1)S(1)}, bf16[320,128]{1,0:T(8,128)(2,1)S(1)}, u32[]{:S(2)}, u32[]{:S(2)}) collective-permute-start(bf16[320,128]{1,0:T(8,128)(2,1)S(1)} %get-tuple-element.54), channel_id=1, source_target_pairs={{0,12},{1,13},{2,14},{3,15},{4,8},{5,9},{6,10},{7,11},{8,4},{9,5},... | collective-permute-start | bytes 245768 | tf_op jit(solution)/shard_map/ppermute | solution.py:356
  61.5 6.7 %collective-permute-start.9 = (bf16[320,128]{1,0:T(8,128)(2,1)S(1)}, bf16[320,128]{1,0:T(8,128)(2,1)S(1)}, u32[]{:S(2)}, u32[]{:S(2)}) collective-permute-start(bf16[320,128]{1,0:T(8,128)(2,1)S(1)} %get-tuple-element.53), channel_id=1, source_target_pairs={{0,2},{1,3},{2,0},{3,1},{4,6},{5,7},{6,4},{7,5},{8,10},{9,11},{10,... | collective-permute-start | bytes 245768 | tf_op jit(solution)/shard_map/ppermute | solution.py:356
  68.3 7.8 %collective-permute-start.13 = (bf16[320,128]{1,0:T(8,128)(2,1)S(1)}, bf16[320,128]{1,0:T(8,128)(2,1)S(1)}, u32[]{:S(2)}, u32[]{:S(2)}) collective-permute-start(bf16[320,128]{1,0:T(8,128)(2,1)S(1)} %get-tuple-element.38), channel_id=1, source_target_pairs={{0,8},{1,9},{2,10},{3,11},{4,12},{5,13},{6,14},{7,15},{8,0},{9,1},... | collective-permute-start | bytes 245768 | tf_op jit(solution)/shard_map/ppermute | solution.py:356
  71.3 5.7 %collective-permute-start.14 = (bf16[320,128]{1,0:T(8,128)(2,1)S(1)}, bf16[320,128]{1,0:T(8,128)(2,1)S(1)}, u32[]{:S(2)}, u32[]{:S(2)}) collective-permute-start(bf16[320,128]{1,0:T(8,128)(2,1)S(1)} %get-tuple-element.38), channel_id=1, source_target_pairs={{0,4},{1,5},{2,6},{3,7},{4,0},{5,1},{6,2},{7,3},{8,12},{9,13},{10,... | collective-permute-start | bytes 245768 | tf_op jit(solution)/shard_map/ppermute | solution.py:356
  71.3 6.8 %collective-permute-start.15 = (bf16[320,128]{1,0:T(8,128)(2,1)S(1)}, bf16[320,128]{1,0:T(8,128)(2,1)S(1)}, u32[]{:S(2)}, u32[]{:S(2)}) collective-permute-start(bf16[320,128]{1,0:T(8,128)(2,1)S(1)} %get-tuple-element.38), channel_id=1, source_target_pairs={{0,12},{1,13},{2,14},{3,15},{4,8},{5,9},{6,10},{7,11},{8,4},{9,5},... | collective-permute-start | bytes 245768 | tf_op jit(solution)/shard_map/ppermute | solution.py:356
  78.1 8.5 %collective-permute-start.16 = (bf16[1280,128]{1,0:T(8,128)(2,1)S(1)}, bf16[1280,128]{1,0:T(8,128)(2,1)S(1)}, u32[]{:S(2)}, u32[]{:S(2)}) collective-permute-start(bf16[1280,128]{1,0:T(8,128)(2,1)S(1)} %pad_maximum_fusion.2), channel_id=1, source_target_pairs={{0,2},{1,3},{2,0},{3,1},{4,6},{5,7},{6,4},{7,5},{8,10},{9,11},{10,... | collective-permute-start | bytes 983048 | tf_op jit(solution)/shard_map/ppermute | solution.py:356
  102.4 7.8 %collective-permute-start.19 = (bf16[320,128]{1,0:T(8,128)(2,1)S(1)}, bf16[320,128]{1,0:T(8,128)(2,1)S(1)}, u32[]{:S(2)}, u32[]{:S(2)}) collective-permute-start(bf16[320,128]{1,0:T(8,128)(2,1)S(1)} %get-tuple-element.42), channel_id=1, source_target_pairs={{0,8},{1,9},{2,10},{3,11},{4,12},{5,13},{6,14},{7,15},{8,0},{9,1},... | collective-permute-start | bytes 245768 | tf_op jit(solution)/shard_map/ppermute | solution.py:356
  105.3 6.6 %collective-permute-start.20 = (bf16[320,128]{1,0:T(8,128)(2,1)S(1)}, bf16[320,128]{1,0:T(8,128)(2,1)S(1)}, u32[]{:S(2)}, u32[]{:S(2)}) collective-permute-start(bf16[320,128]{1,0:T(8,128)(2,1)S(1)} %get-tuple-element.48), channel_id=1, source_target_pairs={{0,4},{1,5},{2,6},{3,7},{4,0},{5,1},{6,2},{7,3},{8,12},{9,13},{10,... | collective-permute-start | bytes 245768 | tf_op jit(solution)/shard_map/ppermute | solution.py:356
  105.7 10.1 %collective-permute-start.21 = (bf16[320,128]{1,0:T(8,128)(2,1)S(1)}, bf16[320,128]{1,0:T(8,128)(2,1)S(1)}, u32[]{:S(2)}, u32[]{:S(2)}) collective-permute-start(bf16[320,128]{1,0:T(8,128)(2,1)S(1)} %get-tuple-element.47), channel_id=1, source_target_pairs={{0,12},{1,13},{2,14},{3,15},{4,8},{5,9},{6,10},{7,11},{8,4},{9,5},... | collective-permute-start | bytes 245768 | tf_op jit(solution)/shard_map/ppermute | solution.py:356
  107.4 8.4 %collective-permute-start.22 = (bf16[320,128]{1,0:T(8,128)(2,1)S(1)}, bf16[320,128]{1,0:T(8,128)(2,1)S(1)}, u32[]{:S(2)}, u32[]{:S(2)}) collective-permute-start(bf16[320,128]{1,0:T(8,128)(2,1)S(1)} %get-tuple-element.46), channel_id=1, source_target_pairs={{0,2},{1,3},{2,0},{3,1},{4,6},{5,7},{6,4},{7,5},{8,10},{9,11},{10,... | collective-permute-start | bytes 245768 | tf_op jit(solution)/shard_map/ppermute | solution.py:356
  108.0 10.3 %collective-permute-start.23 = (bf16[320,128]{1,0:T(8,128)(2,1)S(1)}, bf16[320,128]{1,0:T(8,128)(2,1)S(1)}, u32[]{:S(2)}, u32[]{:S(2)}) collective-permute-start(bf16[320,128]{1,0:T(8,128)(2,1)S(1)} %get-tuple-element.45), channel_id=1, source_target_pairs={{0,10},{1,11},{2,8},{3,9},{4,14},{5,15},{6,12},{7,13},{8,2},{9,3},... | collective-permute-start | bytes 245768 | tf_op jit(solution)/shard_map/ppermute | solution.py:356
  110.2 8.1 %collective-permute-start.24 = (bf16[320,128]{1,0:T(8,128)(2,1)S(1)}, bf16[320,128]{1,0:T(8,128)(2,1)S(1)}, u32[]{:S(2)}, u32[]{:S(2)}) collective-permute-start(bf16[320,128]{1,0:T(8,128)(2,1)S(1)} %get-tuple-element.44), channel_id=1, source_target_pairs={{0,6},{1,7},{2,4},{3,5},{4,2},{5,3},{6,0},{7,1},{8,14},{9,15},{10,... | collective-permute-start | bytes 245768 | tf_op jit(solution)/shard_map/ppermute | solution.py:356
  111.8 7.4 %collective-permute-start.25 = (bf16[320,128]{1,0:T(8,128)(2,1)S(1)}, bf16[320,128]{1,0:T(8,128)(2,1)S(1)}, u32[]{:S(2)}, u32[]{:S(2)}) collective-permute-start(bf16[320,128]{1,0:T(8,128)(2,1)S(1)} %get-tuple-element.43), channel_id=1, source_target_pairs={{0,14},{1,15},{2,12},{3,13},{4,10},{5,11},{6,8},{7,9},{8,6},{9,7},... | collective-permute-start | bytes 245768 | tf_op jit(solution)/shard_map/ppermute | solution.py:356
  119.4 8.2 %collective-permute-start.26 = (bf16[320,128]{1,0:T(8,128)(2,1)S(1)}, bf16[320,128]{1,0:T(8,128)(2,1)S(1)}, u32[]{:S(2)}, u32[]{:S(2)}) collective-permute-start(bf16[320,128]{1,0:T(8,128)(2,1)S(1)} %get-tuple-element.34), channel_id=1, source_target_pairs={{0,8},{1,9},{2,10},{3,11},{4,12},{5,13},{6,14},{7,15},{8,0},{9,1},... | collective-permute-start | bytes 245768 | tf_op jit(solution)/shard_map/ppermute | solution.py:356
  122.4 5.5 %collective-permute-start.27 = (bf16[320,128]{1,0:T(8,128)(2,1)S(1)}, bf16[320,128]{1,0:T(8,128)(2,1)S(1)}, u32[]{:S(2)}, u32[]{:S(2)}) collective-permute-start(bf16[320,128]{1,0:T(8,128)(2,1)S(1)} %get-tuple-element.34), channel_id=1, source_target_pairs={{0,4},{1,5},{2,6},{3,7},{4,0},{5,1},{6,2},{7,3},{8,12},{9,13},{10,... | collective-permute-start | bytes 245768 | tf_op jit(solution)/shard_map/ppermute | solution.py:356
  122.7 6.6 %collective-permute-start.28 = (bf16[320,128]{1,0:T(8,128)(2,1)S(1)}, bf16[320,128]{1,0:T(8,128)(2,1)S(1)}, u32[]{:S(2)}, u32[]{:S(2)}) collective-permute-start(bf16[320,128]{1,0:T(8,128)(2,1)S(1)} %get-tuple-element.34), channel_id=1, source_target_pairs={{0,12},{1,13},{2,14},{3,15},{4,8},{5,9},{6,10},{7,11},{8,4},{9,5},... | collective-permute-start | bytes 245768 | tf_op jit(solution)/shard_map/ppermute | solution.py:356
  129.3 8.1 %collective-permute-start.29 = (bf16[1280,128]{1,0:T(8,128)(2,1)S(1)}, bf16[1280,128]{1,0:T(8,128)(2,1)S(1)}, u32[]{:S(2)}, u32[]{:S(2)}) collective-permute-start(bf16[1280,128]{1,0:T(8,128)(2,1)S(1)} %pad_maximum_fusion.3), channel_id=1, source_target_pairs={{0,2},{1,3},{2,0},{3,1},{4,6},{5,7},{6,4},{7,5},{8,10},{9,11},{10,... | collective-permute-start | bytes 983048 | tf_op jit(solution)/shard_map/ppermute | solution.py:356
  151.7 2.7 %collective-permute-start.31 = (bf16[4096,128]{1,0:T(8,128)(2,1)S(1)}, bf16[4096,128]{1,0:T(8,128)(2,1)S(1)}, u32[]{:S(2)}, u32[]{:S(2)}) collective-permute-start(bf16[4096,128]{1,0:T(8,128)(2,1)S(1)} %get-tuple-element.31), channel_id=1, source_target_pairs={{0,1},{1,0},{2,3},{3,2},{4,5},{5,4},{6,7},{7,6},{8,9},{9,8},{10,11... | collective-permute-start | bytes 3145736 | tf_op jit(solution)/shard_map/ppermute | solution.py:356
  154.6 9.2 %collective-permute-start.32 = (bf16[2048,128]{1,0:T(8,128)(2,1)S(1)}, bf16[2048,128]{1,0:T(8,128)(2,1)S(1)}, u32[]{:S(2)}, u32[]{:S(2)}) collective-permute-start(bf16[2048,128]{1,0:T(8,128)(2,1)S(1)} %slice.161), channel_id=1, source_target_pairs={{0,2},{1,5},{2,0},{3,7},{4,6},{5,1},{6,4},{7,3},{8,10},{9,13},{10,... | collective-permute-start | bytes 1572872 | tf_op jit(solution)/shard_map/ppermute | solution.py:356
  164.0 9.3 %collective-permute-start.33 = (bf16[1024,128]{1,0:T(8,128)(2,1)S(1)}, bf16[1024,128]{1,0:T(8,128)(2,1)S(1)}, u32[]{:S(2)}, u32[]{:S(2)}) collective-permute-start(bf16[1024,128]{1,0:T(8,128)(2,1)S(1)} %slice.162), channel_id=1, source_target_pairs={{0,4},{1,9},{2,6},{3,11},{4,0},{5,13},{6,2},{7,15},{8,12},{9,1},{1... | collective-permute-start | bytes 786440 | tf_op jit(solution)/shard_map/ppermute | solution.py:356
  173.4 7.3 %collective-permute-start.34 = (bf16[512,128]{1,0:T(8,128)(2,1)S(1)}, bf16[512,128]{1,0:T(8,128)(2,1)S(1)}, u32[]{:S(2)}, u32[]{:S(2)}) collective-permute-start(bf16[512,128]{1,0:T(8,128)(2,1)S(1)} %slice.163), channel_id=1, source_target_pairs={{0,8},{1,3},{2,10},{3,1},{4,12},{5,7},{6,14},{7,5},{8,0},{9,11},{1... | collective-permute-start | bytes 393224 | tf_op jit(solution)/shard_map/ppermute | solution.py:356
  (9 other events, 23.6 us)

commit v8 on v7

--- a/solution.py
+++ b/solution.py
@@ -44,14 +44,30 @@
     return lax.broadcasted_iota(jnp.int32, shape, 1) >= BLOCK
 
 
+class Part:
+    def __init__(self, ref, begin, width=1):
+        self.ref, self.begin, self.width = ref, begin, width
+
+    def __getitem__(self, index):
+        if isinstance(index, tuple):
+            index = index[0] * self.width + index[1]
+        return self.ref[self.begin + index]
+
+
+def scalar_parts(scalars, groups):
+    seq, order, counts = (Part(scalars, part * groups) for part in range(3))
+    return seq, order, counts, Part(scalars, 3 * groups, SLOTS), scalars[groups * (3 + SLOTS)]
+
+
 def group_at(index, seq, order, counts):
     position = seq[index]
     group = order[position]
     return position, group, counts[group]
 
 
-def support_kernel(begin, seq, order, support, counts, dictionary, *refs):
+def support_kernel(begin, groups, scalars, dictionary, *refs):
     out, held, picks, ids, sems, out_sems = refs[-6:]
+    seq, order, counts, support, _ = scalar_parts(scalars, groups)
     entries, rows, _ = held.shape
     pairs = entries // 2
 
@@ -71,7 +87,7 @@
         lax.fori_loop(jnp.clip(-offset, 0, live), jnp.clip(entries - offset, 0, live), start_slot, 0)
         return offset + live
 
-    lax.fori_loop(0, order.shape[0], start_group, jnp.int32(-begin))
+    lax.fori_loop(0, groups, start_group, jnp.int32(-begin))
     shape = (2 * LANES, LANES)
     source = lax.broadcasted_iota(jnp.int32, shape, 0)
     target = lax.broadcasted_iota(jnp.int32, shape, 1)
@@ -106,14 +122,14 @@
     lax.fori_loop(0, pairs, drain, 0)
 
 
-def collect_support(seq, order, support, counts, dictionary, pairs, part, *before):
+def collect_support(scalars, groups, dictionary, pairs, part, *before):
     rows = dictionary.shape[0]
     pairs = pairs // SUPPORT_PARTS
     entries = 2 * pairs
     return pl.pallas_call(
-        functools.partial(support_kernel, part * entries),
+        functools.partial(support_kernel, part * entries, groups),
         grid_spec=pltpu.PrefetchScalarGridSpec(
-            num_scalar_prefetch=4,
+            num_scalar_prefetch=1,
             grid=(),
             in_specs=[pl.BlockSpec(memory_space=pltpu.HBM)] * (1 + len(before)),
             out_specs=pl.BlockSpec(memory_space=pltpu.HBM),
@@ -128,9 +144,9 @@
         out_shape=jax.ShapeDtypeStruct((HELD_BYTES // (rows * LANES * 2), rows, LANES), dictionary.dtype),
         compiler_params=pltpu.CompilerParams(vmem_limit_bytes=SUPPORT_VMEM),
         cost_estimate=pl.CostEstimate(flops=0, transcendentals=0, bytes_accessed=6 * pairs * rows * LANES * 2),
-        input_output_aliases={5: 0} if before else {},
+        input_output_aliases={2: 0} if before else {},
         name="collect_support",
-    )(seq, order, support, counts, dictionary, *before)
+    )(scalars, dictionary, *before)
 
 
 def stage_distances(devices):
@@ -147,12 +163,14 @@
     return sum(distance for bit, distance in zip(bits, distances) if slot >> bit & 1)
 
 
-def gradient_kernel(mode, shards, pairs, seq, order, counts, own, blocks, near, far, targets, *refs):
+def gradient_kernel(mode, shards, pairs, groups, scalars, blocks, *refs):
+    seq, order, counts, _, me = scalar_parts(scalars, groups)
     refs = list(refs)
     take = lambda: refs.pop(0)
+    gathered, targets = [take() for _ in range(4)], take()
     if mode in ("first", "final"):
         thresh = take()
-    keep, send = take(), take()
+    keep, send = take(), (take(), take())
     if mode == "first":
         start_out, thresh_out = take(), take()
     if mode == "final":
@@ -162,9 +180,7 @@
         starts, limits = take(), take()
     offsets, sems = refs
 
-    groups = order.shape[0]
     pieces = pairs // PIECE
-    me = own[0]
 
     def load(index):
         span = pl.ds(index * PIECE, PIECE)
@@ -185,11 +201,19 @@
             even, odd = odd, even
         return jnp.where(me % 2 == 0, even, odd) ^ me
 
-    size_in = 2 * near.shape[0] // shards
+    quarter = shards // 4
+    size_in = gathered[0].shape[0] // quarter
     for slot in range(shards):
-        source = near if slot < shards // 2 else far
-        begin = slot % (shards // 2) * size_in
-        codes[shard_span(slot, size_in), :] = source[begin : begin + size_in, :]
+        begin = slot % quarter * size_in
+        codes[shard_span(slot, size_in), :] = gathered[slot // quarter][begin : begin + size_in, :]
+
+    def put(slot, size, begin, value):
+        rows = slice(slot % quarter * size + begin, slot % quarter * size + begin + value.shape[0])
+        if slot < 2 * quarter:
+            first = slot // quarter * quarter * size
+            keep[first + rows.start : first + rows.stop, :] = value
+        else:
+            send[slot // quarter - 2][rows, :] = value.astype(jnp.bfloat16)
 
     def seat(index, offset):
         position, _, live = group_at(index, seq, order, counts)
@@ -256,21 +280,21 @@
 
     def two_groups(step, waited):
         picks = []
-        chunks = 1
+        count_needed = 1
         for index in (2 * step, 2 * step + 1):
             position, group, live = group_at(index, seq, order, counts)
             offset = offsets[position]
             picks.append((position, group, offset, live))
-            chunks = jnp.maximum(chunks, (live + offset % 2 + 3) // 4)
-        reach = jnp.minimum(picks[1][2] // 2 + 2 * chunks - 1, pairs - 1)
+            count_needed = jnp.maximum(count_needed, (live + offset % 2 + 1) // 2)
+        reach = jnp.minimum(picks[1][2] // 2 + count_needed - 1, pairs - 1)
         needed = jnp.maximum(reach // PIECE + 1, waited)
         lax.fori_loop(waited, needed, wait_piece, 0)
-        for count in range(1, SLOTS // 4 + 2):
-
-            @pl.when(chunks == count)
+        for count in range(1, SLOT_PAIRS + 2):
+
+            @pl.when(count_needed == count)
             def _(count=count):
                 for pick in picks:
-                    one_group(*pick, 2 * count)
+                    one_group(*pick, count)
 
         return needed
 
@@ -280,12 +304,7 @@
     if mode != "final":
         size = 2 * keep.shape[0] // shards
         for slot in range(shards):
-            begin = slot % (shards // 2) * size
-            value = total[shard_span(slot, size), :]
-            if slot < shards // 2:
-                keep[begin : begin + size, :] = value
-            else:
-                send[begin : begin + size, :] = value.astype(send.dtype)
+            put(slot, size, 0, total[shard_span(slot, size), :])
     if mode == "first":
         size = start_out.shape[0]
         span = pl.ds(pl.multiple_of(me * size, ROW_TILE), size)
@@ -302,25 +321,19 @@
             offset = offsets[position]
             live = counts[order[position]]
             parts = [total[tile(offset // 2 + pair), :] for pair in range(SLOT_PAIRS + 1)]
-            begin = slot % (shards // 2) * SLOT_PAIRS * PATCHES
             for pair, part in enumerate(shifted(parts, SLOT_PAIRS, offset % 2 == 1, True)):
                 value = jnp.where(2 * pair + side < live, part, 0.0)
-                rows = slice(begin + pair * PATCHES, begin + (pair + 1) * PATCHES)
-                if slot < shards // 2:
-                    keep[rows, :] = value
-                else:
-                    send[rows, :] = value.astype(send.dtype)
-
-
-def gradient_call(mode, shards, pairs, scalars, blocks, near, far, targets, extra=()):
+                put(slot, SLOT_PAIRS * PATCHES, pair * PATCHES, value)
+
+
+def gradient_call(mode, shards, pairs, groups, scalars, blocks, gathered, targets, extra=()):
     rows = blocks.shape[1]
     places = pairs + SPARE
-    groups = scalars[1].shape[0]
     single, double = jnp.bfloat16, jnp.float32
     packed = (places * PATCHES, LANES)
     half_out = (groups * SLOT_PAIRS if mode == "final" else pairs) * PATCHES // 2
     shard = (2 * half_out // shards, LANES)
-    outs = [((half_out, LANES), double), ((half_out, LANES), single)]
+    outs = [((half_out, LANES), double)] + [((half_out // 2, LANES), single)] * 2
     if mode == "first":
         outs += [(shard, single), (shard, double)]
     if mode == "final":
@@ -331,12 +344,12 @@
         scratch += [(packed, single), (packed, double)]
     room = sum(math.prod(shape) * jnp.dtype(kind).itemsize for shape, kind in scratch)
     return pl.pallas_call(
-        functools.partial(gradient_kernel, mode, shards, pairs),
+        functools.partial(gradient_kernel, mode, shards, pairs, groups),
         grid_spec=pltpu.PrefetchScalarGridSpec(
-            num_scalar_prefetch=4,
+            num_scalar_prefetch=1,
             grid=(),
             in_specs=[pl.BlockSpec(memory_space=pltpu.HBM)]
-            + [pl.BlockSpec(memory_space=pltpu.VMEM)] * (3 + len(extra)),
+            + [pl.BlockSpec(memory_space=pltpu.VMEM)] * (5 + len(extra)),
             out_specs=[pl.BlockSpec(memory_space=pltpu.VMEM)] * len(outs),
             scratch_shapes=[pltpu.VMEM(shape, kind) for shape, kind in scratch]
             + [pltpu.SMEM((groups,), jnp.int32), pltpu.SemaphoreType.DMA((pairs // PIECE,))],
@@ -347,7 +360,7 @@
             flops=4 * pairs * rows * LANES * MATRIX_UNIT, transcendentals=0, bytes_accessed=pairs * rows * LANES * 2
         ),
         name="gradient",
-    )(*scalars, blocks, near, far, targets, *extra)
+    )(scalars, blocks, *gathered, targets, *extra)
 
 
 def exchange(value, even, odd=None):
@@ -357,36 +370,44 @@
 
 
 def gather_shards(own, beside=()):
-    distances = stage_distances(lax.axis_size("rows"))
-    apart = [slot_distance(slot, distances[2:]) for slot in range(lax.axis_size("rows") // 4)]
+    core, row, *columns = stage_distances(lax.axis_size("rows"))
+    apart = [slot_distance(slot, columns) for slot in range(lax.axis_size("rows") // 4)]
     made = ()
-    value = jnp.concatenate([own] + [exchange(own, distance) for distance in apart[1:]], axis=0)
+    near = jnp.concatenate([own] + [exchange(own, distance) for distance in apart[1:]], axis=0)
     if beside:
-        value, *made = lax.optimization_barrier((value, beside[0]()))
-    value = jnp.concatenate([value, exchange(value, distances[1])], axis=0)
+        near, *made = lax.optimization_barrier((near, beside[0]()))
+    other = exchange(near, row)
+    far = exchange(near, core)
     if beside:
-        value, *made = lax.optimization_barrier((value, beside[1](*made)))
-    return value, exchange(value, distances[0]), made
-
-
-def reduce_shards(keep, send):
+        other, *made = lax.optimization_barrier((other, beside[1](*made)))
+    return (near, other, far, exchange(other, core)), made
+
+
+def add_cores(keep, *send):
+    middle = keep.shape[0] // 2
+    arrived = [exchange(part, 1).astype(jnp.float32) for part in send]
+    return [part + share for part, share in zip((keep[:middle], keep[middle:]), arrived)]
+
+
+def reduce_shards(keep, *send):
     devices = lax.axis_size("rows")
     distances = stage_distances(devices)
-    half = keep + exchange(send, distances[0]).astype(jnp.float32)
+    quarters = add_cores(keep, *send)
     size = 2 * keep.shape[0] // devices
-    sent = half.astype(jnp.bfloat16)
-    total = half[:size]
+    sent = [quarter.astype(jnp.bfloat16) for quarter in quarters]
+    total = quarters[0][:size]
     for slot in range(1, devices // 2):
-        share = exchange(sent[slot * size : (slot + 1) * size], slot_distance(slot, distances[1:]))
-        total = total + share.astype(jnp.float32)
+        begin = slot % (devices // 4) * size
+        share = sent[slot // (devices // 4)][begin : begin + size]
+        total = total + exchange(share, slot_distance(slot, distances[1:])).astype(jnp.float32)
     return total
 
 
-def last_reduce(keep, send):
-    total = keep + exchange(send, 1).astype(jnp.float32)
+def last_reduce(keep, *send):
+    near, other = add_cores(keep, *send)
     for even, odd in list(zip(*last_orders(lax.axis_size("rows"))))[1:]:
-        middle = total.shape[0] // 2
-        total = total[:middle] + exchange(total[middle:].astype(jnp.bfloat16), even, odd).astype(jnp.float32)
+        total = near + exchange(other.astype(jnp.bfloat16), even, odd).astype(jnp.float32)
+        near, other = total[: total.shape[0] // 2], total[total.shape[0] // 2 :]
     return total
 
 
@@ -410,27 +431,30 @@
 
     laid = initial_codes.reshape(SLOT_PAIRS, 2, PATCHES, BLOCK).transpose(0, 2, 1, 3)
     laid = laid.reshape(SLOT_PAIRS * PATCHES, LANES)
-    seq = packed_order(jnp.take(counts, group_order))
-    collect = functools.partial(collect_support, seq, group_order, support, counts, dictionary, pairs)
-    near, far, (blocks,) = gather_shards(laid, [functools.partial(collect, part) for part in range(SUPPORT_PARTS)])
-
-    scalars = (seq, group_order, counts, position.astype(jnp.int32).reshape(1))
+    live = jnp.sum(jnp.where(group_order[:, None] == jnp.arange(groups)[None, :], counts[None, :], 0), axis=1)
+    own = position.astype(jnp.int32).reshape(1)
+    scalars = jnp.concatenate([packed_order(live), group_order, counts, support.reshape(groups * SLOTS), own])
+    collect = functools.partial(collect_support, scalars, groups, dictionary, pairs)
+    gathered, (blocks,) = gather_shards(laid, [functools.partial(collect, part) for part in range(SUPPORT_PARTS)])
+
     targets = patches.T
     half_penalty = 0.5 * penalty
     thresh_tiles = jnp.broadcast_to(half_penalty[:, :, None], (groups, PATCHES, LANES))
 
-    run = functools.partial(gradient_call, shards=devices, pairs=pairs, scalars=scalars, blocks=blocks, targets=targets)
-    keep, send, start, thresh = run("first", near=near, far=far, extra=(thresh_tiles,))
+    run = functools.partial(
+        gradient_call, shards=devices, pairs=pairs, groups=groups, scalars=scalars, blocks=blocks, targets=targets
+    )
+    *shares, start, thresh = run("first", gathered=gathered, extra=(thresh_tiles,))
     point = previous = start.astype(jnp.float32)
     for turn in range(ITERS - 1):
         if turn:
-            keep, send = run("packed", near=near, far=far)
-        current = shrink(point - 0.5 * reduce_shards(keep, send), thresh)
+            shares = run("packed", gathered=gathered)
+        current = shrink(point - 0.5 * reduce_shards(*shares), thresh)
         point = current + momenta[turn] * (current - previous)
         previous = current
-        near, far, _ = gather_shards(point.astype(jnp.bfloat16))
-    keep, send, sent, thresh = run("final", near=near, far=far, extra=(thresh_tiles,))
-    gradient = last_reduce(keep, send).reshape(SLOT_PAIRS, PATCHES, LANES)
+        gathered, _ = gather_shards(point.astype(jnp.bfloat16))
+    *shares, sent, thresh = run("final", gathered=gathered, extra=(thresh_tiles,))
+    gradient = last_reduce(*shares).reshape(SLOT_PAIRS, PATCHES, LANES)
     sent = sent.astype(jnp.float32)
     result = shrink(sent - 0.5 * gradient, thresh[None])
     result = result.reshape(SLOT_PAIRS, PATCHES, 2, BLOCK).transpose(0, 2, 1, 3)

time: 183 us -> 180 us (0.984)
  local copies, waits for them, and re-layouts: 8.23 us -> 6.2 us
    unnamed x19 -> x3, local copies, waits for them, and re-layouts: 3.61 us -> 1.5 us
    ppermute x35 -> x41, waiting for transfers between devices: 65.9 us -> 64.9 us  [exchange(): lax.ppermute(value, 'rows', [(i, i ^ apart[i % 2]) for i in range(devices)])]
    ppermute x35 -> x41, starting transfers between devices: 52.8 us -> 53.8 us  [exchange(): lax.ppermute(value, 'rows', [(i, i ^ apart[i % 2]) for i in range(devices)])]
  transfers between devices with their start and end apart: 35 -> 41, of which waited for: 21 -> 23; matrix products, arithmetic and copies ran while one was open for 2% -> 2% of each run, Pallas kernels for 10% -> 10%
where the time goes in v8:
time: 180 us; the launch traced here: 179 us
  waiting for transfers between devices  64.9 us (36%)
  starting transfers between devices  53.8 us (30%)
  Pallas kernels  52.1 us (29%)
  local copies, waits for them, and re-layouts  6.2 us (3%)
  other arithmetic  2.22 us (1%)
    ppermute x41, waiting for transfers between devices, exchange(): lax.ppermute(value, 'rows', [(i, i ^ apart[i % 2]) for i in range(devices)])  64.9 us
    ppermute x41, starting transfers between devices, exchange(): lax.ppermute(value, 'rows', [(i, i ^ apart[i % 2]) for i in range(devices)])  53.8 us
    pallas_call x3, Pallas kernels, gradient_call(): pl.pallas_call(functools.partial(gradient_kernel, mode, shards, pairs, gr...  34.8 us
    pallas_call x2, Pallas kernels, collect_support(): pl.pallas_call(functools.partial(support_kernel, part * entries, groups),...  17.2 us
  transfers between devices with their start and end apart: 41, of which 23 were waited for; matrix products, arithmetic and copies ran while one was open for 2% of the time, Pallas kernels for 10%

profile of v8, /device:TPU:0, one launch (start us, length us, event | category | flops | bytes accessed | tf_op | source)
XLA Modules:
  0.0 179.4 jit_solution(3304356030361208455)
XLA Ops:
  1.6 4.1 %collective-permute-start = (bf16[512,128]{1,0:T(8,128)(2,1)S(1)}, bf16[512,128]{1,0:T(8,128)(2,1)S(1)}, u32[]{:S(2)}, u32[]{:S(2)}) collective-permute-start(bf16[512,128]{1,0:T(8,128)(2,1)S(1)} %reshape.33), channel_id=1, source_target_pairs={{0,8},{1,9},{2,10},{3,11},{4,12},{5,13},{6,14},{7,15},{8,0},{9,1},... | collective-permute-start | bytes 393224 | tf_op jit(solution)/shard_map/ppermute | solution.py:369
  10.0 8.5 %collect_support.2.refs_0_ = bf16[520,512,128]{2,1,0:T(8,128)(2,1)} custom-call(s32[305]{0:T(512)S(1)} %concatenate.12.scalars, bf16[512,32768]{1,0:T(8,128)(2,1)} %dictionary.3), custom_call_target="tpu_custom_call" | custom-call | bytes 31457280 | tf_op jit(solution)/shard_map/collect_support/pallas_call | solution.py:129
  18.5 1.8 %collective-permute-start.3 = (bf16[2048,128]{1,0:T(8,128)(2,1)S(1)}, bf16[2048,128]{1,0:T(8,128)(2,1)S(1)}, u32[]{:S(2)}, u32[]{:S(2)}) collective-permute-start(bf16[2048,128]{1,0:T(8,128)(2,1)S(1)} %pad_maximum_fusion.refs_0_), channel_id=1, source_target_pairs={{0,2},{1,3},{2,0},{3,1},{4,6},{5,7},{6,4},{7,5},{8,10},{9,11},{10,... | collective-permute-start | bytes 1572872 | tf_op jit(solution)/shard_map/ppermute | solution.py:369
  20.3 8.8 %collect_support.3.blocks = bf16[520,512,128]{2,1,0:T(8,128)(2,1)} custom-call(s32[305]{0:T(512)S(1)} %concatenate.12.scalars, bf16[512,32768]{1,0:T(8,128)(2,1)} %dictionary.3, bf16[520,512,128]{2,1,0:T(8,128)(2,1)} %collect_support.2.refs_0_), custom_call_target="tpu_custom_call", output_to_operand_aliasing={{}: (2, {})} | custom-call | bytes 31457280 | tf_op jit(solution)/shard_map/collect_support/pallas_call | solution.py:129
  29.1 2.6 %collective-permute-done.3.refs_1_ = bf16[2048,128]{1,0:T(8,128)(2,1)S(1)} collective-permute-done((bf16[2048,128]{1,0:T(8,128)(2,1)S(1)}, bf16[2048,128]{1,0:T(8,128)(2,1)S(1)}, u32[]{:S(2)}, u32[]{:S(2)}) %collective-permute-start.3) | collective-permute-done | bytes 524320 | tf_op jit(solution)/shard_map/ppermute | solution.py:369
  33.8 11.4 %gradient.3 = (f32[2560,128]{1,0:T(8,128)S(1)}, bf16[1280,128]{1,0:T(8,128)(2,1)S(1)}, bf16[1280,128]{1,0:T(8,128)(2,1)S(1)}, bf16[320,128]{1,0:T(8,128)(2,1)S(1)}, f32[320,128]{1,0:T(8,128)S(1)}) custom-call(s32[305]{0:T(512)S(1)} %concatenate.12.scalars, bf16[520,512,128]{2,1,0:T(8,128)(2,1)} %collect_support.3.blocks, ...), custom_call_target="tpu_custom_call" | custom-call | flops 5368709120 | bytes 10485760 | tf_op jit(solution)/shard_map/gradient/pallas_call | solution.py:346
  49.1 2.5 %collective-permute-start.12 = (bf16[320,128]{1,0:T(8,128)(2,1)S(1)}, bf16[320,128]{1,0:T(8,128)(2,1)S(1)}, u32[]{:S(2)}, u32[]{:S(2)}) collective-permute-start(bf16[320,128]{1,0:T(8,128)(2,1)S(1)} %get-tuple-element.60), channel_id=1, source_target_pairs={{0,10},{1,11},{2,8},{3,9},{4,14},{5,15},{6,12},{7,13},{8,2},{9,3},... | collective-permute-start | bytes 245768 | tf_op jit(solution)/shard_map/ppermute | solution.py:369
  51.6 2.5 %collective-permute-start.13 = (bf16[320,128]{1,0:T(8,128)(2,1)S(1)}, bf16[320,128]{1,0:T(8,128)(2,1)S(1)}, u32[]{:S(2)}, u32[]{:S(2)}) collective-permute-start(bf16[320,128]{1,0:T(8,128)(2,1)S(1)} %get-tuple-element.59), channel_id=1, source_target_pairs={{0,6},{1,7},{2,4},{3,5},{4,2},{5,3},{6,0},{7,1},{8,14},{9,15},{10,... | collective-permute-start | bytes 245768 | tf_op jit(solution)/shard_map/ppermute | solution.py:369
  54.4 1.7 collective-permute-start.7
  56.1 2.5 %collective-permute-start.8 = (bf16[320,128]{1,0:T(8,128)(2,1)S(1)}, bf16[320,128]{1,0:T(8,128)(2,1)S(1)}, u32[]{:S(2)}, u32[]{:S(2)}) collective-permute-start(bf16[320,128]{1,0:T(8,128)(2,1)S(1)} %get-tuple-element.56), channel_id=1, source_target_pairs={{0,4},{1,5},{2,6},{3,7},{4,0},{5,1},{6,2},{7,3},{8,12},{9,13},{10,... | collective-permute-start | bytes 245768 | tf_op jit(solution)/shard_map/ppermute | solution.py:369
  58.6 2.7 %collective-permute-start.9 = (bf16[320,128]{1,0:T(8,128)(2,1)S(1)}, bf16[320,128]{1,0:T(8,128)(2,1)S(1)}, u32[]{:S(2)}, u32[]{:S(2)}) collective-permute-start(bf16[320,128]{1,0:T(8,128)(2,1)S(1)} %get-tuple-element.55), channel_id=1, source_target_pairs={{0,12},{1,13},{2,14},{3,15},{4,8},{5,9},{6,10},{7,11},{8,4},{9,5},... | collective-permute-start | bytes 245768 | tf_op jit(solution)/shard_map/ppermute | solution.py:369
  62.2 3.6 %collective-permute-done.7 = bf16[320,128]{1,0:T(8,128)(2,1)S(1)} collective-permute-done((bf16[320,128]{1,0:T(8,128)(2,1)S(1)}, bf16[320,128]{1,0:T(8,128)(2,1)S(1)}, u32[]{:S(2)}, u32[]{:S(2)}) %collective-permute-start.7) | collective-permute-done | bytes 81952 | tf_op jit(solution)/shard_map/ppermute | solution.py:369
  66.0 3.3 %collective-permute-start.15 = (bf16[320,128]{1,0:T(8,128)(2,1)S(1)}, bf16[320,128]{1,0:T(8,128)(2,1)S(1)}, u32[]{:S(2)}, u32[]{:S(2)}) collective-permute-start(bf16[320,128]{1,0:T(8,128)(2,1)S(1)} %get-tuple-element.41), channel_id=1, source_target_pairs={{0,8},{1,9},{2,10},{3,11},{4,12},{5,13},{6,14},{7,15},{8,0},{9,1},... | collective-permute-start | bytes 245768 | tf_op jit(solution)/shard_map/ppermute | solution.py:369
  70.8 3.4 %collective-permute-done.15 = bf16[320,128]{1,0:T(8,128)(2,1)S(1)} collective-permute-done((bf16[320,128]{1,0:T(8,128)(2,1)S(1)}, bf16[320,128]{1,0:T(8,128)(2,1)S(1)}, u32[]{:S(2)}, u32[]{:S(2)}) %collective-permute-start.15) | collective-permute-done | bytes 81952 | tf_op jit(solution)/shard_map/ppermute | solution.py:369
  74.2 2.0 %collective-permute-done.16 = bf16[320,128]{1,0:T(8,128)(2,1)S(1)} collective-permute-done((bf16[320,128]{1,0:T(8,128)(2,1)S(1)}, bf16[320,128]{1,0:T(8,128)(2,1)S(1)}, u32[]{:S(2)}, u32[]{:S(2)}) %collective-permute-start.16) | collective-permute-done | bytes 81952 | tf_op jit(solution)/shard_map/ppermute | solution.py:369
  77.8 6.9 %collective-permute-done.18.refs_1_ = bf16[1280,128]{1,0:T(8,128)(2,1)S(1)} collective-permute-done((bf16[1280,128]{1,0:T(8,128)(2,1)S(1)}, bf16[1280,128]{1,0:T(8,128)(2,1)S(1)}, u32[]{:S(2)}, u32[]{:S(2)}) %collective-permute-start.18) | collective-permute-done | bytes 327712 | tf_op jit(solution)/shard_map/ppermute | solution.py:369
  86.3 11.1 %gradient.4 = (f32[2560,128]{1,0:T(8,128)S(1)}, bf16[1280,128]{1,0:T(8,128)(2,1)S(1)}, bf16[1280,128]{1,0:T(8,128)(2,1)S(1)}) custom-call(s32[305]{0:T(512)S(1)} %concatenate.12.scalars, bf16[520,512,128]{2,1,0:T(8,128)(2,1)} %collect_support.3.blocks, bf16[1280,128]{1,0:T(8,128)(2,1)S(1)} %pad_maximum_fusion.1.refs_0_, ...), custom_call_target="tpu_custom_call" | custom-call | flops 5368709120 | bytes 10485760 | tf_op jit(solution)/shard_map/gradient/pallas_call | solution.py:346
  101.3 3.0 %collective-permute-start.27 = (bf16[320,128]{1,0:T(8,128)(2,1)S(1)}, bf16[320,128]{1,0:T(8,128)(2,1)S(1)}, u32[]{:S(2)}, u32[]{:S(2)}) collective-permute-start(bf16[320,128]{1,0:T(8,128)(2,1)S(1)} %get-tuple-element.53), channel_id=1, source_target_pairs={{0,10},{1,11},{2,8},{3,9},{4,14},{5,15},{6,12},{7,13},{8,2},{9,3},... | collective-permute-start | bytes 245768 | tf_op jit(solution)/shard_map/ppermute | solution.py:369
  107.0 1.9 %collective-permute-start.22 = (bf16[320,128]{1,0:T(8,128)(2,1)S(1)}, bf16[320,128]{1,0:T(8,128)(2,1)S(1)}, u32[]{:S(2)}, u32[]{:S(2)}) collective-permute-start(bf16[320,128]{1,0:T(8,128)(2,1)S(1)} %get-tuple-element.47), channel_id=1, source_target_pairs={{0,8},{1,9},{2,10},{3,11},{4,12},{5,13},{6,14},{7,15},{8,0},{9,1},... | collective-permute-start | bytes 245768 | tf_op jit(solution)/shard_map/ppermute | solution.py:369
  111.4 2.2 %collective-permute-done.29 = bf16[320,128]{1,0:T(8,128)(2,1)S(1)} collective-permute-done((bf16[320,128]{1,0:T(8,128)(2,1)S(1)}, bf16[320,128]{1,0:T(8,128)(2,1)S(1)}, u32[]{:S(2)}, u32[]{:S(2)}) %collective-permute-start.29) | collective-permute-done | bytes 81952 | tf_op jit(solution)/shard_map/ppermute | solution.py:369
  113.6 5.0 %collective-permute-done.22 = bf16[320,128]{1,0:T(8,128)(2,1)S(1)} collective-permute-done((bf16[320,128]{1,0:T(8,128)(2,1)S(1)}, bf16[320,128]{1,0:T(8,128)(2,1)S(1)}, u32[]{:S(2)}, u32[]{:S(2)}) %collective-permute-start.22) | collective-permute-done | bytes 81952 | tf_op jit(solution)/shard_map/ppermute | solution.py:369
  118.8 2.1 %collective-permute-start.30 = (bf16[320,128]{1,0:T(8,128)(2,1)S(1)}, bf16[320,128]{1,0:T(8,128)(2,1)S(1)}, u32[]{:S(2)}, u32[]{:S(2)}) collective-permute-start(bf16[320,128]{1,0:T(8,128)(2,1)S(1)} %add_convert_fusion.3), channel_id=1, source_target_pairs={{0,8},{1,9},{2,10},{3,11},{4,12},{5,13},{6,14},{7,15},{8,0},{9,1},... | collective-permute-start | bytes 245768 | tf_op jit(solution)/shard_map/ppermute | solution.py:369
  121.1 2.1 %collective-permute-start.32 = (bf16[320,128]{1,0:T(8,128)(2,1)S(1)}, bf16[320,128]{1,0:T(8,128)(2,1)S(1)}, u32[]{:S(2)}, u32[]{:S(2)}) collective-permute-start(bf16[320,128]{1,0:T(8,128)(2,1)S(1)} %add_convert_fusion.3), channel_id=1, source_target_pairs={{0,12},{1,13},{2,14},{3,15},{4,8},{5,9},{6,10},{7,11},{8,4},{9,5},... | collective-permute-start | bytes 245768 | tf_op jit(solution)/shard_map/ppermute | solution.py:369
  123.2 2.8 %collective-permute-done.30 = bf16[320,128]{1,0:T(8,128)(2,1)S(1)} collective-permute-done((bf16[320,128]{1,0:T(8,128)(2,1)S(1)}, bf16[320,128]{1,0:T(8,128)(2,1)S(1)}, u32[]{:S(2)}, u32[]{:S(2)}) %collective-permute-start.30) | collective-permute-done | bytes 81952 | tf_op jit(solution)/shard_map/ppermute | solution.py:369
  127.9 1.7 collective-permute-start.33
  129.6 6.3 %collective-permute-done.33.refs_1_ = bf16[1280,128]{1,0:T(8,128)(2,1)S(1)} collective-permute-done((bf16[1280,128]{1,0:T(8,128)(2,1)S(1)}, bf16[1280,128]{1,0:T(8,128)(2,1)S(1)}, u32[]{:S(2)}, u32[]{:S(2)}) %collective-permute-start.33) | collective-permute-done | bytes 327712 | tf_op jit(solution)/shard_map/ppermute | solution.py:369
  137.5 12.3 %gradient.5 = (f32[4096,128]{1,0:T(8,128)S(1)}, bf16[2048,128]{1,0:T(8,128)(2,1)S(1)}, bf16[2048,128]{1,0:T(8,128)(2,1)S(1)}, bf16[8,64,128]{2,1,0:T(8,128)(2,1)S(1)}, f32[64,128]{1,0:T(8,128)S(1)}) custom-call(s32[305]{0:T(512)S(1)} %concatenate.12.scalars, bf16[520,512,128]{2,1,0:T(8,128)(2,1)} %collect_support.3.blocks, ...), custom_call_target="tpu_custom_call" | custom-call | flops 5368709120 | bytes 10485760 | tf_op jit(solution)/shard_map/gradient/pallas_call | solution.py:346
  153.6 7.6 %collective-permute-done.38 = bf16[2048,128]{1,0:T(8,128)(2,1)S(1)} collective-permute-done((bf16[2048,128]{1,0:T(8,128)(2,1)S(1)}, bf16[2048,128]{1,0:T(8,128)(2,1)S(1)}, u32[]{:S(2)}, u32[]{:S(2)}) %collective-permute-start.38) | collective-permute-done | bytes 524320 | tf_op jit(solution)/shard_map/ppermute | solution.py:369
  161.4 2.9 %collective-permute-start.39 = (bf16[1024,128]{1,0:T(8,128)(2,1)S(1)}, bf16[1024,128]{1,0:T(8,128)(2,1)S(1)}, u32[]{:S(2)}, u32[]{:S(2)}) collective-permute-start(bf16[1024,128]{1,0:T(8,128)(2,1)S(1)} %slice.176), channel_id=1, source_target_pairs={{0,4},{1,9},{2,6},{3,11},{4,0},{5,13},{6,2},{7,15},{8,12},{9,1},{1... | collective-permute-start | bytes 786440 | tf_op jit(solution)/shard_map/ppermute | solution.py:369
  164.3 6.4 %collective-permute-done.39 = bf16[1024,128]{1,0:T(8,128)(2,1)S(1)} collective-permute-done((bf16[1024,128]{1,0:T(8,128)(2,1)S(1)}, bf16[1024,128]{1,0:T(8,128)(2,1)S(1)}, u32[]{:S(2)}, u32[]{:S(2)}) %collective-permute-start.39) | collective-permute-done | bytes 262176 | tf_op jit(solution)/shard_map/ppermute | solution.py:369
  170.7 2.1 %collective-permute-start.40 = (bf16[512,128]{1,0:T(8,128)(2,1)S(1)}, bf16[512,128]{1,0:T(8,128)(2,1)S(1)}, u32[]{:S(2)}, u32[]{:S(2)}) collective-permute-start(bf16[512,128]{1,0:T(8,128)(2,1)S(1)} %slice.177), channel_id=1, source_target_pairs={{0,8},{1,3},{2,10},{3,1},{4,12},{5,7},{6,14},{7,5},{8,0},{9,11},{1... | collective-permute-start | bytes 393224 | tf_op jit(solution)/shard_map/ppermute | solution.py:369
  172.8 5.2 %collective-permute-done.40 = bf16[512,128]{1,0:T(8,128)(2,1)S(1)} collective-permute-done((bf16[512,128]{1,0:T(8,128)(2,1)S(1)}, bf16[512,128]{1,0:T(8,128)(2,1)S(1)}, u32[]{:S(2)}, u32[]{:S(2)}) %collective-permute-start.40) | collective-permute-done | bytes 131104 | tf_op jit(solution)/shard_map/ppermute | solution.py:369
  (90 shorter events, 36.3 us)
Async XLA Ops:
  1.6 16.8 %collective-permute-start = (bf16[512,128]{1,0:T(8,128)(2,1)S(1)}, bf16[512,128]{1,0:T(8,128)(2,1)S(1)}, u32[]{:S(2)}, u32[]{:S(2)}) collective-permute-start(bf16[512,128]{1,0:T(8,128)(2,1)S(1)} %reshape.33), channel_id=1, source_target_pairs={{0,8},{1,9},{2,10},{3,11},{4,12},{5,13},{6,14},{7,15},{8,0},{9,1},... | collective-permute-start | bytes 393224 | tf_op jit(solution)/shard_map/ppermute | solution.py:369
  5.7 12.7 %collective-permute-start.1 = (bf16[512,128]{1,0:T(8,128)(2,1)S(1)}, bf16[512,128]{1,0:T(8,128)(2,1)S(1)}, u32[]{:S(2)}, u32[]{:S(2)}) collective-permute-start(bf16[512,128]{1,0:T(8,128)(2,1)S(1)} %reshape.33), channel_id=1, source_target_pairs={{0,4},{1,5},{2,6},{3,7},{4,0},{5,1},{6,2},{7,3},{8,12},{9,13},{10,... | collective-permute-start | bytes 393224 | tf_op jit(solution)/shard_map/ppermute | solution.py:369
  7.3 11.2 %collective-permute-start.2 = (bf16[512,128]{1,0:T(8,128)(2,1)S(1)}, bf16[512,128]{1,0:T(8,128)(2,1)S(1)}, u32[]{:S(2)}, u32[]{:S(2)}) collective-permute-start(bf16[512,128]{1,0:T(8,128)(2,1)S(1)} %reshape.33), channel_id=1, source_target_pairs={{0,12},{1,13},{2,14},{3,15},{4,8},{5,9},{6,10},{7,11},{8,4},{9,5},... | collective-permute-start | bytes 393224 | tf_op jit(solution)/shard_map/ppermute | solution.py:369
  18.5 13.2 %collective-permute-start.3 = (bf16[2048,128]{1,0:T(8,128)(2,1)S(1)}, bf16[2048,128]{1,0:T(8,128)(2,1)S(1)}, u32[]{:S(2)}, u32[]{:S(2)}) collective-permute-start(bf16[2048,128]{1,0:T(8,128)(2,1)S(1)} %pad_maximum_fusion.refs_0_), channel_id=1, source_target_pairs={{0,2},{1,3},{2,0},{3,1},{4,6},{5,7},{6,4},{7,5},{8,10},{9,11},{10,... | collective-permute-start | bytes 1572872 | tf_op jit(solution)/shard_map/ppermute | solution.py:369
  20.3 12.9 %collective-permute-start.4 = (bf16[2048,128]{1,0:T(8,128)(2,1)S(1)}, bf16[2048,128]{1,0:T(8,128)(2,1)S(1)}, u32[]{:S(2)}, u32[]{:S(2)}) collective-permute-start(bf16[2048,128]{1,0:T(8,128)(2,1)S(1)} %pad_maximum_fusion.refs_0_), channel_id=1, source_target_pairs={{0,1},{1,0},{2,3},{3,2},{4,5},{5,4},{6,7},{7,6},{8,9},{9,8},{10,11... | collective-permute-start | bytes 1572872 | tf_op jit(solution)/shard_map/ppermute | solution.py:369
  47.6 8.5 %collective-permute-start.11 = (bf16[320,128]{1,0:T(8,128)(2,1)S(1)}, bf16[320,128]{1,0:T(8,128)(2,1)S(1)}, u32[]{:S(2)}, u32[]{:S(2)}) collective-permute-start(bf16[320,128]{1,0:T(8,128)(2,1)S(1)} %get-tuple-element.57), channel_id=1, source_target_pairs={{0,2},{1,3},{2,0},{3,1},{4,6},{5,7},{6,4},{7,5},{8,10},{9,11},{10,... | collective-permute-start | bytes 245768 | tf_op jit(solution)/shard_map/ppermute | solution.py:369
  49.1 9.4 %collective-permute-start.12 = (bf16[320,128]{1,0:T(8,128)(2,1)S(1)}, bf16[320,128]{1,0:T(8,128)(2,1)S(1)}, u32[]{:S(2)}, u32[]{:S(2)}) collective-permute-start(bf16[320,128]{1,0:T(8,128)(2,1)S(1)} %get-tuple-element.60), channel_id=1, source_target_pairs={{0,10},{1,11},{2,8},{3,9},{4,14},{5,15},{6,12},{7,13},{8,2},{9,3},... | collective-permute-start | bytes 245768 | tf_op jit(solution)/shard_map/ppermute | solution.py:369
  51.6 9.7 %collective-permute-start.13 = (bf16[320,128]{1,0:T(8,128)(2,1)S(1)}, bf16[320,128]{1,0:T(8,128)(2,1)S(1)}, u32[]{:S(2)}, u32[]{:S(2)}) collective-permute-start(bf16[320,128]{1,0:T(8,128)(2,1)S(1)} %get-tuple-element.59), channel_id=1, source_target_pairs={{0,6},{1,7},{2,4},{3,5},{4,2},{5,3},{6,0},{7,1},{8,14},{9,15},{10,... | collective-permute-start | bytes 245768 | tf_op jit(solution)/shard_map/ppermute | solution.py:369
  54.1 8.1 %collective-permute-start.14 = (bf16[320,128]{1,0:T(8,128)(2,1)S(1)}, bf16[320,128]{1,0:T(8,128)(2,1)S(1)}, u32[]{:S(2)}, u32[]{:S(2)}) collective-permute-start(bf16[320,128]{1,0:T(8,128)(2,1)S(1)} %get-tuple-element.58), channel_id=1, source_target_pairs={{0,14},{1,15},{2,12},{3,13},{4,10},{5,11},{6,8},{7,9},{8,6},{9,7},... | collective-permute-start | bytes 245768 | tf_op jit(solution)/shard_map/ppermute | solution.py:369
  54.4 11.4 %collective-permute-start.7 = (bf16[320,128]{1,0:T(8,128)(2,1)S(1)}, bf16[320,128]{1,0:T(8,128)(2,1)S(1)}, u32[]{:S(2)}, u32[]{:S(2)}) collective-permute-start(bf16[320,128]{1,0:T(8,128)(2,1)S(1)} %get-tuple-element.54), channel_id=1, source_target_pairs={{0,8},{1,9},{2,10},{3,11},{4,12},{5,13},{6,14},{7,15},{8,0},{9,1},... | collective-permute-start | bytes 245768 | tf_op jit(solution)/shard_map/ppermute | solution.py:369
  56.1 9.7 %collective-permute-start.8 = (bf16[320,128]{1,0:T(8,128)(2,1)S(1)}, bf16[320,128]{1,0:T(8,128)(2,1)S(1)}, u32[]{:S(2)}, u32[]{:S(2)}) collective-permute-start(bf16[320,128]{1,0:T(8,128)(2,1)S(1)} %get-tuple-element.56), channel_id=1, source_target_pairs={{0,4},{1,5},{2,6},{3,7},{4,0},{5,1},{6,2},{7,3},{8,12},{9,13},{10,... | collective-permute-start | bytes 245768 | tf_op jit(solution)/shard_map/ppermute | solution.py:369
  58.6 7.2 %collective-permute-start.9 = (bf16[320,128]{1,0:T(8,128)(2,1)S(1)}, bf16[320,128]{1,0:T(8,128)(2,1)S(1)}, u32[]{:S(2)}, u32[]{:S(2)}) collective-permute-start(bf16[320,128]{1,0:T(8,128)(2,1)S(1)} %get-tuple-element.55), channel_id=1, source_target_pairs={{0,12},{1,13},{2,14},{3,15},{4,8},{5,9},{6,10},{7,11},{8,4},{9,5},... | collective-permute-start | bytes 245768 | tf_op jit(solution)/shard_map/ppermute | solution.py:369
  66.0 8.2 %collective-permute-start.15 = (bf16[320,128]{1,0:T(8,128)(2,1)S(1)}, bf16[320,128]{1,0:T(8,128)(2,1)S(1)}, u32[]{:S(2)}, u32[]{:S(2)}) collective-permute-start(bf16[320,128]{1,0:T(8,128)(2,1)S(1)} %get-tuple-element.41), channel_id=1, source_target_pairs={{0,8},{1,9},{2,10},{3,11},{4,12},{5,13},{6,14},{7,15},{8,0},{9,1},... | collective-permute-start | bytes 245768 | tf_op jit(solution)/shard_map/ppermute | solution.py:369
  69.2 6.9 %collective-permute-start.16 = (bf16[320,128]{1,0:T(8,128)(2,1)S(1)}, bf16[320,128]{1,0:T(8,128)(2,1)S(1)}, u32[]{:S(2)}, u32[]{:S(2)}) collective-permute-start(bf16[320,128]{1,0:T(8,128)(2,1)S(1)} %get-tuple-element.41), channel_id=1, source_target_pairs={{0,4},{1,5},{2,6},{3,7},{4,0},{5,1},{6,2},{7,3},{8,12},{9,13},{10,... | collective-permute-start | bytes 245768 | tf_op jit(solution)/shard_map/ppermute | solution.py:369
  69.2 6.9 %collective-permute-start.17 = (bf16[320,128]{1,0:T(8,128)(2,1)S(1)}, bf16[320,128]{1,0:T(8,128)(2,1)S(1)}, u32[]{:S(2)}, u32[]{:S(2)}) collective-permute-start(bf16[320,128]{1,0:T(8,128)(2,1)S(1)} %get-tuple-element.41), channel_id=1, source_target_pairs={{0,12},{1,13},{2,14},{3,15},{4,8},{5,9},{6,10},{7,11},{8,4},{9,5},... | collective-permute-start | bytes 245768 | tf_op jit(solution)/shard_map/ppermute | solution.py:369
  76.2 8.5 %collective-permute-start.18 = (bf16[1280,128]{1,0:T(8,128)(2,1)S(1)}, bf16[1280,128]{1,0:T(8,128)(2,1)S(1)}, u32[]{:S(2)}, u32[]{:S(2)}) collective-permute-start(bf16[1280,128]{1,0:T(8,128)(2,1)S(1)} %pad_maximum_fusion.1.refs_0_), channel_id=1, source_target_pairs={{0,2},{1,3},{2,0},{3,1},{4,6},{5,7},{6,4},{7,5},{8,10},{9,11},{10,... | collective-permute-start | bytes 983048 | tf_op jit(solution)/shard_map/ppermute | solution.py:369
  77.8 6.9 %collective-permute-start.19 = (bf16[1280,128]{1,0:T(8,128)(2,1)S(1)}, bf16[1280,128]{1,0:T(8,128)(2,1)S(1)}, u32[]{:S(2)}, u32[]{:S(2)}) collective-permute-start(bf16[1280,128]{1,0:T(8,128)(2,1)S(1)} %pad_maximum_fusion.1.refs_0_), channel_id=1, source_target_pairs={{0,1},{1,0},{2,3},{3,2},{4,5},{5,4},{6,7},{7,6},{8,9},{9,8},{10,11... | collective-permute-start | bytes 983048 | tf_op jit(solution)/shard_map/ppermute | solution.py:369
  99.7 9.1 %collective-permute-start.26 = (bf16[320,128]{1,0:T(8,128)(2,1)S(1)}, bf16[320,128]{1,0:T(8,128)(2,1)S(1)}, u32[]{:S(2)}, u32[]{:S(2)}) collective-permute-start(bf16[320,128]{1,0:T(8,128)(2,1)S(1)} %get-tuple-element.50), channel_id=1, source_target_pairs={{0,2},{1,3},{2,0},{3,1},{4,6},{5,7},{6,4},{7,5},{8,10},{9,11},{10,... | collective-permute-start | bytes 245768 | tf_op jit(solution)/shard_map/ppermute | solution.py:369
  101.3 8.5 %collective-permute-start.27 = (bf16[320,128]{1,0:T(8,128)(2,1)S(1)}, bf16[320,128]{1,0:T(8,128)(2,1)S(1)}, u32[]{:S(2)}, u32[]{:S(2)}) collective-permute-start(bf16[320,128]{1,0:T(8,128)(2,1)S(1)} %get-tuple-element.53), channel_id=1, source_target_pairs={{0,10},{1,11},{2,8},{3,9},{4,14},{5,15},{6,12},{7,13},{8,2},{9,3},... | collective-permute-start | bytes 245768 | tf_op jit(solution)/shard_map/ppermute | solution.py:369
  104.4 7.1 %collective-permute-start.28 = (bf16[320,128]{1,0:T(8,128)(2,1)S(1)}, bf16[320,128]{1,0:T(8,128)(2,1)S(1)}, u32[]{:S(2)}, u32[]{:S(2)}) collective-permute-start(bf16[320,128]{1,0:T(8,128)(2,1)S(1)} %get-tuple-element.52), channel_id=1, source_target_pairs={{0,6},{1,7},{2,4},{3,5},{4,2},{5,3},{6,0},{7,1},{8,14},{9,15},{10,... | collective-permute-start | bytes 245768 | tf_op jit(solution)/shard_map/ppermute | solution.py:369
  105.3 8.3 %collective-permute-start.29 = (bf16[320,128]{1,0:T(8,128)(2,1)S(1)}, bf16[320,128]{1,0:T(8,128)(2,1)S(1)}, u32[]{:S(2)}, u32[]{:S(2)}) collective-permute-start(bf16[320,128]{1,0:T(8,128)(2,1)S(1)} %get-tuple-element.51), channel_id=1, source_target_pairs={{0,14},{1,15},{2,12},{3,13},{4,10},{5,11},{6,8},{7,9},{8,6},{9,7},... | collective-permute-start | bytes 245768 | tf_op jit(solution)/shard_map/ppermute | solution.py:369
  107.0 11.6 %collective-permute-start.22 = (bf16[320,128]{1,0:T(8,128)(2,1)S(1)}, bf16[320,128]{1,0:T(8,128)(2,1)S(1)}, u32[]{:S(2)}, u32[]{:S(2)}) collective-permute-start(bf16[320,128]{1,0:T(8,128)(2,1)S(1)} %get-tuple-element.47), channel_id=1, source_target_pairs={{0,8},{1,9},{2,10},{3,11},{4,12},{5,13},{6,14},{7,15},{8,0},{9,1},... | collective-permute-start | bytes 245768 | tf_op jit(solution)/shard_map/ppermute | solution.py:369
  108.8 9.8 %collective-permute-start.23 = (bf16[320,128]{1,0:T(8,128)(2,1)S(1)}, bf16[320,128]{1,0:T(8,128)(2,1)S(1)}, u32[]{:S(2)}, u32[]{:S(2)}) collective-permute-start(bf16[320,128]{1,0:T(8,128)(2,1)S(1)} %get-tuple-element.49), channel_id=1, source_target_pairs={{0,4},{1,5},{2,6},{3,7},{4,0},{5,1},{6,2},{7,3},{8,12},{9,13},{10,... | collective-permute-start | bytes 245768 | tf_op jit(solution)/shard_map/ppermute | solution.py:369
  109.8 8.8 %collective-permute-start.24 = (bf16[320,128]{1,0:T(8,128)(2,1)S(1)}, bf16[320,128]{1,0:T(8,128)(2,1)S(1)}, u32[]{:S(2)}, u32[]{:S(2)}) collective-permute-start(bf16[320,128]{1,0:T(8,128)(2,1)S(1)} %get-tuple-element.48), channel_id=1, source_target_pairs={{0,12},{1,13},{2,14},{3,15},{4,8},{5,9},{6,10},{7,11},{8,4},{9,5},... | collective-permute-start | bytes 245768 | tf_op jit(solution)/shard_map/ppermute | solution.py:369
  118.8 7.3 %collective-permute-start.30 = (bf16[320,128]{1,0:T(8,128)(2,1)S(1)}, bf16[320,128]{1,0:T(8,128)(2,1)S(1)}, u32[]{:S(2)}, u32[]{:S(2)}) collective-permute-start(bf16[320,128]{1,0:T(8,128)(2,1)S(1)} %add_convert_fusion.3), channel_id=1, source_target_pairs={{0,8},{1,9},{2,10},{3,11},{4,12},{5,13},{6,14},{7,15},{8,0},{9,1},... | collective-permute-start | bytes 245768 | tf_op jit(solution)/shard_map/ppermute | solution.py:369
  120.9 5.5 %collective-permute-start.31 = (bf16[320,128]{1,0:T(8,128)(2,1)S(1)}, bf16[320,128]{1,0:T(8,128)(2,1)S(1)}, u32[]{:S(2)}, u32[]{:S(2)}) collective-permute-start(bf16[320,128]{1,0:T(8,128)(2,1)S(1)} %add_convert_fusion.3), channel_id=1, source_target_pairs={{0,4},{1,5},{2,6},{3,7},{4,0},{5,1},{6,2},{7,3},{8,12},{9,13},{10,... | collective-permute-start | bytes 245768 | tf_op jit(solution)/shard_map/ppermute | solution.py:369
  121.1 6.7 %collective-permute-start.32 = (bf16[320,128]{1,0:T(8,128)(2,1)S(1)}, bf16[320,128]{1,0:T(8,128)(2,1)S(1)}, u32[]{:S(2)}, u32[]{:S(2)}) collective-permute-start(bf16[320,128]{1,0:T(8,128)(2,1)S(1)} %add_convert_fusion.3), channel_id=1, source_target_pairs={{0,12},{1,13},{2,14},{3,15},{4,8},{5,9},{6,10},{7,11},{8,4},{9,5},... | collective-permute-start | bytes 245768 | tf_op jit(solution)/shard_map/ppermute | solution.py:369
  127.9 8.0 %collective-permute-start.33 = (bf16[1280,128]{1,0:T(8,128)(2,1)S(1)}, bf16[1280,128]{1,0:T(8,128)(2,1)S(1)}, u32[]{:S(2)}, u32[]{:S(2)}) collective-permute-start(bf16[1280,128]{1,0:T(8,128)(2,1)S(1)} %pad_maximum_fusion.2.refs_0_), channel_id=1, source_target_pairs={{0,2},{1,3},{2,0},{3,1},{4,6},{5,7},{6,4},{7,5},{8,10},{9,11},{10,... | collective-permute-start | bytes 983048 | tf_op jit(solution)/shard_map/ppermute | solution.py:369
  129.6 6.3 %collective-permute-start.34 = (bf16[1280,128]{1,0:T(8,128)(2,1)S(1)}, bf16[1280,128]{1,0:T(8,128)(2,1)S(1)}, u32[]{:S(2)}, u32[]{:S(2)}) collective-permute-start(bf16[1280,128]{1,0:T(8,128)(2,1)S(1)} %pad_maximum_fusion.2.refs_0_), channel_id=1, source_target_pairs={{0,1},{1,0},{2,3},{3,2},{4,5},{5,4},{6,7},{7,6},{8,9},{9,8},{10,11... | collective-permute-start | bytes 983048 | tf_op jit(solution)/shard_map/ppermute | solution.py:369
  151.9 9.2 %collective-permute-start.38 = (bf16[2048,128]{1,0:T(8,128)(2,1)S(1)}, bf16[2048,128]{1,0:T(8,128)(2,1)S(1)}, u32[]{:S(2)}, u32[]{:S(2)}) collective-permute-start(bf16[2048,128]{1,0:T(8,128)(2,1)S(1)} %add_convert_fusion), channel_id=1, source_target_pairs={{0,2},{1,5},{2,0},{3,7},{4,6},{5,1},{6,4},{7,3},{8,10},{9,13},{10,... | collective-permute-start | bytes 1572872 | tf_op jit(solution)/shard_map/ppermute | solution.py:369
  161.4 9.3 %collective-permute-start.39 = (bf16[1024,128]{1,0:T(8,128)(2,1)S(1)}, bf16[1024,128]{1,0:T(8,128)(2,1)S(1)}, u32[]{:S(2)}, u32[]{:S(2)}) collective-permute-start(bf16[1024,128]{1,0:T(8,128)(2,1)S(1)} %slice.176), channel_id=1, source_target_pairs={{0,4},{1,9},{2,6},{3,11},{4,0},{5,13},{6,2},{7,15},{8,12},{9,1},{1... | collective-permute-start | bytes 786440 | tf_op jit(solution)/shard_map/ppermute | solution.py:369
  170.7 7.3 %collective-permute-start.40 = (bf16[512,128]{1,0:T(8,128)(2,1)S(1)}, bf16[512,128]{1,0:T(8,128)(2,1)S(1)}, u32[]{:S(2)}, u32[]{:S(2)}) collective-permute-start(bf16[512,128]{1,0:T(8,128)(2,1)S(1)} %slice.177), channel_id=1, source_target_pairs={{0,8},{1,3},{2,10},{3,1},{4,12},{5,7},{6,14},{7,5},{8,0},{9,11},{1... | collective-permute-start | bytes 393224 | tf_op jit(solution)/shard_map/ppermute | solution.py:369
  (10 other events, 22.1 us)

commit v9 on v8

--- a/solution.py
+++ b/solution.py
@@ -202,10 +202,12 @@
         return jnp.where(me % 2 == 0, even, odd) ^ me
 
     quarter = shards // 4
-    size_in = gathered[0].shape[0] // quarter
+    size_in = gathered[0].shape[0] // (quarter + 1)
     for slot in range(shards):
-        begin = slot % quarter * size_in
-        codes[shard_span(slot, size_in), :] = gathered[slot // quarter][begin : begin + size_in, :]
+        half, inside = divmod(slot, 2 * quarter)
+        second = inside > quarter
+        begin = (inside - (quarter + 1) * second) * size_in
+        codes[shard_span(slot, size_in), :] = gathered[2 * half + second][begin : begin + size_in, :]
 
     def put(slot, size, begin, value):
         rows = slice(slot % quarter * size + begin, slot % quarter * size + begin + value.shape[0])
@@ -268,7 +270,7 @@
             write_packed(limits, [thresh[group]] * count, offset)
         matrix = jnp.concatenate([held[first + pair] for pair in range(count)], axis=1)
         point = jnp.concatenate(parts, axis=1)
-        residual = lax.dot_general(point, matrix, (((1,), (1,)), ((), ())), preferred_element_type=jnp.float32)
+        residual = lax.dot_general(matrix, point, (((1,), (1,)), ((), ())), preferred_element_type=jnp.float32).T
         target = targets[tile(group), :].astype(jnp.float32)
         residual = (residual - target).astype(jnp.bfloat16)
         gradient = jnp.dot(residual, matrix, preferred_element_type=jnp.float32)
@@ -373,10 +375,10 @@
     core, row, *columns = stage_distances(lax.axis_size("rows"))
     apart = [slot_distance(slot, columns) for slot in range(lax.axis_size("rows") // 4)]
     made = ()
-    near = jnp.concatenate([own] + [exchange(own, distance) for distance in apart[1:]], axis=0)
+    near = jnp.concatenate([own] + [exchange(own, distance) for distance in apart[1:] + [row]], axis=0)
     if beside:
         near, *made = lax.optimization_barrier((near, beside[0]()))
-    other = exchange(near, row)
+    other = exchange(near[own.shape[0] : len(apart) * own.shape[0]], row)
     far = exchange(near, core)
     if beside:
         other, *made = lax.optimization_barrier((other, beside[1](*made)))

time: 180 us -> 185 us (1.028)
  Pallas kernels: 52.1 us -> 63.4 us
  waiting for transfers between devices: 64.9 us -> 60.2 us
    pallas_call x3, Pallas kernels: 34.8 us -> 46.2 us  [gradient_call(): pl.pallas_call(functools.partial(gradient_kernel, mode, shards, pairs, gr...]
    ppermute x41 -> x44, waiting for transfers between devices: 64.9 us -> 60.2 us  [exchange(): lax.ppermute(value, 'rows', [(i, i ^ apart[i % 2]) for i in range(devices)])]
    ppermute x41 -> x44, starting transfers between devices: 53.8 us -> 52 us  [exchange(): lax.ppermute(value, 'rows', [(i, i ^ apart[i % 2]) for i in range(devices)])]
  transfers between devices with their start and end apart: 41 -> 44, of which waited for: 23 -> 26; matrix products, arithmetic and copies ran while one was open for 2% -> 2% of each run, Pallas kernels for 10% -> 9%
where the time goes in v9:
time: 185 us
  Pallas kernels  63.4 us (34%)
  waiting for transfers between devices  60.2 us (33%)
  starting transfers between devices  52 us (28%)
  local copies, waits for them, and re-layouts  6.44 us (3%)
  other arithmetic  2.17 us (1%)
    ppermute x44, waiting for transfers between devices, exchange(): lax.ppermute(value, 'rows', [(i, i ^ apart[i % 2]) for i in range(devices)])  60.2 us
    ppermute x44, starting transfers between devices, exchange(): lax.ppermute(value, 'rows', [(i, i ^ apart[i % 2]) for i in range(devices)])  52 us
    pallas_call x3, Pallas kernels, gradient_call(): pl.pallas_call(functools.partial(gradient_kernel, mode, shards, pairs, gr...  46.2 us
    pallas_call x2, Pallas kernels, collect_support(): pl.pallas_call(functools.partial(support_kernel, part * entries, groups),...  17.3 us
  transfers between devices with their start and end apart: 44, of which 26 were waited for; matrix products, arithmetic and copies ran while one was open for 2% of the time, Pallas kernels for 9%

profile of v9, /device:TPU:0, one launch (start us, length us, event | category | flops | bytes accessed | tf_op | source)
XLA Modules:
  0.0 184.6 jit_solution(11739508775546272362)
XLA Ops:
  1.6 4.1 %collective-permute-start = (bf16[512,128]{1,0:T(8,128)(2,1)S(1)}, bf16[512,128]{1,0:T(8,128)(2,1)S(1)}, u32[]{:S(2)}, u32[]{:S(2)}) collective-permute-start(bf16[512,128]{1,0:T(8,128)(2,1)S(1)} %reshape.33), channel_id=1, source_target_pairs={{0,8},{1,9},{2,10},{3,11},{4,12},{5,13},{6,14},{7,15},{8,0},{9,1},... | collective-permute-start | bytes 393224 | tf_op jit(solution)/shard_map/ppermute | solution.py:371
  5.7 1.6 collective-permute-start.1
  7.3 1.7 collective-permute-start.3
  11.7 8.5 %collect_support.2.refs_0_ = bf16[520,512,128]{2,1,0:T(8,128)(2,1)} custom-call(s32[305]{0:T(512)S(1)} %concatenate.18.scalars, bf16[512,32768]{1,0:T(8,128)(2,1)} %dictionary.3), custom_call_target="tpu_custom_call" | custom-call | bytes 31457280 | tf_op jit(solution)/shard_map/collect_support/pallas_call | solution.py:129
  20.8 8.8 %collect_support.3.blocks = bf16[520,512,128]{2,1,0:T(8,128)(2,1)} custom-call(s32[305]{0:T(512)S(1)} %concatenate.18.scalars, bf16[512,32768]{1,0:T(8,128)(2,1)} %dictionary.3, bf16[520,512,128]{2,1,0:T(8,128)(2,1)} %collect_support.2.refs_0_), custom_call_target="tpu_custom_call", output_to_operand_aliasing={{}: (2, {})} | custom-call | bytes 31457280 | tf_op jit(solution)/shard_map/collect_support/pallas_call | solution.py:129
  32.2 15.5 %gradient.3 = (f32[2560,128]{1,0:T(8,128)S(1)}, bf16[1280,128]{1,0:T(8,128)(2,1)S(1)}, bf16[1280,128]{1,0:T(8,128)(2,1)S(1)}, bf16[320,128]{1,0:T(8,128)(2,1)S(1)}, f32[320,128]{1,0:T(8,128)S(1)}) custom-call(s32[305]{0:T(512)S(1)} %concatenate.18.scalars, bf16[520,512,128]{2,1,0:T(8,128)(2,1)} %collect_support.3.blocks, ...), custom_call_target="tpu_custom_call" | custom-call | flops 5368709120 | bytes 10485760 | tf_op jit(solution)/shard_map/gradient/pallas_call | solution.py:348
  51.5 1.7 collective-permute-start.13
  53.2 3.4 %collective-permute-start.14 = (bf16[320,128]{1,0:T(8,128)(2,1)S(1)}, bf16[320,128]{1,0:T(8,128)(2,1)S(1)}, u32[]{:S(2)}, u32[]{:S(2)}) collective-permute-start(bf16[320,128]{1,0:T(8,128)(2,1)S(1)} %get-tuple-element.62), channel_id=1, source_target_pairs={{0,6},{1,7},{2,4},{3,5},{4,2},{5,3},{6,0},{7,1},{8,14},{9,15},{10,... | collective-permute-start | bytes 245768 | tf_op jit(solution)/shard_map/ppermute | solution.py:371
  56.9 3.6 %collective-permute-start.10 = (bf16[320,128]{1,0:T(8,128)(2,1)S(1)}, bf16[320,128]{1,0:T(8,128)(2,1)S(1)}, u32[]{:S(2)}, u32[]{:S(2)}) collective-permute-start(bf16[320,128]{1,0:T(8,128)(2,1)S(1)} %get-tuple-element.58), channel_id=1, source_target_pairs={{0,12},{1,13},{2,14},{3,15},{4,8},{5,9},{6,10},{7,11},{8,4},{9,5},... | collective-permute-start | bytes 245768 | tf_op jit(solution)/shard_map/ppermute | solution.py:371
  61.3 3.4 %collective-permute-done.15 = bf16[320,128]{1,0:T(8,128)(2,1)S(1)} collective-permute-done((bf16[320,128]{1,0:T(8,128)(2,1)S(1)}, bf16[320,128]{1,0:T(8,128)(2,1)S(1)}, u32[]{:S(2)}, u32[]{:S(2)}) %collective-permute-start.15) | collective-permute-done | bytes 81952 | tf_op jit(solution)/shard_map/ppermute | solution.py:371
  65.5 3.6 %collective-permute-done.8 = bf16[320,128]{1,0:T(8,128)(2,1)S(1)} collective-permute-done((bf16[320,128]{1,0:T(8,128)(2,1)S(1)}, bf16[320,128]{1,0:T(8,128)(2,1)S(1)}, u32[]{:S(2)}, u32[]{:S(2)}) %collective-permute-start.8) | collective-permute-done | bytes 81952 | tf_op jit(solution)/shard_map/ppermute | solution.py:371
  69.5 3.1 %collective-permute-start.17 = (bf16[320,128]{1,0:T(8,128)(2,1)S(1)}, bf16[320,128]{1,0:T(8,128)(2,1)S(1)}, u32[]{:S(2)}, u32[]{:S(2)}) collective-permute-start(bf16[320,128]{1,0:T(8,128)(2,1)S(1)} %get-tuple-element.44), channel_id=1, source_target_pairs={{0,4},{1,5},{2,6},{3,7},{4,0},{5,1},{6,2},{7,3},{8,12},{9,13},{10,... | collective-permute-start | bytes 245768 | tf_op jit(solution)/shard_map/ppermute | solution.py:371
  76.1 2.8 %collective-permute-done.18 = bf16[320,128]{1,0:T(8,128)(2,1)S(1)} collective-permute-done((bf16[320,128]{1,0:T(8,128)(2,1)S(1)}, bf16[320,128]{1,0:T(8,128)(2,1)S(1)}, u32[]{:S(2)}, u32[]{:S(2)}) %collective-permute-start.18) | collective-permute-done | bytes 81952 | tf_op jit(solution)/shard_map/ppermute | solution.py:371
  80.5 4.7 %collective-permute-done.20.refs_1_ = bf16[960,128]{1,0:T(8,128)(2,1)S(1)} collective-permute-done((bf16[960,128]{1,0:T(8,128)(2,1)S(1)}, bf16[960,128]{1,0:T(8,128)(2,1)S(1)}, u32[]{:S(2)}, u32[]{:S(2)}) %collective-permute-start.20) | collective-permute-done | bytes 245792 | tf_op jit(solution)/shard_map/ppermute | solution.py:371
  85.2 1.5 collective-permute-done.22.refs_3_
  86.7 15.0 %gradient.4 = (f32[2560,128]{1,0:T(8,128)S(1)}, bf16[1280,128]{1,0:T(8,128)(2,1)S(1)}, bf16[1280,128]{1,0:T(8,128)(2,1)S(1)}) custom-call(s32[305]{0:T(512)S(1)} %concatenate.18.scalars, bf16[520,512,128]{2,1,0:T(8,128)(2,1)} %collect_support.3.blocks, bf16[1600,128]{1,0:T(8,128)(2,1)S(1)} %constant_dynamic-update-slice_fusion.5.refs_0_, ...), custom_call_target="tpu_custom_call" | custom-call | flops 5368709120 | bytes 10485760 | tf_op jit(solution)/shard_map/gradient/pallas_call | solution.py:348
  105.4 2.4 %collective-permute-start.29 = (bf16[320,128]{1,0:T(8,128)(2,1)S(1)}, bf16[320,128]{1,0:T(8,128)(2,1)S(1)}, u32[]{:S(2)}, u32[]{:S(2)}) collective-permute-start(bf16[320,128]{1,0:T(8,128)(2,1)S(1)} %get-tuple-element.56), channel_id=1, source_target_pairs={{0,10},{1,11},{2,8},{3,9},{4,14},{5,15},{6,12},{7,13},{8,2},{9,3},... | collective-permute-start | bytes 245768 | tf_op jit(solution)/shard_map/ppermute | solution.py:371
  108.2 2.6 %collective-permute-start.31 = (bf16[320,128]{1,0:T(8,128)(2,1)S(1)}, bf16[320,128]{1,0:T(8,128)(2,1)S(1)}, u32[]{:S(2)}, u32[]{:S(2)}) collective-permute-start(bf16[320,128]{1,0:T(8,128)(2,1)S(1)} %get-tuple-element.54), channel_id=1, source_target_pairs={{0,14},{1,15},{2,12},{3,13},{4,10},{5,11},{6,8},{7,9},{8,6},{9,7},... | collective-permute-start | bytes 245768 | tf_op jit(solution)/shard_map/ppermute | solution.py:371
  116.3 5.7 %collective-permute-done.24 = bf16[320,128]{1,0:T(8,128)(2,1)S(1)} collective-permute-done((bf16[320,128]{1,0:T(8,128)(2,1)S(1)}, bf16[320,128]{1,0:T(8,128)(2,1)S(1)}, u32[]{:S(2)}, u32[]{:S(2)}) %collective-permute-start.24) | collective-permute-done | bytes 81952 | tf_op jit(solution)/shard_map/ppermute | solution.py:371
  122.2 2.3 %collective-permute-start.32 = (bf16[320,128]{1,0:T(8,128)(2,1)S(1)}, bf16[320,128]{1,0:T(8,128)(2,1)S(1)}, u32[]{:S(2)}, u32[]{:S(2)}) collective-permute-start(bf16[320,128]{1,0:T(8,128)(2,1)S(1)} %get-tuple-element.40), channel_id=1, source_target_pairs={{0,8},{1,9},{2,10},{3,11},{4,12},{5,13},{6,14},{7,15},{8,0},{9,1},... | collective-permute-start | bytes 245768 | tf_op jit(solution)/shard_map/ppermute | solution.py:371
  124.6 2.0 %collective-permute-start.34 = (bf16[320,128]{1,0:T(8,128)(2,1)S(1)}, bf16[320,128]{1,0:T(8,128)(2,1)S(1)}, u32[]{:S(2)}, u32[]{:S(2)}) collective-permute-start(bf16[320,128]{1,0:T(8,128)(2,1)S(1)} %get-tuple-element.40), channel_id=1, source_target_pairs={{0,12},{1,13},{2,14},{3,15},{4,8},{5,9},{6,10},{7,11},{8,4},{9,5},... | collective-permute-start | bytes 245768 | tf_op jit(solution)/shard_map/ppermute | solution.py:371
  127.7 2.2 %collective-permute-done.33 = bf16[320,128]{1,0:T(8,128)(2,1)S(1)} collective-permute-done((bf16[320,128]{1,0:T(8,128)(2,1)S(1)}, bf16[320,128]{1,0:T(8,128)(2,1)S(1)}, u32[]{:S(2)}, u32[]{:S(2)}) %collective-permute-start.33) | collective-permute-done | bytes 81952 | tf_op jit(solution)/shard_map/ppermute | solution.py:371
  131.2 1.9 %collective-permute-start.36 = (bf16[960,128]{1,0:T(8,128)(2,1)S(1)}, bf16[960,128]{1,0:T(8,128)(2,1)S(1)}, u32[]{:S(2)}, u32[]{:S(2)}) collective-permute-start(bf16[960,128]{1,0:T(8,128)(2,1)S(1)} %pad_maximum_fusion.1), channel_id=1, source_target_pairs={{0,2},{1,3},{2,0},{3,1},{4,6},{5,7},{6,4},{7,5},{8,10},{9,11},{10,... | collective-permute-start | bytes 737288 | tf_op jit(solution)/shard_map/ppermute | solution.py:371
  133.3 4.5 %collective-permute-done.36.refs_1_ = bf16[960,128]{1,0:T(8,128)(2,1)S(1)} collective-permute-done((bf16[960,128]{1,0:T(8,128)(2,1)S(1)}, bf16[960,128]{1,0:T(8,128)(2,1)S(1)}, u32[]{:S(2)}, u32[]{:S(2)}) %collective-permute-start.36) | collective-permute-done | bytes 245792 | tf_op jit(solution)/shard_map/ppermute | solution.py:371
  137.7 1.5 collective-permute-done.38.refs_3_
  139.2 15.7 %gradient.5 = (f32[4096,128]{1,0:T(8,128)S(1)}, bf16[2048,128]{1,0:T(8,128)(2,1)S(1)}, bf16[2048,128]{1,0:T(8,128)(2,1)S(1)}, bf16[8,64,128]{2,1,0:T(8,128)(2,1)S(1)}, f32[64,128]{1,0:T(8,128)S(1)}) custom-call(s32[305]{0:T(512)S(1)} %concatenate.18.scalars, bf16[520,512,128]{2,1,0:T(8,128)(2,1)} %collect_support.3.blocks, ...), custom_call_target="tpu_custom_call" | custom-call | flops 5368709120 | bytes 10485760 | tf_op jit(solution)/shard_map/gradient/pallas_call | solution.py:348
  157.1 1.7 collective-permute-start.41
  158.7 7.6 %collective-permute-done.41 = bf16[2048,128]{1,0:T(8,128)(2,1)S(1)} collective-permute-done((bf16[2048,128]{1,0:T(8,128)(2,1)S(1)}, bf16[2048,128]{1,0:T(8,128)(2,1)S(1)}, u32[]{:S(2)}, u32[]{:S(2)}) %collective-permute-start.41) | collective-permute-done | bytes 524320 | tf_op jit(solution)/shard_map/ppermute | solution.py:371
  166.5 2.6 %collective-permute-start.42 = (bf16[1024,128]{1,0:T(8,128)(2,1)S(1)}, bf16[1024,128]{1,0:T(8,128)(2,1)S(1)}, u32[]{:S(2)}, u32[]{:S(2)}) collective-permute-start(bf16[1024,128]{1,0:T(8,128)(2,1)S(1)} %slice.184), channel_id=1, source_target_pairs={{0,4},{1,9},{2,6},{3,11},{4,0},{5,13},{6,2},{7,15},{8,12},{9,1},{1... | collective-permute-start | bytes 786440 | tf_op jit(solution)/shard_map/ppermute | solution.py:371
  169.2 6.7 %collective-permute-done.42 = bf16[1024,128]{1,0:T(8,128)(2,1)S(1)} collective-permute-done((bf16[1024,128]{1,0:T(8,128)(2,1)S(1)}, bf16[1024,128]{1,0:T(8,128)(2,1)S(1)}, u32[]{:S(2)}, u32[]{:S(2)}) %collective-permute-start.42) | collective-permute-done | bytes 262176 | tf_op jit(solution)/shard_map/ppermute | solution.py:371
  175.9 1.8 collective-permute-start.43
  177.7 5.5 %collective-permute-done.43 = bf16[512,128]{1,0:T(8,128)(2,1)S(1)} collective-permute-done((bf16[512,128]{1,0:T(8,128)(2,1)S(1)}, bf16[512,128]{1,0:T(8,128)(2,1)S(1)}, u32[]{:S(2)}, u32[]{:S(2)}) %collective-permute-start.43) | collective-permute-done | bytes 131104 | tf_op jit(solution)/shard_map/ppermute | solution.py:371
  (109 shorter events, 34.7 us)
Async XLA Ops:
  1.6 18.6 %collective-permute-start = (bf16[512,128]{1,0:T(8,128)(2,1)S(1)}, bf16[512,128]{1,0:T(8,128)(2,1)S(1)}, u32[]{:S(2)}, u32[]{:S(2)}) collective-permute-start(bf16[512,128]{1,0:T(8,128)(2,1)S(1)} %reshape.33), channel_id=1, source_target_pairs={{0,8},{1,9},{2,10},{3,11},{4,12},{5,13},{6,14},{7,15},{8,0},{9,1},... | collective-permute-start | bytes 393224 | tf_op jit(solution)/shard_map/ppermute | solution.py:371
  5.7 14.5 %collective-permute-start.1 = (bf16[512,128]{1,0:T(8,128)(2,1)S(1)}, bf16[512,128]{1,0:T(8,128)(2,1)S(1)}, u32[]{:S(2)}, u32[]{:S(2)}) collective-permute-start(bf16[512,128]{1,0:T(8,128)(2,1)S(1)} %reshape.33), channel_id=1, source_target_pairs={{0,4},{1,5},{2,6},{3,7},{4,0},{5,1},{6,2},{7,3},{8,12},{9,13},{10,... | collective-permute-start | bytes 393224 | tf_op jit(solution)/shard_map/ppermute | solution.py:371
  7.3 13.0 %collective-permute-start.2 = (bf16[512,128]{1,0:T(8,128)(2,1)S(1)}, bf16[512,128]{1,0:T(8,128)(2,1)S(1)}, u32[]{:S(2)}, u32[]{:S(2)}) collective-permute-start(bf16[512,128]{1,0:T(8,128)(2,1)S(1)} %reshape.33), channel_id=1, source_target_pairs={{0,12},{1,13},{2,14},{3,15},{4,8},{5,9},{6,10},{7,11},{8,4},{9,5},... | collective-permute-start | bytes 393224 | tf_op jit(solution)/shard_map/ppermute | solution.py:371
  7.3 13.0 %collective-permute-start.3 = (bf16[512,128]{1,0:T(8,128)(2,1)S(1)}, bf16[512,128]{1,0:T(8,128)(2,1)S(1)}, u32[]{:S(2)}, u32[]{:S(2)}) collective-permute-start(bf16[512,128]{1,0:T(8,128)(2,1)S(1)} %reshape.33), channel_id=1, source_target_pairs={{0,2},{1,3},{2,0},{3,1},{4,6},{5,7},{6,4},{7,5},{8,10},{9,11},{10,... | collective-permute-start | bytes 393224 | tf_op jit(solution)/shard_map/ppermute | solution.py:371
  20.4 9.9 %collective-permute-start.4 = (bf16[1536,128]{1,0:T(8,128)(2,1)S(1)}, bf16[1536,128]{1,0:T(8,128)(2,1)S(1)}, u32[]{:S(2)}, u32[]{:S(2)}) collective-permute-start(bf16[1536,128]{1,0:T(8,128)(2,1)S(1)} %slice.87), channel_id=1, source_target_pairs={{0,2},{1,3},{2,0},{3,1},{4,6},{5,7},{6,4},{7,5},{8,10},{9,11},{10,... | collective-permute-start | bytes 1179656 | tf_op jit(solution)/shard_map/ppermute | solution.py:371
  20.8 11.0 %collective-permute-start.5 = (bf16[2560,128]{1,0:T(8,128)(2,1)S(1)}, bf16[2560,128]{1,0:T(8,128)(2,1)S(1)}, u32[]{:S(2)}, u32[]{:S(2)}) collective-permute-start(bf16[2560,128]{1,0:T(8,128)(2,1)S(1)} %constant_dynamic-update-slice_fusion.refs_0_), channel_id=1, source_target_pairs={{0,1},{1,0},{2,3},{3,2},{4,5},{5,4},{6,7},{7,6},{8,9},{9,8},{10,11... | collective-permute-start | bytes 1966088 | tf_op jit(solution)/shard_map/ppermute | solution.py:371
  50.0 10.4 %collective-permute-start.12 = (bf16[320,128]{1,0:T(8,128)(2,1)S(1)}, bf16[320,128]{1,0:T(8,128)(2,1)S(1)}, u32[]{:S(2)}, u32[]{:S(2)}) collective-permute-start(bf16[320,128]{1,0:T(8,128)(2,1)S(1)} %get-tuple-element.60), channel_id=1, source_target_pairs={{0,2},{1,3},{2,0},{3,1},{4,6},{5,7},{6,4},{7,5},{8,10},{9,11},{10,... | collective-permute-start | bytes 245768 | tf_op jit(solution)/shard_map/ppermute | solution.py:371
  51.5 9.0 %collective-permute-start.13 = (bf16[320,128]{1,0:T(8,128)(2,1)S(1)}, bf16[320,128]{1,0:T(8,128)(2,1)S(1)}, u32[]{:S(2)}, u32[]{:S(2)}) collective-permute-start(bf16[320,128]{1,0:T(8,128)(2,1)S(1)} %get-tuple-element.63), channel_id=1, source_target_pairs={{0,10},{1,11},{2,8},{3,9},{4,14},{5,15},{6,12},{7,13},{8,2},{9,3},... | collective-permute-start | bytes 245768 | tf_op jit(solution)/shard_map/ppermute | solution.py:371
  53.2 8.1 %collective-permute-start.14 = (bf16[320,128]{1,0:T(8,128)(2,1)S(1)}, bf16[320,128]{1,0:T(8,128)(2,1)S(1)}, u32[]{:S(2)}, u32[]{:S(2)}) collective-permute-start(bf16[320,128]{1,0:T(8,128)(2,1)S(1)} %get-tuple-element.62), channel_id=1, source_target_pairs={{0,6},{1,7},{2,4},{3,5},{4,2},{5,3},{6,0},{7,1},{8,14},{9,15},{10,... | collective-permute-start | bytes 245768 | tf_op jit(solution)/shard_map/ppermute | solution.py:371
  56.6 8.1 %collective-permute-start.15 = (bf16[320,128]{1,0:T(8,128)(2,1)S(1)}, bf16[320,128]{1,0:T(8,128)(2,1)S(1)}, u32[]{:S(2)}, u32[]{:S(2)}) collective-permute-start(bf16[320,128]{1,0:T(8,128)(2,1)S(1)} %get-tuple-element.61), channel_id=1, source_target_pairs={{0,14},{1,15},{2,12},{3,13},{4,10},{5,11},{6,8},{7,9},{8,6},{9,7},... | collective-permute-start | bytes 245768 | tf_op jit(solution)/shard_map/ppermute | solution.py:371
  56.9 8.6 %collective-permute-start.10 = (bf16[320,128]{1,0:T(8,128)(2,1)S(1)}, bf16[320,128]{1,0:T(8,128)(2,1)S(1)}, u32[]{:S(2)}, u32[]{:S(2)}) collective-permute-start(bf16[320,128]{1,0:T(8,128)(2,1)S(1)} %get-tuple-element.58), channel_id=1, source_target_pairs={{0,12},{1,13},{2,14},{3,15},{4,8},{5,9},{6,10},{7,11},{8,4},{9,5},... | collective-permute-start | bytes 245768 | tf_op jit(solution)/shard_map/ppermute | solution.py:371
  60.5 8.7 %collective-permute-start.8 = (bf16[320,128]{1,0:T(8,128)(2,1)S(1)}, bf16[320,128]{1,0:T(8,128)(2,1)S(1)}, u32[]{:S(2)}, u32[]{:S(2)}) collective-permute-start(bf16[320,128]{1,0:T(8,128)(2,1)S(1)} %get-tuple-element.57), channel_id=1, source_target_pairs={{0,8},{1,9},{2,10},{3,11},{4,12},{5,13},{6,14},{7,15},{8,0},{9,1},... | collective-permute-start | bytes 245768 | tf_op jit(solution)/shard_map/ppermute | solution.py:371
  60.5 8.7 %collective-permute-start.9 = (bf16[320,128]{1,0:T(8,128)(2,1)S(1)}, bf16[320,128]{1,0:T(8,128)(2,1)S(1)}, u32[]{:S(2)}, u32[]{:S(2)}) collective-permute-start(bf16[320,128]{1,0:T(8,128)(2,1)S(1)} %get-tuple-element.59), channel_id=1, source_target_pairs={{0,4},{1,5},{2,6},{3,7},{4,0},{5,1},{6,2},{7,3},{8,12},{9,13},{10,... | collective-permute-start | bytes 245768 | tf_op jit(solution)/shard_map/ppermute | solution.py:371
  69.3 6.8 %collective-permute-start.16 = (bf16[320,128]{1,0:T(8,128)(2,1)S(1)}, bf16[320,128]{1,0:T(8,128)(2,1)S(1)}, u32[]{:S(2)}, u32[]{:S(2)}) collective-permute-start(bf16[320,128]{1,0:T(8,128)(2,1)S(1)} %get-tuple-element.44), channel_id=1, source_target_pairs={{0,8},{1,9},{2,10},{3,11},{4,12},{5,13},{6,14},{7,15},{8,0},{9,1},... | collective-permute-start | bytes 245768 | tf_op jit(solution)/shard_map/ppermute | solution.py:371
  69.5 6.7 %collective-permute-start.17 = (bf16[320,128]{1,0:T(8,128)(2,1)S(1)}, bf16[320,128]{1,0:T(8,128)(2,1)S(1)}, u32[]{:S(2)}, u32[]{:S(2)}) collective-permute-start(bf16[320,128]{1,0:T(8,128)(2,1)S(1)} %get-tuple-element.44), channel_id=1, source_target_pairs={{0,4},{1,5},{2,6},{3,7},{4,0},{5,1},{6,2},{7,3},{8,12},{9,13},{10,... | collective-permute-start | bytes 245768 | tf_op jit(solution)/shard_map/ppermute | solution.py:371
  72.5 6.3 %collective-permute-start.18 = (bf16[320,128]{1,0:T(8,128)(2,1)S(1)}, bf16[320,128]{1,0:T(8,128)(2,1)S(1)}, u32[]{:S(2)}, u32[]{:S(2)}) collective-permute-start(bf16[320,128]{1,0:T(8,128)(2,1)S(1)} %get-tuple-element.44), channel_id=1, source_target_pairs={{0,12},{1,13},{2,14},{3,15},{4,8},{5,9},{6,10},{7,11},{8,4},{9,5},... | collective-permute-start | bytes 245768 | tf_op jit(solution)/shard_map/ppermute | solution.py:371
  73.7 6.7 %collective-permute-start.19 = (bf16[320,128]{1,0:T(8,128)(2,1)S(1)}, bf16[320,128]{1,0:T(8,128)(2,1)S(1)}, u32[]{:S(2)}, u32[]{:S(2)}) collective-permute-start(bf16[320,128]{1,0:T(8,128)(2,1)S(1)} %get-tuple-element.44), channel_id=1, source_target_pairs={{0,2},{1,3},{2,0},{3,1},{4,6},{5,7},{6,4},{7,5},{8,10},{9,11},{10,... | collective-permute-start | bytes 245768 | tf_op jit(solution)/shard_map/ppermute | solution.py:371
  78.9 6.3 %collective-permute-start.20 = (bf16[960,128]{1,0:T(8,128)(2,1)S(1)}, bf16[960,128]{1,0:T(8,128)(2,1)S(1)}, u32[]{:S(2)}, u32[]{:S(2)}) collective-permute-start(bf16[960,128]{1,0:T(8,128)(2,1)S(1)} %pad_maximum_fusion), channel_id=1, source_target_pairs={{0,2},{1,3},{2,0},{3,1},{4,6},{5,7},{6,4},{7,5},{8,10},{9,11},{10,... | collective-permute-start | bytes 737288 | tf_op jit(solution)/shard_map/ppermute | solution.py:371
  104.0 8.3 %collective-permute-start.28 = (bf16[320,128]{1,0:T(8,128)(2,1)S(1)}, bf16[320,128]{1,0:T(8,128)(2,1)S(1)}, u32[]{:S(2)}, u32[]{:S(2)}) collective-permute-start(bf16[320,128]{1,0:T(8,128)(2,1)S(1)} %get-tuple-element.53), channel_id=1, source_target_pairs={{0,2},{1,3},{2,0},{3,1},{4,6},{5,7},{6,4},{7,5},{8,10},{9,11},{10,... | collective-permute-start | bytes 245768 | tf_op jit(solution)/shard_map/ppermute | solution.py:371
  105.4 8.5 %collective-permute-start.29 = (bf16[320,128]{1,0:T(8,128)(2,1)S(1)}, bf16[320,128]{1,0:T(8,128)(2,1)S(1)}, u32[]{:S(2)}, u32[]{:S(2)}) collective-permute-start(bf16[320,128]{1,0:T(8,128)(2,1)S(1)} %get-tuple-element.56), channel_id=1, source_target_pairs={{0,10},{1,11},{2,8},{3,9},{4,14},{5,15},{6,12},{7,13},{8,2},{9,3},... | collective-permute-start | bytes 245768 | tf_op jit(solution)/shard_map/ppermute | solution.py:371
  107.8 7.9 %collective-permute-start.30 = (bf16[320,128]{1,0:T(8,128)(2,1)S(1)}, bf16[320,128]{1,0:T(8,128)(2,1)S(1)}, u32[]{:S(2)}, u32[]{:S(2)}) collective-permute-start(bf16[320,128]{1,0:T(8,128)(2,1)S(1)} %get-tuple-element.55), channel_id=1, source_target_pairs={{0,6},{1,7},{2,4},{3,5},{4,2},{5,3},{6,0},{7,1},{8,14},{9,15},{10,... | collective-permute-start | bytes 245768 | tf_op jit(solution)/shard_map/ppermute | solution.py:371
  108.2 8.1 %collective-permute-start.31 = (bf16[320,128]{1,0:T(8,128)(2,1)S(1)}, bf16[320,128]{1,0:T(8,128)(2,1)S(1)}, u32[]{:S(2)}, u32[]{:S(2)}) collective-permute-start(bf16[320,128]{1,0:T(8,128)(2,1)S(1)} %get-tuple-element.54), channel_id=1, source_target_pairs={{0,14},{1,15},{2,12},{3,13},{4,10},{5,11},{6,8},{7,9},{8,6},{9,7},... | collective-permute-start | bytes 245768 | tf_op jit(solution)/shard_map/ppermute | solution.py:371
  110.8 11.2 %collective-permute-start.24 = (bf16[320,128]{1,0:T(8,128)(2,1)S(1)}, bf16[320,128]{1,0:T(8,128)(2,1)S(1)}, u32[]{:S(2)}, u32[]{:S(2)}) collective-permute-start(bf16[320,128]{1,0:T(8,128)(2,1)S(1)} %get-tuple-element.50), channel_id=1, source_target_pairs={{0,8},{1,9},{2,10},{3,11},{4,12},{5,13},{6,14},{7,15},{8,0},{9,1},... | collective-permute-start | bytes 245768 | tf_op jit(solution)/shard_map/ppermute | solution.py:371
  112.3 9.7 %collective-permute-start.25 = (bf16[320,128]{1,0:T(8,128)(2,1)S(1)}, bf16[320,128]{1,0:T(8,128)(2,1)S(1)}, u32[]{:S(2)}, u32[]{:S(2)}) collective-permute-start(bf16[320,128]{1,0:T(8,128)(2,1)S(1)} %get-tuple-element.52), channel_id=1, source_target_pairs={{0,4},{1,5},{2,6},{3,7},{4,0},{5,1},{6,2},{7,3},{8,12},{9,13},{10,... | collective-permute-start | bytes 245768 | tf_op jit(solution)/shard_map/ppermute | solution.py:371
  114.0 8.0 %collective-permute-start.26 = (bf16[320,128]{1,0:T(8,128)(2,1)S(1)}, bf16[320,128]{1,0:T(8,128)(2,1)S(1)}, u32[]{:S(2)}, u32[]{:S(2)}) collective-permute-start(bf16[320,128]{1,0:T(8,128)(2,1)S(1)} %get-tuple-element.51), channel_id=1, source_target_pairs={{0,12},{1,13},{2,14},{3,15},{4,8},{5,9},{6,10},{7,11},{8,4},{9,5},... | collective-permute-start | bytes 245768 | tf_op jit(solution)/shard_map/ppermute | solution.py:371
  122.2 5.6 %collective-permute-start.32 = (bf16[320,128]{1,0:T(8,128)(2,1)S(1)}, bf16[320,128]{1,0:T(8,128)(2,1)S(1)}, u32[]{:S(2)}, u32[]{:S(2)}) collective-permute-start(bf16[320,128]{1,0:T(8,128)(2,1)S(1)} %get-tuple-element.40), channel_id=1, source_target_pairs={{0,8},{1,9},{2,10},{3,11},{4,12},{5,13},{6,14},{7,15},{8,0},{9,1},... | collective-permute-start | bytes 245768 | tf_op jit(solution)/shard_map/ppermute | solution.py:371
  124.6 6.6 %collective-permute-start.34 = (bf16[320,128]{1,0:T(8,128)(2,1)S(1)}, bf16[320,128]{1,0:T(8,128)(2,1)S(1)}, u32[]{:S(2)}, u32[]{:S(2)}) collective-permute-start(bf16[320,128]{1,0:T(8,128)(2,1)S(1)} %get-tuple-element.40), channel_id=1, source_target_pairs={{0,12},{1,13},{2,14},{3,15},{4,8},{5,9},{6,10},{7,11},{8,4},{9,5},... | collective-permute-start | bytes 245768 | tf_op jit(solution)/shard_map/ppermute | solution.py:371
  126.6 6.6 %collective-permute-start.35 = (bf16[320,128]{1,0:T(8,128)(2,1)S(1)}, bf16[320,128]{1,0:T(8,128)(2,1)S(1)}, u32[]{:S(2)}, u32[]{:S(2)}) collective-permute-start(bf16[320,128]{1,0:T(8,128)(2,1)S(1)} %get-tuple-element.40), channel_id=1, source_target_pairs={{0,2},{1,3},{2,0},{3,1},{4,6},{5,7},{6,4},{7,5},{8,10},{9,11},{10,... | collective-permute-start | bytes 245768 | tf_op jit(solution)/shard_map/ppermute | solution.py:371
  131.2 6.5 %collective-permute-start.36 = (bf16[960,128]{1,0:T(8,128)(2,1)S(1)}, bf16[960,128]{1,0:T(8,128)(2,1)S(1)}, u32[]{:S(2)}, u32[]{:S(2)}) collective-permute-start(bf16[960,128]{1,0:T(8,128)(2,1)S(1)} %pad_maximum_fusion.1), channel_id=1, source_target_pairs={{0,2},{1,3},{2,0},{3,1},{4,6},{5,7},{6,4},{7,5},{8,10},{9,11},{10,... | collective-permute-start | bytes 737288 | tf_op jit(solution)/shard_map/ppermute | solution.py:371
  157.1 9.2 %collective-permute-start.41 = (bf16[2048,128]{1,0:T(8,128)(2,1)S(1)}, bf16[2048,128]{1,0:T(8,128)(2,1)S(1)}, u32[]{:S(2)}, u32[]{:S(2)}) collective-permute-start(bf16[2048,128]{1,0:T(8,128)(2,1)S(1)} %add_convert_fusion), channel_id=1, source_target_pairs={{0,2},{1,5},{2,0},{3,7},{4,6},{5,1},{6,4},{7,3},{8,10},{9,13},{10,... | collective-permute-start | bytes 1572872 | tf_op jit(solution)/shard_map/ppermute | solution.py:371
  166.5 9.3 %collective-permute-start.42 = (bf16[1024,128]{1,0:T(8,128)(2,1)S(1)}, bf16[1024,128]{1,0:T(8,128)(2,1)S(1)}, u32[]{:S(2)}, u32[]{:S(2)}) collective-permute-start(bf16[1024,128]{1,0:T(8,128)(2,1)S(1)} %slice.184), channel_id=1, source_target_pairs={{0,4},{1,9},{2,6},{3,11},{4,0},{5,13},{6,2},{7,15},{8,12},{9,1},{1... | collective-permute-start | bytes 786440 | tf_op jit(solution)/shard_map/ppermute | solution.py:371
  175.9 7.3 %collective-permute-start.43 = (bf16[512,128]{1,0:T(8,128)(2,1)S(1)}, bf16[512,128]{1,0:T(8,128)(2,1)S(1)}, u32[]{:S(2)}, u32[]{:S(2)}) collective-permute-start(bf16[512,128]{1,0:T(8,128)(2,1)S(1)} %slice.185), channel_id=1, source_target_pairs={{0,8},{1,3},{2,10},{3,1},{4,12},{5,7},{6,14},{7,5},{8,0},{9,11},{1... | collective-permute-start | bytes 393224 | tf_op jit(solution)/shard_map/ppermute | solution.py:371
  (13 other events, 34.4 us)

commit v10 on v9

--- a/solution.py
+++ b/solution.py
@@ -19,6 +19,7 @@
 ROW_TILE = 16
 SUPPORT_PARTS = 2
 SUPPORT_STEP = 4
+SUPPORT_AHEAD = 3
 PIECE = 5
 MATRIX_UNIT = 256
 VMEM_MARGIN = 3 * 1024 * 1024
@@ -79,15 +80,22 @@
         _, group, live = group_at(index, seq, order, counts)
 
         def start_slot(slot, carry):
-            block = support[group, slot]
-            ids[offset + slot] = block
-            fetch(offset + slot, block).start()
+            ids[offset + slot] = support[group, slot]
             return carry
 
         lax.fori_loop(jnp.clip(-offset, 0, live), jnp.clip(entries - offset, 0, live), start_slot, 0)
         return offset + live
 
     lax.fori_loop(0, groups, start_group, jnp.int32(-begin))
+    steps = pairs // SUPPORT_STEP
+
+    def start_step(step):
+        for entry in range(2 * SUPPORT_STEP):
+            index = 2 * SUPPORT_STEP * step + entry
+            fetch(index, ids[index]).start()
+
+    for step in range(min(SUPPORT_AHEAD, steps)):
+        start_step(step)
     shape = (2 * LANES, LANES)
     source = lax.broadcasted_iota(jnp.int32, shape, 0)
     target = lax.broadcasted_iota(jnp.int32, shape, 1)
@@ -99,6 +107,10 @@
         return pltpu.make_async_copy(held.at[2 * pair], out.at[begin // 2 + pair], out_sems.at[pair])
 
     def pack(step, carry):
+        @pl.when(step + SUPPORT_AHEAD < steps)
+        def _():
+            start_step(step + SUPPORT_AHEAD)
+
         span = [SUPPORT_STEP * step + pair for pair in range(SUPPORT_STEP)]
         for pair in span:
             fetch(2 * pair, ids[2 * pair]).wait()
@@ -113,7 +125,7 @@
             store(pair).start()
         return carry
 
-    lax.fori_loop(0, pairs // SUPPORT_STEP, pack, 0)
+    lax.fori_loop(0, steps, pack, 0)
 
     def drain(pair, carry):
         store(pair).wait()
@@ -270,7 +282,7 @@
             write_packed(limits, [thresh[group]] * count, offset)
         matrix = jnp.concatenate([held[first + pair] for pair in range(count)], axis=1)
         point = jnp.concatenate(parts, axis=1)
-        residual = lax.dot_general(matrix, point, (((1,), (1,)), ((), ())), preferred_element_type=jnp.float32).T
+        residual = lax.dot_general(point, matrix, (((1,), (1,)), ((), ())), preferred_element_type=jnp.float32)
         target = targets[tile(group), :].astype(jnp.float32)
         residual = (residual - target).astype(jnp.bfloat16)
         gradient = jnp.dot(residual, matrix, preferred_element_type=jnp.float32)
@@ -393,15 +405,15 @@
 
 def reduce_shards(keep, *send):
     devices = lax.axis_size("rows")
-    distances = stage_distances(devices)
-    quarters = add_cores(keep, *send)
-    size = 2 * keep.shape[0] // devices
-    sent = [quarter.astype(jnp.bfloat16) for quarter in quarters]
-    total = quarters[0][:size]
-    for slot in range(1, devices // 2):
-        begin = slot % (devices // 4) * size
-        share = sent[slot // (devices // 4)][begin : begin + size]
-        total = total + exchange(share, slot_distance(slot, distances[1:])).astype(jnp.float32)
+    _, row, *columns = stage_distances(devices)
+    near, other = add_cores(keep, *send)
+    size = near.shape[0] // (devices // 4)
+    sums = near[size:] + exchange(other[size:].astype(jnp.bfloat16), row).astype(jnp.float32)
+    last, sums = lax.optimization_barrier((other[:size].astype(jnp.bfloat16), sums.astype(jnp.bfloat16)))
+    total = near[:size] + exchange(last, row).astype(jnp.float32)
+    for slot in range(1, devices // 4):
+        share = exchange(sums[(slot - 1) * size : slot * size], slot_distance(slot, columns))
+        total = total + share.astype(jnp.float32)
     return total
 
 

time: 185 us -> 172 us (0.930)
  Pallas kernels: 63.4 us -> 53.4 us
  starting transfers between devices: 52 us -> 46.9 us
  waiting for transfers between devices: 60.2 us -> 62.3 us
    pallas_call x3, Pallas kernels: 46.2 us -> 34.1 us  [gradient_call(): pl.pallas_call(functools.partial(gradient_kernel, mode, shards, pairs, gr...]
    ppermute x44 -> x40, starting transfers between devices: 52 us -> 46.9 us  [exchange(): lax.ppermute(value, 'rows', [(i, i ^ apart[i % 2]) for i in range(devices)])]
    ppermute x44 -> x40, waiting for transfers between devices: 60.2 us -> 62.3 us  [exchange(): lax.ppermute(value, 'rows', [(i, i ^ apart[i % 2]) for i in range(devices)])]
    pallas_call x2, Pallas kernels: 17.3 us -> 19.3 us  [collect_support(): pl.pallas_call(functools.partial(support_kernel, part * entries, groups),...]
  transfers between devices with their start and end apart: 44 -> 40, of which waited for: 26 -> 22; matrix products, arithmetic and copies ran while one was open for 2% -> 3% of each run, Pallas kernels for 9% -> 11%
where the time goes in v10:
time: 172 us
  waiting for transfers between devices  62.3 us (36%)
  Pallas kernels  53.4 us (31%)
  starting transfers between devices  46.9 us (27%)
  local copies, waits for them, and re-layouts  6.44 us (4%)
  other arithmetic  2.24 us (1%)
    ppermute x40, waiting for transfers between devices, exchange(): lax.ppermute(value, 'rows', [(i, i ^ apart[i % 2]) for i in range(devices)])  62.3 us
    ppermute x40, starting transfers between devices, exchange(): lax.ppermute(value, 'rows', [(i, i ^ apart[i % 2]) for i in range(devices)])  46.9 us
    pallas_call x3, Pallas kernels, gradient_call(): pl.pallas_call(functools.partial(gradient_kernel, mode, shards, pairs, gr...  34.1 us
    pallas_call x2, Pallas kernels, collect_support(): pl.pallas_call(functools.partial(support_kernel, part * entries, groups),...  19.3 us
  transfers between devices with their start and end apart: 40, of which 22 were waited for; matrix products, arithmetic and copies ran while one was open for 3% of the time, Pallas kernels for 11%

profile of v10, /device:TPU:0, one launch (start us, length us, event | category | flops | bytes accessed | tf_op | source)
XLA Modules:
  0.0 171.8 jit_solution(2092889873043833713)
XLA Ops:
  1.6 4.1 %collective-permute-start = (bf16[512,128]{1,0:T(8,128)(2,1)S(1)}, bf16[512,128]{1,0:T(8,128)(2,1)S(1)}, u32[]{:S(2)}, u32[]{:S(2)}) collective-permute-start(bf16[512,128]{1,0:T(8,128)(2,1)S(1)} %reshape.33), channel_id=1, source_target_pairs={{0,8},{1,9},{2,10},{3,11},{4,12},{5,13},{6,14},{7,15},{8,0},{9,1},... | collective-permute-start | bytes 393224 | tf_op jit(solution)/shard_map/ppermute | solution.py:383
  7.3 1.7 %collective-permute-start.3 = (bf16[512,128]{1,0:T(8,128)(2,1)S(1)}, bf16[512,128]{1,0:T(8,128)(2,1)S(1)}, u32[]{:S(2)}, u32[]{:S(2)}) collective-permute-start(bf16[512,128]{1,0:T(8,128)(2,1)S(1)} %reshape.33), channel_id=1, source_target_pairs={{0,2},{1,3},{2,0},{3,1},{4,6},{5,7},{6,4},{7,5},{8,10},{9,11},{10,... | collective-permute-start | bytes 393224 | tf_op jit(solution)/shard_map/ppermute | solution.py:383
  11.7 9.7 %collect_support.2.refs_0_ = bf16[520,512,128]{2,1,0:T(8,128)(2,1)} custom-call(s32[305]{0:T(512)S(1)} %concatenate.18.scalars, bf16[512,32768]{1,0:T(8,128)(2,1)} %dictionary.3), custom_call_target="tpu_custom_call" | custom-call | bytes 31457280 | tf_op jit(solution)/shard_map/collect_support/pallas_call | solution.py:141
  21.9 9.6 %collect_support.3.blocks = bf16[520,512,128]{2,1,0:T(8,128)(2,1)} custom-call(s32[305]{0:T(512)S(1)} %concatenate.18.scalars, bf16[512,32768]{1,0:T(8,128)(2,1)} %dictionary.3, bf16[520,512,128]{2,1,0:T(8,128)(2,1)} %collect_support.2.refs_0_), custom_call_target="tpu_custom_call", output_to_operand_aliasing={{}: (2, {})} | custom-call | bytes 31457280 | tf_op jit(solution)/shard_map/collect_support/pallas_call | solution.py:141
  33.9 11.2 %gradient.3 = (f32[2560,128]{1,0:T(8,128)S(1)}, bf16[1280,128]{1,0:T(8,128)(2,1)S(1)}, bf16[1280,128]{1,0:T(8,128)(2,1)S(1)}, bf16[320,128]{1,0:T(8,128)(2,1)S(1)}, f32[320,128]{1,0:T(8,128)S(1)}) custom-call(s32[305]{0:T(512)S(1)} %concatenate.18.scalars, bf16[520,512,128]{2,1,0:T(8,128)(2,1)} %collect_support.3.blocks, ...), custom_call_target="tpu_custom_call" | custom-call | flops 5368709120 | bytes 10485760 | tf_op jit(solution)/shard_map/gradient/pallas_call | solution.py:360
  47.4 1.8 %collective-permute-start.9 = (bf16[960,128]{1,0:T(8,128)(2,1)S(1)}, bf16[960,128]{1,0:T(8,128)(2,1)S(1)}, u32[]{:S(2)}, u32[]{:S(2)}) collective-permute-start(bf16[960,128]{1,0:T(8,128)(2,1)S(1)} %slice.113), channel_id=1, source_target_pairs={{0,2},{1,3},{2,0},{3,1},{4,6},{5,7},{6,4},{7,5},{8,10},{9,11},{10,... | collective-permute-start | bytes 737288 | tf_op jit(solution)/shard_map/ppermute | solution.py:383
  49.2 6.3 %collective-permute-done.9 = bf16[960,128]{1,0:T(8,128)(2,1)S(1)} collective-permute-done((bf16[960,128]{1,0:T(8,128)(2,1)S(1)}, bf16[960,128]{1,0:T(8,128)(2,1)S(1)}, u32[]{:S(2)}, u32[]{:S(2)}) %collective-permute-start.9) | collective-permute-done | bytes 245792 | tf_op jit(solution)/shard_map/ppermute | solution.py:383
  55.6 2.0 %collective-permute-start.11 = (bf16[320,128]{1,0:T(8,128)(2,1)S(1)}, bf16[320,128]{1,0:T(8,128)(2,1)S(1)}, u32[]{:S(2)}, u32[]{:S(2)}) collective-permute-start(bf16[320,128]{1,0:T(8,128)(2,1)S(1)} %get-tuple-element.58), channel_id=1, source_target_pairs={{0,8},{1,9},{2,10},{3,11},{4,12},{5,13},{6,14},{7,15},{8,0},{9,1},... | collective-permute-start | bytes 245768 | tf_op jit(solution)/shard_map/ppermute | solution.py:383
  57.6 2.5 %collective-permute-start.12 = (bf16[320,128]{1,0:T(8,128)(2,1)S(1)}, bf16[320,128]{1,0:T(8,128)(2,1)S(1)}, u32[]{:S(2)}, u32[]{:S(2)}) collective-permute-start(bf16[320,128]{1,0:T(8,128)(2,1)S(1)} %get-tuple-element.60), channel_id=1, source_target_pairs={{0,4},{1,5},{2,6},{3,7},{4,0},{5,1},{6,2},{7,3},{8,12},{9,13},{10,... | collective-permute-start | bytes 245768 | tf_op jit(solution)/shard_map/ppermute | solution.py:383
  60.1 1.7 collective-permute-start.10
  62.7 3.6 %collective-permute-done.13 = bf16[320,128]{1,0:T(8,128)(2,1)S(1)} collective-permute-done((bf16[320,128]{1,0:T(8,128)(2,1)S(1)}, bf16[320,128]{1,0:T(8,128)(2,1)S(1)}, u32[]{:S(2)}, u32[]{:S(2)}) %collective-permute-start.13) | collective-permute-done | bytes 81952 | tf_op jit(solution)/shard_map/ppermute | solution.py:383
  69.1 1.8 %collective-permute-start.16 = (bf16[320,128]{1,0:T(8,128)(2,1)S(1)}, bf16[320,128]{1,0:T(8,128)(2,1)S(1)}, u32[]{:S(2)}, u32[]{:S(2)}) collective-permute-start(bf16[320,128]{1,0:T(8,128)(2,1)S(1)} %get-tuple-element.50), channel_id=1, source_target_pairs={{0,12},{1,13},{2,14},{3,15},{4,8},{5,9},{6,10},{7,11},{8,4},{9,5},... | collective-permute-start | bytes 245768 | tf_op jit(solution)/shard_map/ppermute | solution.py:383
  73.6 1.7 collective-permute-done.16
  75.3 1.6 collective-permute-start.18
  77.1 4.5 %collective-permute-done.18.refs_1_ = bf16[960,128]{1,0:T(8,128)(2,1)S(1)} collective-permute-done((bf16[960,128]{1,0:T(8,128)(2,1)S(1)}, bf16[960,128]{1,0:T(8,128)(2,1)S(1)}, u32[]{:S(2)}, u32[]{:S(2)}) %collective-permute-start.18) | collective-permute-done | bytes 245792 | tf_op jit(solution)/shard_map/ppermute | solution.py:383
  83.1 10.9 %gradient.4 = (f32[2560,128]{1,0:T(8,128)S(1)}, bf16[1280,128]{1,0:T(8,128)(2,1)S(1)}, bf16[1280,128]{1,0:T(8,128)(2,1)S(1)}) custom-call(s32[305]{0:T(512)S(1)} %concatenate.18.scalars, bf16[520,512,128]{2,1,0:T(8,128)(2,1)} %collect_support.3.blocks, bf16[1600,128]{1,0:T(8,128)(2,1)S(1)} %constant_dynamic-update-slice_fusion.5.refs_0_, ...), custom_call_target="tpu_custom_call" | custom-call | flops 5368709120 | bytes 10485760 | tf_op jit(solution)/shard_map/gradient/pallas_call | solution.py:360
  96.3 1.6 collective-permute-start.23
  97.9 6.5 %collective-permute-done.23 = bf16[960,128]{1,0:T(8,128)(2,1)S(1)} collective-permute-done((bf16[960,128]{1,0:T(8,128)(2,1)S(1)}, bf16[960,128]{1,0:T(8,128)(2,1)S(1)}, u32[]{:S(2)}, u32[]{:S(2)}) %collective-permute-start.23) | collective-permute-done | bytes 245792 | tf_op jit(solution)/shard_map/ppermute | solution.py:383
  107.0 1.9 %collective-permute-start.27 = (bf16[320,128]{1,0:T(8,128)(2,1)S(1)}, bf16[320,128]{1,0:T(8,128)(2,1)S(1)}, u32[]{:S(2)}, u32[]{:S(2)}) collective-permute-start(bf16[320,128]{1,0:T(8,128)(2,1)S(1)} %get-tuple-element.56), channel_id=1, source_target_pairs={{0,12},{1,13},{2,14},{3,15},{4,8},{5,9},{6,10},{7,11},{8,4},{9,5},... | collective-permute-start | bytes 245768 | tf_op jit(solution)/shard_map/ppermute | solution.py:383
  110.4 3.0 %collective-permute-done.25 = bf16[320,128]{1,0:T(8,128)(2,1)S(1)} collective-permute-done((bf16[320,128]{1,0:T(8,128)(2,1)S(1)}, bf16[320,128]{1,0:T(8,128)(2,1)S(1)}, u32[]{:S(2)}, u32[]{:S(2)}) %collective-permute-start.25) | collective-permute-done | bytes 81952 | tf_op jit(solution)/shard_map/ppermute | solution.py:383
  113.6 2.0 %collective-permute-start.28 = (bf16[320,128]{1,0:T(8,128)(2,1)S(1)}, bf16[320,128]{1,0:T(8,128)(2,1)S(1)}, u32[]{:S(2)}, u32[]{:S(2)}) collective-permute-start(bf16[320,128]{1,0:T(8,128)(2,1)S(1)} %get-tuple-element.48), channel_id=1, source_target_pairs={{0,8},{1,9},{2,10},{3,11},{4,12},{5,13},{6,14},{7,15},{8,0},{9,1},... | collective-permute-start | bytes 245768 | tf_op jit(solution)/shard_map/ppermute | solution.py:383
  116.2 1.9 %collective-permute-start.30 = (bf16[320,128]{1,0:T(8,128)(2,1)S(1)}, bf16[320,128]{1,0:T(8,128)(2,1)S(1)}, u32[]{:S(2)}, u32[]{:S(2)}) collective-permute-start(bf16[320,128]{1,0:T(8,128)(2,1)S(1)} %get-tuple-element.48), channel_id=1, source_target_pairs={{0,12},{1,13},{2,14},{3,15},{4,8},{5,9},{6,10},{7,11},{8,4},{9,5},... | collective-permute-start | bytes 245768 | tf_op jit(solution)/shard_map/ppermute | solution.py:383
  119.6 1.8 %collective-permute-done.28 = bf16[320,128]{1,0:T(8,128)(2,1)S(1)} collective-permute-done((bf16[320,128]{1,0:T(8,128)(2,1)S(1)}, bf16[320,128]{1,0:T(8,128)(2,1)S(1)}, u32[]{:S(2)}, u32[]{:S(2)}) %collective-permute-start.28) | collective-permute-done | bytes 81952 | tf_op jit(solution)/shard_map/ppermute | solution.py:383
  122.7 1.7 collective-permute-start.32
  124.5 4.4 %collective-permute-done.32.refs_1_ = bf16[960,128]{1,0:T(8,128)(2,1)S(1)} collective-permute-done((bf16[960,128]{1,0:T(8,128)(2,1)S(1)}, bf16[960,128]{1,0:T(8,128)(2,1)S(1)}, u32[]{:S(2)}, u32[]{:S(2)}) %collective-permute-start.32) | collective-permute-done | bytes 245792 | tf_op jit(solution)/shard_map/ppermute | solution.py:383
  130.4 12.1 %gradient.5 = (f32[4096,128]{1,0:T(8,128)S(1)}, bf16[2048,128]{1,0:T(8,128)(2,1)S(1)}, bf16[2048,128]{1,0:T(8,128)(2,1)S(1)}, bf16[8,64,128]{2,1,0:T(8,128)(2,1)S(1)}, f32[64,128]{1,0:T(8,128)S(1)}) custom-call(s32[305]{0:T(512)S(1)} %concatenate.18.scalars, bf16[520,512,128]{2,1,0:T(8,128)(2,1)} %collect_support.3.blocks, ...), custom_call_target="tpu_custom_call" | custom-call | flops 5368709120 | bytes 10485760 | tf_op jit(solution)/shard_map/gradient/pallas_call | solution.py:360
  144.6 1.7 collective-permute-start.37
  146.3 7.6 %collective-permute-done.37 = bf16[2048,128]{1,0:T(8,128)(2,1)S(1)} collective-permute-done((bf16[2048,128]{1,0:T(8,128)(2,1)S(1)}, bf16[2048,128]{1,0:T(8,128)(2,1)S(1)}, u32[]{:S(2)}, u32[]{:S(2)}) %collective-permute-start.37) | collective-permute-done | bytes 524320 | tf_op jit(solution)/shard_map/ppermute | solution.py:383
  154.1 2.5 %collective-permute-start.38 = (bf16[1024,128]{1,0:T(8,128)(2,1)S(1)}, bf16[1024,128]{1,0:T(8,128)(2,1)S(1)}, u32[]{:S(2)}, u32[]{:S(2)}) collective-permute-start(bf16[1024,128]{1,0:T(8,128)(2,1)S(1)} %slice.170), channel_id=1, source_target_pairs={{0,4},{1,9},{2,6},{3,11},{4,0},{5,13},{6,2},{7,15},{8,12},{9,1},{1... | collective-permute-start | bytes 786440 | tf_op jit(solution)/shard_map/ppermute | solution.py:383
  156.6 6.7 %collective-permute-done.38 = bf16[1024,128]{1,0:T(8,128)(2,1)S(1)} collective-permute-done((bf16[1024,128]{1,0:T(8,128)(2,1)S(1)}, bf16[1024,128]{1,0:T(8,128)(2,1)S(1)}, u32[]{:S(2)}, u32[]{:S(2)}) %collective-permute-start.38) | collective-permute-done | bytes 262176 | tf_op jit(solution)/shard_map/ppermute | solution.py:383
  163.3 1.8 %collective-permute-start.39 = (bf16[512,128]{1,0:T(8,128)(2,1)S(1)}, bf16[512,128]{1,0:T(8,128)(2,1)S(1)}, u32[]{:S(2)}, u32[]{:S(2)}) collective-permute-start(bf16[512,128]{1,0:T(8,128)(2,1)S(1)} %slice.171), channel_id=1, source_target_pairs={{0,8},{1,3},{2,10},{3,1},{4,12},{5,7},{6,14},{7,5},{8,0},{9,11},{1... | collective-permute-start | bytes 393224 | tf_op jit(solution)/shard_map/ppermute | solution.py:383
  165.2 5.3 %collective-permute-done.39 = bf16[512,128]{1,0:T(8,128)(2,1)S(1)} collective-permute-done((bf16[512,128]{1,0:T(8,128)(2,1)S(1)}, bf16[512,128]{1,0:T(8,128)(2,1)S(1)}, u32[]{:S(2)}, u32[]{:S(2)}) %collective-permute-start.39) | collective-permute-done | bytes 131104 | tf_op jit(solution)/shard_map/ppermute | solution.py:383
  (105 shorter events, 34.5 us)
Async XLA Ops:
  1.6 19.8 %collective-permute-start = (bf16[512,128]{1,0:T(8,128)(2,1)S(1)}, bf16[512,128]{1,0:T(8,128)(2,1)S(1)}, u32[]{:S(2)}, u32[]{:S(2)}) collective-permute-start(bf16[512,128]{1,0:T(8,128)(2,1)S(1)} %reshape.33), channel_id=1, source_target_pairs={{0,8},{1,9},{2,10},{3,11},{4,12},{5,13},{6,14},{7,15},{8,0},{9,1},... | collective-permute-start | bytes 393224 | tf_op jit(solution)/shard_map/ppermute | solution.py:383
  5.7 15.7 %collective-permute-start.1 = (bf16[512,128]{1,0:T(8,128)(2,1)S(1)}, bf16[512,128]{1,0:T(8,128)(2,1)S(1)}, u32[]{:S(2)}, u32[]{:S(2)}) collective-permute-start(bf16[512,128]{1,0:T(8,128)(2,1)S(1)} %reshape.33), channel_id=1, source_target_pairs={{0,4},{1,5},{2,6},{3,7},{4,0},{5,1},{6,2},{7,3},{8,12},{9,13},{10,... | collective-permute-start | bytes 393224 | tf_op jit(solution)/shard_map/ppermute | solution.py:383
  7.3 14.2 %collective-permute-start.2 = (bf16[512,128]{1,0:T(8,128)(2,1)S(1)}, bf16[512,128]{1,0:T(8,128)(2,1)S(1)}, u32[]{:S(2)}, u32[]{:S(2)}) collective-permute-start(bf16[512,128]{1,0:T(8,128)(2,1)S(1)} %reshape.33), channel_id=1, source_target_pairs={{0,12},{1,13},{2,14},{3,15},{4,8},{5,9},{6,10},{7,11},{8,4},{9,5},... | collective-permute-start | bytes 393224 | tf_op jit(solution)/shard_map/ppermute | solution.py:383
  7.3 14.2 %collective-permute-start.3 = (bf16[512,128]{1,0:T(8,128)(2,1)S(1)}, bf16[512,128]{1,0:T(8,128)(2,1)S(1)}, u32[]{:S(2)}, u32[]{:S(2)}) collective-permute-start(bf16[512,128]{1,0:T(8,128)(2,1)S(1)} %reshape.33), channel_id=1, source_target_pairs={{0,2},{1,3},{2,0},{3,1},{4,6},{5,7},{6,4},{7,5},{8,10},{9,11},{10,... | collective-permute-start | bytes 393224 | tf_op jit(solution)/shard_map/ppermute | solution.py:383
  21.6 10.0 %collective-permute-start.4 = (bf16[1536,128]{1,0:T(8,128)(2,1)S(1)}, bf16[1536,128]{1,0:T(8,128)(2,1)S(1)}, u32[]{:S(2)}, u32[]{:S(2)}) collective-permute-start(bf16[1536,128]{1,0:T(8,128)(2,1)S(1)} %slice.85), channel_id=1, source_target_pairs={{0,2},{1,3},{2,0},{3,1},{4,6},{5,7},{6,4},{7,5},{8,10},{9,11},{10,... | collective-permute-start | bytes 1179656 | tf_op jit(solution)/shard_map/ppermute | solution.py:383
  21.9 11.8 %collective-permute-start.5 = (bf16[2560,128]{1,0:T(8,128)(2,1)S(1)}, bf16[2560,128]{1,0:T(8,128)(2,1)S(1)}, u32[]{:S(2)}, u32[]{:S(2)}) collective-permute-start(bf16[2560,128]{1,0:T(8,128)(2,1)S(1)} %constant_dynamic-update-slice_fusion.refs_0_), channel_id=1, source_target_pairs={{0,1},{1,0},{2,3},{3,2},{4,5},{5,4},{6,7},{7,6},{8,9},{9,8},{10,11... | collective-permute-start | bytes 1966088 | tf_op jit(solution)/shard_map/ppermute | solution.py:383
  47.4 8.1 %collective-permute-start.9 = (bf16[960,128]{1,0:T(8,128)(2,1)S(1)}, bf16[960,128]{1,0:T(8,128)(2,1)S(1)}, u32[]{:S(2)}, u32[]{:S(2)}) collective-permute-start(bf16[960,128]{1,0:T(8,128)(2,1)S(1)} %slice.113), channel_id=1, source_target_pairs={{0,2},{1,3},{2,0},{3,1},{4,6},{5,7},{6,4},{7,5},{8,10},{9,11},{10,... | collective-permute-start | bytes 737288 | tf_op jit(solution)/shard_map/ppermute | solution.py:383
  55.6 7.1 %collective-permute-start.11 = (bf16[320,128]{1,0:T(8,128)(2,1)S(1)}, bf16[320,128]{1,0:T(8,128)(2,1)S(1)}, u32[]{:S(2)}, u32[]{:S(2)}) collective-permute-start(bf16[320,128]{1,0:T(8,128)(2,1)S(1)} %get-tuple-element.58), channel_id=1, source_target_pairs={{0,8},{1,9},{2,10},{3,11},{4,12},{5,13},{6,14},{7,15},{8,0},{9,1},... | collective-permute-start | bytes 245768 | tf_op jit(solution)/shard_map/ppermute | solution.py:383
  57.6 5.1 %collective-permute-start.12 = (bf16[320,128]{1,0:T(8,128)(2,1)S(1)}, bf16[320,128]{1,0:T(8,128)(2,1)S(1)}, u32[]{:S(2)}, u32[]{:S(2)}) collective-permute-start(bf16[320,128]{1,0:T(8,128)(2,1)S(1)} %get-tuple-element.60), channel_id=1, source_target_pairs={{0,4},{1,5},{2,6},{3,7},{4,0},{5,1},{6,2},{7,3},{8,12},{9,13},{10,... | collective-permute-start | bytes 245768 | tf_op jit(solution)/shard_map/ppermute | solution.py:383
  60.1 6.2 %collective-permute-start.13 = (bf16[320,128]{1,0:T(8,128)(2,1)S(1)}, bf16[320,128]{1,0:T(8,128)(2,1)S(1)}, u32[]{:S(2)}, u32[]{:S(2)}) collective-permute-start(bf16[320,128]{1,0:T(8,128)(2,1)S(1)} %get-tuple-element.59), channel_id=1, source_target_pairs={{0,12},{1,13},{2,14},{3,15},{4,8},{5,9},{6,10},{7,11},{8,4},{9,5},... | collective-permute-start | bytes 245768 | tf_op jit(solution)/shard_map/ppermute | solution.py:383
  60.1 6.2 %collective-permute-start.10 = (bf16[320,128]{1,0:T(8,128)(2,1)S(1)}, bf16[320,128]{1,0:T(8,128)(2,1)S(1)}, u32[]{:S(2)}, u32[]{:S(2)}) collective-permute-start(bf16[320,128]{1,0:T(8,128)(2,1)S(1)} %slice.111), channel_id=1, source_target_pairs={{0,2},{1,3},{2,0},{3,1},{4,6},{5,7},{6,4},{7,5},{8,10},{9,11},{10,... | collective-permute-start | bytes 245768 | tf_op jit(solution)/shard_map/ppermute | solution.py:383
  66.4 7.1 %collective-permute-start.14 = (bf16[320,128]{1,0:T(8,128)(2,1)S(1)}, bf16[320,128]{1,0:T(8,128)(2,1)S(1)}, u32[]{:S(2)}, u32[]{:S(2)}) collective-permute-start(bf16[320,128]{1,0:T(8,128)(2,1)S(1)} %get-tuple-element.50), channel_id=1, source_target_pairs={{0,8},{1,9},{2,10},{3,11},{4,12},{5,13},{6,14},{7,15},{8,0},{9,1},... | collective-permute-start | bytes 245768 | tf_op jit(solution)/shard_map/ppermute | solution.py:383
  67.8 5.9 %collective-permute-start.15 = (bf16[320,128]{1,0:T(8,128)(2,1)S(1)}, bf16[320,128]{1,0:T(8,128)(2,1)S(1)}, u32[]{:S(2)}, u32[]{:S(2)}) collective-permute-start(bf16[320,128]{1,0:T(8,128)(2,1)S(1)} %get-tuple-element.50), channel_id=1, source_target_pairs={{0,4},{1,5},{2,6},{3,7},{4,0},{5,1},{6,2},{7,3},{8,12},{9,13},{10,... | collective-permute-start | bytes 245768 | tf_op jit(solution)/shard_map/ppermute | solution.py:383
  69.1 6.2 %collective-permute-start.16 = (bf16[320,128]{1,0:T(8,128)(2,1)S(1)}, bf16[320,128]{1,0:T(8,128)(2,1)S(1)}, u32[]{:S(2)}, u32[]{:S(2)}) collective-permute-start(bf16[320,128]{1,0:T(8,128)(2,1)S(1)} %get-tuple-element.50), channel_id=1, source_target_pairs={{0,12},{1,13},{2,14},{3,15},{4,8},{5,9},{6,10},{7,11},{8,4},{9,5},... | collective-permute-start | bytes 245768 | tf_op jit(solution)/shard_map/ppermute | solution.py:383
  70.9 6.1 %collective-permute-start.17 = (bf16[320,128]{1,0:T(8,128)(2,1)S(1)}, bf16[320,128]{1,0:T(8,128)(2,1)S(1)}, u32[]{:S(2)}, u32[]{:S(2)}) collective-permute-start(bf16[320,128]{1,0:T(8,128)(2,1)S(1)} %get-tuple-element.50), channel_id=1, source_target_pairs={{0,2},{1,3},{2,0},{3,1},{4,6},{5,7},{6,4},{7,5},{8,10},{9,11},{10,... | collective-permute-start | bytes 245768 | tf_op jit(solution)/shard_map/ppermute | solution.py:383
  75.3 6.3 %collective-permute-start.18 = (bf16[960,128]{1,0:T(8,128)(2,1)S(1)}, bf16[960,128]{1,0:T(8,128)(2,1)S(1)}, u32[]{:S(2)}, u32[]{:S(2)}) collective-permute-start(bf16[960,128]{1,0:T(8,128)(2,1)S(1)} %pad_maximum_fusion), channel_id=1, source_target_pairs={{0,2},{1,3},{2,0},{3,1},{4,6},{5,7},{6,4},{7,5},{8,10},{9,11},{10,... | collective-permute-start | bytes 737288 | tf_op jit(solution)/shard_map/ppermute | solution.py:383
  77.0 4.6 %collective-permute-start.19 = (bf16[1600,128]{1,0:T(8,128)(2,1)S(1)}, bf16[1600,128]{1,0:T(8,128)(2,1)S(1)}, u32[]{:S(2)}, u32[]{:S(2)}) collective-permute-start(bf16[1600,128]{1,0:T(8,128)(2,1)S(1)} %constant_dynamic-update-slice_fusion.5.refs_0_), channel_id=1, source_target_pairs={{0,1},{1,0},{2,3},{3,2},{4,5},{5,4},{6,7},{7,6},{8,9},{9,8},{10,11... | collective-permute-start | bytes 1228808 | tf_op jit(solution)/shard_map/ppermute | solution.py:383
  96.3 8.1 %collective-permute-start.23 = (bf16[960,128]{1,0:T(8,128)(2,1)S(1)}, bf16[960,128]{1,0:T(8,128)(2,1)S(1)}, u32[]{:S(2)}, u32[]{:S(2)}) collective-permute-start(bf16[960,128]{1,0:T(8,128)(2,1)S(1)} %slice.117), channel_id=1, source_target_pairs={{0,2},{1,3},{2,0},{3,1},{4,6},{5,7},{6,4},{7,5},{8,10},{9,11},{10,... | collective-permute-start | bytes 737288 | tf_op jit(solution)/shard_map/ppermute | solution.py:383
  104.4 9.0 %collective-permute-start.25 = (bf16[320,128]{1,0:T(8,128)(2,1)S(1)}, bf16[320,128]{1,0:T(8,128)(2,1)S(1)}, u32[]{:S(2)}, u32[]{:S(2)}) collective-permute-start(bf16[320,128]{1,0:T(8,128)(2,1)S(1)} %get-tuple-element.55), channel_id=1, source_target_pairs={{0,8},{1,9},{2,10},{3,11},{4,12},{5,13},{6,14},{7,15},{8,0},{9,1},... | collective-permute-start | bytes 245768 | tf_op jit(solution)/shard_map/ppermute | solution.py:383
  105.7 7.8 %collective-permute-start.26 = (bf16[320,128]{1,0:T(8,128)(2,1)S(1)}, bf16[320,128]{1,0:T(8,128)(2,1)S(1)}, u32[]{:S(2)}, u32[]{:S(2)}) collective-permute-start(bf16[320,128]{1,0:T(8,128)(2,1)S(1)} %get-tuple-element.57), channel_id=1, source_target_pairs={{0,4},{1,5},{2,6},{3,7},{4,0},{5,1},{6,2},{7,3},{8,12},{9,13},{10,... | collective-permute-start | bytes 245768 | tf_op jit(solution)/shard_map/ppermute | solution.py:383
  107.0 6.4 %collective-permute-start.27 = (bf16[320,128]{1,0:T(8,128)(2,1)S(1)}, bf16[320,128]{1,0:T(8,128)(2,1)S(1)}, u32[]{:S(2)}, u32[]{:S(2)}) collective-permute-start(bf16[320,128]{1,0:T(8,128)(2,1)S(1)} %get-tuple-element.56), channel_id=1, source_target_pairs={{0,12},{1,13},{2,14},{3,15},{4,8},{5,9},{6,10},{7,11},{8,4},{9,5},... | collective-permute-start | bytes 245768 | tf_op jit(solution)/shard_map/ppermute | solution.py:383
  108.9 4.5 %collective-permute-start.24 = (bf16[320,128]{1,0:T(8,128)(2,1)S(1)}, bf16[320,128]{1,0:T(8,128)(2,1)S(1)}, u32[]{:S(2)}, u32[]{:S(2)}) collective-permute-start(bf16[320,128]{1,0:T(8,128)(2,1)S(1)} %slice.115), channel_id=1, source_target_pairs={{0,2},{1,3},{2,0},{3,1},{4,6},{5,7},{6,4},{7,5},{8,10},{9,11},{10,... | collective-permute-start | bytes 245768 | tf_op jit(solution)/shard_map/ppermute | solution.py:383
  113.6 7.8 %collective-permute-start.28 = (bf16[320,128]{1,0:T(8,128)(2,1)S(1)}, bf16[320,128]{1,0:T(8,128)(2,1)S(1)}, u32[]{:S(2)}, u32[]{:S(2)}) collective-permute-start(bf16[320,128]{1,0:T(8,128)(2,1)S(1)} %get-tuple-element.48), channel_id=1, source_target_pairs={{0,8},{1,9},{2,10},{3,11},{4,12},{5,13},{6,14},{7,15},{8,0},{9,1},... | collective-permute-start | bytes 245768 | tf_op jit(solution)/shard_map/ppermute | solution.py:383
  115.6 5.8 %collective-permute-start.29 = (bf16[320,128]{1,0:T(8,128)(2,1)S(1)}, bf16[320,128]{1,0:T(8,128)(2,1)S(1)}, u32[]{:S(2)}, u32[]{:S(2)}) collective-permute-start(bf16[320,128]{1,0:T(8,128)(2,1)S(1)} %get-tuple-element.48), channel_id=1, source_target_pairs={{0,4},{1,5},{2,6},{3,7},{4,0},{5,1},{6,2},{7,3},{8,12},{9,13},{10,... | collective-permute-start | bytes 245768 | tf_op jit(solution)/shard_map/ppermute | solution.py:383
  116.2 6.5 %collective-permute-start.30 = (bf16[320,128]{1,0:T(8,128)(2,1)S(1)}, bf16[320,128]{1,0:T(8,128)(2,1)S(1)}, u32[]{:S(2)}, u32[]{:S(2)}) collective-permute-start(bf16[320,128]{1,0:T(8,128)(2,1)S(1)} %get-tuple-element.48), channel_id=1, source_target_pairs={{0,12},{1,13},{2,14},{3,15},{4,8},{5,9},{6,10},{7,11},{8,4},{9,5},... | collective-permute-start | bytes 245768 | tf_op jit(solution)/shard_map/ppermute | solution.py:383
  118.1 6.3 %collective-permute-start.31 = (bf16[320,128]{1,0:T(8,128)(2,1)S(1)}, bf16[320,128]{1,0:T(8,128)(2,1)S(1)}, u32[]{:S(2)}, u32[]{:S(2)}) collective-permute-start(bf16[320,128]{1,0:T(8,128)(2,1)S(1)} %get-tuple-element.48), channel_id=1, source_target_pairs={{0,2},{1,3},{2,0},{3,1},{4,6},{5,7},{6,4},{7,5},{8,10},{9,11},{10,... | collective-permute-start | bytes 245768 | tf_op jit(solution)/shard_map/ppermute | solution.py:383
  122.7 6.3 %collective-permute-start.32 = (bf16[960,128]{1,0:T(8,128)(2,1)S(1)}, bf16[960,128]{1,0:T(8,128)(2,1)S(1)}, u32[]{:S(2)}, u32[]{:S(2)}) collective-permute-start(bf16[960,128]{1,0:T(8,128)(2,1)S(1)} %pad_maximum_fusion.1), channel_id=1, source_target_pairs={{0,2},{1,3},{2,0},{3,1},{4,6},{5,7},{6,4},{7,5},{8,10},{9,11},{10,... | collective-permute-start | bytes 737288 | tf_op jit(solution)/shard_map/ppermute | solution.py:383
  124.4 4.5 %collective-permute-start.33 = (bf16[1600,128]{1,0:T(8,128)(2,1)S(1)}, bf16[1600,128]{1,0:T(8,128)(2,1)S(1)}, u32[]{:S(2)}, u32[]{:S(2)}) collective-permute-start(bf16[1600,128]{1,0:T(8,128)(2,1)S(1)} %constant_dynamic-update-slice_fusion.10.refs_0_), channel_id=1, source_target_pairs={{0,1},{1,0},{2,3},{3,2},{4,5},{5,4},{6,7},{7,6},{8,9},{9,8},{10,11... | collective-permute-start | bytes 1228808 | tf_op jit(solution)/shard_map/ppermute | solution.py:383
  142.7 3.6 %collective-permute-start.35 = (bf16[2048,128]{1,0:T(8,128)(2,1)S(1)}, bf16[2048,128]{1,0:T(8,128)(2,1)S(1)}, u32[]{:S(2)}, u32[]{:S(2)}) collective-permute-start(bf16[2048,128]{1,0:T(8,128)(2,1)S(1)} %get-tuple-element.44), channel_id=1, source_target_pairs={{0,1},{1,0},{2,3},{3,2},{4,5},{5,4},{6,7},{7,6},{8,9},{9,8},{10,11... | collective-permute-start | bytes 1572872 | tf_op jit(solution)/shard_map/ppermute | solution.py:383
  144.6 9.2 %collective-permute-start.37 = (bf16[2048,128]{1,0:T(8,128)(2,1)S(1)}, bf16[2048,128]{1,0:T(8,128)(2,1)S(1)}, u32[]{:S(2)}, u32[]{:S(2)}) collective-permute-start(bf16[2048,128]{1,0:T(8,128)(2,1)S(1)} %add_convert_fusion), channel_id=1, source_target_pairs={{0,2},{1,5},{2,0},{3,7},{4,6},{5,1},{6,4},{7,3},{8,10},{9,13},{10,... | collective-permute-start | bytes 1572872 | tf_op jit(solution)/shard_map/ppermute | solution.py:383
  154.1 9.2 %collective-permute-start.38 = (bf16[1024,128]{1,0:T(8,128)(2,1)S(1)}, bf16[1024,128]{1,0:T(8,128)(2,1)S(1)}, u32[]{:S(2)}, u32[]{:S(2)}) collective-permute-start(bf16[1024,128]{1,0:T(8,128)(2,1)S(1)} %slice.170), channel_id=1, source_target_pairs={{0,4},{1,9},{2,6},{3,11},{4,0},{5,13},{6,2},{7,15},{8,12},{9,1},{1... | collective-permute-start | bytes 786440 | tf_op jit(solution)/shard_map/ppermute | solution.py:383
  163.3 7.1 %collective-permute-start.39 = (bf16[512,128]{1,0:T(8,128)(2,1)S(1)}, bf16[512,128]{1,0:T(8,128)(2,1)S(1)}, u32[]{:S(2)}, u32[]{:S(2)}) collective-permute-start(bf16[512,128]{1,0:T(8,128)(2,1)S(1)} %slice.171), channel_id=1, source_target_pairs={{0,8},{1,3},{2,10},{3,1},{4,12},{5,7},{6,14},{7,5},{8,0},{9,11},{1... | collective-permute-start | bytes 393224 | tf_op jit(solution)/shard_map/ppermute | solution.py:383
  (9 other events, 16.5 us)

commit v11 on v10

--- a/solution.py
+++ b/solution.py
@@ -19,7 +19,6 @@
 ROW_TILE = 16
 SUPPORT_PARTS = 2
 SUPPORT_STEP = 4
-SUPPORT_AHEAD = 3
 PIECE = 5
 MATRIX_UNIT = 256
 VMEM_MARGIN = 3 * 1024 * 1024
@@ -94,8 +93,11 @@
             index = 2 * SUPPORT_STEP * step + entry
             fetch(index, ids[index]).start()
 
-    for step in range(min(SUPPORT_AHEAD, steps)):
+    def start_all(step, carry):
         start_step(step)
+        return carry
+
+    lax.fori_loop(0, steps, start_all, 0)
     shape = (2 * LANES, LANES)
     source = lax.broadcasted_iota(jnp.int32, shape, 0)
     target = lax.broadcasted_iota(jnp.int32, shape, 1)
@@ -107,10 +109,6 @@
         return pltpu.make_async_copy(held.at[2 * pair], out.at[begin // 2 + pair], out_sems.at[pair])
 
     def pack(step, carry):
-        @pl.when(step + SUPPORT_AHEAD < steps)
-        def _():
-            start_step(step + SUPPORT_AHEAD)
-
         span = [SUPPORT_STEP * step + pair for pair in range(SUPPORT_STEP)]
         for pair in span:
             fetch(2 * pair, ids[2 * pair]).wait()
@@ -222,12 +220,15 @@
         codes[shard_span(slot, size_in), :] = gathered[2 * half + second][begin : begin + size_in, :]
 
     def put(slot, size, begin, value):
-        rows = slice(slot % quarter * size + begin, slot % quarter * size + begin + value.shape[0])
-        if slot < 2 * quarter:
-            first = slot // quarter * quarter * size
-            keep[first + rows.start : first + rows.stop, :] = value
+        far, inside = divmod(slot, 2 * quarter)
+        if far:
+            ahead = send[0].shape[0] // size
+            second = inside >= ahead
+            start = (inside - ahead * second) * size + begin
+            send[second][start : start + value.shape[0], :] = value.astype(jnp.bfloat16)
         else:
-            send[slot // quarter - 2][rows, :] = value.astype(jnp.bfloat16)
+            start = inside * size + begin
+            keep[start : start + value.shape[0], :] = value
 
     def seat(index, offset):
         position, _, live = group_at(index, seq, order, counts)
@@ -347,7 +348,8 @@
     packed = (places * PATCHES, LANES)
     half_out = (groups * SLOT_PAIRS if mode == "final" else pairs) * PATCHES // 2
     shard = (2 * half_out // shards, LANES)
-    outs = [((half_out, LANES), double)] + [((half_out // 2, LANES), single)] * 2
+    ahead = half_out // 2 + (0 if mode == "final" else shard[0])
+    outs = [((half_out, LANES), double), ((ahead, LANES), single), ((half_out - ahead, LANES), single)]
     if mode == "first":
         outs += [(shard, single), (shard, double)]
     if mode == "final":
@@ -398,18 +400,18 @@
 
 
 def add_cores(keep, *send):
-    middle = keep.shape[0] // 2
-    arrived = [exchange(part, 1).astype(jnp.float32) for part in send]
-    return [part + share for part, share in zip((keep[:middle], keep[middle:]), arrived)]
+    ahead = send[0].shape[0]
+    after = keep[ahead:] + exchange(send[1], 1).astype(jnp.float32)
+    return keep[:ahead] + exchange(send[0], 1).astype(jnp.float32), after
 
 
 def reduce_shards(keep, *send):
     devices = lax.axis_size("rows")
     _, row, *columns = stage_distances(devices)
+    size = 2 * keep.shape[0] // devices
     near, other = add_cores(keep, *send)
-    size = near.shape[0] // (devices // 4)
-    sums = near[size:] + exchange(other[size:].astype(jnp.bfloat16), row).astype(jnp.float32)
-    last, sums = lax.optimization_barrier((other[:size].astype(jnp.bfloat16), sums.astype(jnp.bfloat16)))
+    sums = near[size:-size] + exchange(other.astype(jnp.bfloat16), row).astype(jnp.float32)
+    last, sums = lax.optimization_barrier((near[-size:].astype(jnp.bfloat16), sums.astype(jnp.bfloat16)))
     total = near[:size] + exchange(last, row).astype(jnp.float32)
     for slot in range(1, devices // 4):
         share = exchange(sums[(slot - 1) * size : slot * size], slot_distance(slot, columns))
@@ -427,7 +429,7 @@
 
 def packed_order(live):
     index = jnp.arange(live.shape[0])
-    ahead = (live[None, :] > live[:, None]) | ((live[None, :] == live[:, None]) & (index[None, :] < index[:, None]))
+    ahead = (live[None, :] < live[:, None]) | ((live[None, :] == live[:, None]) & (index[None, :] < index[:, None]))
     rank = jnp.sum(ahead.astype(jnp.int32), axis=1)
     return jnp.sum(jnp.where(rank[:, None] == index[None, :], index[:, None], 0), axis=0).astype(jnp.int32)
 

time: 172 us -> 169 us (0.983)
  transfers between devices with their start and end apart: 40 -> 40, of which waited for: 22 -> 21; matrix products, arithmetic and copies ran while one was open for 3% -> 3% of each run, Pallas kernels for 11% -> 11%
where the time goes in v11:
time: 169 us; the launch traced here: 170 us
  waiting for transfers between devices  61.1 us (36%)
  Pallas kernels  52.8 us (31%)
  starting transfers between devices  46.8 us (28%)
  local copies, waits for them, and re-layouts  6.41 us (4%)
  other arithmetic  2.28 us (1%)
    ppermute x40, waiting for transfers between devices, exchange(): lax.ppermute(value, 'rows', [(i, i ^ apart[i % 2]) for i in range(devices)])  61.1 us
    ppermute x40, starting transfers between devices, exchange(): lax.ppermute(value, 'rows', [(i, i ^ apart[i % 2]) for i in range(devices)])  46.8 us
    pallas_call x3, Pallas kernels, gradient_call(): pl.pallas_call(functools.partial(gradient_kernel, mode, shards, pairs, gr...  34 us
    pallas_call x2, Pallas kernels, collect_support(): pl.pallas_call(functools.partial(support_kernel, part * entries, groups),...  18.8 us
  transfers between devices with their start and end apart: 40, of which 21 were waited for; matrix products, arithmetic and copies ran while one was open for 3% of the time, Pallas kernels for 11%

profile of v11, /device:TPU:0, one launch (start us, length us, event | category | flops | bytes accessed | tf_op | source)
XLA Modules:
  0.0 169.8 jit_solution(5324845483396058921)
XLA Ops:
  1.6 4.1 %collective-permute-start = (bf16[512,128]{1,0:T(8,128)(2,1)S(1)}, bf16[512,128]{1,0:T(8,128)(2,1)S(1)}, u32[]{:S(2)}, u32[]{:S(2)}) collective-permute-start(bf16[512,128]{1,0:T(8,128)(2,1)S(1)} %reshape.33), channel_id=1, source_target_pairs={{0,8},{1,9},{2,10},{3,11},{4,12},{5,13},{6,14},{7,15},{8,0},{9,1},... | collective-permute-start | bytes 393224 | tf_op jit(solution)/shard_map/ppermute | solution.py:385
  7.3 1.7 %collective-permute-start.3 = (bf16[512,128]{1,0:T(8,128)(2,1)S(1)}, bf16[512,128]{1,0:T(8,128)(2,1)S(1)}, u32[]{:S(2)}, u32[]{:S(2)}) collective-permute-start(bf16[512,128]{1,0:T(8,128)(2,1)S(1)} %reshape.33), channel_id=1, source_target_pairs={{0,2},{1,3},{2,0},{3,1},{4,6},{5,7},{6,4},{7,5},{8,10},{9,11},{10,... | collective-permute-start | bytes 393224 | tf_op jit(solution)/shard_map/ppermute | solution.py:385
  11.7 9.4 %collect_support.2.refs_0_ = bf16[520,512,128]{2,1,0:T(8,128)(2,1)} custom-call(s32[305]{0:T(512)S(1)} %concatenate.18.scalars, bf16[512,32768]{1,0:T(8,128)(2,1)} %dictionary.3), custom_call_target="tpu_custom_call" | custom-call | bytes 31457280 | tf_op jit(solution)/shard_map/collect_support/pallas_call | solution.py:139
  21.7 9.4 %collect_support.3.blocks = bf16[520,512,128]{2,1,0:T(8,128)(2,1)} custom-call(s32[305]{0:T(512)S(1)} %concatenate.18.scalars, bf16[512,32768]{1,0:T(8,128)(2,1)} %dictionary.3, bf16[520,512,128]{2,1,0:T(8,128)(2,1)} %collect_support.2.refs_0_), custom_call_target="tpu_custom_call", output_to_operand_aliasing={{}: (2, {})} | custom-call | bytes 31457280 | tf_op jit(solution)/shard_map/collect_support/pallas_call | solution.py:139
  33.4 11.1 %gradient.3 = (f32[2560,128]{1,0:T(8,128)S(1)}, bf16[1600,128]{1,0:T(8,128)(2,1)S(1)}, bf16[960,128]{1,0:T(8,128)(2,1)S(1)}, bf16[320,128]{1,0:T(8,128)(2,1)S(1)}, f32[320,128]{1,0:T(8,128)S(1)}) custom-call(s32[305]{0:T(512)S(1)} %concatenate.18.scalars, bf16[520,512,128]{2,1,0:T(8,128)(2,1)} %collect_support.3.blocks, ...), custom_call_target="tpu_custom_call" | custom-call | flops 5368709120 | bytes 10485760 | tf_op jit(solution)/shard_map/gradient/pallas_call | solution.py:362
  46.2 1.8 %collective-permute-start.9 = (bf16[960,128]{1,0:T(8,128)(2,1)S(1)}, bf16[960,128]{1,0:T(8,128)(2,1)S(1)}, u32[]{:S(2)}, u32[]{:S(2)}) collective-permute-start(bf16[960,128]{1,0:T(8,128)(2,1)S(1)} %add_convert_fusion.2), channel_id=1, source_target_pairs={{0,2},{1,3},{2,0},{3,1},{4,6},{5,7},{6,4},{7,5},{8,10},{9,11},{10,... | collective-permute-start | bytes 737288 | tf_op jit(solution)/shard_map/ppermute | solution.py:385
  48.1 6.2 %collective-permute-done.9 = bf16[960,128]{1,0:T(8,128)(2,1)S(1)} collective-permute-done((bf16[960,128]{1,0:T(8,128)(2,1)S(1)}, bf16[960,128]{1,0:T(8,128)(2,1)S(1)}, u32[]{:S(2)}, u32[]{:S(2)}) %collective-permute-start.9) | collective-permute-done | bytes 245792 | tf_op jit(solution)/shard_map/ppermute | solution.py:385
  54.4 2.0 %collective-permute-start.11 = (bf16[320,128]{1,0:T(8,128)(2,1)S(1)}, bf16[320,128]{1,0:T(8,128)(2,1)S(1)}, u32[]{:S(2)}, u32[]{:S(2)}) collective-permute-start(bf16[320,128]{1,0:T(8,128)(2,1)S(1)} %get-tuple-element.54), channel_id=1, source_target_pairs={{0,8},{1,9},{2,10},{3,11},{4,12},{5,13},{6,14},{7,15},{8,0},{9,1},... | collective-permute-start | bytes 245768 | tf_op jit(solution)/shard_map/ppermute | solution.py:385
  56.4 2.5 %collective-permute-start.12 = (bf16[320,128]{1,0:T(8,128)(2,1)S(1)}, bf16[320,128]{1,0:T(8,128)(2,1)S(1)}, u32[]{:S(2)}, u32[]{:S(2)}) collective-permute-start(bf16[320,128]{1,0:T(8,128)(2,1)S(1)} %get-tuple-element.56), channel_id=1, source_target_pairs={{0,4},{1,5},{2,6},{3,7},{4,0},{5,1},{6,2},{7,3},{8,12},{9,13},{10,... | collective-permute-start | bytes 245768 | tf_op jit(solution)/shard_map/ppermute | solution.py:385
  58.9 1.7 %collective-permute-start.10 = (bf16[320,128]{1,0:T(8,128)(2,1)S(1)}, bf16[320,128]{1,0:T(8,128)(2,1)S(1)}, u32[]{:S(2)}, u32[]{:S(2)}) collective-permute-start(bf16[320,128]{1,0:T(8,128)(2,1)S(1)} %slice.163), channel_id=1, source_target_pairs={{0,2},{1,3},{2,0},{3,1},{4,6},{5,7},{6,4},{7,5},{8,10},{9,11},{10,... | collective-permute-start | bytes 245768 | tf_op jit(solution)/shard_map/ppermute | solution.py:385
  61.5 3.6 %collective-permute-done.13 = bf16[320,128]{1,0:T(8,128)(2,1)S(1)} collective-permute-done((bf16[320,128]{1,0:T(8,128)(2,1)S(1)}, bf16[320,128]{1,0:T(8,128)(2,1)S(1)}, u32[]{:S(2)}, u32[]{:S(2)}) %collective-permute-start.13) | collective-permute-done | bytes 81952 | tf_op jit(solution)/shard_map/ppermute | solution.py:385
  67.9 1.8 %collective-permute-start.16 = (bf16[320,128]{1,0:T(8,128)(2,1)S(1)}, bf16[320,128]{1,0:T(8,128)(2,1)S(1)}, u32[]{:S(2)}, u32[]{:S(2)}) collective-permute-start(bf16[320,128]{1,0:T(8,128)(2,1)S(1)} %get-tuple-element.50), channel_id=1, source_target_pairs={{0,12},{1,13},{2,14},{3,15},{4,8},{5,9},{6,10},{7,11},{8,4},{9,5},... | collective-permute-start | bytes 245768 | tf_op jit(solution)/shard_map/ppermute | solution.py:385
  72.4 1.7 collective-permute-done.16
  74.1 1.6 collective-permute-start.18
  75.9 4.5 %collective-permute-done.18.refs_1_ = bf16[960,128]{1,0:T(8,128)(2,1)S(1)} collective-permute-done((bf16[960,128]{1,0:T(8,128)(2,1)S(1)}, bf16[960,128]{1,0:T(8,128)(2,1)S(1)}, u32[]{:S(2)}, u32[]{:S(2)}) %collective-permute-start.18) | collective-permute-done | bytes 245792 | tf_op jit(solution)/shard_map/ppermute | solution.py:385
  81.9 10.8 %gradient.4 = (f32[2560,128]{1,0:T(8,128)S(1)}, bf16[1600,128]{1,0:T(8,128)(2,1)S(1)}, bf16[960,128]{1,0:T(8,128)(2,1)S(1)}) custom-call(s32[305]{0:T(512)S(1)} %concatenate.18.scalars, bf16[520,512,128]{2,1,0:T(8,128)(2,1)} %collect_support.3.blocks, bf16[1600,128]{1,0:T(8,128)(2,1)S(1)} %constant_dynamic-update-slice_fusion.5.refs_0_, ...), custom_call_target="tpu_custom_call" | custom-call | flops 5368709120 | bytes 10485760 | tf_op jit(solution)/shard_map/gradient/pallas_call | solution.py:362
  94.4 1.6 collective-permute-start.23
  96.1 6.4 %collective-permute-done.23 = bf16[960,128]{1,0:T(8,128)(2,1)S(1)} collective-permute-done((bf16[960,128]{1,0:T(8,128)(2,1)S(1)}, bf16[960,128]{1,0:T(8,128)(2,1)S(1)}, u32[]{:S(2)}, u32[]{:S(2)}) %collective-permute-start.23) | collective-permute-done | bytes 245792 | tf_op jit(solution)/shard_map/ppermute | solution.py:385
  105.0 1.9 %collective-permute-start.27 = (bf16[320,128]{1,0:T(8,128)(2,1)S(1)}, bf16[320,128]{1,0:T(8,128)(2,1)S(1)}, u32[]{:S(2)}, u32[]{:S(2)}) collective-permute-start(bf16[320,128]{1,0:T(8,128)(2,1)S(1)} %get-tuple-element.52), channel_id=1, source_target_pairs={{0,12},{1,13},{2,14},{3,15},{4,8},{5,9},{6,10},{7,11},{8,4},{9,5},... | collective-permute-start | bytes 245768 | tf_op jit(solution)/shard_map/ppermute | solution.py:385
  108.5 3.0 %collective-permute-done.25 = bf16[320,128]{1,0:T(8,128)(2,1)S(1)} collective-permute-done((bf16[320,128]{1,0:T(8,128)(2,1)S(1)}, bf16[320,128]{1,0:T(8,128)(2,1)S(1)}, u32[]{:S(2)}, u32[]{:S(2)}) %collective-permute-start.25) | collective-permute-done | bytes 81952 | tf_op jit(solution)/shard_map/ppermute | solution.py:385
  111.7 2.0 %collective-permute-start.28 = (bf16[320,128]{1,0:T(8,128)(2,1)S(1)}, bf16[320,128]{1,0:T(8,128)(2,1)S(1)}, u32[]{:S(2)}, u32[]{:S(2)}) collective-permute-start(bf16[320,128]{1,0:T(8,128)(2,1)S(1)} %get-tuple-element.48), channel_id=1, source_target_pairs={{0,8},{1,9},{2,10},{3,11},{4,12},{5,13},{6,14},{7,15},{8,0},{9,1},... | collective-permute-start | bytes 245768 | tf_op jit(solution)/shard_map/ppermute | solution.py:385
  114.2 1.9 %collective-permute-start.30 = (bf16[320,128]{1,0:T(8,128)(2,1)S(1)}, bf16[320,128]{1,0:T(8,128)(2,1)S(1)}, u32[]{:S(2)}, u32[]{:S(2)}) collective-permute-start(bf16[320,128]{1,0:T(8,128)(2,1)S(1)} %get-tuple-element.48), channel_id=1, source_target_pairs={{0,12},{1,13},{2,14},{3,15},{4,8},{5,9},{6,10},{7,11},{8,4},{9,5},... | collective-permute-start | bytes 245768 | tf_op jit(solution)/shard_map/ppermute | solution.py:385
  117.7 1.8 %collective-permute-done.28 = bf16[320,128]{1,0:T(8,128)(2,1)S(1)} collective-permute-done((bf16[320,128]{1,0:T(8,128)(2,1)S(1)}, bf16[320,128]{1,0:T(8,128)(2,1)S(1)}, u32[]{:S(2)}, u32[]{:S(2)}) %collective-permute-start.28) | collective-permute-done | bytes 81952 | tf_op jit(solution)/shard_map/ppermute | solution.py:385
  120.7 1.6 collective-permute-start.32
  122.5 4.5 %collective-permute-done.32.refs_1_ = bf16[960,128]{1,0:T(8,128)(2,1)S(1)} collective-permute-done((bf16[960,128]{1,0:T(8,128)(2,1)S(1)}, bf16[960,128]{1,0:T(8,128)(2,1)S(1)}, u32[]{:S(2)}, u32[]{:S(2)}) %collective-permute-start.32) | collective-permute-done | bytes 245792 | tf_op jit(solution)/shard_map/ppermute | solution.py:385
  128.5 12.0 %gradient.5 = (f32[4096,128]{1,0:T(8,128)S(1)}, bf16[2048,128]{1,0:T(8,128)(2,1)S(1)}, bf16[2048,128]{1,0:T(8,128)(2,1)S(1)}, bf16[8,64,128]{2,1,0:T(8,128)(2,1)S(1)}, f32[64,128]{1,0:T(8,128)S(1)}) custom-call(s32[305]{0:T(512)S(1)} %concatenate.18.scalars, bf16[520,512,128]{2,1,0:T(8,128)(2,1)} %collect_support.3.blocks, ...), custom_call_target="tpu_custom_call" | custom-call | flops 5368709120 | bytes 10485760 | tf_op jit(solution)/shard_map/gradient/pallas_call | solution.py:362
  142.6 1.6 collective-permute-start.37
  144.2 7.6 %collective-permute-done.37 = bf16[2048,128]{1,0:T(8,128)(2,1)S(1)} collective-permute-done((bf16[2048,128]{1,0:T(8,128)(2,1)S(1)}, bf16[2048,128]{1,0:T(8,128)(2,1)S(1)}, u32[]{:S(2)}, u32[]{:S(2)}) %collective-permute-start.37) | collective-permute-done | bytes 524320 | tf_op jit(solution)/shard_map/ppermute | solution.py:385
  152.1 2.5 %collective-permute-start.38 = (bf16[1024,128]{1,0:T(8,128)(2,1)S(1)}, bf16[1024,128]{1,0:T(8,128)(2,1)S(1)}, u32[]{:S(2)}, u32[]{:S(2)}) collective-permute-start(bf16[1024,128]{1,0:T(8,128)(2,1)S(1)} %slice.160), channel_id=1, source_target_pairs={{0,4},{1,9},{2,6},{3,11},{4,0},{5,13},{6,2},{7,15},{8,12},{9,1},{1... | collective-permute-start | bytes 786440 | tf_op jit(solution)/shard_map/ppermute | solution.py:385
  154.6 6.7 %collective-permute-done.38 = bf16[1024,128]{1,0:T(8,128)(2,1)S(1)} collective-permute-done((bf16[1024,128]{1,0:T(8,128)(2,1)S(1)}, bf16[1024,128]{1,0:T(8,128)(2,1)S(1)}, u32[]{:S(2)}, u32[]{:S(2)}) %collective-permute-start.38) | collective-permute-done | bytes 262176 | tf_op jit(solution)/shard_map/ppermute | solution.py:385
  161.3 1.8 %collective-permute-start.39 = (bf16[512,128]{1,0:T(8,128)(2,1)S(1)}, bf16[512,128]{1,0:T(8,128)(2,1)S(1)}, u32[]{:S(2)}, u32[]{:S(2)}) collective-permute-start(bf16[512,128]{1,0:T(8,128)(2,1)S(1)} %slice.161), channel_id=1, source_target_pairs={{0,8},{1,3},{2,10},{3,1},{4,12},{5,7},{6,14},{7,5},{8,0},{9,11},{1... | collective-permute-start | bytes 393224 | tf_op jit(solution)/shard_map/ppermute | solution.py:385
  163.1 5.3 %collective-permute-done.39 = bf16[512,128]{1,0:T(8,128)(2,1)S(1)} collective-permute-done((bf16[512,128]{1,0:T(8,128)(2,1)S(1)}, bf16[512,128]{1,0:T(8,128)(2,1)S(1)}, u32[]{:S(2)}, u32[]{:S(2)}) %collective-permute-start.39) | collective-permute-done | bytes 131104 | tf_op jit(solution)/shard_map/ppermute | solution.py:385
  (105 shorter events, 33.2 us)
Async XLA Ops:
  1.6 19.5 %collective-permute-start = (bf16[512,128]{1,0:T(8,128)(2,1)S(1)}, bf16[512,128]{1,0:T(8,128)(2,1)S(1)}, u32[]{:S(2)}, u32[]{:S(2)}) collective-permute-start(bf16[512,128]{1,0:T(8,128)(2,1)S(1)} %reshape.33), channel_id=1, source_target_pairs={{0,8},{1,9},{2,10},{3,11},{4,12},{5,13},{6,14},{7,15},{8,0},{9,1},... | collective-permute-start | bytes 393224 | tf_op jit(solution)/shard_map/ppermute | solution.py:385
  5.7 15.5 %collective-permute-start.1 = (bf16[512,128]{1,0:T(8,128)(2,1)S(1)}, bf16[512,128]{1,0:T(8,128)(2,1)S(1)}, u32[]{:S(2)}, u32[]{:S(2)}) collective-permute-start(bf16[512,128]{1,0:T(8,128)(2,1)S(1)} %reshape.33), channel_id=1, source_target_pairs={{0,4},{1,5},{2,6},{3,7},{4,0},{5,1},{6,2},{7,3},{8,12},{9,13},{10,... | collective-permute-start | bytes 393224 | tf_op jit(solution)/shard_map/ppermute | solution.py:385
  7.3 13.9 %collective-permute-start.2 = (bf16[512,128]{1,0:T(8,128)(2,1)S(1)}, bf16[512,128]{1,0:T(8,128)(2,1)S(1)}, u32[]{:S(2)}, u32[]{:S(2)}) collective-permute-start(bf16[512,128]{1,0:T(8,128)(2,1)S(1)} %reshape.33), channel_id=1, source_target_pairs={{0,12},{1,13},{2,14},{3,15},{4,8},{5,9},{6,10},{7,11},{8,4},{9,5},... | collective-permute-start | bytes 393224 | tf_op jit(solution)/shard_map/ppermute | solution.py:385
  7.3 14.0 %collective-permute-start.3 = (bf16[512,128]{1,0:T(8,128)(2,1)S(1)}, bf16[512,128]{1,0:T(8,128)(2,1)S(1)}, u32[]{:S(2)}, u32[]{:S(2)}) collective-permute-start(bf16[512,128]{1,0:T(8,128)(2,1)S(1)} %reshape.33), channel_id=1, source_target_pairs={{0,2},{1,3},{2,0},{3,1},{4,6},{5,7},{6,4},{7,5},{8,10},{9,11},{10,... | collective-permute-start | bytes 393224 | tf_op jit(solution)/shard_map/ppermute | solution.py:385
  21.3 9.9 %collective-permute-start.4 = (bf16[1536,128]{1,0:T(8,128)(2,1)S(1)}, bf16[1536,128]{1,0:T(8,128)(2,1)S(1)}, u32[]{:S(2)}, u32[]{:S(2)}) collective-permute-start(bf16[1536,128]{1,0:T(8,128)(2,1)S(1)} %slice.77), channel_id=1, source_target_pairs={{0,2},{1,3},{2,0},{3,1},{4,6},{5,7},{6,4},{7,5},{8,10},{9,11},{10,... | collective-permute-start | bytes 1179656 | tf_op jit(solution)/shard_map/ppermute | solution.py:385
  21.7 11.6 %collective-permute-start.5 = (bf16[2560,128]{1,0:T(8,128)(2,1)S(1)}, bf16[2560,128]{1,0:T(8,128)(2,1)S(1)}, u32[]{:S(2)}, u32[]{:S(2)}) collective-permute-start(bf16[2560,128]{1,0:T(8,128)(2,1)S(1)} %constant_dynamic-update-slice_fusion.refs_0_), channel_id=1, source_target_pairs={{0,1},{1,0},{2,3},{3,2},{4,5},{5,4},{6,7},{7,6},{8,9},{9,8},{10,11... | collective-permute-start | bytes 1966088 | tf_op jit(solution)/shard_map/ppermute | solution.py:385
  46.2 8.1 %collective-permute-start.9 = (bf16[960,128]{1,0:T(8,128)(2,1)S(1)}, bf16[960,128]{1,0:T(8,128)(2,1)S(1)}, u32[]{:S(2)}, u32[]{:S(2)}) collective-permute-start(bf16[960,128]{1,0:T(8,128)(2,1)S(1)} %add_convert_fusion.2), channel_id=1, source_target_pairs={{0,2},{1,3},{2,0},{3,1},{4,6},{5,7},{6,4},{7,5},{8,10},{9,11},{10,... | collective-permute-start | bytes 737288 | tf_op jit(solution)/shard_map/ppermute | solution.py:385
  54.4 7.1 %collective-permute-start.11 = (bf16[320,128]{1,0:T(8,128)(2,1)S(1)}, bf16[320,128]{1,0:T(8,128)(2,1)S(1)}, u32[]{:S(2)}, u32[]{:S(2)}) collective-permute-start(bf16[320,128]{1,0:T(8,128)(2,1)S(1)} %get-tuple-element.54), channel_id=1, source_target_pairs={{0,8},{1,9},{2,10},{3,11},{4,12},{5,13},{6,14},{7,15},{8,0},{9,1},... | collective-permute-start | bytes 245768 | tf_op jit(solution)/shard_map/ppermute | solution.py:385
  56.4 5.1 %collective-permute-start.12 = (bf16[320,128]{1,0:T(8,128)(2,1)S(1)}, bf16[320,128]{1,0:T(8,128)(2,1)S(1)}, u32[]{:S(2)}, u32[]{:S(2)}) collective-permute-start(bf16[320,128]{1,0:T(8,128)(2,1)S(1)} %get-tuple-element.56), channel_id=1, source_target_pairs={{0,4},{1,5},{2,6},{3,7},{4,0},{5,1},{6,2},{7,3},{8,12},{9,13},{10,... | collective-permute-start | bytes 245768 | tf_op jit(solution)/shard_map/ppermute | solution.py:385
  58.8 6.2 %collective-permute-start.13 = (bf16[320,128]{1,0:T(8,128)(2,1)S(1)}, bf16[320,128]{1,0:T(8,128)(2,1)S(1)}, u32[]{:S(2)}, u32[]{:S(2)}) collective-permute-start(bf16[320,128]{1,0:T(8,128)(2,1)S(1)} %get-tuple-element.55), channel_id=1, source_target_pairs={{0,12},{1,13},{2,14},{3,15},{4,8},{5,9},{6,10},{7,11},{8,4},{9,5},... | collective-permute-start | bytes 245768 | tf_op jit(solution)/shard_map/ppermute | solution.py:385
  58.9 6.2 %collective-permute-start.10 = (bf16[320,128]{1,0:T(8,128)(2,1)S(1)}, bf16[320,128]{1,0:T(8,128)(2,1)S(1)}, u32[]{:S(2)}, u32[]{:S(2)}) collective-permute-start(bf16[320,128]{1,0:T(8,128)(2,1)S(1)} %slice.163), channel_id=1, source_target_pairs={{0,2},{1,3},{2,0},{3,1},{4,6},{5,7},{6,4},{7,5},{8,10},{9,11},{10,... | collective-permute-start | bytes 245768 | tf_op jit(solution)/shard_map/ppermute | solution.py:385
  65.2 7.1 %collective-permute-start.14 = (bf16[320,128]{1,0:T(8,128)(2,1)S(1)}, bf16[320,128]{1,0:T(8,128)(2,1)S(1)}, u32[]{:S(2)}, u32[]{:S(2)}) collective-permute-start(bf16[320,128]{1,0:T(8,128)(2,1)S(1)} %get-tuple-element.50), channel_id=1, source_target_pairs={{0,8},{1,9},{2,10},{3,11},{4,12},{5,13},{6,14},{7,15},{8,0},{9,1},... | collective-permute-start | bytes 245768 | tf_op jit(solution)/shard_map/ppermute | solution.py:385
  66.6 5.9 %collective-permute-start.15 = (bf16[320,128]{1,0:T(8,128)(2,1)S(1)}, bf16[320,128]{1,0:T(8,128)(2,1)S(1)}, u32[]{:S(2)}, u32[]{:S(2)}) collective-permute-start(bf16[320,128]{1,0:T(8,128)(2,1)S(1)} %get-tuple-element.50), channel_id=1, source_target_pairs={{0,4},{1,5},{2,6},{3,7},{4,0},{5,1},{6,2},{7,3},{8,12},{9,13},{10,... | collective-permute-start | bytes 245768 | tf_op jit(solution)/shard_map/ppermute | solution.py:385
  67.9 6.2 %collective-permute-start.16 = (bf16[320,128]{1,0:T(8,128)(2,1)S(1)}, bf16[320,128]{1,0:T(8,128)(2,1)S(1)}, u32[]{:S(2)}, u32[]{:S(2)}) collective-permute-start(bf16[320,128]{1,0:T(8,128)(2,1)S(1)} %get-tuple-element.50), channel_id=1, source_target_pairs={{0,12},{1,13},{2,14},{3,15},{4,8},{5,9},{6,10},{7,11},{8,4},{9,5},... | collective-permute-start | bytes 245768 | tf_op jit(solution)/shard_map/ppermute | solution.py:385
  69.7 6.1 %collective-permute-start.17 = (bf16[320,128]{1,0:T(8,128)(2,1)S(1)}, bf16[320,128]{1,0:T(8,128)(2,1)S(1)}, u32[]{:S(2)}, u32[]{:S(2)}) collective-permute-start(bf16[320,128]{1,0:T(8,128)(2,1)S(1)} %get-tuple-element.50), channel_id=1, source_target_pairs={{0,2},{1,3},{2,0},{3,1},{4,6},{5,7},{6,4},{7,5},{8,10},{9,11},{10,... | collective-permute-start | bytes 245768 | tf_op jit(solution)/shard_map/ppermute | solution.py:385
  74.1 6.3 %collective-permute-start.18 = (bf16[960,128]{1,0:T(8,128)(2,1)S(1)}, bf16[960,128]{1,0:T(8,128)(2,1)S(1)}, u32[]{:S(2)}, u32[]{:S(2)}) collective-permute-start(bf16[960,128]{1,0:T(8,128)(2,1)S(1)} %pad_maximum_fusion), channel_id=1, source_target_pairs={{0,2},{1,3},{2,0},{3,1},{4,6},{5,7},{6,4},{7,5},{8,10},{9,11},{10,... | collective-permute-start | bytes 737288 | tf_op jit(solution)/shard_map/ppermute | solution.py:385
  75.8 4.6 %collective-permute-start.19 = (bf16[1600,128]{1,0:T(8,128)(2,1)S(1)}, bf16[1600,128]{1,0:T(8,128)(2,1)S(1)}, u32[]{:S(2)}, u32[]{:S(2)}) collective-permute-start(bf16[1600,128]{1,0:T(8,128)(2,1)S(1)} %constant_dynamic-update-slice_fusion.5.refs_0_), channel_id=1, source_target_pairs={{0,1},{1,0},{2,3},{3,2},{4,5},{5,4},{6,7},{7,6},{8,9},{9,8},{10,11... | collective-permute-start | bytes 1228808 | tf_op jit(solution)/shard_map/ppermute | solution.py:385
  94.4 8.1 %collective-permute-start.23 = (bf16[960,128]{1,0:T(8,128)(2,1)S(1)}, bf16[960,128]{1,0:T(8,128)(2,1)S(1)}, u32[]{:S(2)}, u32[]{:S(2)}) collective-permute-start(bf16[960,128]{1,0:T(8,128)(2,1)S(1)} %add_convert_fusion.1), channel_id=1, source_target_pairs={{0,2},{1,3},{2,0},{3,1},{4,6},{5,7},{6,4},{7,5},{8,10},{9,11},{10,... | collective-permute-start | bytes 737288 | tf_op jit(solution)/shard_map/ppermute | solution.py:385
  102.5 9.0 %collective-permute-start.25 = (bf16[320,128]{1,0:T(8,128)(2,1)S(1)}, bf16[320,128]{1,0:T(8,128)(2,1)S(1)}, u32[]{:S(2)}, u32[]{:S(2)}) collective-permute-start(bf16[320,128]{1,0:T(8,128)(2,1)S(1)} %get-tuple-element.51), channel_id=1, source_target_pairs={{0,8},{1,9},{2,10},{3,11},{4,12},{5,13},{6,14},{7,15},{8,0},{9,1},... | collective-permute-start | bytes 245768 | tf_op jit(solution)/shard_map/ppermute | solution.py:385
  103.6 7.9 %collective-permute-start.26 = (bf16[320,128]{1,0:T(8,128)(2,1)S(1)}, bf16[320,128]{1,0:T(8,128)(2,1)S(1)}, u32[]{:S(2)}, u32[]{:S(2)}) collective-permute-start(bf16[320,128]{1,0:T(8,128)(2,1)S(1)} %get-tuple-element.53), channel_id=1, source_target_pairs={{0,4},{1,5},{2,6},{3,7},{4,0},{5,1},{6,2},{7,3},{8,12},{9,13},{10,... | collective-permute-start | bytes 245768 | tf_op jit(solution)/shard_map/ppermute | solution.py:385
  105.0 6.4 %collective-permute-start.27 = (bf16[320,128]{1,0:T(8,128)(2,1)S(1)}, bf16[320,128]{1,0:T(8,128)(2,1)S(1)}, u32[]{:S(2)}, u32[]{:S(2)}) collective-permute-start(bf16[320,128]{1,0:T(8,128)(2,1)S(1)} %get-tuple-element.52), channel_id=1, source_target_pairs={{0,12},{1,13},{2,14},{3,15},{4,8},{5,9},{6,10},{7,11},{8,4},{9,5},... | collective-permute-start | bytes 245768 | tf_op jit(solution)/shard_map/ppermute | solution.py:385
  107.0 4.5 %collective-permute-start.24 = (bf16[320,128]{1,0:T(8,128)(2,1)S(1)}, bf16[320,128]{1,0:T(8,128)(2,1)S(1)}, u32[]{:S(2)}, u32[]{:S(2)}) collective-permute-start(bf16[320,128]{1,0:T(8,128)(2,1)S(1)} %slice.162), channel_id=1, source_target_pairs={{0,2},{1,3},{2,0},{3,1},{4,6},{5,7},{6,4},{7,5},{8,10},{9,11},{10,... | collective-permute-start | bytes 245768 | tf_op jit(solution)/shard_map/ppermute | solution.py:385
  111.7 7.8 %collective-permute-start.28 = (bf16[320,128]{1,0:T(8,128)(2,1)S(1)}, bf16[320,128]{1,0:T(8,128)(2,1)S(1)}, u32[]{:S(2)}, u32[]{:S(2)}) collective-permute-start(bf16[320,128]{1,0:T(8,128)(2,1)S(1)} %get-tuple-element.48), channel_id=1, source_target_pairs={{0,8},{1,9},{2,10},{3,11},{4,12},{5,13},{6,14},{7,15},{8,0},{9,1},... | collective-permute-start | bytes 245768 | tf_op jit(solution)/shard_map/ppermute | solution.py:385
  113.7 5.9 %collective-permute-start.29 = (bf16[320,128]{1,0:T(8,128)(2,1)S(1)}, bf16[320,128]{1,0:T(8,128)(2,1)S(1)}, u32[]{:S(2)}, u32[]{:S(2)}) collective-permute-start(bf16[320,128]{1,0:T(8,128)(2,1)S(1)} %get-tuple-element.48), channel_id=1, source_target_pairs={{0,4},{1,5},{2,6},{3,7},{4,0},{5,1},{6,2},{7,3},{8,12},{9,13},{10,... | collective-permute-start | bytes 245768 | tf_op jit(solution)/shard_map/ppermute | solution.py:385
  114.2 6.5 %collective-permute-start.30 = (bf16[320,128]{1,0:T(8,128)(2,1)S(1)}, bf16[320,128]{1,0:T(8,128)(2,1)S(1)}, u32[]{:S(2)}, u32[]{:S(2)}) collective-permute-start(bf16[320,128]{1,0:T(8,128)(2,1)S(1)} %get-tuple-element.48), channel_id=1, source_target_pairs={{0,12},{1,13},{2,14},{3,15},{4,8},{5,9},{6,10},{7,11},{8,4},{9,5},... | collective-permute-start | bytes 245768 | tf_op jit(solution)/shard_map/ppermute | solution.py:385
  116.1 6.2 %collective-permute-start.31 = (bf16[320,128]{1,0:T(8,128)(2,1)S(1)}, bf16[320,128]{1,0:T(8,128)(2,1)S(1)}, u32[]{:S(2)}, u32[]{:S(2)}) collective-permute-start(bf16[320,128]{1,0:T(8,128)(2,1)S(1)} %get-tuple-element.48), channel_id=1, source_target_pairs={{0,2},{1,3},{2,0},{3,1},{4,6},{5,7},{6,4},{7,5},{8,10},{9,11},{10,... | collective-permute-start | bytes 245768 | tf_op jit(solution)/shard_map/ppermute | solution.py:385
  120.7 6.3 %collective-permute-start.32 = (bf16[960,128]{1,0:T(8,128)(2,1)S(1)}, bf16[960,128]{1,0:T(8,128)(2,1)S(1)}, u32[]{:S(2)}, u32[]{:S(2)}) collective-permute-start(bf16[960,128]{1,0:T(8,128)(2,1)S(1)} %pad_maximum_fusion.1), channel_id=1, source_target_pairs={{0,2},{1,3},{2,0},{3,1},{4,6},{5,7},{6,4},{7,5},{8,10},{9,11},{10,... | collective-permute-start | bytes 737288 | tf_op jit(solution)/shard_map/ppermute | solution.py:385
  122.4 4.6 %collective-permute-start.33 = (bf16[1600,128]{1,0:T(8,128)(2,1)S(1)}, bf16[1600,128]{1,0:T(8,128)(2,1)S(1)}, u32[]{:S(2)}, u32[]{:S(2)}) collective-permute-start(bf16[1600,128]{1,0:T(8,128)(2,1)S(1)} %constant_dynamic-update-slice_fusion.10.refs_0_), channel_id=1, source_target_pairs={{0,1},{1,0},{2,3},{3,2},{4,5},{5,4},{6,7},{7,6},{8,9},{9,8},{10,11... | collective-permute-start | bytes 1228808 | tf_op jit(solution)/shard_map/ppermute | solution.py:385
  140.7 3.5 %collective-permute-start.35 = (bf16[2048,128]{1,0:T(8,128)(2,1)S(1)}, bf16[2048,128]{1,0:T(8,128)(2,1)S(1)}, u32[]{:S(2)}, u32[]{:S(2)}) collective-permute-start(bf16[2048,128]{1,0:T(8,128)(2,1)S(1)} %get-tuple-element.44), channel_id=1, source_target_pairs={{0,1},{1,0},{2,3},{3,2},{4,5},{5,4},{6,7},{7,6},{8,9},{9,8},{10,11... | collective-permute-start | bytes 1572872 | tf_op jit(solution)/shard_map/ppermute | solution.py:385
  142.6 9.2 %collective-permute-start.37 = (bf16[2048,128]{1,0:T(8,128)(2,1)S(1)}, bf16[2048,128]{1,0:T(8,128)(2,1)S(1)}, u32[]{:S(2)}, u32[]{:S(2)}) collective-permute-start(bf16[2048,128]{1,0:T(8,128)(2,1)S(1)} %add_convert_fusion), channel_id=1, source_target_pairs={{0,2},{1,5},{2,0},{3,7},{4,6},{5,1},{6,4},{7,3},{8,10},{9,13},{10,... | collective-permute-start | bytes 1572872 | tf_op jit(solution)/shard_map/ppermute | solution.py:385
  152.1 9.2 %collective-permute-start.38 = (bf16[1024,128]{1,0:T(8,128)(2,1)S(1)}, bf16[1024,128]{1,0:T(8,128)(2,1)S(1)}, u32[]{:S(2)}, u32[]{:S(2)}) collective-permute-start(bf16[1024,128]{1,0:T(8,128)(2,1)S(1)} %slice.160), channel_id=1, source_target_pairs={{0,4},{1,9},{2,6},{3,11},{4,0},{5,13},{6,2},{7,15},{8,12},{9,1},{1... | collective-permute-start | bytes 786440 | tf_op jit(solution)/shard_map/ppermute | solution.py:385
  161.3 7.1 %collective-permute-start.39 = (bf16[512,128]{1,0:T(8,128)(2,1)S(1)}, bf16[512,128]{1,0:T(8,128)(2,1)S(1)}, u32[]{:S(2)}, u32[]{:S(2)}) collective-permute-start(bf16[512,128]{1,0:T(8,128)(2,1)S(1)} %slice.161), channel_id=1, source_target_pairs={{0,8},{1,3},{2,10},{3,1},{4,12},{5,7},{6,14},{7,5},{8,0},{9,11},{1... | collective-permute-start | bytes 393224 | tf_op jit(solution)/shard_map/ppermute | solution.py:385
  (9 other events, 18.5 us)

commit v12 on v11

--- a/solution.py
+++ b/solution.py
@@ -79,7 +79,9 @@
         _, group, live = group_at(index, seq, order, counts)
 
         def start_slot(slot, carry):
-            ids[offset + slot] = support[group, slot]
+            block = support[group, slot]
+            ids[offset + slot] = block
+            fetch(offset + slot, block).start()
             return carry
 
         lax.fori_loop(jnp.clip(-offset, 0, live), jnp.clip(entries - offset, 0, live), start_slot, 0)
@@ -87,17 +89,6 @@
 
     lax.fori_loop(0, groups, start_group, jnp.int32(-begin))
     steps = pairs // SUPPORT_STEP
-
-    def start_step(step):
-        for entry in range(2 * SUPPORT_STEP):
-            index = 2 * SUPPORT_STEP * step + entry
-            fetch(index, ids[index]).start()
-
-    def start_all(step, carry):
-        start_step(step)
-        return carry
-
-    lax.fori_loop(0, steps, start_all, 0)
     shape = (2 * LANES, LANES)
     source = lax.broadcasted_iota(jnp.int32, shape, 0)
     target = lax.broadcasted_iota(jnp.int32, shape, 1)
@@ -420,16 +411,23 @@
 
 
 def last_reduce(keep, *send):
+    devices = lax.axis_size("rows")
+    even, odd = last_orders(devices)
     near, other = add_cores(keep, *send)
-    for even, odd in list(zip(*last_orders(lax.axis_size("rows"))))[1:]:
-        total = near + exchange(other.astype(jnp.bfloat16), even, odd).astype(jnp.float32)
-        near, other = total[: total.shape[0] // 2], total[total.shape[0] // 2 :]
+    sums = near + exchange(other.astype(jnp.bfloat16), even[1], odd[1]).astype(jnp.float32)
+    size = 2 * keep.shape[0] // devices
+    sent = sums.astype(jnp.bfloat16)
+    total = sums[:size]
+    for slot in range(1, devices // 4):
+        share = sent[slot * size : (slot + 1) * size]
+        total = total + exchange(share, slot_distance(slot, even[2:]), slot_distance(slot, odd[2:])).astype(jnp.float32)
     return total
 
 
 def packed_order(live):
     index = jnp.arange(live.shape[0])
-    ahead = (live[None, :] < live[:, None]) | ((live[None, :] == live[:, None]) & (index[None, :] < index[:, None]))
+    key = (live + live % 2 * (SLOTS + 1)) * live.shape[0] + index
+    ahead = key[None, :] < key[:, None]
     rank = jnp.sum(ahead.astype(jnp.int32), axis=1)
     return jnp.sum(jnp.where(rank[:, None] == index[None, :], index[:, None], 0), axis=0).astype(jnp.int32)
 

time: 169 us -> 166 us (0.982); the launches traced: 170 us -> 164 us
  starting transfers between devices: 46.8 us -> 44 us
  Pallas kernels: 52.8 us -> 50.4 us
    ppermute x40 -> x41, starting transfers between devices: 46.8 us -> 44 us  [exchange(): lax.ppermute(value, 'rows', [(i, i ^ apart[i % 2]) for i in range(devices)])]
    ppermute x40 -> x41, waiting for transfers between devices: 61.1 us -> 60.9 us  [exchange(): lax.ppermute(value, 'rows', [(i, i ^ apart[i % 2]) for i in range(devices)])]
  transfers between devices with their start and end apart: 40 -> 41, of which waited for: 21 -> 21; matrix products, arithmetic and copies ran while one was open for 3% -> 3% of each run, Pallas kernels for 11% -> 11%
where the time goes in v12:
time: 166 us; the launch traced here: 164 us
  waiting for transfers between devices  60.9 us (37%)
  Pallas kernels  50.4 us (30%)
  starting transfers between devices  44 us (27%)
  local copies, waits for them, and re-layouts  6.4 us (4%)
  other arithmetic  2.29 us (1%)
    ppermute x41, waiting for transfers between devices, exchange(): lax.ppermute(value, 'rows', [(i, i ^ apart[i % 2]) for i in range(devices)])  60.9 us
    ppermute x41, starting transfers between devices, exchange(): lax.ppermute(value, 'rows', [(i, i ^ apart[i % 2]) for i in range(devices)])  44 us
    pallas_call x3, Pallas kernels, gradient_call(): pl.pallas_call(functools.partial(gradient_kernel, mode, shards, pairs, gr...  33 us
    pallas_call x2, Pallas kernels, collect_support(): pl.pallas_call(functools.partial(support_kernel, part * entries, groups),...  17.3 us
  transfers between devices with their start and end apart: 41, of which 21 were waited for; matrix products, arithmetic and copies ran while one was open for 3% of the time, Pallas kernels for 11%

profile of v12, /device:TPU:0, one launch (start us, length us, event | category | flops | bytes accessed | tf_op | source)
XLA Modules:
  0.0 164.4 jit_solution(6446047353391536294)
XLA Ops:
  1.6 4.1 %collective-permute-start = (bf16[512,128]{1,0:T(8,128)(2,1)S(1)}, bf16[512,128]{1,0:T(8,128)(2,1)S(1)}, u32[]{:S(2)}, u32[]{:S(2)}) collective-permute-start(bf16[512,128]{1,0:T(8,128)(2,1)S(1)} %reshape.71), channel_id=1, source_target_pairs={{0,8},{1,9},{2,10},{3,11},{4,12},{5,13},{6,14},{7,15},{8,0},{9,1},... | collective-permute-start | bytes 393224 | tf_op jit(solution)/shard_map/ppermute | solution.py:376
  5.7 1.6 collective-permute-start.1
  7.3 1.7 %collective-permute-start.3 = (bf16[512,128]{1,0:T(8,128)(2,1)S(1)}, bf16[512,128]{1,0:T(8,128)(2,1)S(1)}, u32[]{:S(2)}, u32[]{:S(2)}) collective-permute-start(bf16[512,128]{1,0:T(8,128)(2,1)S(1)} %reshape.71), channel_id=1, source_target_pairs={{0,2},{1,3},{2,0},{3,1},{4,6},{5,7},{6,4},{7,5},{8,10},{9,11},{10,... | collective-permute-start | bytes 393224 | tf_op jit(solution)/shard_map/ppermute | solution.py:376
  11.7 8.5 %collect_support.2.refs_0_ = bf16[520,512,128]{2,1,0:T(8,128)(2,1)} custom-call(s32[305]{0:T(512)S(1)} %concatenate.18.scalars, bf16[512,32768]{1,0:T(8,128)(2,1)} %dictionary.3), custom_call_target="tpu_custom_call" | custom-call | bytes 31457280 | tf_op jit(solution)/shard_map/collect_support/pallas_call | solution.py:130
  20.8 8.8 %collect_support.3.blocks = bf16[520,512,128]{2,1,0:T(8,128)(2,1)} custom-call(s32[305]{0:T(512)S(1)} %concatenate.18.scalars, bf16[512,32768]{1,0:T(8,128)(2,1)} %dictionary.3, bf16[520,512,128]{2,1,0:T(8,128)(2,1)} %collect_support.2.refs_0_), custom_call_target="tpu_custom_call", output_to_operand_aliasing={{}: (2, {})} | custom-call | bytes 31457280 | tf_op jit(solution)/shard_map/collect_support/pallas_call | solution.py:130
  30.3 1.5 copy.13
  32.2 10.8 %gradient.3 = (f32[2560,128]{1,0:T(8,128)S(1)}, bf16[1600,128]{1,0:T(8,128)(2,1)S(1)}, bf16[960,128]{1,0:T(8,128)(2,1)S(1)}, bf16[320,128]{1,0:T(8,128)(2,1)S(1)}, f32[320,128]{1,0:T(8,128)S(1)}) custom-call(s32[305]{0:T(512)S(1)} %concatenate.18.scalars, bf16[520,512,128]{2,1,0:T(8,128)(2,1)} %collect_support.3.blocks, ...), custom_call_target="tpu_custom_call" | custom-call | flops 5368709120 | bytes 10485760 | tf_op jit(solution)/shard_map/gradient/pallas_call | solution.py:353
  44.7 1.5 collective-permute-start.9
  46.3 6.6 %collective-permute-done.9 = bf16[960,128]{1,0:T(8,128)(2,1)S(1)} collective-permute-done((bf16[960,128]{1,0:T(8,128)(2,1)S(1)}, bf16[960,128]{1,0:T(8,128)(2,1)S(1)}, u32[]{:S(2)}, u32[]{:S(2)}) %collective-permute-start.9) | collective-permute-done | bytes 245792 | tf_op jit(solution)/shard_map/ppermute | solution.py:376
  53.0 1.7 %collective-permute-start.11 = (bf16[320,128]{1,0:T(8,128)(2,1)S(1)}, bf16[320,128]{1,0:T(8,128)(2,1)S(1)}, u32[]{:S(2)}, u32[]{:S(2)}) collective-permute-start(bf16[320,128]{1,0:T(8,128)(2,1)S(1)} %get-tuple-element.59), channel_id=1, source_target_pairs={{0,8},{1,9},{2,10},{3,11},{4,12},{5,13},{6,14},{7,15},{8,0},{9,1},... | collective-permute-start | bytes 245768 | tf_op jit(solution)/shard_map/ppermute | solution.py:376
  54.7 2.5 %collective-permute-start.12 = (bf16[320,128]{1,0:T(8,128)(2,1)S(1)}, bf16[320,128]{1,0:T(8,128)(2,1)S(1)}, u32[]{:S(2)}, u32[]{:S(2)}) collective-permute-start(bf16[320,128]{1,0:T(8,128)(2,1)S(1)} %get-tuple-element.61), channel_id=1, source_target_pairs={{0,4},{1,5},{2,6},{3,7},{4,0},{5,1},{6,2},{7,3},{8,12},{9,13},{10,... | collective-permute-start | bytes 245768 | tf_op jit(solution)/shard_map/ppermute | solution.py:376
  60.1 3.4 %collective-permute-done.13 = bf16[320,128]{1,0:T(8,128)(2,1)S(1)} collective-permute-done((bf16[320,128]{1,0:T(8,128)(2,1)S(1)}, bf16[320,128]{1,0:T(8,128)(2,1)S(1)}, u32[]{:S(2)}, u32[]{:S(2)}) %collective-permute-start.13) | collective-permute-done | bytes 81952 | tf_op jit(solution)/shard_map/ppermute | solution.py:376
  63.5 1.5 collective-permute-start.14
  66.2 1.8 %collective-permute-start.16 = (bf16[320,128]{1,0:T(8,128)(2,1)S(1)}, bf16[320,128]{1,0:T(8,128)(2,1)S(1)}, u32[]{:S(2)}, u32[]{:S(2)}) collective-permute-start(bf16[320,128]{1,0:T(8,128)(2,1)S(1)} %get-tuple-element.52), channel_id=1, source_target_pairs={{0,12},{1,13},{2,14},{3,15},{4,8},{5,9},{6,10},{7,11},{8,4},{9,5},... | collective-permute-start | bytes 245768 | tf_op jit(solution)/shard_map/ppermute | solution.py:376
  69.4 1.6 collective-permute-done.14
  74.1 4.7 %collective-permute-done.18.refs_1_ = bf16[960,128]{1,0:T(8,128)(2,1)S(1)} collective-permute-done((bf16[960,128]{1,0:T(8,128)(2,1)S(1)}, bf16[960,128]{1,0:T(8,128)(2,1)S(1)}, u32[]{:S(2)}, u32[]{:S(2)}) %collective-permute-start.18) | collective-permute-done | bytes 245792 | tf_op jit(solution)/shard_map/ppermute | solution.py:376
  78.8 1.5 collective-permute-done.20.refs_3_
  80.3 10.5 %gradient.4 = (f32[2560,128]{1,0:T(8,128)S(1)}, bf16[1600,128]{1,0:T(8,128)(2,1)S(1)}, bf16[960,128]{1,0:T(8,128)(2,1)S(1)}) custom-call(s32[305]{0:T(512)S(1)} %concatenate.18.scalars, bf16[520,512,128]{2,1,0:T(8,128)(2,1)} %collect_support.3.blocks, bf16[1600,128]{1,0:T(8,128)(2,1)S(1)} %constant_dynamic-update-slice_fusion.5.refs_0_, ...), custom_call_target="tpu_custom_call" | custom-call | flops 5368709120 | bytes 10485760 | tf_op jit(solution)/shard_map/gradient/pallas_call | solution.py:353
  94.0 6.6 %collective-permute-done.23 = bf16[960,128]{1,0:T(8,128)(2,1)S(1)} collective-permute-done((bf16[960,128]{1,0:T(8,128)(2,1)S(1)}, bf16[960,128]{1,0:T(8,128)(2,1)S(1)}, u32[]{:S(2)}, u32[]{:S(2)}) %collective-permute-start.23) | collective-permute-done | bytes 245792 | tf_op jit(solution)/shard_map/ppermute | solution.py:376
  100.6 1.7 %collective-permute-start.25 = (bf16[320,128]{1,0:T(8,128)(2,1)S(1)}, bf16[320,128]{1,0:T(8,128)(2,1)S(1)}, u32[]{:S(2)}, u32[]{:S(2)}) collective-permute-start(bf16[320,128]{1,0:T(8,128)(2,1)S(1)} %get-tuple-element.56), channel_id=1, source_target_pairs={{0,8},{1,9},{2,10},{3,11},{4,12},{5,13},{6,14},{7,15},{8,0},{9,1},... | collective-permute-start | bytes 245768 | tf_op jit(solution)/shard_map/ppermute | solution.py:376
  103.1 2.0 %collective-permute-start.27 = (bf16[320,128]{1,0:T(8,128)(2,1)S(1)}, bf16[320,128]{1,0:T(8,128)(2,1)S(1)}, u32[]{:S(2)}, u32[]{:S(2)}) collective-permute-start(bf16[320,128]{1,0:T(8,128)(2,1)S(1)} %get-tuple-element.57), channel_id=1, source_target_pairs={{0,12},{1,13},{2,14},{3,15},{4,8},{5,9},{6,10},{7,11},{8,4},{9,5},... | collective-permute-start | bytes 245768 | tf_op jit(solution)/shard_map/ppermute | solution.py:376
  106.4 3.2 %collective-permute-done.25 = bf16[320,128]{1,0:T(8,128)(2,1)S(1)} collective-permute-done((bf16[320,128]{1,0:T(8,128)(2,1)S(1)}, bf16[320,128]{1,0:T(8,128)(2,1)S(1)}, u32[]{:S(2)}, u32[]{:S(2)}) %collective-permute-start.25) | collective-permute-done | bytes 81952 | tf_op jit(solution)/shard_map/ppermute | solution.py:376
  109.8 1.9 %collective-permute-start.28 = (bf16[320,128]{1,0:T(8,128)(2,1)S(1)}, bf16[320,128]{1,0:T(8,128)(2,1)S(1)}, u32[]{:S(2)}, u32[]{:S(2)}) collective-permute-start(bf16[320,128]{1,0:T(8,128)(2,1)S(1)} %get-tuple-element.50), channel_id=1, source_target_pairs={{0,8},{1,9},{2,10},{3,11},{4,12},{5,13},{6,14},{7,15},{8,0},{9,1},... | collective-permute-start | bytes 245768 | tf_op jit(solution)/shard_map/ppermute | solution.py:376
  112.3 2.0 %collective-permute-start.30 = (bf16[320,128]{1,0:T(8,128)(2,1)S(1)}, bf16[320,128]{1,0:T(8,128)(2,1)S(1)}, u32[]{:S(2)}, u32[]{:S(2)}) collective-permute-start(bf16[320,128]{1,0:T(8,128)(2,1)S(1)} %get-tuple-element.50), channel_id=1, source_target_pairs={{0,12},{1,13},{2,14},{3,15},{4,8},{5,9},{6,10},{7,11},{8,4},{9,5},... | collective-permute-start | bytes 245768 | tf_op jit(solution)/shard_map/ppermute | solution.py:376
  115.6 2.3 %collective-permute-done.28 = bf16[320,128]{1,0:T(8,128)(2,1)S(1)} collective-permute-done((bf16[320,128]{1,0:T(8,128)(2,1)S(1)}, bf16[320,128]{1,0:T(8,128)(2,1)S(1)}, u32[]{:S(2)}, u32[]{:S(2)}) %collective-permute-start.28) | collective-permute-done | bytes 81952 | tf_op jit(solution)/shard_map/ppermute | solution.py:376
  120.4 4.8 %collective-permute-done.32.refs_1_ = bf16[960,128]{1,0:T(8,128)(2,1)S(1)} collective-permute-done((bf16[960,128]{1,0:T(8,128)(2,1)S(1)}, bf16[960,128]{1,0:T(8,128)(2,1)S(1)}, u32[]{:S(2)}, u32[]{:S(2)}) %collective-permute-start.32) | collective-permute-done | bytes 245792 | tf_op jit(solution)/shard_map/ppermute | solution.py:376
  125.2 1.5 collective-permute-done.34.refs_3_
  126.8 11.7 %gradient.5 = (f32[4096,128]{1,0:T(8,128)S(1)}, bf16[2048,128]{1,0:T(8,128)(2,1)S(1)}, bf16[2048,128]{1,0:T(8,128)(2,1)S(1)}, bf16[8,64,128]{2,1,0:T(8,128)(2,1)S(1)}, f32[64,128]{1,0:T(8,128)S(1)}) custom-call(s32[305]{0:T(512)S(1)} %concatenate.18.scalars, bf16[520,512,128]{2,1,0:T(8,128)(2,1)} %collect_support.3.blocks, ...), custom_call_target="tpu_custom_call" | custom-call | flops 5368709120 | bytes 10485760 | tf_op jit(solution)/shard_map/gradient/pallas_call | solution.py:353
  141.8 8.0 %collective-permute-done.37 = bf16[2048,128]{1,0:T(8,128)(2,1)S(1)} collective-permute-done((bf16[2048,128]{1,0:T(8,128)(2,1)S(1)}, bf16[2048,128]{1,0:T(8,128)(2,1)S(1)}, u32[]{:S(2)}, u32[]{:S(2)}) %collective-permute-start.37) | collective-permute-done | bytes 524320 | tf_op jit(solution)/shard_map/ppermute | solution.py:376
  150.0 2.9 %collective-permute-start.38 = (bf16[512,128]{1,0:T(8,128)(2,1)S(1)}, bf16[512,128]{1,0:T(8,128)(2,1)S(1)}, u32[]{:S(2)}, u32[]{:S(2)}) collective-permute-start(bf16[512,128]{1,0:T(8,128)(2,1)S(1)} %get-tuple-element.53), channel_id=1, source_target_pairs={{0,8},{1,3},{2,10},{3,1},{4,12},{5,7},{6,14},{7,5},{8,0},{9,11},{1... | collective-permute-start | bytes 393224 | tf_op jit(solution)/shard_map/ppermute | solution.py:376
  152.9 1.6 collective-permute-start.40
  154.5 8.5 %collective-permute-done.38 = bf16[512,128]{1,0:T(8,128)(2,1)S(1)} collective-permute-done((bf16[512,128]{1,0:T(8,128)(2,1)S(1)}, bf16[512,128]{1,0:T(8,128)(2,1)S(1)}, u32[]{:S(2)}, u32[]{:S(2)}) %collective-permute-start.38) | collective-permute-done | bytes 131104 | tf_op jit(solution)/shard_map/ppermute | solution.py:376
  (106 shorter events, 31.0 us)
Async XLA Ops:
  1.6 18.7 %collective-permute-start = (bf16[512,128]{1,0:T(8,128)(2,1)S(1)}, bf16[512,128]{1,0:T(8,128)(2,1)S(1)}, u32[]{:S(2)}, u32[]{:S(2)}) collective-permute-start(bf16[512,128]{1,0:T(8,128)(2,1)S(1)} %reshape.71), channel_id=1, source_target_pairs={{0,8},{1,9},{2,10},{3,11},{4,12},{5,13},{6,14},{7,15},{8,0},{9,1},... | collective-permute-start | bytes 393224 | tf_op jit(solution)/shard_map/ppermute | solution.py:376
  5.7 14.6 %collective-permute-start.1 = (bf16[512,128]{1,0:T(8,128)(2,1)S(1)}, bf16[512,128]{1,0:T(8,128)(2,1)S(1)}, u32[]{:S(2)}, u32[]{:S(2)}) collective-permute-start(bf16[512,128]{1,0:T(8,128)(2,1)S(1)} %reshape.71), channel_id=1, source_target_pairs={{0,4},{1,5},{2,6},{3,7},{4,0},{5,1},{6,2},{7,3},{8,12},{9,13},{10,... | collective-permute-start | bytes 393224 | tf_op jit(solution)/shard_map/ppermute | solution.py:376
  7.3 13.1 %collective-permute-start.2 = (bf16[512,128]{1,0:T(8,128)(2,1)S(1)}, bf16[512,128]{1,0:T(8,128)(2,1)S(1)}, u32[]{:S(2)}, u32[]{:S(2)}) collective-permute-start(bf16[512,128]{1,0:T(8,128)(2,1)S(1)} %reshape.71), channel_id=1, source_target_pairs={{0,12},{1,13},{2,14},{3,15},{4,8},{5,9},{6,10},{7,11},{8,4},{9,5},... | collective-permute-start | bytes 393224 | tf_op jit(solution)/shard_map/ppermute | solution.py:376
  7.3 13.1 %collective-permute-start.3 = (bf16[512,128]{1,0:T(8,128)(2,1)S(1)}, bf16[512,128]{1,0:T(8,128)(2,1)S(1)}, u32[]{:S(2)}, u32[]{:S(2)}) collective-permute-start(bf16[512,128]{1,0:T(8,128)(2,1)S(1)} %reshape.71), channel_id=1, source_target_pairs={{0,2},{1,3},{2,0},{3,1},{4,6},{5,7},{6,4},{7,5},{8,10},{9,11},{10,... | collective-permute-start | bytes 393224 | tf_op jit(solution)/shard_map/ppermute | solution.py:376
  20.5 9.9 %collective-permute-start.4 = (bf16[1536,128]{1,0:T(8,128)(2,1)S(1)}, bf16[1536,128]{1,0:T(8,128)(2,1)S(1)}, u32[]{:S(2)}, u32[]{:S(2)}) collective-permute-start(bf16[1536,128]{1,0:T(8,128)(2,1)S(1)} %slice.75), channel_id=1, source_target_pairs={{0,2},{1,3},{2,0},{3,1},{4,6},{5,7},{6,4},{7,5},{8,10},{9,11},{10,... | collective-permute-start | bytes 1179656 | tf_op jit(solution)/shard_map/ppermute | solution.py:376
  20.8 11.0 %collective-permute-start.5 = (bf16[2560,128]{1,0:T(8,128)(2,1)S(1)}, bf16[2560,128]{1,0:T(8,128)(2,1)S(1)}, u32[]{:S(2)}, u32[]{:S(2)}) collective-permute-start(bf16[2560,128]{1,0:T(8,128)(2,1)S(1)} %constant_dynamic-update-slice_fusion.refs_0_), channel_id=1, source_target_pairs={{0,1},{1,0},{2,3},{3,2},{4,5},{5,4},{6,7},{7,6},{8,9},{9,8},{10,11... | collective-permute-start | bytes 1966088 | tf_op jit(solution)/shard_map/ppermute | solution.py:376
  44.7 8.2 %collective-permute-start.9 = (bf16[960,128]{1,0:T(8,128)(2,1)S(1)}, bf16[960,128]{1,0:T(8,128)(2,1)S(1)}, u32[]{:S(2)}, u32[]{:S(2)}) collective-permute-start(bf16[960,128]{1,0:T(8,128)(2,1)S(1)} %add_convert_fusion.2), channel_id=1, source_target_pairs={{0,2},{1,3},{2,0},{3,1},{4,6},{5,7},{6,4},{7,5},{8,10},{9,11},{10,... | collective-permute-start | bytes 737288 | tf_op jit(solution)/shard_map/ppermute | solution.py:376
  53.0 7.0 %collective-permute-start.11 = (bf16[320,128]{1,0:T(8,128)(2,1)S(1)}, bf16[320,128]{1,0:T(8,128)(2,1)S(1)}, u32[]{:S(2)}, u32[]{:S(2)}) collective-permute-start(bf16[320,128]{1,0:T(8,128)(2,1)S(1)} %get-tuple-element.59), channel_id=1, source_target_pairs={{0,8},{1,9},{2,10},{3,11},{4,12},{5,13},{6,14},{7,15},{8,0},{9,1},... | collective-permute-start | bytes 245768 | tf_op jit(solution)/shard_map/ppermute | solution.py:376
  54.7 5.3 %collective-permute-start.12 = (bf16[320,128]{1,0:T(8,128)(2,1)S(1)}, bf16[320,128]{1,0:T(8,128)(2,1)S(1)}, u32[]{:S(2)}, u32[]{:S(2)}) collective-permute-start(bf16[320,128]{1,0:T(8,128)(2,1)S(1)} %get-tuple-element.61), channel_id=1, source_target_pairs={{0,4},{1,5},{2,6},{3,7},{4,0},{5,1},{6,2},{7,3},{8,12},{9,13},{10,... | collective-permute-start | bytes 245768 | tf_op jit(solution)/shard_map/ppermute | solution.py:376
  57.2 6.2 %collective-permute-start.13 = (bf16[320,128]{1,0:T(8,128)(2,1)S(1)}, bf16[320,128]{1,0:T(8,128)(2,1)S(1)}, u32[]{:S(2)}, u32[]{:S(2)}) collective-permute-start(bf16[320,128]{1,0:T(8,128)(2,1)S(1)} %get-tuple-element.60), channel_id=1, source_target_pairs={{0,12},{1,13},{2,14},{3,15},{4,8},{5,9},{6,10},{7,11},{8,4},{9,5},... | collective-permute-start | bytes 245768 | tf_op jit(solution)/shard_map/ppermute | solution.py:376
  57.5 5.9 %collective-permute-start.10 = (bf16[320,128]{1,0:T(8,128)(2,1)S(1)}, bf16[320,128]{1,0:T(8,128)(2,1)S(1)}, u32[]{:S(2)}, u32[]{:S(2)}) collective-permute-start(bf16[320,128]{1,0:T(8,128)(2,1)S(1)} %slice.160), channel_id=1, source_target_pairs={{0,2},{1,3},{2,0},{3,1},{4,6},{5,7},{6,4},{7,5},{8,10},{9,11},{10,... | collective-permute-start | bytes 245768 | tf_op jit(solution)/shard_map/ppermute | solution.py:376
  63.5 7.4 %collective-permute-start.14 = (bf16[320,128]{1,0:T(8,128)(2,1)S(1)}, bf16[320,128]{1,0:T(8,128)(2,1)S(1)}, u32[]{:S(2)}, u32[]{:S(2)}) collective-permute-start(bf16[320,128]{1,0:T(8,128)(2,1)S(1)} %get-tuple-element.52), channel_id=1, source_target_pairs={{0,8},{1,9},{2,10},{3,11},{4,12},{5,13},{6,14},{7,15},{8,0},{9,1},... | collective-permute-start | bytes 245768 | tf_op jit(solution)/shard_map/ppermute | solution.py:376
  65.0 6.1 %collective-permute-start.15 = (bf16[320,128]{1,0:T(8,128)(2,1)S(1)}, bf16[320,128]{1,0:T(8,128)(2,1)S(1)}, u32[]{:S(2)}, u32[]{:S(2)}) collective-permute-start(bf16[320,128]{1,0:T(8,128)(2,1)S(1)} %get-tuple-element.52), channel_id=1, source_target_pairs={{0,4},{1,5},{2,6},{3,7},{4,0},{5,1},{6,2},{7,3},{8,12},{9,13},{10,... | collective-permute-start | bytes 245768 | tf_op jit(solution)/shard_map/ppermute | solution.py:376
  66.2 6.3 %collective-permute-start.16 = (bf16[320,128]{1,0:T(8,128)(2,1)S(1)}, bf16[320,128]{1,0:T(8,128)(2,1)S(1)}, u32[]{:S(2)}, u32[]{:S(2)}) collective-permute-start(bf16[320,128]{1,0:T(8,128)(2,1)S(1)} %get-tuple-element.52), channel_id=1, source_target_pairs={{0,12},{1,13},{2,14},{3,15},{4,8},{5,9},{6,10},{7,11},{8,4},{9,5},... | collective-permute-start | bytes 245768 | tf_op jit(solution)/shard_map/ppermute | solution.py:376
  68.0 6.0 %collective-permute-start.17 = (bf16[320,128]{1,0:T(8,128)(2,1)S(1)}, bf16[320,128]{1,0:T(8,128)(2,1)S(1)}, u32[]{:S(2)}, u32[]{:S(2)}) collective-permute-start(bf16[320,128]{1,0:T(8,128)(2,1)S(1)} %get-tuple-element.52), channel_id=1, source_target_pairs={{0,2},{1,3},{2,0},{3,1},{4,6},{5,7},{6,4},{7,5},{8,10},{9,11},{10,... | collective-permute-start | bytes 245768 | tf_op jit(solution)/shard_map/ppermute | solution.py:376
  72.5 6.3 %collective-permute-start.18 = (bf16[960,128]{1,0:T(8,128)(2,1)S(1)}, bf16[960,128]{1,0:T(8,128)(2,1)S(1)}, u32[]{:S(2)}, u32[]{:S(2)}) collective-permute-start(bf16[960,128]{1,0:T(8,128)(2,1)S(1)} %pad_maximum_fusion), channel_id=1, source_target_pairs={{0,2},{1,3},{2,0},{3,1},{4,6},{5,7},{6,4},{7,5},{8,10},{9,11},{10,... | collective-permute-start | bytes 737288 | tf_op jit(solution)/shard_map/ppermute | solution.py:376
  74.0 4.8 %collective-permute-start.19 = (bf16[1600,128]{1,0:T(8,128)(2,1)S(1)}, bf16[1600,128]{1,0:T(8,128)(2,1)S(1)}, u32[]{:S(2)}, u32[]{:S(2)}) collective-permute-start(bf16[1600,128]{1,0:T(8,128)(2,1)S(1)} %constant_dynamic-update-slice_fusion.5.refs_0_), channel_id=1, source_target_pairs={{0,1},{1,0},{2,3},{3,2},{4,5},{5,4},{6,7},{7,6},{8,9},{9,8},{10,11... | collective-permute-start | bytes 1228808 | tf_op jit(solution)/shard_map/ppermute | solution.py:376
  92.5 8.1 %collective-permute-start.23 = (bf16[960,128]{1,0:T(8,128)(2,1)S(1)}, bf16[960,128]{1,0:T(8,128)(2,1)S(1)}, u32[]{:S(2)}, u32[]{:S(2)}) collective-permute-start(bf16[960,128]{1,0:T(8,128)(2,1)S(1)} %add_convert_fusion.1), channel_id=1, source_target_pairs={{0,2},{1,3},{2,0},{3,1},{4,6},{5,7},{6,4},{7,5},{8,10},{9,11},{10,... | collective-permute-start | bytes 737288 | tf_op jit(solution)/shard_map/ppermute | solution.py:376
  100.6 9.0 %collective-permute-start.25 = (bf16[320,128]{1,0:T(8,128)(2,1)S(1)}, bf16[320,128]{1,0:T(8,128)(2,1)S(1)}, u32[]{:S(2)}, u32[]{:S(2)}) collective-permute-start(bf16[320,128]{1,0:T(8,128)(2,1)S(1)} %get-tuple-element.56), channel_id=1, source_target_pairs={{0,8},{1,9},{2,10},{3,11},{4,12},{5,13},{6,14},{7,15},{8,0},{9,1},... | collective-permute-start | bytes 245768 | tf_op jit(solution)/shard_map/ppermute | solution.py:376
  102.3 7.3 %collective-permute-start.26 = (bf16[320,128]{1,0:T(8,128)(2,1)S(1)}, bf16[320,128]{1,0:T(8,128)(2,1)S(1)}, u32[]{:S(2)}, u32[]{:S(2)}) collective-permute-start(bf16[320,128]{1,0:T(8,128)(2,1)S(1)} %get-tuple-element.58), channel_id=1, source_target_pairs={{0,4},{1,5},{2,6},{3,7},{4,0},{5,1},{6,2},{7,3},{8,12},{9,13},{10,... | collective-permute-start | bytes 245768 | tf_op jit(solution)/shard_map/ppermute | solution.py:376
  103.1 6.6 %collective-permute-start.27 = (bf16[320,128]{1,0:T(8,128)(2,1)S(1)}, bf16[320,128]{1,0:T(8,128)(2,1)S(1)}, u32[]{:S(2)}, u32[]{:S(2)}) collective-permute-start(bf16[320,128]{1,0:T(8,128)(2,1)S(1)} %get-tuple-element.57), channel_id=1, source_target_pairs={{0,12},{1,13},{2,14},{3,15},{4,8},{5,9},{6,10},{7,11},{8,4},{9,5},... | collective-permute-start | bytes 245768 | tf_op jit(solution)/shard_map/ppermute | solution.py:376
  105.1 4.5 %collective-permute-start.24 = (bf16[320,128]{1,0:T(8,128)(2,1)S(1)}, bf16[320,128]{1,0:T(8,128)(2,1)S(1)}, u32[]{:S(2)}, u32[]{:S(2)}) collective-permute-start(bf16[320,128]{1,0:T(8,128)(2,1)S(1)} %slice.159), channel_id=1, source_target_pairs={{0,2},{1,3},{2,0},{3,1},{4,6},{5,7},{6,4},{7,5},{8,10},{9,11},{10,... | collective-permute-start | bytes 245768 | tf_op jit(solution)/shard_map/ppermute | solution.py:376
  109.8 8.1 %collective-permute-start.28 = (bf16[320,128]{1,0:T(8,128)(2,1)S(1)}, bf16[320,128]{1,0:T(8,128)(2,1)S(1)}, u32[]{:S(2)}, u32[]{:S(2)}) collective-permute-start(bf16[320,128]{1,0:T(8,128)(2,1)S(1)} %get-tuple-element.50), channel_id=1, source_target_pairs={{0,8},{1,9},{2,10},{3,11},{4,12},{5,13},{6,14},{7,15},{8,0},{9,1},... | collective-permute-start | bytes 245768 | tf_op jit(solution)/shard_map/ppermute | solution.py:376
  111.7 6.2 %collective-permute-start.29 = (bf16[320,128]{1,0:T(8,128)(2,1)S(1)}, bf16[320,128]{1,0:T(8,128)(2,1)S(1)}, u32[]{:S(2)}, u32[]{:S(2)}) collective-permute-start(bf16[320,128]{1,0:T(8,128)(2,1)S(1)} %get-tuple-element.50), channel_id=1, source_target_pairs={{0,4},{1,5},{2,6},{3,7},{4,0},{5,1},{6,2},{7,3},{8,12},{9,13},{10,... | collective-permute-start | bytes 245768 | tf_op jit(solution)/shard_map/ppermute | solution.py:376
  112.3 6.7 %collective-permute-start.30 = (bf16[320,128]{1,0:T(8,128)(2,1)S(1)}, bf16[320,128]{1,0:T(8,128)(2,1)S(1)}, u32[]{:S(2)}, u32[]{:S(2)}) collective-permute-start(bf16[320,128]{1,0:T(8,128)(2,1)S(1)} %get-tuple-element.50), channel_id=1, source_target_pairs={{0,12},{1,13},{2,14},{3,15},{4,8},{5,9},{6,10},{7,11},{8,4},{9,5},... | collective-permute-start | bytes 245768 | tf_op jit(solution)/shard_map/ppermute | solution.py:376
  114.3 6.0 %collective-permute-start.31 = (bf16[320,128]{1,0:T(8,128)(2,1)S(1)}, bf16[320,128]{1,0:T(8,128)(2,1)S(1)}, u32[]{:S(2)}, u32[]{:S(2)}) collective-permute-start(bf16[320,128]{1,0:T(8,128)(2,1)S(1)} %get-tuple-element.50), channel_id=1, source_target_pairs={{0,2},{1,3},{2,0},{3,1},{4,6},{5,7},{6,4},{7,5},{8,10},{9,11},{10,... | collective-permute-start | bytes 245768 | tf_op jit(solution)/shard_map/ppermute | solution.py:376
  119.0 6.3 %collective-permute-start.32 = (bf16[960,128]{1,0:T(8,128)(2,1)S(1)}, bf16[960,128]{1,0:T(8,128)(2,1)S(1)}, u32[]{:S(2)}, u32[]{:S(2)}) collective-permute-start(bf16[960,128]{1,0:T(8,128)(2,1)S(1)} %pad_maximum_fusion.1), channel_id=1, source_target_pairs={{0,2},{1,3},{2,0},{3,1},{4,6},{5,7},{6,4},{7,5},{8,10},{9,11},{10,... | collective-permute-start | bytes 737288 | tf_op jit(solution)/shard_map/ppermute | solution.py:376
  120.3 4.9 %collective-permute-start.33 = (bf16[1600,128]{1,0:T(8,128)(2,1)S(1)}, bf16[1600,128]{1,0:T(8,128)(2,1)S(1)}, u32[]{:S(2)}, u32[]{:S(2)}) collective-permute-start(bf16[1600,128]{1,0:T(8,128)(2,1)S(1)} %constant_dynamic-update-slice_fusion.10.refs_0_), channel_id=1, source_target_pairs={{0,1},{1,0},{2,3},{3,2},{4,5},{5,4},{6,7},{7,6},{8,9},{9,8},{10,11... | collective-permute-start | bytes 1228808 | tf_op jit(solution)/shard_map/ppermute | solution.py:376
  140.6 9.2 %collective-permute-start.37 = (bf16[2048,128]{1,0:T(8,128)(2,1)S(1)}, bf16[2048,128]{1,0:T(8,128)(2,1)S(1)}, u32[]{:S(2)}, u32[]{:S(2)}) collective-permute-start(bf16[2048,128]{1,0:T(8,128)(2,1)S(1)} %add_convert_fusion), channel_id=1, source_target_pairs={{0,2},{1,5},{2,0},{3,7},{4,6},{5,1},{6,4},{7,3},{8,10},{9,13},{10,... | collective-permute-start | bytes 1572872 | tf_op jit(solution)/shard_map/ppermute | solution.py:376
  150.0 13.0 %collective-permute-start.38 = (bf16[512,128]{1,0:T(8,128)(2,1)S(1)}, bf16[512,128]{1,0:T(8,128)(2,1)S(1)}, u32[]{:S(2)}, u32[]{:S(2)}) collective-permute-start(bf16[512,128]{1,0:T(8,128)(2,1)S(1)} %get-tuple-element.53), channel_id=1, source_target_pairs={{0,8},{1,3},{2,10},{3,1},{4,12},{5,7},{6,14},{7,5},{8,0},{9,11},{1... | collective-permute-start | bytes 393224 | tf_op jit(solution)/shard_map/ppermute | solution.py:376
  152.9 10.1 %collective-permute-start.39 = (bf16[512,128]{1,0:T(8,128)(2,1)S(1)}, bf16[512,128]{1,0:T(8,128)(2,1)S(1)}, u32[]{:S(2)}, u32[]{:S(2)}) collective-permute-start(bf16[512,128]{1,0:T(8,128)(2,1)S(1)} %get-tuple-element.55), channel_id=1, source_target_pairs={{0,4},{1,9},{2,6},{3,11},{4,0},{5,13},{6,2},{7,15},{8,12},{9,1},{1... | collective-permute-start | bytes 393224 | tf_op jit(solution)/shard_map/ppermute | solution.py:376
  152.9 10.1 %collective-permute-start.40 = (bf16[512,128]{1,0:T(8,128)(2,1)S(1)}, bf16[512,128]{1,0:T(8,128)(2,1)S(1)}, u32[]{:S(2)}, u32[]{:S(2)}) collective-permute-start(bf16[512,128]{1,0:T(8,128)(2,1)S(1)} %get-tuple-element.54), channel_id=1, source_target_pairs={{0,12},{1,11},{2,14},{3,9},{4,8},{5,15},{6,10},{7,13},{8,4},{9,3},... | collective-permute-start | bytes 393224 | tf_op jit(solution)/shard_map/ppermute | solution.py:376
  (10 other events, 20.8 us)

commit v13 on v12

--- a/solution.py
+++ b/solution.py
@@ -154,7 +154,7 @@
     return [2**bit for bit in range(devices.bit_length() - 1)]
 
 
-def last_orders(devices):
+def reduce_orders(devices):
     distances = stage_distances(devices)
     return distances, distances[:1] + distances[2:] + distances[1:2]
 
@@ -196,8 +196,8 @@
     def shard_span(slot, size):
         return pl.ds(pl.multiple_of((slot_distance(slot, distances) ^ me) * size, ROW_TILE), size)
 
-    def last_holder(slot):
-        even, odd = (slot_distance(slot, order) for order in last_orders(shards))
+    def reduce_holder(slot):
+        even, odd = (slot_distance(slot, order) for order in reduce_orders(shards))
         if slot >= shards // 2:
             even, odd = odd, even
         return jnp.where(me % 2 == 0, even, odd) ^ me
@@ -310,7 +310,7 @@
     if mode != "final":
         size = 2 * keep.shape[0] // shards
         for slot in range(shards):
-            put(slot, size, 0, total[shard_span(slot, size), :])
+            put(slot, size, 0, total[pl.ds(pl.multiple_of(reduce_holder(slot) * size, ROW_TILE), size), :])
     if mode == "first":
         size = start_out.shape[0]
         span = pl.ds(pl.multiple_of(me * size, ROW_TILE), size)
@@ -323,7 +323,7 @@
             sent[pair] = part
         thresh_out[...] = thresh[order[me]]
         for slot in range(shards):
-            position = last_holder(slot)
+            position = reduce_holder(slot)
             offset = offsets[position]
             live = counts[order[position]]
             parts = [total[tile(offset // 2 + pair), :] for pair in range(SLOT_PAIRS + 1)]
@@ -339,8 +339,7 @@
     packed = (places * PATCHES, LANES)
     half_out = (groups * SLOT_PAIRS if mode == "final" else pairs) * PATCHES // 2
     shard = (2 * half_out // shards, LANES)
-    ahead = half_out // 2 + (0 if mode == "final" else shard[0])
-    outs = [((half_out, LANES), double), ((ahead, LANES), single), ((half_out - ahead, LANES), single)]
+    outs = [((half_out, LANES), double)] + [((half_out // 2, LANES), single)] * 2
     if mode == "first":
         outs += [(shard, single), (shard, double)]
     if mode == "final":
@@ -398,21 +397,7 @@
 
 def reduce_shards(keep, *send):
     devices = lax.axis_size("rows")
-    _, row, *columns = stage_distances(devices)
-    size = 2 * keep.shape[0] // devices
-    near, other = add_cores(keep, *send)
-    sums = near[size:-size] + exchange(other.astype(jnp.bfloat16), row).astype(jnp.float32)
-    last, sums = lax.optimization_barrier((near[-size:].astype(jnp.bfloat16), sums.astype(jnp.bfloat16)))
-    total = near[:size] + exchange(last, row).astype(jnp.float32)
-    for slot in range(1, devices // 4):
-        share = exchange(sums[(slot - 1) * size : slot * size], slot_distance(slot, columns))
-        total = total + share.astype(jnp.float32)
-    return total
-
-
-def last_reduce(keep, *send):
-    devices = lax.axis_size("rows")
-    even, odd = last_orders(devices)
+    even, odd = reduce_orders(devices)
     near, other = add_cores(keep, *send)
     sums = near + exchange(other.astype(jnp.bfloat16), even[1], odd[1]).astype(jnp.float32)
     size = 2 * keep.shape[0] // devices
@@ -468,7 +453,7 @@
         previous = current
         gathered, _ = gather_shards(point.astype(jnp.bfloat16))
     *shares, sent, thresh = run("final", gathered=gathered, extra=(thresh_tiles,))
-    gradient = last_reduce(*shares).reshape(SLOT_PAIRS, PATCHES, LANES)
+    gradient = reduce_shards(*shares).reshape(SLOT_PAIRS, PATCHES, LANES)
     sent = sent.astype(jnp.float32)
     result = shrink(sent - 0.5 * gradient, thresh[None])
     result = result.reshape(SLOT_PAIRS, PATCHES, 2, BLOCK).transpose(0, 2, 1, 3)

time: 166 us -> 169 us (1.018)
  waiting for transfers between devices: 60.9 us -> 69.6 us
  starting transfers between devices: 44 us -> 39.1 us
    ppermute x41 -> x39, waiting for transfers between devices: 60.9 us -> 69.6 us  [exchange(): lax.ppermute(value, 'rows', [(i, i ^ apart[i % 2]) for i in range(devices)])]
    ppermute x41 -> x39, starting transfers between devices: 44 us -> 39.1 us  [exchange(): lax.ppermute(value, 'rows', [(i, i ^ apart[i % 2]) for i in range(devices)])]
  transfers between devices with their start and end apart: 41 -> 39, of which waited for: 21 -> 21; matrix products, arithmetic and copies ran while one was open for 3% -> 3% of each run, Pallas kernels for 11% -> 10%
where the time goes in v13:
time: 169 us; the launch traced here: 167 us
  waiting for transfers between devices  69.6 us (41%)
  Pallas kernels  49.7 us (29%)
  starting transfers between devices  39.1 us (23%)
  local copies, waits for them, and re-layouts  6.37 us (4%)
  other arithmetic  2.25 us (1%)
    ppermute x39, waiting for transfers between devices, exchange(): lax.ppermute(value, 'rows', [(i, i ^ apart[i % 2]) for i in range(devices)])  69.6 us
    ppermute x39, starting transfers between devices, exchange(): lax.ppermute(value, 'rows', [(i, i ^ apart[i % 2]) for i in range(devices)])  39.1 us
    pallas_call x3, Pallas kernels, gradient_call(): pl.pallas_call(functools.partial(gradient_kernel, mode, shards, pairs, gr...  32.4 us
    pallas_call x2, Pallas kernels, collect_support(): pl.pallas_call(functools.partial(support_kernel, part * entries, groups),...  17.3 us
  transfers between devices with their start and end apart: 39, of which 21 were waited for; matrix products, arithmetic and copies ran while one was open for 3% of the time, Pallas kernels for 10%

profile of v13, /device:TPU:0, one launch (start us, length us, event | category | flops | bytes accessed | tf_op | source)
XLA Modules:
  0.0 167.4 jit_solution(904710640244196974)
XLA Ops:
  1.6 4.1 %collective-permute-start = (bf16[512,128]{1,0:T(8,128)(2,1)S(1)}, bf16[512,128]{1,0:T(8,128)(2,1)S(1)}, u32[]{:S(2)}, u32[]{:S(2)}) collective-permute-start(bf16[512,128]{1,0:T(8,128)(2,1)S(1)} %reshape.71), channel_id=1, source_target_pairs={{0,8},{1,9},{2,10},{3,11},{4,12},{5,13},{6,14},{7,15},{8,0},{9,1},... | collective-permute-start | bytes 393224 | tf_op jit(solution)/shard_map/ppermute | solution.py:375
  5.7 1.6 collective-permute-start.1
  7.3 1.7 %collective-permute-start.3 = (bf16[512,128]{1,0:T(8,128)(2,1)S(1)}, bf16[512,128]{1,0:T(8,128)(2,1)S(1)}, u32[]{:S(2)}, u32[]{:S(2)}) collective-permute-start(bf16[512,128]{1,0:T(8,128)(2,1)S(1)} %reshape.71), channel_id=1, source_target_pairs={{0,2},{1,3},{2,0},{3,1},{4,6},{5,7},{6,4},{7,5},{8,10},{9,11},{10,... | collective-permute-start | bytes 393224 | tf_op jit(solution)/shard_map/ppermute | solution.py:375
  11.7 8.5 %collect_support.2.refs_0_ = bf16[520,512,128]{2,1,0:T(8,128)(2,1)} custom-call(s32[305]{0:T(512)S(1)} %concatenate.18.scalars, bf16[512,32768]{1,0:T(8,128)(2,1)} %dictionary.3), custom_call_target="tpu_custom_call" | custom-call | bytes 31457280 | tf_op jit(solution)/shard_map/collect_support/pallas_call | solution.py:130
  20.8 8.8 %collect_support.3.blocks = bf16[520,512,128]{2,1,0:T(8,128)(2,1)} custom-call(s32[305]{0:T(512)S(1)} %concatenate.18.scalars, bf16[512,32768]{1,0:T(8,128)(2,1)} %dictionary.3, bf16[520,512,128]{2,1,0:T(8,128)(2,1)} %collect_support.2.refs_0_), custom_call_target="tpu_custom_call", output_to_operand_aliasing={{}: (2, {})} | custom-call | bytes 31457280 | tf_op jit(solution)/shard_map/collect_support/pallas_call | solution.py:130
  32.2 10.6 %gradient.3 = (f32[2560,128]{1,0:T(8,128)S(1)}, bf16[1280,128]{1,0:T(8,128)(2,1)S(1)}, bf16[1280,128]{1,0:T(8,128)(2,1)S(1)}, bf16[320,128]{1,0:T(8,128)(2,1)S(1)}, f32[320,128]{1,0:T(8,128)S(1)}) custom-call(s32[305]{0:T(512)S(1)} %concatenate.18.scalars, bf16[520,512,128]{2,1,0:T(8,128)(2,1)} %collect_support.3.blocks, ...), custom_call_target="tpu_custom_call" | custom-call | flops 5368709120 | bytes 10485760 | tf_op jit(solution)/shard_map/gradient/pallas_call | solution.py:352
  44.6 1.5 collective-permute-start.9
  46.1 5.6 %collective-permute-done.9 = bf16[1280,128]{1,0:T(8,128)(2,1)S(1)} collective-permute-done((bf16[1280,128]{1,0:T(8,128)(2,1)S(1)}, bf16[1280,128]{1,0:T(8,128)(2,1)S(1)}, u32[]{:S(2)}, u32[]{:S(2)}) %collective-permute-start.9) | collective-permute-done | bytes 327712 | tf_op jit(solution)/shard_map/ppermute | solution.py:375
  51.8 1.7 %collective-permute-start.10 = (bf16[320,128]{1,0:T(8,128)(2,1)S(1)}, bf16[320,128]{1,0:T(8,128)(2,1)S(1)}, u32[]{:S(2)}, u32[]{:S(2)}) collective-permute-start(bf16[320,128]{1,0:T(8,128)(2,1)S(1)} %get-tuple-element.55), channel_id=1, source_target_pairs={{0,8},{1,3},{2,10},{3,1},{4,12},{5,7},{6,14},{7,5},{8,0},{9,11},{1... | collective-permute-start | bytes 245768 | tf_op jit(solution)/shard_map/ppermute | solution.py:375
  53.6 2.5 %collective-permute-start.11 = (bf16[320,128]{1,0:T(8,128)(2,1)S(1)}, bf16[320,128]{1,0:T(8,128)(2,1)S(1)}, u32[]{:S(2)}, u32[]{:S(2)}) collective-permute-start(bf16[320,128]{1,0:T(8,128)(2,1)S(1)} %get-tuple-element.57), channel_id=1, source_target_pairs={{0,4},{1,9},{2,6},{3,11},{4,0},{5,13},{6,2},{7,15},{8,12},{9,1},{1... | collective-permute-start | bytes 245768 | tf_op jit(solution)/shard_map/ppermute | solution.py:375
  56.3 4.4 %collective-permute-done.10 = bf16[320,128]{1,0:T(8,128)(2,1)S(1)} collective-permute-done((bf16[320,128]{1,0:T(8,128)(2,1)S(1)}, bf16[320,128]{1,0:T(8,128)(2,1)S(1)}, u32[]{:S(2)}, u32[]{:S(2)}) %collective-permute-start.10) | collective-permute-done | bytes 81952 | tf_op jit(solution)/shard_map/ppermute | solution.py:375
  60.7 1.7 %collective-permute-done.12 = bf16[320,128]{1,0:T(8,128)(2,1)S(1)} collective-permute-done((bf16[320,128]{1,0:T(8,128)(2,1)S(1)}, bf16[320,128]{1,0:T(8,128)(2,1)S(1)}, u32[]{:S(2)}, u32[]{:S(2)}) %collective-permute-start.12) | collective-permute-done | bytes 81952 | tf_op jit(solution)/shard_map/ppermute | solution.py:375
  62.5 2.8 %collective-permute-start.13 = (bf16[320,128]{1,0:T(8,128)(2,1)S(1)}, bf16[320,128]{1,0:T(8,128)(2,1)S(1)}, u32[]{:S(2)}, u32[]{:S(2)}) collective-permute-start(bf16[320,128]{1,0:T(8,128)(2,1)S(1)} %get-tuple-element.46), channel_id=1, source_target_pairs={{0,8},{1,9},{2,10},{3,11},{4,12},{5,13},{6,14},{7,15},{8,0},{9,1},... | collective-permute-start | bytes 245768 | tf_op jit(solution)/shard_map/ppermute | solution.py:375
  65.2 1.7 %collective-permute-start.15 = (bf16[320,128]{1,0:T(8,128)(2,1)S(1)}, bf16[320,128]{1,0:T(8,128)(2,1)S(1)}, u32[]{:S(2)}, u32[]{:S(2)}) collective-permute-start(bf16[320,128]{1,0:T(8,128)(2,1)S(1)} %get-tuple-element.46), channel_id=1, source_target_pairs={{0,12},{1,13},{2,14},{3,15},{4,8},{5,9},{6,10},{7,11},{8,4},{9,5},... | collective-permute-start | bytes 245768 | tf_op jit(solution)/shard_map/ppermute | solution.py:375
  68.4 2.0 %collective-permute-done.13 = bf16[320,128]{1,0:T(8,128)(2,1)S(1)} collective-permute-done((bf16[320,128]{1,0:T(8,128)(2,1)S(1)}, bf16[320,128]{1,0:T(8,128)(2,1)S(1)}, u32[]{:S(2)}, u32[]{:S(2)}) %collective-permute-start.13) | collective-permute-done | bytes 81952 | tf_op jit(solution)/shard_map/ppermute | solution.py:375
  70.4 2.1 %collective-permute-done.15 = bf16[320,128]{1,0:T(8,128)(2,1)S(1)} collective-permute-done((bf16[320,128]{1,0:T(8,128)(2,1)S(1)}, bf16[320,128]{1,0:T(8,128)(2,1)S(1)}, u32[]{:S(2)}, u32[]{:S(2)}) %collective-permute-start.15) | collective-permute-done | bytes 81952 | tf_op jit(solution)/shard_map/ppermute | solution.py:375
  73.6 6.9 %collective-permute-done.17.refs_1_ = bf16[960,128]{1,0:T(8,128)(2,1)S(1)} collective-permute-done((bf16[960,128]{1,0:T(8,128)(2,1)S(1)}, bf16[960,128]{1,0:T(8,128)(2,1)S(1)}, u32[]{:S(2)}, u32[]{:S(2)}) %collective-permute-start.17) | collective-permute-done | bytes 245792 | tf_op jit(solution)/shard_map/ppermute | solution.py:375
  81.9 10.3 %gradient.4 = (f32[2560,128]{1,0:T(8,128)S(1)}, bf16[1280,128]{1,0:T(8,128)(2,1)S(1)}, bf16[1280,128]{1,0:T(8,128)(2,1)S(1)}) custom-call(s32[305]{0:T(512)S(1)} %concatenate.18.scalars, bf16[520,512,128]{2,1,0:T(8,128)(2,1)} %collect_support.3.blocks, bf16[1600,128]{1,0:T(8,128)(2,1)S(1)} %constant_dynamic-update-slice_fusion.5.refs_0_, ...), custom_call_target="tpu_custom_call" | custom-call | flops 5368709120 | bytes 10485760 | tf_op jit(solution)/shard_map/gradient/pallas_call | solution.py:352
  95.0 6.2 %collective-permute-done.22 = bf16[1280,128]{1,0:T(8,128)(2,1)S(1)} collective-permute-done((bf16[1280,128]{1,0:T(8,128)(2,1)S(1)}, bf16[1280,128]{1,0:T(8,128)(2,1)S(1)}, u32[]{:S(2)}, u32[]{:S(2)}) %collective-permute-start.22) | collective-permute-done | bytes 327712 | tf_op jit(solution)/shard_map/ppermute | solution.py:375
  102.3 1.6 collective-permute-start.24
  103.9 1.8 %collective-permute-start.25 = (bf16[320,128]{1,0:T(8,128)(2,1)S(1)}, bf16[320,128]{1,0:T(8,128)(2,1)S(1)}, u32[]{:S(2)}, u32[]{:S(2)}) collective-permute-start(bf16[320,128]{1,0:T(8,128)(2,1)S(1)} %get-tuple-element.53), channel_id=1, source_target_pairs={{0,12},{1,11},{2,14},{3,9},{4,8},{5,15},{6,10},{7,13},{8,4},{9,3},... | collective-permute-start | bytes 245768 | tf_op jit(solution)/shard_map/ppermute | solution.py:375
  105.8 5.1 %collective-permute-done.23 = bf16[320,128]{1,0:T(8,128)(2,1)S(1)} collective-permute-done((bf16[320,128]{1,0:T(8,128)(2,1)S(1)}, bf16[320,128]{1,0:T(8,128)(2,1)S(1)}, u32[]{:S(2)}, u32[]{:S(2)}) %collective-permute-start.23) | collective-permute-done | bytes 81952 | tf_op jit(solution)/shard_map/ppermute | solution.py:375
  111.1 2.3 %collective-permute-start.26 = (bf16[320,128]{1,0:T(8,128)(2,1)S(1)}, bf16[320,128]{1,0:T(8,128)(2,1)S(1)}, u32[]{:S(2)}, u32[]{:S(2)}) collective-permute-start(bf16[320,128]{1,0:T(8,128)(2,1)S(1)} %get-tuple-element.42), channel_id=1, source_target_pairs={{0,8},{1,9},{2,10},{3,11},{4,12},{5,13},{6,14},{7,15},{8,0},{9,1},... | collective-permute-start | bytes 245768 | tf_op jit(solution)/shard_map/ppermute | solution.py:375
  113.6 1.9 %collective-permute-start.28 = (bf16[320,128]{1,0:T(8,128)(2,1)S(1)}, bf16[320,128]{1,0:T(8,128)(2,1)S(1)}, u32[]{:S(2)}, u32[]{:S(2)}) collective-permute-start(bf16[320,128]{1,0:T(8,128)(2,1)S(1)} %get-tuple-element.42), channel_id=1, source_target_pairs={{0,12},{1,13},{2,14},{3,15},{4,8},{5,9},{6,10},{7,11},{8,4},{9,5},... | collective-permute-start | bytes 245768 | tf_op jit(solution)/shard_map/ppermute | solution.py:375
  116.1 2.4 %collective-permute-done.26 = bf16[320,128]{1,0:T(8,128)(2,1)S(1)} collective-permute-done((bf16[320,128]{1,0:T(8,128)(2,1)S(1)}, bf16[320,128]{1,0:T(8,128)(2,1)S(1)}, u32[]{:S(2)}, u32[]{:S(2)}) %collective-permute-start.26) | collective-permute-done | bytes 81952 | tf_op jit(solution)/shard_map/ppermute | solution.py:375
  119.0 2.0 %collective-permute-done.28 = bf16[320,128]{1,0:T(8,128)(2,1)S(1)} collective-permute-done((bf16[320,128]{1,0:T(8,128)(2,1)S(1)}, bf16[320,128]{1,0:T(8,128)(2,1)S(1)}, u32[]{:S(2)}, u32[]{:S(2)}) %collective-permute-start.28) | collective-permute-done | bytes 81952 | tf_op jit(solution)/shard_map/ppermute | solution.py:375
  121.9 6.6 %collective-permute-done.30.refs_1_ = bf16[960,128]{1,0:T(8,128)(2,1)S(1)} collective-permute-done((bf16[960,128]{1,0:T(8,128)(2,1)S(1)}, bf16[960,128]{1,0:T(8,128)(2,1)S(1)}, u32[]{:S(2)}, u32[]{:S(2)}) %collective-permute-start.30) | collective-permute-done | bytes 245792 | tf_op jit(solution)/shard_map/ppermute | solution.py:375
  130.0 11.5 %gradient.5 = (f32[4096,128]{1,0:T(8,128)S(1)}, bf16[2048,128]{1,0:T(8,128)(2,1)S(1)}, bf16[2048,128]{1,0:T(8,128)(2,1)S(1)}, bf16[8,64,128]{2,1,0:T(8,128)(2,1)S(1)}, f32[64,128]{1,0:T(8,128)S(1)}) custom-call(s32[305]{0:T(512)S(1)} %concatenate.18.scalars, bf16[520,512,128]{2,1,0:T(8,128)(2,1)} %collect_support.3.blocks, ...), custom_call_target="tpu_custom_call" | custom-call | flops 5368709120 | bytes 10485760 | tf_op jit(solution)/shard_map/gradient/pallas_call | solution.py:352
  144.6 8.3 %collective-permute-done.35 = bf16[2048,128]{1,0:T(8,128)(2,1)S(1)} collective-permute-done((bf16[2048,128]{1,0:T(8,128)(2,1)S(1)}, bf16[2048,128]{1,0:T(8,128)(2,1)S(1)}, u32[]{:S(2)}, u32[]{:S(2)}) %collective-permute-start.35) | collective-permute-done | bytes 524320 | tf_op jit(solution)/shard_map/ppermute | solution.py:375
  153.1 2.7 %collective-permute-start.36 = (bf16[512,128]{1,0:T(8,128)(2,1)S(1)}, bf16[512,128]{1,0:T(8,128)(2,1)S(1)}, u32[]{:S(2)}, u32[]{:S(2)}) collective-permute-start(bf16[512,128]{1,0:T(8,128)(2,1)S(1)} %get-tuple-element.49), channel_id=1, source_target_pairs={{0,8},{1,3},{2,10},{3,1},{4,12},{5,7},{6,14},{7,5},{8,0},{9,11},{1... | collective-permute-start | bytes 393224 | tf_op jit(solution)/shard_map/ppermute | solution.py:375
  155.8 1.7 %collective-permute-start.38 = (bf16[512,128]{1,0:T(8,128)(2,1)S(1)}, bf16[512,128]{1,0:T(8,128)(2,1)S(1)}, u32[]{:S(2)}, u32[]{:S(2)}) collective-permute-start(bf16[512,128]{1,0:T(8,128)(2,1)S(1)} %get-tuple-element.50), channel_id=1, source_target_pairs={{0,12},{1,11},{2,14},{3,9},{4,8},{5,15},{6,10},{7,13},{8,4},{9,3},... | collective-permute-start | bytes 393224 | tf_op jit(solution)/shard_map/ppermute | solution.py:375
  157.5 8.4 %collective-permute-done.36 = bf16[512,128]{1,0:T(8,128)(2,1)S(1)} collective-permute-done((bf16[512,128]{1,0:T(8,128)(2,1)S(1)}, bf16[512,128]{1,0:T(8,128)(2,1)S(1)}, u32[]{:S(2)}, u32[]{:S(2)}) %collective-permute-start.36) | collective-permute-done | bytes 131104 | tf_op jit(solution)/shard_map/ppermute | solution.py:375
  (98 shorter events, 26.0 us)
Async XLA Ops:
  1.6 18.6 %collective-permute-start = (bf16[512,128]{1,0:T(8,128)(2,1)S(1)}, bf16[512,128]{1,0:T(8,128)(2,1)S(1)}, u32[]{:S(2)}, u32[]{:S(2)}) collective-permute-start(bf16[512,128]{1,0:T(8,128)(2,1)S(1)} %reshape.71), channel_id=1, source_target_pairs={{0,8},{1,9},{2,10},{3,11},{4,12},{5,13},{6,14},{7,15},{8,0},{9,1},... | collective-permute-start | bytes 393224 | tf_op jit(solution)/shard_map/ppermute | solution.py:375
  5.7 14.6 %collective-permute-start.1 = (bf16[512,128]{1,0:T(8,128)(2,1)S(1)}, bf16[512,128]{1,0:T(8,128)(2,1)S(1)}, u32[]{:S(2)}, u32[]{:S(2)}) collective-permute-start(bf16[512,128]{1,0:T(8,128)(2,1)S(1)} %reshape.71), channel_id=1, source_target_pairs={{0,4},{1,5},{2,6},{3,7},{4,0},{5,1},{6,2},{7,3},{8,12},{9,13},{10,... | collective-permute-start | bytes 393224 | tf_op jit(solution)/shard_map/ppermute | solution.py:375
  7.3 13.0 %collective-permute-start.2 = (bf16[512,128]{1,0:T(8,128)(2,1)S(1)}, bf16[512,128]{1,0:T(8,128)(2,1)S(1)}, u32[]{:S(2)}, u32[]{:S(2)}) collective-permute-start(bf16[512,128]{1,0:T(8,128)(2,1)S(1)} %reshape.71), channel_id=1, source_target_pairs={{0,12},{1,13},{2,14},{3,15},{4,8},{5,9},{6,10},{7,11},{8,4},{9,5},... | collective-permute-start | bytes 393224 | tf_op jit(solution)/shard_map/ppermute | solution.py:375
  7.3 13.1 %collective-permute-start.3 = (bf16[512,128]{1,0:T(8,128)(2,1)S(1)}, bf16[512,128]{1,0:T(8,128)(2,1)S(1)}, u32[]{:S(2)}, u32[]{:S(2)}) collective-permute-start(bf16[512,128]{1,0:T(8,128)(2,1)S(1)} %reshape.71), channel_id=1, source_target_pairs={{0,2},{1,3},{2,0},{3,1},{4,6},{5,7},{6,4},{7,5},{8,10},{9,11},{10,... | collective-permute-start | bytes 393224 | tf_op jit(solution)/shard_map/ppermute | solution.py:375
  20.4 9.9 %collective-permute-start.4 = (bf16[1536,128]{1,0:T(8,128)(2,1)S(1)}, bf16[1536,128]{1,0:T(8,128)(2,1)S(1)}, u32[]{:S(2)}, u32[]{:S(2)}) collective-permute-start(bf16[1536,128]{1,0:T(8,128)(2,1)S(1)} %slice.61), channel_id=1, source_target_pairs={{0,2},{1,3},{2,0},{3,1},{4,6},{5,7},{6,4},{7,5},{8,10},{9,11},{10,... | collective-permute-start | bytes 1179656 | tf_op jit(solution)/shard_map/ppermute | solution.py:375
  20.8 11.0 %collective-permute-start.5 = (bf16[2560,128]{1,0:T(8,128)(2,1)S(1)}, bf16[2560,128]{1,0:T(8,128)(2,1)S(1)}, u32[]{:S(2)}, u32[]{:S(2)}) collective-permute-start(bf16[2560,128]{1,0:T(8,128)(2,1)S(1)} %constant_dynamic-update-slice_fusion.refs_0_), channel_id=1, source_target_pairs={{0,1},{1,0},{2,3},{3,2},{4,5},{5,4},{6,7},{7,6},{8,9},{9,8},{10,11... | collective-permute-start | bytes 1966088 | tf_op jit(solution)/shard_map/ppermute | solution.py:375
  43.2 2.9 %collective-permute-start.7 = (bf16[1280,128]{1,0:T(8,128)(2,1)S(1)}, bf16[1280,128]{1,0:T(8,128)(2,1)S(1)}, u32[]{:S(2)}, u32[]{:S(2)}) collective-permute-start(bf16[1280,128]{1,0:T(8,128)(2,1)S(1)} %get-tuple-element.28), channel_id=1, source_target_pairs={{0,1},{1,0},{2,3},{3,2},{4,5},{5,4},{6,7},{7,6},{8,9},{9,8},{10,11... | collective-permute-start | bytes 983048 | tf_op jit(solution)/shard_map/ppermute | solution.py:375
  44.6 7.1 %collective-permute-start.9 = (bf16[1280,128]{1,0:T(8,128)(2,1)S(1)}, bf16[1280,128]{1,0:T(8,128)(2,1)S(1)}, u32[]{:S(2)}, u32[]{:S(2)}) collective-permute-start(bf16[1280,128]{1,0:T(8,128)(2,1)S(1)} %add_convert_fusion.2), channel_id=1, source_target_pairs={{0,2},{1,5},{2,0},{3,7},{4,6},{5,1},{6,4},{7,3},{8,10},{9,13},{10,... | collective-permute-start | bytes 983048 | tf_op jit(solution)/shard_map/ppermute | solution.py:375
  51.8 8.8 %collective-permute-start.10 = (bf16[320,128]{1,0:T(8,128)(2,1)S(1)}, bf16[320,128]{1,0:T(8,128)(2,1)S(1)}, u32[]{:S(2)}, u32[]{:S(2)}) collective-permute-start(bf16[320,128]{1,0:T(8,128)(2,1)S(1)} %get-tuple-element.55), channel_id=1, source_target_pairs={{0,8},{1,3},{2,10},{3,1},{4,12},{5,7},{6,14},{7,5},{8,0},{9,11},{1... | collective-permute-start | bytes 245768 | tf_op jit(solution)/shard_map/ppermute | solution.py:375
  53.6 7.1 %collective-permute-start.11 = (bf16[320,128]{1,0:T(8,128)(2,1)S(1)}, bf16[320,128]{1,0:T(8,128)(2,1)S(1)}, u32[]{:S(2)}, u32[]{:S(2)}) collective-permute-start(bf16[320,128]{1,0:T(8,128)(2,1)S(1)} %get-tuple-element.57), channel_id=1, source_target_pairs={{0,4},{1,9},{2,6},{3,11},{4,0},{5,13},{6,2},{7,15},{8,12},{9,1},{1... | collective-permute-start | bytes 245768 | tf_op jit(solution)/shard_map/ppermute | solution.py:375
  56.0 6.3 %collective-permute-start.12 = (bf16[320,128]{1,0:T(8,128)(2,1)S(1)}, bf16[320,128]{1,0:T(8,128)(2,1)S(1)}, u32[]{:S(2)}, u32[]{:S(2)}) collective-permute-start(bf16[320,128]{1,0:T(8,128)(2,1)S(1)} %get-tuple-element.56), channel_id=1, source_target_pairs={{0,12},{1,11},{2,14},{3,9},{4,8},{5,15},{6,10},{7,13},{8,4},{9,3},... | collective-permute-start | bytes 245768 | tf_op jit(solution)/shard_map/ppermute | solution.py:375
  62.5 7.9 %collective-permute-start.13 = (bf16[320,128]{1,0:T(8,128)(2,1)S(1)}, bf16[320,128]{1,0:T(8,128)(2,1)S(1)}, u32[]{:S(2)}, u32[]{:S(2)}) collective-permute-start(bf16[320,128]{1,0:T(8,128)(2,1)S(1)} %get-tuple-element.46), channel_id=1, source_target_pairs={{0,8},{1,9},{2,10},{3,11},{4,12},{5,13},{6,14},{7,15},{8,0},{9,1},... | collective-permute-start | bytes 245768 | tf_op jit(solution)/shard_map/ppermute | solution.py:375
  65.2 5.1 %collective-permute-start.14 = (bf16[320,128]{1,0:T(8,128)(2,1)S(1)}, bf16[320,128]{1,0:T(8,128)(2,1)S(1)}, u32[]{:S(2)}, u32[]{:S(2)}) collective-permute-start(bf16[320,128]{1,0:T(8,128)(2,1)S(1)} %get-tuple-element.46), channel_id=1, source_target_pairs={{0,4},{1,5},{2,6},{3,7},{4,0},{5,1},{6,2},{7,3},{8,12},{9,13},{10,... | collective-permute-start | bytes 245768 | tf_op jit(solution)/shard_map/ppermute | solution.py:375
  65.2 7.2 %collective-permute-start.15 = (bf16[320,128]{1,0:T(8,128)(2,1)S(1)}, bf16[320,128]{1,0:T(8,128)(2,1)S(1)}, u32[]{:S(2)}, u32[]{:S(2)}) collective-permute-start(bf16[320,128]{1,0:T(8,128)(2,1)S(1)} %get-tuple-element.46), channel_id=1, source_target_pairs={{0,12},{1,13},{2,14},{3,15},{4,8},{5,9},{6,10},{7,11},{8,4},{9,5},... | collective-permute-start | bytes 245768 | tf_op jit(solution)/shard_map/ppermute | solution.py:375
  66.9 6.6 %collective-permute-start.16 = (bf16[320,128]{1,0:T(8,128)(2,1)S(1)}, bf16[320,128]{1,0:T(8,128)(2,1)S(1)}, u32[]{:S(2)}, u32[]{:S(2)}) collective-permute-start(bf16[320,128]{1,0:T(8,128)(2,1)S(1)} %get-tuple-element.46), channel_id=1, source_target_pairs={{0,2},{1,3},{2,0},{3,1},{4,6},{5,7},{6,4},{7,5},{8,10},{9,11},{10,... | collective-permute-start | bytes 245768 | tf_op jit(solution)/shard_map/ppermute | solution.py:375
  72.5 8.0 %collective-permute-start.17 = (bf16[960,128]{1,0:T(8,128)(2,1)S(1)}, bf16[960,128]{1,0:T(8,128)(2,1)S(1)}, u32[]{:S(2)}, u32[]{:S(2)}) collective-permute-start(bf16[960,128]{1,0:T(8,128)(2,1)S(1)} %pad_maximum_fusion), channel_id=1, source_target_pairs={{0,2},{1,3},{2,0},{3,1},{4,6},{5,7},{6,4},{7,5},{8,10},{9,11},{10,... | collective-permute-start | bytes 737288 | tf_op jit(solution)/shard_map/ppermute | solution.py:375
  73.5 6.9 %collective-permute-start.18 = (bf16[1600,128]{1,0:T(8,128)(2,1)S(1)}, bf16[1600,128]{1,0:T(8,128)(2,1)S(1)}, u32[]{:S(2)}, u32[]{:S(2)}) collective-permute-start(bf16[1600,128]{1,0:T(8,128)(2,1)S(1)} %constant_dynamic-update-slice_fusion.5.refs_0_), channel_id=1, source_target_pairs={{0,1},{1,0},{2,3},{3,2},{4,5},{5,4},{6,7},{7,6},{8,9},{9,8},{10,11... | collective-permute-start | bytes 1228808 | tf_op jit(solution)/shard_map/ppermute | solution.py:375
  94.0 7.1 %collective-permute-start.22 = (bf16[1280,128]{1,0:T(8,128)(2,1)S(1)}, bf16[1280,128]{1,0:T(8,128)(2,1)S(1)}, u32[]{:S(2)}, u32[]{:S(2)}) collective-permute-start(bf16[1280,128]{1,0:T(8,128)(2,1)S(1)} %add_convert_fusion.1), channel_id=1, source_target_pairs={{0,2},{1,5},{2,0},{3,7},{4,6},{5,1},{6,4},{7,3},{8,10},{9,13},{10,... | collective-permute-start | bytes 983048 | tf_op jit(solution)/shard_map/ppermute | solution.py:375
  101.3 9.6 %collective-permute-start.23 = (bf16[320,128]{1,0:T(8,128)(2,1)S(1)}, bf16[320,128]{1,0:T(8,128)(2,1)S(1)}, u32[]{:S(2)}, u32[]{:S(2)}) collective-permute-start(bf16[320,128]{1,0:T(8,128)(2,1)S(1)} %get-tuple-element.52), channel_id=1, source_target_pairs={{0,8},{1,3},{2,10},{3,1},{4,12},{5,7},{6,14},{7,5},{8,0},{9,11},{1... | collective-permute-start | bytes 245768 | tf_op jit(solution)/shard_map/ppermute | solution.py:375
  102.3 8.5 %collective-permute-start.24 = (bf16[320,128]{1,0:T(8,128)(2,1)S(1)}, bf16[320,128]{1,0:T(8,128)(2,1)S(1)}, u32[]{:S(2)}, u32[]{:S(2)}) collective-permute-start(bf16[320,128]{1,0:T(8,128)(2,1)S(1)} %get-tuple-element.54), channel_id=1, source_target_pairs={{0,4},{1,9},{2,6},{3,11},{4,0},{5,13},{6,2},{7,15},{8,12},{9,1},{1... | collective-permute-start | bytes 245768 | tf_op jit(solution)/shard_map/ppermute | solution.py:375
  103.9 7.0 %collective-permute-start.25 = (bf16[320,128]{1,0:T(8,128)(2,1)S(1)}, bf16[320,128]{1,0:T(8,128)(2,1)S(1)}, u32[]{:S(2)}, u32[]{:S(2)}) collective-permute-start(bf16[320,128]{1,0:T(8,128)(2,1)S(1)} %get-tuple-element.53), channel_id=1, source_target_pairs={{0,12},{1,11},{2,14},{3,9},{4,8},{5,15},{6,10},{7,13},{8,4},{9,3},... | collective-permute-start | bytes 245768 | tf_op jit(solution)/shard_map/ppermute | solution.py:375
  111.1 7.4 %collective-permute-start.26 = (bf16[320,128]{1,0:T(8,128)(2,1)S(1)}, bf16[320,128]{1,0:T(8,128)(2,1)S(1)}, u32[]{:S(2)}, u32[]{:S(2)}) collective-permute-start(bf16[320,128]{1,0:T(8,128)(2,1)S(1)} %get-tuple-element.42), channel_id=1, source_target_pairs={{0,8},{1,9},{2,10},{3,11},{4,12},{5,13},{6,14},{7,15},{8,0},{9,1},... | collective-permute-start | bytes 245768 | tf_op jit(solution)/shard_map/ppermute | solution.py:375
  113.4 5.5 %collective-permute-start.27 = (bf16[320,128]{1,0:T(8,128)(2,1)S(1)}, bf16[320,128]{1,0:T(8,128)(2,1)S(1)}, u32[]{:S(2)}, u32[]{:S(2)}) collective-permute-start(bf16[320,128]{1,0:T(8,128)(2,1)S(1)} %get-tuple-element.42), channel_id=1, source_target_pairs={{0,4},{1,5},{2,6},{3,7},{4,0},{5,1},{6,2},{7,3},{8,12},{9,13},{10,... | collective-permute-start | bytes 245768 | tf_op jit(solution)/shard_map/ppermute | solution.py:375
  113.6 7.4 %collective-permute-start.28 = (bf16[320,128]{1,0:T(8,128)(2,1)S(1)}, bf16[320,128]{1,0:T(8,128)(2,1)S(1)}, u32[]{:S(2)}, u32[]{:S(2)}) collective-permute-start(bf16[320,128]{1,0:T(8,128)(2,1)S(1)} %get-tuple-element.42), channel_id=1, source_target_pairs={{0,12},{1,13},{2,14},{3,15},{4,8},{5,9},{6,10},{7,11},{8,4},{9,5},... | collective-permute-start | bytes 245768 | tf_op jit(solution)/shard_map/ppermute | solution.py:375
  115.5 6.3 %collective-permute-start.29 = (bf16[320,128]{1,0:T(8,128)(2,1)S(1)}, bf16[320,128]{1,0:T(8,128)(2,1)S(1)}, u32[]{:S(2)}, u32[]{:S(2)}) collective-permute-start(bf16[320,128]{1,0:T(8,128)(2,1)S(1)} %get-tuple-element.42), channel_id=1, source_target_pairs={{0,2},{1,3},{2,0},{3,1},{4,6},{5,7},{6,4},{7,5},{8,10},{9,11},{10,... | collective-permute-start | bytes 245768 | tf_op jit(solution)/shard_map/ppermute | solution.py:375
  121.0 7.5 %collective-permute-start.30 = (bf16[960,128]{1,0:T(8,128)(2,1)S(1)}, bf16[960,128]{1,0:T(8,128)(2,1)S(1)}, u32[]{:S(2)}, u32[]{:S(2)}) collective-permute-start(bf16[960,128]{1,0:T(8,128)(2,1)S(1)} %pad_maximum_fusion.1), channel_id=1, source_target_pairs={{0,2},{1,3},{2,0},{3,1},{4,6},{5,7},{6,4},{7,5},{8,10},{9,11},{10,... | collective-permute-start | bytes 737288 | tf_op jit(solution)/shard_map/ppermute | solution.py:375
  121.8 6.7 %collective-permute-start.31 = (bf16[1600,128]{1,0:T(8,128)(2,1)S(1)}, bf16[1600,128]{1,0:T(8,128)(2,1)S(1)}, u32[]{:S(2)}, u32[]{:S(2)}) collective-permute-start(bf16[1600,128]{1,0:T(8,128)(2,1)S(1)} %constant_dynamic-update-slice_fusion.10.refs_0_), channel_id=1, source_target_pairs={{0,1},{1,0},{2,3},{3,2},{4,5},{5,4},{6,7},{7,6},{8,9},{9,8},{10,11... | collective-permute-start | bytes 1228808 | tf_op jit(solution)/shard_map/ppermute | solution.py:375
  141.7 2.9 %collective-permute-start.33 = (bf16[2048,128]{1,0:T(8,128)(2,1)S(1)}, bf16[2048,128]{1,0:T(8,128)(2,1)S(1)}, u32[]{:S(2)}, u32[]{:S(2)}) collective-permute-start(bf16[2048,128]{1,0:T(8,128)(2,1)S(1)} %get-tuple-element.36), channel_id=1, source_target_pairs={{0,1},{1,0},{2,3},{3,2},{4,5},{5,4},{6,7},{7,6},{8,9},{9,8},{10,11... | collective-permute-start | bytes 1572872 | tf_op jit(solution)/shard_map/ppermute | solution.py:375
  143.6 9.2 %collective-permute-start.35 = (bf16[2048,128]{1,0:T(8,128)(2,1)S(1)}, bf16[2048,128]{1,0:T(8,128)(2,1)S(1)}, u32[]{:S(2)}, u32[]{:S(2)}) collective-permute-start(bf16[2048,128]{1,0:T(8,128)(2,1)S(1)} %add_convert_fusion), channel_id=1, source_target_pairs={{0,2},{1,5},{2,0},{3,7},{4,6},{5,1},{6,4},{7,3},{8,10},{9,13},{10,... | collective-permute-start | bytes 1572872 | tf_op jit(solution)/shard_map/ppermute | solution.py:375
  153.1 12.9 %collective-permute-start.36 = (bf16[512,128]{1,0:T(8,128)(2,1)S(1)}, bf16[512,128]{1,0:T(8,128)(2,1)S(1)}, u32[]{:S(2)}, u32[]{:S(2)}) collective-permute-start(bf16[512,128]{1,0:T(8,128)(2,1)S(1)} %get-tuple-element.49), channel_id=1, source_target_pairs={{0,8},{1,3},{2,10},{3,1},{4,12},{5,7},{6,14},{7,5},{8,0},{9,11},{1... | collective-permute-start | bytes 393224 | tf_op jit(solution)/shard_map/ppermute | solution.py:375
  155.8 10.2 %collective-permute-start.37 = (bf16[512,128]{1,0:T(8,128)(2,1)S(1)}, bf16[512,128]{1,0:T(8,128)(2,1)S(1)}, u32[]{:S(2)}, u32[]{:S(2)}) collective-permute-start(bf16[512,128]{1,0:T(8,128)(2,1)S(1)} %get-tuple-element.51), channel_id=1, source_target_pairs={{0,4},{1,9},{2,6},{3,11},{4,0},{5,13},{6,2},{7,15},{8,12},{9,1},{1... | collective-permute-start | bytes 393224 | tf_op jit(solution)/shard_map/ppermute | solution.py:375
  155.8 10.2 %collective-permute-start.38 = (bf16[512,128]{1,0:T(8,128)(2,1)S(1)}, bf16[512,128]{1,0:T(8,128)(2,1)S(1)}, u32[]{:S(2)}, u32[]{:S(2)}) collective-permute-start(bf16[512,128]{1,0:T(8,128)(2,1)S(1)} %get-tuple-element.50), channel_id=1, source_target_pairs={{0,12},{1,11},{2,14},{3,9},{4,8},{5,15},{6,10},{7,13},{8,4},{9,3},... | collective-permute-start | bytes 393224 | tf_op jit(solution)/shard_map/ppermute | solution.py:375
  (8 other events, 14.8 us)

commit v14 on v12

--- a/solution.py
+++ b/solution.py
@@ -380,7 +380,8 @@
     core, row, *columns = stage_distances(lax.axis_size("rows"))
     apart = [slot_distance(slot, columns) for slot in range(lax.axis_size("rows") // 4)]
     made = ()
-    near = jnp.concatenate([own] + [exchange(own, distance) for distance in apart[1:] + [row]], axis=0)
+    arrived = {distance: exchange(own, distance) for distance in sorted(apart[1:] + [row], reverse=True)}
+    near = jnp.concatenate([own] + [arrived[distance] for distance in apart[1:] + [row]], axis=0)
     if beside:
         near, *made = lax.optimization_barrier((near, beside[0]()))
     other = exchange(near[own.shape[0] : len(apart) * own.shape[0]], row)
@@ -403,11 +404,11 @@
     near, other = add_cores(keep, *send)
     sums = near[size:-size] + exchange(other.astype(jnp.bfloat16), row).astype(jnp.float32)
     last, sums = lax.optimization_barrier((near[-size:].astype(jnp.bfloat16), sums.astype(jnp.bfloat16)))
-    total = near[:size] + exchange(last, row).astype(jnp.float32)
-    for slot in range(1, devices // 4):
+    total = near[:size]
+    for slot in sorted(range(1, devices // 4), key=lambda slot: -slot_distance(slot, columns)):
         share = exchange(sums[(slot - 1) * size : slot * size], slot_distance(slot, columns))
         total = total + share.astype(jnp.float32)
-    return total
+    return total + exchange(last, row).astype(jnp.float32)
 
 
 def last_reduce(keep, *send):
@@ -418,7 +419,7 @@
     size = 2 * keep.shape[0] // devices
     sent = sums.astype(jnp.bfloat16)
     total = sums[:size]
-    for slot in range(1, devices // 4):
+    for slot in sorted(range(1, devices // 4), key=lambda slot: -slot_distance(slot, even[2:])):
         share = sent[slot * size : (slot + 1) * size]
         total = total + exchange(share, slot_distance(slot, even[2:]), slot_distance(slot, odd[2:])).astype(jnp.float32)
     return total

time: 166 us -> 167 us (level)
  waiting for transfers between devices: 60.9 us -> 63.9 us
    ppermute x41, waiting for transfers between devices: 60.9 us -> 63.9 us  [exchange(): lax.ppermute(value, 'rows', [(i, i ^ apart[i % 2]) for i in range(devices)])]
  transfers between devices with their start and end apart: 41 -> 41, of which waited for: 21 -> 22; matrix products, arithmetic and copies ran while one was open for 3% -> 3% of each run, Pallas kernels for 11% -> 10%
where the time goes in v14:
time: 167 us; the launch traced here: 166 us
  waiting for transfers between devices  63.9 us (38%)
  Pallas kernels  49.2 us (29%)
  starting transfers between devices  43.8 us (26%)
  local copies, waits for them, and re-layouts  6.4 us (4%)
  other arithmetic  2.28 us (1%)
    ppermute x41, waiting for transfers between devices, exchange(): lax.ppermute(value, 'rows', [(i, i ^ apart[i % 2]) for i in range(devices)])  63.9 us
    ppermute x41, starting transfers between devices, exchange(): lax.ppermute(value, 'rows', [(i, i ^ apart[i % 2]) for i in range(devices)])  43.8 us
    pallas_call x3, Pallas kernels, gradient_call(): pl.pallas_call(functools.partial(gradient_kernel, mode, shards, pairs, gr...  31.9 us
    pallas_call x2, Pallas kernels, collect_support(): pl.pallas_call(functools.partial(support_kernel, part * entries, groups),...  17.3 us
  transfers between devices with their start and end apart: 41, of which 22 were waited for; matrix products, arithmetic and copies ran while one was open for 3% of the time, Pallas kernels for 10%

profile of v14, /device:TPU:0, one launch (start us, length us, event | category | flops | bytes accessed | tf_op | source)
XLA Modules:
  0.0 166.1 jit_solution(9138694287221580180)
XLA Ops:
  1.6 4.1 %collective-permute-start = (bf16[512,128]{1,0:T(8,128)(2,1)S(1)}, bf16[512,128]{1,0:T(8,128)(2,1)S(1)}, u32[]{:S(2)}, u32[]{:S(2)}) collective-permute-start(bf16[512,128]{1,0:T(8,128)(2,1)S(1)} %reshape.71), channel_id=1, source_target_pairs={{0,8},{1,9},{2,10},{3,11},{4,12},{5,13},{6,14},{7,15},{8,0},{9,1},... | collective-permute-start | bytes 393224 | tf_op jit(solution)/shard_map/ppermute | solution.py:376
  5.7 1.6 collective-permute-start.1
  7.3 1.7 %collective-permute-start.3 = (bf16[512,128]{1,0:T(8,128)(2,1)S(1)}, bf16[512,128]{1,0:T(8,128)(2,1)S(1)}, u32[]{:S(2)}, u32[]{:S(2)}) collective-permute-start(bf16[512,128]{1,0:T(8,128)(2,1)S(1)} %reshape.71), channel_id=1, source_target_pairs={{0,2},{1,3},{2,0},{3,1},{4,6},{5,7},{6,4},{7,5},{8,10},{9,11},{10,... | collective-permute-start | bytes 393224 | tf_op jit(solution)/shard_map/ppermute | solution.py:376
  11.7 8.5 %collect_support.2.refs_0_ = bf16[520,512,128]{2,1,0:T(8,128)(2,1)} custom-call(s32[305]{0:T(512)S(1)} %concatenate.18.scalars, bf16[512,32768]{1,0:T(8,128)(2,1)} %dictionary.3), custom_call_target="tpu_custom_call" | custom-call | bytes 31457280 | tf_op jit(solution)/shard_map/collect_support/pallas_call | solution.py:130
  20.8 8.8 %collect_support.3.blocks = bf16[520,512,128]{2,1,0:T(8,128)(2,1)} custom-call(s32[305]{0:T(512)S(1)} %concatenate.18.scalars, bf16[512,32768]{1,0:T(8,128)(2,1)} %dictionary.3, bf16[520,512,128]{2,1,0:T(8,128)(2,1)} %collect_support.2.refs_0_), custom_call_target="tpu_custom_call", output_to_operand_aliasing={{}: (2, {})} | custom-call | bytes 31457280 | tf_op jit(solution)/shard_map/collect_support/pallas_call | solution.py:130
  30.3 1.5 copy.13
  32.2 10.4 %gradient.3 = (f32[2560,128]{1,0:T(8,128)S(1)}, bf16[1600,128]{1,0:T(8,128)(2,1)S(1)}, bf16[960,128]{1,0:T(8,128)(2,1)S(1)}, bf16[320,128]{1,0:T(8,128)(2,1)S(1)}, f32[320,128]{1,0:T(8,128)S(1)}) custom-call(s32[305]{0:T(512)S(1)} %concatenate.18.scalars, bf16[520,512,128]{2,1,0:T(8,128)(2,1)} %collect_support.3.blocks, ...), custom_call_target="tpu_custom_call" | custom-call | flops 5368709120 | bytes 10485760 | tf_op jit(solution)/shard_map/gradient/pallas_call | solution.py:353
  44.3 1.5 collective-permute-start.9
  45.9 6.6 %collective-permute-done.9 = bf16[960,128]{1,0:T(8,128)(2,1)S(1)} collective-permute-done((bf16[960,128]{1,0:T(8,128)(2,1)S(1)}, bf16[960,128]{1,0:T(8,128)(2,1)S(1)}, u32[]{:S(2)}, u32[]{:S(2)}) %collective-permute-start.9) | collective-permute-done | bytes 245792 | tf_op jit(solution)/shard_map/ppermute | solution.py:376
  52.6 3.6 %collective-permute-start.10 = (bf16[320,128]{1,0:T(8,128)(2,1)S(1)}, bf16[320,128]{1,0:T(8,128)(2,1)S(1)}, u32[]{:S(2)}, u32[]{:S(2)}) collective-permute-start(bf16[320,128]{1,0:T(8,128)(2,1)S(1)} %get-tuple-element.59), channel_id=1, source_target_pairs={{0,12},{1,13},{2,14},{3,15},{4,8},{5,9},{6,10},{7,11},{8,4},{9,5},... | collective-permute-start | bytes 245768 | tf_op jit(solution)/shard_map/ppermute | solution.py:376
  59.5 3.0 %collective-permute-done.11 = bf16[320,128]{1,0:T(8,128)(2,1)S(1)} collective-permute-done((bf16[320,128]{1,0:T(8,128)(2,1)S(1)}, bf16[320,128]{1,0:T(8,128)(2,1)S(1)}, u32[]{:S(2)}, u32[]{:S(2)}) %collective-permute-start.11) | collective-permute-done | bytes 81952 | tf_op jit(solution)/shard_map/ppermute | solution.py:376
  63.9 2.0 %collective-permute-start.15 = (bf16[320,128]{1,0:T(8,128)(2,1)S(1)}, bf16[320,128]{1,0:T(8,128)(2,1)S(1)}, u32[]{:S(2)}, u32[]{:S(2)}) collective-permute-start(bf16[320,128]{1,0:T(8,128)(2,1)S(1)} %get-tuple-element.52), channel_id=1, source_target_pairs={{0,4},{1,5},{2,6},{3,7},{4,0},{5,1},{6,2},{7,3},{8,12},{9,13},{10,... | collective-permute-start | bytes 245768 | tf_op jit(solution)/shard_map/ppermute | solution.py:376
  68.4 2.2 %collective-permute-done.14 = bf16[320,128]{1,0:T(8,128)(2,1)S(1)} collective-permute-done((bf16[320,128]{1,0:T(8,128)(2,1)S(1)}, bf16[320,128]{1,0:T(8,128)(2,1)S(1)}, u32[]{:S(2)}, u32[]{:S(2)}) %collective-permute-start.14) | collective-permute-done | bytes 81952 | tf_op jit(solution)/shard_map/ppermute | solution.py:376
  70.7 1.5 collective-permute-done.16
  73.8 4.7 %collective-permute-done.18.refs_1_ = bf16[960,128]{1,0:T(8,128)(2,1)S(1)} collective-permute-done((bf16[960,128]{1,0:T(8,128)(2,1)S(1)}, bf16[960,128]{1,0:T(8,128)(2,1)S(1)}, u32[]{:S(2)}, u32[]{:S(2)}) %collective-permute-start.18) | collective-permute-done | bytes 245792 | tf_op jit(solution)/shard_map/ppermute | solution.py:376
  78.4 1.5 collective-permute-done.20.refs_3_
  79.9 10.1 %gradient.4 = (f32[2560,128]{1,0:T(8,128)S(1)}, bf16[1600,128]{1,0:T(8,128)(2,1)S(1)}, bf16[960,128]{1,0:T(8,128)(2,1)S(1)}) custom-call(s32[305]{0:T(512)S(1)} %concatenate.18.scalars, bf16[520,512,128]{2,1,0:T(8,128)(2,1)} %collect_support.3.blocks, bf16[1600,128]{1,0:T(8,128)(2,1)S(1)} %constant_dynamic-update-slice_fusion.5.refs_0_, ...), custom_call_target="tpu_custom_call" | custom-call | flops 5368709120 | bytes 10485760 | tf_op jit(solution)/shard_map/gradient/pallas_call | solution.py:353
  93.3 6.5 %collective-permute-done.23 = bf16[960,128]{1,0:T(8,128)(2,1)S(1)} collective-permute-done((bf16[960,128]{1,0:T(8,128)(2,1)S(1)}, bf16[960,128]{1,0:T(8,128)(2,1)S(1)}, u32[]{:S(2)}, u32[]{:S(2)}) %collective-permute-start.23) | collective-permute-done | bytes 245792 | tf_op jit(solution)/shard_map/ppermute | solution.py:376
  102.2 2.1 %collective-permute-start.26 = (bf16[320,128]{1,0:T(8,128)(2,1)S(1)}, bf16[320,128]{1,0:T(8,128)(2,1)S(1)}, u32[]{:S(2)}, u32[]{:S(2)}) collective-permute-start(bf16[320,128]{1,0:T(8,128)(2,1)S(1)} %get-tuple-element.57), channel_id=1, source_target_pairs={{0,4},{1,5},{2,6},{3,7},{4,0},{5,1},{6,2},{7,3},{8,12},{9,13},{10,... | collective-permute-start | bytes 245768 | tf_op jit(solution)/shard_map/ppermute | solution.py:376
  105.7 1.4 collective-permute-done.24
  107.1 2.6 %collective-permute-done.25 = bf16[320,128]{1,0:T(8,128)(2,1)S(1)} collective-permute-done((bf16[320,128]{1,0:T(8,128)(2,1)S(1)}, bf16[320,128]{1,0:T(8,128)(2,1)S(1)}, u32[]{:S(2)}, u32[]{:S(2)}) %collective-permute-start.25) | collective-permute-done | bytes 81952 | tf_op jit(solution)/shard_map/ppermute | solution.py:376
  110.1 1.8 %collective-permute-start.29 = (bf16[320,128]{1,0:T(8,128)(2,1)S(1)}, bf16[320,128]{1,0:T(8,128)(2,1)S(1)}, u32[]{:S(2)}, u32[]{:S(2)}) collective-permute-start(bf16[320,128]{1,0:T(8,128)(2,1)S(1)} %get-tuple-element.50), channel_id=1, source_target_pairs={{0,4},{1,5},{2,6},{3,7},{4,0},{5,1},{6,2},{7,3},{8,12},{9,13},{10,... | collective-permute-start | bytes 245768 | tf_op jit(solution)/shard_map/ppermute | solution.py:376
  111.9 2.6 %collective-permute-start.30 = (bf16[320,128]{1,0:T(8,128)(2,1)S(1)}, bf16[320,128]{1,0:T(8,128)(2,1)S(1)}, u32[]{:S(2)}, u32[]{:S(2)}) collective-permute-start(bf16[320,128]{1,0:T(8,128)(2,1)S(1)} %get-tuple-element.50), channel_id=1, source_target_pairs={{0,12},{1,13},{2,14},{3,15},{4,8},{5,9},{6,10},{7,11},{8,4},{9,5},... | collective-permute-start | bytes 245768 | tf_op jit(solution)/shard_map/ppermute | solution.py:376
  115.1 1.8 %collective-permute-done.28 = bf16[320,128]{1,0:T(8,128)(2,1)S(1)} collective-permute-done((bf16[320,128]{1,0:T(8,128)(2,1)S(1)}, bf16[320,128]{1,0:T(8,128)(2,1)S(1)}, u32[]{:S(2)}, u32[]{:S(2)}) %collective-permute-start.28) | collective-permute-done | bytes 81952 | tf_op jit(solution)/shard_map/ppermute | solution.py:376
  119.8 4.7 %collective-permute-done.32.refs_1_ = bf16[960,128]{1,0:T(8,128)(2,1)S(1)} collective-permute-done((bf16[960,128]{1,0:T(8,128)(2,1)S(1)}, bf16[960,128]{1,0:T(8,128)(2,1)S(1)}, u32[]{:S(2)}, u32[]{:S(2)}) %collective-permute-start.32) | collective-permute-done | bytes 245792 | tf_op jit(solution)/shard_map/ppermute | solution.py:376
  124.5 1.5 collective-permute-done.34.refs_3_
  126.0 11.3 %gradient.5 = (f32[4096,128]{1,0:T(8,128)S(1)}, bf16[2048,128]{1,0:T(8,128)(2,1)S(1)}, bf16[2048,128]{1,0:T(8,128)(2,1)S(1)}, bf16[8,64,128]{2,1,0:T(8,128)(2,1)S(1)}, f32[64,128]{1,0:T(8,128)S(1)}) custom-call(s32[305]{0:T(512)S(1)} %concatenate.18.scalars, bf16[520,512,128]{2,1,0:T(8,128)(2,1)} %collect_support.3.blocks, ...), custom_call_target="tpu_custom_call" | custom-call | flops 5368709120 | bytes 10485760 | tf_op jit(solution)/shard_map/gradient/pallas_call | solution.py:353
  140.9 7.8 %collective-permute-done.37 = bf16[2048,128]{1,0:T(8,128)(2,1)S(1)} collective-permute-done((bf16[2048,128]{1,0:T(8,128)(2,1)S(1)}, bf16[2048,128]{1,0:T(8,128)(2,1)S(1)}, u32[]{:S(2)}, u32[]{:S(2)}) %collective-permute-start.37) | collective-permute-done | bytes 524320 | tf_op jit(solution)/shard_map/ppermute | solution.py:376
  149.0 2.5 %collective-permute-start.38 = (bf16[512,128]{1,0:T(8,128)(2,1)S(1)}, bf16[512,128]{1,0:T(8,128)(2,1)S(1)}, u32[]{:S(2)}, u32[]{:S(2)}) collective-permute-start(bf16[512,128]{1,0:T(8,128)(2,1)S(1)} %get-tuple-element.53), channel_id=1, source_target_pairs={{0,12},{1,11},{2,14},{3,9},{4,8},{5,15},{6,10},{7,13},{8,4},{9,3},... | collective-permute-start | bytes 393224 | tf_op jit(solution)/shard_map/ppermute | solution.py:376
  151.5 1.5 collective-permute-start.39
  153.4 3.4 %collective-permute-done.38 = bf16[512,128]{1,0:T(8,128)(2,1)S(1)} collective-permute-done((bf16[512,128]{1,0:T(8,128)(2,1)S(1)}, bf16[512,128]{1,0:T(8,128)(2,1)S(1)}, u32[]{:S(2)}, u32[]{:S(2)}) %collective-permute-start.38) | collective-permute-done | bytes 131104 | tf_op jit(solution)/shard_map/ppermute | solution.py:376
  156.8 7.8 %collective-permute-done.39 = bf16[512,128]{1,0:T(8,128)(2,1)S(1)} collective-permute-done((bf16[512,128]{1,0:T(8,128)(2,1)S(1)}, bf16[512,128]{1,0:T(8,128)(2,1)S(1)}, u32[]{:S(2)}, u32[]{:S(2)}) %collective-permute-start.39) | collective-permute-done | bytes 131104 | tf_op jit(solution)/shard_map/ppermute | solution.py:376
  (106 shorter events, 32.7 us)
Async XLA Ops:
  1.6 18.6 %collective-permute-start = (bf16[512,128]{1,0:T(8,128)(2,1)S(1)}, bf16[512,128]{1,0:T(8,128)(2,1)S(1)}, u32[]{:S(2)}, u32[]{:S(2)}) collective-permute-start(bf16[512,128]{1,0:T(8,128)(2,1)S(1)} %reshape.71), channel_id=1, source_target_pairs={{0,8},{1,9},{2,10},{3,11},{4,12},{5,13},{6,14},{7,15},{8,0},{9,1},... | collective-permute-start | bytes 393224 | tf_op jit(solution)/shard_map/ppermute | solution.py:376
  5.7 14.6 %collective-permute-start.1 = (bf16[512,128]{1,0:T(8,128)(2,1)S(1)}, bf16[512,128]{1,0:T(8,128)(2,1)S(1)}, u32[]{:S(2)}, u32[]{:S(2)}) collective-permute-start(bf16[512,128]{1,0:T(8,128)(2,1)S(1)} %reshape.71), channel_id=1, source_target_pairs={{0,4},{1,5},{2,6},{3,7},{4,0},{5,1},{6,2},{7,3},{8,12},{9,13},{10,... | collective-permute-start | bytes 393224 | tf_op jit(solution)/shard_map/ppermute | solution.py:376
  7.3 13.0 %collective-permute-start.2 = (bf16[512,128]{1,0:T(8,128)(2,1)S(1)}, bf16[512,128]{1,0:T(8,128)(2,1)S(1)}, u32[]{:S(2)}, u32[]{:S(2)}) collective-permute-start(bf16[512,128]{1,0:T(8,128)(2,1)S(1)} %reshape.71), channel_id=1, source_target_pairs={{0,12},{1,13},{2,14},{3,15},{4,8},{5,9},{6,10},{7,11},{8,4},{9,5},... | collective-permute-start | bytes 393224 | tf_op jit(solution)/shard_map/ppermute | solution.py:376
  7.3 13.1 %collective-permute-start.3 = (bf16[512,128]{1,0:T(8,128)(2,1)S(1)}, bf16[512,128]{1,0:T(8,128)(2,1)S(1)}, u32[]{:S(2)}, u32[]{:S(2)}) collective-permute-start(bf16[512,128]{1,0:T(8,128)(2,1)S(1)} %reshape.71), channel_id=1, source_target_pairs={{0,2},{1,3},{2,0},{3,1},{4,6},{5,7},{6,4},{7,5},{8,10},{9,11},{10,... | collective-permute-start | bytes 393224 | tf_op jit(solution)/shard_map/ppermute | solution.py:376
  20.4 9.9 %collective-permute-start.4 = (bf16[1536,128]{1,0:T(8,128)(2,1)S(1)}, bf16[1536,128]{1,0:T(8,128)(2,1)S(1)}, u32[]{:S(2)}, u32[]{:S(2)}) collective-permute-start(bf16[1536,128]{1,0:T(8,128)(2,1)S(1)} %slice.75), channel_id=1, source_target_pairs={{0,2},{1,3},{2,0},{3,1},{4,6},{5,7},{6,4},{7,5},{8,10},{9,11},{10,... | collective-permute-start | bytes 1179656 | tf_op jit(solution)/shard_map/ppermute | solution.py:376
  20.8 11.0 %collective-permute-start.5 = (bf16[2560,128]{1,0:T(8,128)(2,1)S(1)}, bf16[2560,128]{1,0:T(8,128)(2,1)S(1)}, u32[]{:S(2)}, u32[]{:S(2)}) collective-permute-start(bf16[2560,128]{1,0:T(8,128)(2,1)S(1)} %constant_dynamic-update-slice_fusion.refs_0_), channel_id=1, source_target_pairs={{0,1},{1,0},{2,3},{3,2},{4,5},{5,4},{6,7},{7,6},{8,9},{9,8},{10,11... | collective-permute-start | bytes 1966088 | tf_op jit(solution)/shard_map/ppermute | solution.py:376
  44.3 8.3 %collective-permute-start.9 = (bf16[960,128]{1,0:T(8,128)(2,1)S(1)}, bf16[960,128]{1,0:T(8,128)(2,1)S(1)}, u32[]{:S(2)}, u32[]{:S(2)}) collective-permute-start(bf16[960,128]{1,0:T(8,128)(2,1)S(1)} %add_convert_fusion.2), channel_id=1, source_target_pairs={{0,2},{1,3},{2,0},{3,1},{4,6},{5,7},{6,4},{7,5},{8,10},{9,11},{10,... | collective-permute-start | bytes 737288 | tf_op jit(solution)/shard_map/ppermute | solution.py:376
  52.6 6.8 %collective-permute-start.10 = (bf16[320,128]{1,0:T(8,128)(2,1)S(1)}, bf16[320,128]{1,0:T(8,128)(2,1)S(1)}, u32[]{:S(2)}, u32[]{:S(2)}) collective-permute-start(bf16[320,128]{1,0:T(8,128)(2,1)S(1)} %get-tuple-element.59), channel_id=1, source_target_pairs={{0,12},{1,13},{2,14},{3,15},{4,8},{5,9},{6,10},{7,11},{8,4},{9,5},... | collective-permute-start | bytes 245768 | tf_op jit(solution)/shard_map/ppermute | solution.py:376
  56.2 6.3 %collective-permute-start.11 = (bf16[320,128]{1,0:T(8,128)(2,1)S(1)}, bf16[320,128]{1,0:T(8,128)(2,1)S(1)}, u32[]{:S(2)}, u32[]{:S(2)}) collective-permute-start(bf16[320,128]{1,0:T(8,128)(2,1)S(1)} %get-tuple-element.61), channel_id=1, source_target_pairs={{0,8},{1,9},{2,10},{3,11},{4,12},{5,13},{6,14},{7,15},{8,0},{9,1},... | collective-permute-start | bytes 245768 | tf_op jit(solution)/shard_map/ppermute | solution.py:376
  56.2 6.3 %collective-permute-start.12 = (bf16[320,128]{1,0:T(8,128)(2,1)S(1)}, bf16[320,128]{1,0:T(8,128)(2,1)S(1)}, u32[]{:S(2)}, u32[]{:S(2)}) collective-permute-start(bf16[320,128]{1,0:T(8,128)(2,1)S(1)} %get-tuple-element.60), channel_id=1, source_target_pairs={{0,4},{1,5},{2,6},{3,7},{4,0},{5,1},{6,2},{7,3},{8,12},{9,13},{10,... | collective-permute-start | bytes 245768 | tf_op jit(solution)/shard_map/ppermute | solution.py:376
  57.1 5.4 %collective-permute-start.13 = (bf16[320,128]{1,0:T(8,128)(2,1)S(1)}, bf16[320,128]{1,0:T(8,128)(2,1)S(1)}, u32[]{:S(2)}, u32[]{:S(2)}) collective-permute-start(bf16[320,128]{1,0:T(8,128)(2,1)S(1)} %slice.160), channel_id=1, source_target_pairs={{0,2},{1,3},{2,0},{3,1},{4,6},{5,7},{6,4},{7,5},{8,10},{9,11},{10,... | collective-permute-start | bytes 245768 | tf_op jit(solution)/shard_map/ppermute | solution.py:376
  62.6 8.0 %collective-permute-start.14 = (bf16[320,128]{1,0:T(8,128)(2,1)S(1)}, bf16[320,128]{1,0:T(8,128)(2,1)S(1)}, u32[]{:S(2)}, u32[]{:S(2)}) collective-permute-start(bf16[320,128]{1,0:T(8,128)(2,1)S(1)} %get-tuple-element.52), channel_id=1, source_target_pairs={{0,8},{1,9},{2,10},{3,11},{4,12},{5,13},{6,14},{7,15},{8,0},{9,1},... | collective-permute-start | bytes 245768 | tf_op jit(solution)/shard_map/ppermute | solution.py:376
  63.9 6.8 %collective-permute-start.15 = (bf16[320,128]{1,0:T(8,128)(2,1)S(1)}, bf16[320,128]{1,0:T(8,128)(2,1)S(1)}, u32[]{:S(2)}, u32[]{:S(2)}) collective-permute-start(bf16[320,128]{1,0:T(8,128)(2,1)S(1)} %get-tuple-element.52), channel_id=1, source_target_pairs={{0,4},{1,5},{2,6},{3,7},{4,0},{5,1},{6,2},{7,3},{8,12},{9,13},{10,... | collective-permute-start | bytes 245768 | tf_op jit(solution)/shard_map/ppermute | solution.py:376
  65.8 6.3 %collective-permute-start.16 = (bf16[320,128]{1,0:T(8,128)(2,1)S(1)}, bf16[320,128]{1,0:T(8,128)(2,1)S(1)}, u32[]{:S(2)}, u32[]{:S(2)}) collective-permute-start(bf16[320,128]{1,0:T(8,128)(2,1)S(1)} %get-tuple-element.52), channel_id=1, source_target_pairs={{0,12},{1,13},{2,14},{3,15},{4,8},{5,9},{6,10},{7,11},{8,4},{9,5},... | collective-permute-start | bytes 245768 | tf_op jit(solution)/shard_map/ppermute | solution.py:376
  67.1 6.6 %collective-permute-start.17 = (bf16[320,128]{1,0:T(8,128)(2,1)S(1)}, bf16[320,128]{1,0:T(8,128)(2,1)S(1)}, u32[]{:S(2)}, u32[]{:S(2)}) collective-permute-start(bf16[320,128]{1,0:T(8,128)(2,1)S(1)} %get-tuple-element.52), channel_id=1, source_target_pairs={{0,2},{1,3},{2,0},{3,1},{4,6},{5,7},{6,4},{7,5},{8,10},{9,11},{10,... | collective-permute-start | bytes 245768 | tf_op jit(solution)/shard_map/ppermute | solution.py:376
  72.2 6.3 %collective-permute-start.18 = (bf16[960,128]{1,0:T(8,128)(2,1)S(1)}, bf16[960,128]{1,0:T(8,128)(2,1)S(1)}, u32[]{:S(2)}, u32[]{:S(2)}) collective-permute-start(bf16[960,128]{1,0:T(8,128)(2,1)S(1)} %pad_maximum_fusion), channel_id=1, source_target_pairs={{0,2},{1,3},{2,0},{3,1},{4,6},{5,7},{6,4},{7,5},{8,10},{9,11},{10,... | collective-permute-start | bytes 737288 | tf_op jit(solution)/shard_map/ppermute | solution.py:376
  73.7 4.7 %collective-permute-start.19 = (bf16[1600,128]{1,0:T(8,128)(2,1)S(1)}, bf16[1600,128]{1,0:T(8,128)(2,1)S(1)}, u32[]{:S(2)}, u32[]{:S(2)}) collective-permute-start(bf16[1600,128]{1,0:T(8,128)(2,1)S(1)} %constant_dynamic-update-slice_fusion.5.refs_0_), channel_id=1, source_target_pairs={{0,1},{1,0},{2,3},{3,2},{4,5},{5,4},{6,7},{7,6},{8,9},{9,8},{10,11... | collective-permute-start | bytes 1228808 | tf_op jit(solution)/shard_map/ppermute | solution.py:376
  91.7 8.1 %collective-permute-start.23 = (bf16[960,128]{1,0:T(8,128)(2,1)S(1)}, bf16[960,128]{1,0:T(8,128)(2,1)S(1)}, u32[]{:S(2)}, u32[]{:S(2)}) collective-permute-start(bf16[960,128]{1,0:T(8,128)(2,1)S(1)} %add_convert_fusion.1), channel_id=1, source_target_pairs={{0,2},{1,3},{2,0},{3,1},{4,6},{5,7},{6,4},{7,5},{8,10},{9,11},{10,... | collective-permute-start | bytes 737288 | tf_op jit(solution)/shard_map/ppermute | solution.py:376
  99.9 7.3 %collective-permute-start.24 = (bf16[320,128]{1,0:T(8,128)(2,1)S(1)}, bf16[320,128]{1,0:T(8,128)(2,1)S(1)}, u32[]{:S(2)}, u32[]{:S(2)}) collective-permute-start(bf16[320,128]{1,0:T(8,128)(2,1)S(1)} %get-tuple-element.56), channel_id=1, source_target_pairs={{0,12},{1,13},{2,14},{3,15},{4,8},{5,9},{6,10},{7,11},{8,4},{9,5},... | collective-permute-start | bytes 245768 | tf_op jit(solution)/shard_map/ppermute | solution.py:376
  101.2 8.6 %collective-permute-start.25 = (bf16[320,128]{1,0:T(8,128)(2,1)S(1)}, bf16[320,128]{1,0:T(8,128)(2,1)S(1)}, u32[]{:S(2)}, u32[]{:S(2)}) collective-permute-start(bf16[320,128]{1,0:T(8,128)(2,1)S(1)} %get-tuple-element.58), channel_id=1, source_target_pairs={{0,8},{1,9},{2,10},{3,11},{4,12},{5,13},{6,14},{7,15},{8,0},{9,1},... | collective-permute-start | bytes 245768 | tf_op jit(solution)/shard_map/ppermute | solution.py:376
  102.2 7.6 %collective-permute-start.26 = (bf16[320,128]{1,0:T(8,128)(2,1)S(1)}, bf16[320,128]{1,0:T(8,128)(2,1)S(1)}, u32[]{:S(2)}, u32[]{:S(2)}) collective-permute-start(bf16[320,128]{1,0:T(8,128)(2,1)S(1)} %get-tuple-element.57), channel_id=1, source_target_pairs={{0,4},{1,5},{2,6},{3,7},{4,0},{5,1},{6,2},{7,3},{8,12},{9,13},{10,... | collective-permute-start | bytes 245768 | tf_op jit(solution)/shard_map/ppermute | solution.py:376
  104.3 5.5 %collective-permute-start.27 = (bf16[320,128]{1,0:T(8,128)(2,1)S(1)}, bf16[320,128]{1,0:T(8,128)(2,1)S(1)}, u32[]{:S(2)}, u32[]{:S(2)}) collective-permute-start(bf16[320,128]{1,0:T(8,128)(2,1)S(1)} %slice.159), channel_id=1, source_target_pairs={{0,2},{1,3},{2,0},{3,1},{4,6},{5,7},{6,4},{7,5},{8,10},{9,11},{10,... | collective-permute-start | bytes 245768 | tf_op jit(solution)/shard_map/ppermute | solution.py:376
  110.0 6.9 %collective-permute-start.28 = (bf16[320,128]{1,0:T(8,128)(2,1)S(1)}, bf16[320,128]{1,0:T(8,128)(2,1)S(1)}, u32[]{:S(2)}, u32[]{:S(2)}) collective-permute-start(bf16[320,128]{1,0:T(8,128)(2,1)S(1)} %get-tuple-element.50), channel_id=1, source_target_pairs={{0,8},{1,9},{2,10},{3,11},{4,12},{5,13},{6,14},{7,15},{8,0},{9,1},... | collective-permute-start | bytes 245768 | tf_op jit(solution)/shard_map/ppermute | solution.py:376
  110.1 6.8 %collective-permute-start.29 = (bf16[320,128]{1,0:T(8,128)(2,1)S(1)}, bf16[320,128]{1,0:T(8,128)(2,1)S(1)}, u32[]{:S(2)}, u32[]{:S(2)}) collective-permute-start(bf16[320,128]{1,0:T(8,128)(2,1)S(1)} %get-tuple-element.50), channel_id=1, source_target_pairs={{0,4},{1,5},{2,6},{3,7},{4,0},{5,1},{6,2},{7,3},{8,12},{9,13},{10,... | collective-permute-start | bytes 245768 | tf_op jit(solution)/shard_map/ppermute | solution.py:376
  111.9 6.3 %collective-permute-start.30 = (bf16[320,128]{1,0:T(8,128)(2,1)S(1)}, bf16[320,128]{1,0:T(8,128)(2,1)S(1)}, u32[]{:S(2)}, u32[]{:S(2)}) collective-permute-start(bf16[320,128]{1,0:T(8,128)(2,1)S(1)} %get-tuple-element.50), channel_id=1, source_target_pairs={{0,12},{1,13},{2,14},{3,15},{4,8},{5,9},{6,10},{7,11},{8,4},{9,5},... | collective-permute-start | bytes 245768 | tf_op jit(solution)/shard_map/ppermute | solution.py:376
  114.5 5.3 %collective-permute-start.31 = (bf16[320,128]{1,0:T(8,128)(2,1)S(1)}, bf16[320,128]{1,0:T(8,128)(2,1)S(1)}, u32[]{:S(2)}, u32[]{:S(2)}) collective-permute-start(bf16[320,128]{1,0:T(8,128)(2,1)S(1)} %get-tuple-element.50), channel_id=1, source_target_pairs={{0,2},{1,3},{2,0},{3,1},{4,6},{5,7},{6,4},{7,5},{8,10},{9,11},{10,... | collective-permute-start | bytes 245768 | tf_op jit(solution)/shard_map/ppermute | solution.py:376
  118.3 6.3 %collective-permute-start.32 = (bf16[960,128]{1,0:T(8,128)(2,1)S(1)}, bf16[960,128]{1,0:T(8,128)(2,1)S(1)}, u32[]{:S(2)}, u32[]{:S(2)}) collective-permute-start(bf16[960,128]{1,0:T(8,128)(2,1)S(1)} %pad_maximum_fusion.1), channel_id=1, source_target_pairs={{0,2},{1,3},{2,0},{3,1},{4,6},{5,7},{6,4},{7,5},{8,10},{9,11},{10,... | collective-permute-start | bytes 737288 | tf_op jit(solution)/shard_map/ppermute | solution.py:376
  119.8 4.8 %collective-permute-start.33 = (bf16[1600,128]{1,0:T(8,128)(2,1)S(1)}, bf16[1600,128]{1,0:T(8,128)(2,1)S(1)}, u32[]{:S(2)}, u32[]{:S(2)}) collective-permute-start(bf16[1600,128]{1,0:T(8,128)(2,1)S(1)} %constant_dynamic-update-slice_fusion.10.refs_0_), channel_id=1, source_target_pairs={{0,1},{1,0},{2,3},{3,2},{4,5},{5,4},{6,7},{7,6},{8,9},{9,8},{10,11... | collective-permute-start | bytes 1228808 | tf_op jit(solution)/shard_map/ppermute | solution.py:376
  139.5 9.2 %collective-permute-start.37 = (bf16[2048,128]{1,0:T(8,128)(2,1)S(1)}, bf16[2048,128]{1,0:T(8,128)(2,1)S(1)}, u32[]{:S(2)}, u32[]{:S(2)}) collective-permute-start(bf16[2048,128]{1,0:T(8,128)(2,1)S(1)} %add_convert_fusion), channel_id=1, source_target_pairs={{0,2},{1,5},{2,0},{3,7},{4,6},{5,1},{6,4},{7,3},{8,10},{9,13},{10,... | collective-permute-start | bytes 1572872 | tf_op jit(solution)/shard_map/ppermute | solution.py:376
  149.0 7.9 %collective-permute-start.38 = (bf16[512,128]{1,0:T(8,128)(2,1)S(1)}, bf16[512,128]{1,0:T(8,128)(2,1)S(1)}, u32[]{:S(2)}, u32[]{:S(2)}) collective-permute-start(bf16[512,128]{1,0:T(8,128)(2,1)S(1)} %get-tuple-element.53), channel_id=1, source_target_pairs={{0,12},{1,11},{2,14},{3,9},{4,8},{5,15},{6,10},{7,13},{8,4},{9,3},... | collective-permute-start | bytes 393224 | tf_op jit(solution)/shard_map/ppermute | solution.py:376
  151.5 13.2 %collective-permute-start.39 = (bf16[512,128]{1,0:T(8,128)(2,1)S(1)}, bf16[512,128]{1,0:T(8,128)(2,1)S(1)}, u32[]{:S(2)}, u32[]{:S(2)}) collective-permute-start(bf16[512,128]{1,0:T(8,128)(2,1)S(1)} %get-tuple-element.55), channel_id=1, source_target_pairs={{0,8},{1,3},{2,10},{3,1},{4,12},{5,7},{6,14},{7,5},{8,0},{9,11},{1... | collective-permute-start | bytes 393224 | tf_op jit(solution)/shard_map/ppermute | solution.py:376
  153.0 11.7 %collective-permute-start.40 = (bf16[512,128]{1,0:T(8,128)(2,1)S(1)}, bf16[512,128]{1,0:T(8,128)(2,1)S(1)}, u32[]{:S(2)}, u32[]{:S(2)}) collective-permute-start(bf16[512,128]{1,0:T(8,128)(2,1)S(1)} %get-tuple-element.54), channel_id=1, source_target_pairs={{0,4},{1,9},{2,6},{3,11},{4,0},{5,13},{6,2},{7,15},{8,12},{9,1},{1... | collective-permute-start | bytes 393224 | tf_op jit(solution)/shard_map/ppermute | solution.py:376
  (10 other events, 21.0 us)

commit v15 on v14

--- a/solution.py
+++ b/solution.py
@@ -45,18 +45,16 @@
 
 
 class Part:
-    def __init__(self, ref, begin, width=1):
-        self.ref, self.begin, self.width = ref, begin, width
+    def __init__(self, ref, begin):
+        self.ref, self.begin = ref, begin
 
     def __getitem__(self, index):
-        if isinstance(index, tuple):
-            index = index[0] * self.width + index[1]
         return self.ref[self.begin + index]
 
 
 def scalar_parts(scalars, groups):
     seq, order, counts = (Part(scalars, part * groups) for part in range(3))
-    return seq, order, counts, Part(scalars, 3 * groups, SLOTS), scalars[groups * (3 + SLOTS)]
+    return seq, order, counts, scalars[3 * groups]
 
 
 def group_at(index, seq, order, counts):
@@ -65,9 +63,9 @@
     return position, group, counts[group]
 
 
-def support_kernel(begin, groups, scalars, dictionary, *refs):
+def support_kernel(begin, groups, scalars, support, dictionary, *refs):
     out, held, picks, ids, sems, out_sems = refs[-6:]
-    seq, order, counts, support, _ = scalar_parts(scalars, groups)
+    seq, order, counts, _ = scalar_parts(scalars, groups)
     entries, rows, _ = held.shape
     pairs = entries // 2
 
@@ -123,14 +121,14 @@
     lax.fori_loop(0, pairs, drain, 0)
 
 
-def collect_support(scalars, groups, dictionary, pairs, part, *before):
+def collect_support(scalars, support, groups, dictionary, pairs, part, *before):
     rows = dictionary.shape[0]
     pairs = pairs // SUPPORT_PARTS
     entries = 2 * pairs
     return pl.pallas_call(
         functools.partial(support_kernel, part * entries, groups),
         grid_spec=pltpu.PrefetchScalarGridSpec(
-            num_scalar_prefetch=1,
+            num_scalar_prefetch=2,
             grid=(),
             in_specs=[pl.BlockSpec(memory_space=pltpu.HBM)] * (1 + len(before)),
             out_specs=pl.BlockSpec(memory_space=pltpu.HBM),
@@ -145,9 +143,9 @@
         out_shape=jax.ShapeDtypeStruct((HELD_BYTES // (rows * LANES * 2), rows, LANES), dictionary.dtype),
         compiler_params=pltpu.CompilerParams(vmem_limit_bytes=SUPPORT_VMEM),
         cost_estimate=pl.CostEstimate(flops=0, transcendentals=0, bytes_accessed=6 * pairs * rows * LANES * 2),
-        input_output_aliases={2: 0} if before else {},
+        input_output_aliases={3: 0} if before else {},
         name="collect_support",
-    )(scalars, dictionary, *before)
+    )(scalars, support, dictionary, *before)
 
 
 def stage_distances(devices):
@@ -165,7 +163,7 @@
 
 
 def gradient_kernel(mode, shards, pairs, groups, scalars, blocks, *refs):
-    seq, order, counts, _, me = scalar_parts(scalars, groups)
+    seq, order, counts, me = scalar_parts(scalars, groups)
     refs = list(refs)
     take = lambda: refs.pop(0)
     gathered, targets = [take() for _ in range(4)], take()
@@ -380,8 +378,7 @@
     core, row, *columns = stage_distances(lax.axis_size("rows"))
     apart = [slot_distance(slot, columns) for slot in range(lax.axis_size("rows") // 4)]
     made = ()
-    arrived = {distance: exchange(own, distance) for distance in sorted(apart[1:] + [row], reverse=True)}
-    near = jnp.concatenate([own] + [arrived[distance] for distance in apart[1:] + [row]], axis=0)
+    near = jnp.concatenate([own] + [exchange(own, distance) for distance in apart[1:] + [row]], axis=0)
     if beside:
         near, *made = lax.optimization_barrier((near, beside[0]()))
     other = exchange(near[own.shape[0] : len(apart) * own.shape[0]], row)
@@ -419,7 +416,7 @@
     size = 2 * keep.shape[0] // devices
     sent = sums.astype(jnp.bfloat16)
     total = sums[:size]
-    for slot in sorted(range(1, devices // 4), key=lambda slot: -slot_distance(slot, even[2:])):
+    for slot in range(1, devices // 4):
         share = sent[slot * size : (slot + 1) * size]
         total = total + exchange(share, slot_distance(slot, even[2:]), slot_distance(slot, odd[2:])).astype(jnp.float32)
     return total
@@ -448,8 +445,8 @@
     laid = laid.reshape(SLOT_PAIRS * PATCHES, LANES)
     live = jnp.sum(jnp.where(group_order[:, None] == jnp.arange(groups)[None, :], counts[None, :], 0), axis=1)
     own = position.astype(jnp.int32).reshape(1)
-    scalars = jnp.concatenate([packed_order(live), group_order, counts, support.reshape(groups * SLOTS), own])
-    collect = functools.partial(collect_support, scalars, groups, dictionary, pairs)
+    scalars = jnp.concatenate([packed_order(live), group_order, counts, own])
+    collect = functools.partial(collect_support, scalars, support, groups, dictionary, pairs)
     gathered, (blocks,) = gather_shards(laid, [functools.partial(collect, part) for part in range(SUPPORT_PARTS)])
 
     targets = patches.T

time: 167 us -> 166 us (level)
  waiting for transfers between devices: 63.9 us -> 60.8 us
    ppermute x41, waiting for transfers between devices: 63.9 us -> 60.8 us  [exchange(): lax.ppermute(value, 'rows', [(i, i ^ apart[i % 2]) for i in range(devices)])]
  transfers between devices with their start and end apart: 41 -> 41, of which waited for: 22 -> 22; matrix products, arithmetic and copies ran while one was open for 3% -> 2% of each run, Pallas kernels for 10% -> 11%
where the time goes in v15:
time: 166 us; the launch traced here: 164 us
  waiting for transfers between devices  60.8 us (37%)
  Pallas kernels  49.7 us (30%)
  starting transfers between devices  44.6 us (27%)
  local copies, waits for them, and re-layouts  5.56 us (3%)
  other arithmetic  3.03 us (2%)
    ppermute x41, waiting for transfers between devices, exchange(): lax.ppermute(value, 'rows', [(i, i ^ apart[i % 2]) for i in range(devices)])  60.8 us
    ppermute x41, starting transfers between devices, exchange(): lax.ppermute(value, 'rows', [(i, i ^ apart[i % 2]) for i in range(devices)])  44.6 us
    pallas_call x3, Pallas kernels, gradient_call(): pl.pallas_call(functools.partial(gradient_kernel, mode, shards, pairs, gr...  32.1 us
    pallas_call x2, Pallas kernels, collect_support(): pl.pallas_call(functools.partial(support_kernel, part * entries, groups),...  17.6 us
  transfers between devices with their start and end apart: 41, of which 22 were waited for; matrix products, arithmetic and copies ran while one was open for 2% of the time, Pallas kernels for 11%

profile of v15, /device:TPU:0, one launch (start us, length us, event | category | flops | bytes accessed | tf_op | source)
XLA Modules:
  0.0 164.0 jit_solution(3048935285875577027)
XLA Ops:
  1.6 4.1 %collective-permute-start = (bf16[512,128]{1,0:T(8,128)(2,1)S(1)}, bf16[512,128]{1,0:T(8,128)(2,1)S(1)}, u32[]{:S(2)}, u32[]{:S(2)}) collective-permute-start(bf16[512,128]{1,0:T(8,128)(2,1)S(1)} %reshape.67), channel_id=1, source_target_pairs={{0,8},{1,9},{2,10},{3,11},{4,12},{5,13},{6,14},{7,15},{8,0},{9,1},... | collective-permute-start | bytes 393224 | tf_op jit(solution)/shard_map/ppermute | solution.py:374
  5.7 1.6 collective-permute-start.1
  7.3 1.7 %collective-permute-start.3 = (bf16[512,128]{1,0:T(8,128)(2,1)S(1)}, bf16[512,128]{1,0:T(8,128)(2,1)S(1)}, u32[]{:S(2)}, u32[]{:S(2)}) collective-permute-start(bf16[512,128]{1,0:T(8,128)(2,1)S(1)} %reshape.67), channel_id=1, source_target_pairs={{0,2},{1,3},{2,0},{3,1},{4,6},{5,7},{6,4},{7,5},{8,10},{9,11},{10,... | collective-permute-start | bytes 393224 | tf_op jit(solution)/shard_map/ppermute | solution.py:374
  11.7 8.6 %collect_support.2.refs_0_ = bf16[520,512,128]{2,1,0:T(8,128)(2,1)} custom-call(s32[49]{0:T(128)S(1)} %pad_add_fusion.scalars, s32[16,16]{1,0:T(8,128)S(1)} %copy-done, bf16[512,32768]{1,0:T(8,128)(2,1)} %dictionary.3), custom_call_target="tpu_custom_call" | custom-call | bytes 31457280 | tf_op jit(solution)/shard_map/collect_support/pallas_call | solution.py:128
  20.8 9.0 %collect_support.3.blocks = bf16[520,512,128]{2,1,0:T(8,128)(2,1)} custom-call(s32[49]{0:T(128)S(1)} %pad_add_fusion.scalars, s32[16,16]{1,0:T(8,128)S(1)} %copy-done, bf16[512,32768]{1,0:T(8,128)(2,1)} %dictionary.3, bf16[520,512,128]{2,1,0:T(8,128)(2,1)} %collect_support.2.refs_0_), custom_call_target="tpu_custom_call", output_to_operand_aliasing={{}: (3, {})} | custom-call | bytes 31457280 | tf_op jit(solution)/shard_map/collect_support/pallas_call | solution.py:128
  32.3 10.5 %gradient.3 = (f32[2560,128]{1,0:T(8,128)S(1)}, bf16[1600,128]{1,0:T(8,128)(2,1)S(1)}, bf16[960,128]{1,0:T(8,128)(2,1)S(1)}, bf16[320,128]{1,0:T(8,128)(2,1)S(1)}, f32[320,128]{1,0:T(8,128)S(1)}) custom-call(s32[49]{0:T(128)S(1)} %pad_add_fusion.scalars, bf16[520,512,128]{2,1,0:T(8,128)(2,1)} %collect_support.3.blocks, ...), custom_call_target="tpu_custom_call" | custom-call | flops 5368709120 | bytes 10485760 | tf_op jit(solution)/shard_map/gradient/pallas_call | solution.py:351
  44.4 1.7 %collective-permute-start.9 = (bf16[960,128]{1,0:T(8,128)(2,1)S(1)}, bf16[960,128]{1,0:T(8,128)(2,1)S(1)}, u32[]{:S(2)}, u32[]{:S(2)}) collective-permute-start(bf16[960,128]{1,0:T(8,128)(2,1)S(1)} %add_convert_fusion.2), channel_id=1, source_target_pairs={{0,2},{1,3},{2,0},{3,1},{4,6},{5,7},{6,4},{7,5},{8,10},{9,11},{10,... | collective-permute-start | bytes 737288 | tf_op jit(solution)/shard_map/ppermute | solution.py:374
  46.1 6.5 %collective-permute-done.9 = bf16[960,128]{1,0:T(8,128)(2,1)S(1)} collective-permute-done((bf16[960,128]{1,0:T(8,128)(2,1)S(1)}, bf16[960,128]{1,0:T(8,128)(2,1)S(1)}, u32[]{:S(2)}, u32[]{:S(2)}) %collective-permute-start.9) | collective-permute-done | bytes 245792 | tf_op jit(solution)/shard_map/ppermute | solution.py:374
  52.7 3.6 %collective-permute-start.10 = (bf16[320,128]{1,0:T(8,128)(2,1)S(1)}, bf16[320,128]{1,0:T(8,128)(2,1)S(1)}, u32[]{:S(2)}, u32[]{:S(2)}) collective-permute-start(bf16[320,128]{1,0:T(8,128)(2,1)S(1)} %get-tuple-element.59), channel_id=1, source_target_pairs={{0,12},{1,13},{2,14},{3,15},{4,8},{5,9},{6,10},{7,11},{8,4},{9,5},... | collective-permute-start | bytes 245768 | tf_op jit(solution)/shard_map/ppermute | solution.py:374
  59.6 3.0 %collective-permute-done.11 = bf16[320,128]{1,0:T(8,128)(2,1)S(1)} collective-permute-done((bf16[320,128]{1,0:T(8,128)(2,1)S(1)}, bf16[320,128]{1,0:T(8,128)(2,1)S(1)}, u32[]{:S(2)}, u32[]{:S(2)}) %collective-permute-start.11) | collective-permute-done | bytes 81952 | tf_op jit(solution)/shard_map/ppermute | solution.py:374
  63.9 2.0 %collective-permute-start.15 = (bf16[320,128]{1,0:T(8,128)(2,1)S(1)}, bf16[320,128]{1,0:T(8,128)(2,1)S(1)}, u32[]{:S(2)}, u32[]{:S(2)}) collective-permute-start(bf16[320,128]{1,0:T(8,128)(2,1)S(1)} %get-tuple-element.52), channel_id=1, source_target_pairs={{0,4},{1,5},{2,6},{3,7},{4,0},{5,1},{6,2},{7,3},{8,12},{9,13},{10,... | collective-permute-start | bytes 245768 | tf_op jit(solution)/shard_map/ppermute | solution.py:374
  67.1 1.5 collective-permute-start.17
  68.7 2.2 %collective-permute-done.14 = bf16[320,128]{1,0:T(8,128)(2,1)S(1)} collective-permute-done((bf16[320,128]{1,0:T(8,128)(2,1)S(1)}, bf16[320,128]{1,0:T(8,128)(2,1)S(1)}, u32[]{:S(2)}, u32[]{:S(2)}) %collective-permute-start.14) | collective-permute-done | bytes 81952 | tf_op jit(solution)/shard_map/ppermute | solution.py:374
  72.3 1.5 collective-permute-start.18
  74.0 4.6 %collective-permute-done.18.refs_1_ = bf16[960,128]{1,0:T(8,128)(2,1)S(1)} collective-permute-done((bf16[960,128]{1,0:T(8,128)(2,1)S(1)}, bf16[960,128]{1,0:T(8,128)(2,1)S(1)}, u32[]{:S(2)}, u32[]{:S(2)}) %collective-permute-start.18) | collective-permute-done | bytes 245792 | tf_op jit(solution)/shard_map/ppermute | solution.py:374
  78.5 1.5 collective-permute-done.20.refs_3_
  80.1 10.2 %gradient.4 = (f32[2560,128]{1,0:T(8,128)S(1)}, bf16[1600,128]{1,0:T(8,128)(2,1)S(1)}, bf16[960,128]{1,0:T(8,128)(2,1)S(1)}) custom-call(s32[49]{0:T(128)S(1)} %pad_add_fusion.scalars, bf16[520,512,128]{2,1,0:T(8,128)(2,1)} %collect_support.3.blocks, bf16[1600,128]{1,0:T(8,128)(2,1)S(1)} %constant_dynamic-update-slice_fusion.5.refs_0_, ...), custom_call_target="tpu_custom_call" | custom-call | flops 5368709120 | bytes 10485760 | tf_op jit(solution)/shard_map/gradient/pallas_call | solution.py:351
  91.9 1.5 collective-permute-start.23
  93.5 6.4 %collective-permute-done.23 = bf16[960,128]{1,0:T(8,128)(2,1)S(1)} collective-permute-done((bf16[960,128]{1,0:T(8,128)(2,1)S(1)}, bf16[960,128]{1,0:T(8,128)(2,1)S(1)}, u32[]{:S(2)}, u32[]{:S(2)}) %collective-permute-start.23) | collective-permute-done | bytes 245792 | tf_op jit(solution)/shard_map/ppermute | solution.py:374
  100.0 1.7 %collective-permute-start.24 = (bf16[320,128]{1,0:T(8,128)(2,1)S(1)}, bf16[320,128]{1,0:T(8,128)(2,1)S(1)}, u32[]{:S(2)}, u32[]{:S(2)}) collective-permute-start(bf16[320,128]{1,0:T(8,128)(2,1)S(1)} %get-tuple-element.56), channel_id=1, source_target_pairs={{0,12},{1,13},{2,14},{3,15},{4,8},{5,9},{6,10},{7,11},{8,4},{9,5},... | collective-permute-start | bytes 245768 | tf_op jit(solution)/shard_map/ppermute | solution.py:374
  102.9 1.6 %collective-permute-start.26 = (bf16[320,128]{1,0:T(8,128)(2,1)S(1)}, bf16[320,128]{1,0:T(8,128)(2,1)S(1)}, u32[]{:S(2)}, u32[]{:S(2)}) collective-permute-start(bf16[320,128]{1,0:T(8,128)(2,1)S(1)} %get-tuple-element.57), channel_id=1, source_target_pairs={{0,4},{1,5},{2,6},{3,7},{4,0},{5,1},{6,2},{7,3},{8,12},{9,13},{10,... | collective-permute-start | bytes 245768 | tf_op jit(solution)/shard_map/ppermute | solution.py:374
  107.3 2.7 %collective-permute-done.25 = bf16[320,128]{1,0:T(8,128)(2,1)S(1)} collective-permute-done((bf16[320,128]{1,0:T(8,128)(2,1)S(1)}, bf16[320,128]{1,0:T(8,128)(2,1)S(1)}, u32[]{:S(2)}, u32[]{:S(2)}) %collective-permute-start.25) | collective-permute-done | bytes 81952 | tf_op jit(solution)/shard_map/ppermute | solution.py:374
  110.2 2.2 %collective-permute-start.29 = (bf16[320,128]{1,0:T(8,128)(2,1)S(1)}, bf16[320,128]{1,0:T(8,128)(2,1)S(1)}, u32[]{:S(2)}, u32[]{:S(2)}) collective-permute-start(bf16[320,128]{1,0:T(8,128)(2,1)S(1)} %get-tuple-element.50), channel_id=1, source_target_pairs={{0,4},{1,5},{2,6},{3,7},{4,0},{5,1},{6,2},{7,3},{8,12},{9,13},{10,... | collective-permute-start | bytes 245768 | tf_op jit(solution)/shard_map/ppermute | solution.py:374
  112.4 2.2 %collective-permute-start.30 = (bf16[320,128]{1,0:T(8,128)(2,1)S(1)}, bf16[320,128]{1,0:T(8,128)(2,1)S(1)}, u32[]{:S(2)}, u32[]{:S(2)}) collective-permute-start(bf16[320,128]{1,0:T(8,128)(2,1)S(1)} %get-tuple-element.50), channel_id=1, source_target_pairs={{0,12},{1,13},{2,14},{3,15},{4,8},{5,9},{6,10},{7,11},{8,4},{9,5},... | collective-permute-start | bytes 245768 | tf_op jit(solution)/shard_map/ppermute | solution.py:374
  115.5 1.8 %collective-permute-done.28 = bf16[320,128]{1,0:T(8,128)(2,1)S(1)} collective-permute-done((bf16[320,128]{1,0:T(8,128)(2,1)S(1)}, bf16[320,128]{1,0:T(8,128)(2,1)S(1)}, u32[]{:S(2)}, u32[]{:S(2)}) %collective-permute-start.28) | collective-permute-done | bytes 81952 | tf_op jit(solution)/shard_map/ppermute | solution.py:374
  120.1 4.9 %collective-permute-done.32.refs_1_ = bf16[960,128]{1,0:T(8,128)(2,1)S(1)} collective-permute-done((bf16[960,128]{1,0:T(8,128)(2,1)S(1)}, bf16[960,128]{1,0:T(8,128)(2,1)S(1)}, u32[]{:S(2)}, u32[]{:S(2)}) %collective-permute-start.32) | collective-permute-done | bytes 245792 | tf_op jit(solution)/shard_map/ppermute | solution.py:374
  125.1 1.5 collective-permute-done.34.refs_3_
  126.6 11.4 %gradient.5 = (f32[4096,128]{1,0:T(8,128)S(1)}, bf16[2048,128]{1,0:T(8,128)(2,1)S(1)}, bf16[2048,128]{1,0:T(8,128)(2,1)S(1)}, bf16[8,64,128]{2,1,0:T(8,128)(2,1)S(1)}, f32[64,128]{1,0:T(8,128)S(1)}) custom-call(s32[49]{0:T(128)S(1)} %pad_add_fusion.scalars, bf16[520,512,128]{2,1,0:T(8,128)(2,1)} %collect_support.3.blocks, ...), custom_call_target="tpu_custom_call" | custom-call | flops 5368709120 | bytes 10485760 | tf_op jit(solution)/shard_map/gradient/pallas_call | solution.py:351
  141.3 8.1 %collective-permute-done.37 = bf16[2048,128]{1,0:T(8,128)(2,1)S(1)} collective-permute-done((bf16[2048,128]{1,0:T(8,128)(2,1)S(1)}, bf16[2048,128]{1,0:T(8,128)(2,1)S(1)}, u32[]{:S(2)}, u32[]{:S(2)}) %collective-permute-start.37) | collective-permute-done | bytes 524320 | tf_op jit(solution)/shard_map/ppermute | solution.py:374
  149.6 2.5 %collective-permute-start.38 = (bf16[512,128]{1,0:T(8,128)(2,1)S(1)}, bf16[512,128]{1,0:T(8,128)(2,1)S(1)}, u32[]{:S(2)}, u32[]{:S(2)}) collective-permute-start(bf16[512,128]{1,0:T(8,128)(2,1)S(1)} %get-tuple-element.53), channel_id=1, source_target_pairs={{0,8},{1,3},{2,10},{3,1},{4,12},{5,7},{6,14},{7,5},{8,0},{9,11},{1... | collective-permute-start | bytes 393224 | tf_op jit(solution)/shard_map/ppermute | solution.py:374
  152.3 2.0 %collective-permute-start.40 = (bf16[512,128]{1,0:T(8,128)(2,1)S(1)}, bf16[512,128]{1,0:T(8,128)(2,1)S(1)}, u32[]{:S(2)}, u32[]{:S(2)}) collective-permute-start(bf16[512,128]{1,0:T(8,128)(2,1)S(1)} %get-tuple-element.54), channel_id=1, source_target_pairs={{0,12},{1,11},{2,14},{3,9},{4,8},{5,15},{6,10},{7,13},{8,4},{9,3},... | collective-permute-start | bytes 393224 | tf_op jit(solution)/shard_map/ppermute | solution.py:374
  154.2 6.9 %collective-permute-done.38 = bf16[512,128]{1,0:T(8,128)(2,1)S(1)} collective-permute-done((bf16[512,128]{1,0:T(8,128)(2,1)S(1)}, bf16[512,128]{1,0:T(8,128)(2,1)S(1)}, u32[]{:S(2)}, u32[]{:S(2)}) %collective-permute-start.38) | collective-permute-done | bytes 131104 | tf_op jit(solution)/shard_map/ppermute | solution.py:374
  (107 shorter events, 32.4 us)
Async XLA Ops:
  1.6 18.7 %collective-permute-start = (bf16[512,128]{1,0:T(8,128)(2,1)S(1)}, bf16[512,128]{1,0:T(8,128)(2,1)S(1)}, u32[]{:S(2)}, u32[]{:S(2)}) collective-permute-start(bf16[512,128]{1,0:T(8,128)(2,1)S(1)} %reshape.67), channel_id=1, source_target_pairs={{0,8},{1,9},{2,10},{3,11},{4,12},{5,13},{6,14},{7,15},{8,0},{9,1},... | collective-permute-start | bytes 393224 | tf_op jit(solution)/shard_map/ppermute | solution.py:374
  5.7 14.6 %collective-permute-start.1 = (bf16[512,128]{1,0:T(8,128)(2,1)S(1)}, bf16[512,128]{1,0:T(8,128)(2,1)S(1)}, u32[]{:S(2)}, u32[]{:S(2)}) collective-permute-start(bf16[512,128]{1,0:T(8,128)(2,1)S(1)} %reshape.67), channel_id=1, source_target_pairs={{0,4},{1,5},{2,6},{3,7},{4,0},{5,1},{6,2},{7,3},{8,12},{9,13},{10,... | collective-permute-start | bytes 393224 | tf_op jit(solution)/shard_map/ppermute | solution.py:374
  7.3 13.1 %collective-permute-start.2 = (bf16[512,128]{1,0:T(8,128)(2,1)S(1)}, bf16[512,128]{1,0:T(8,128)(2,1)S(1)}, u32[]{:S(2)}, u32[]{:S(2)}) collective-permute-start(bf16[512,128]{1,0:T(8,128)(2,1)S(1)} %reshape.67), channel_id=1, source_target_pairs={{0,12},{1,13},{2,14},{3,15},{4,8},{5,9},{6,10},{7,11},{8,4},{9,5},... | collective-permute-start | bytes 393224 | tf_op jit(solution)/shard_map/ppermute | solution.py:374
  7.3 13.1 %collective-permute-start.3 = (bf16[512,128]{1,0:T(8,128)(2,1)S(1)}, bf16[512,128]{1,0:T(8,128)(2,1)S(1)}, u32[]{:S(2)}, u32[]{:S(2)}) collective-permute-start(bf16[512,128]{1,0:T(8,128)(2,1)S(1)} %reshape.67), channel_id=1, source_target_pairs={{0,2},{1,3},{2,0},{3,1},{4,6},{5,7},{6,4},{7,5},{8,10},{9,11},{10,... | collective-permute-start | bytes 393224 | tf_op jit(solution)/shard_map/ppermute | solution.py:374
  20.5 9.9 %collective-permute-start.4 = (bf16[1536,128]{1,0:T(8,128)(2,1)S(1)}, bf16[1536,128]{1,0:T(8,128)(2,1)S(1)}, u32[]{:S(2)}, u32[]{:S(2)}) collective-permute-start(bf16[1536,128]{1,0:T(8,128)(2,1)S(1)} %slice.75), channel_id=1, source_target_pairs={{0,2},{1,3},{2,0},{3,1},{4,6},{5,7},{6,4},{7,5},{8,10},{9,11},{10,... | collective-permute-start | bytes 1179656 | tf_op jit(solution)/shard_map/ppermute | solution.py:374
  20.8 11.1 %collective-permute-start.5 = (bf16[2560,128]{1,0:T(8,128)(2,1)S(1)}, bf16[2560,128]{1,0:T(8,128)(2,1)S(1)}, u32[]{:S(2)}, u32[]{:S(2)}) collective-permute-start(bf16[2560,128]{1,0:T(8,128)(2,1)S(1)} %constant_dynamic-update-slice_fusion.refs_0_), channel_id=1, source_target_pairs={{0,1},{1,0},{2,3},{3,2},{4,5},{5,4},{6,7},{7,6},{8,9},{9,8},{10,11... | collective-permute-start | bytes 1966088 | tf_op jit(solution)/shard_map/ppermute | solution.py:374
  44.4 8.3 %collective-permute-start.9 = (bf16[960,128]{1,0:T(8,128)(2,1)S(1)}, bf16[960,128]{1,0:T(8,128)(2,1)S(1)}, u32[]{:S(2)}, u32[]{:S(2)}) collective-permute-start(bf16[960,128]{1,0:T(8,128)(2,1)S(1)} %add_convert_fusion.2), channel_id=1, source_target_pairs={{0,2},{1,3},{2,0},{3,1},{4,6},{5,7},{6,4},{7,5},{8,10},{9,11},{10,... | collective-permute-start | bytes 737288 | tf_op jit(solution)/shard_map/ppermute | solution.py:374
  52.7 6.8 %collective-permute-start.10 = (bf16[320,128]{1,0:T(8,128)(2,1)S(1)}, bf16[320,128]{1,0:T(8,128)(2,1)S(1)}, u32[]{:S(2)}, u32[]{:S(2)}) collective-permute-start(bf16[320,128]{1,0:T(8,128)(2,1)S(1)} %get-tuple-element.59), channel_id=1, source_target_pairs={{0,12},{1,13},{2,14},{3,15},{4,8},{5,9},{6,10},{7,11},{8,4},{9,5},... | collective-permute-start | bytes 245768 | tf_op jit(solution)/shard_map/ppermute | solution.py:374
  56.3 6.2 %collective-permute-start.11 = (bf16[320,128]{1,0:T(8,128)(2,1)S(1)}, bf16[320,128]{1,0:T(8,128)(2,1)S(1)}, u32[]{:S(2)}, u32[]{:S(2)}) collective-permute-start(bf16[320,128]{1,0:T(8,128)(2,1)S(1)} %get-tuple-element.61), channel_id=1, source_target_pairs={{0,8},{1,9},{2,10},{3,11},{4,12},{5,13},{6,14},{7,15},{8,0},{9,1},... | collective-permute-start | bytes 245768 | tf_op jit(solution)/shard_map/ppermute | solution.py:374
  56.3 6.2 %collective-permute-start.12 = (bf16[320,128]{1,0:T(8,128)(2,1)S(1)}, bf16[320,128]{1,0:T(8,128)(2,1)S(1)}, u32[]{:S(2)}, u32[]{:S(2)}) collective-permute-start(bf16[320,128]{1,0:T(8,128)(2,1)S(1)} %get-tuple-element.60), channel_id=1, source_target_pairs={{0,4},{1,5},{2,6},{3,7},{4,0},{5,1},{6,2},{7,3},{8,12},{9,13},{10,... | collective-permute-start | bytes 245768 | tf_op jit(solution)/shard_map/ppermute | solution.py:374
  57.2 5.4 %collective-permute-start.13 = (bf16[320,128]{1,0:T(8,128)(2,1)S(1)}, bf16[320,128]{1,0:T(8,128)(2,1)S(1)}, u32[]{:S(2)}, u32[]{:S(2)}) collective-permute-start(bf16[320,128]{1,0:T(8,128)(2,1)S(1)} %slice.160), channel_id=1, source_target_pairs={{0,2},{1,3},{2,0},{3,1},{4,6},{5,7},{6,4},{7,5},{8,10},{9,11},{10,... | collective-permute-start | bytes 245768 | tf_op jit(solution)/shard_map/ppermute | solution.py:374
  62.7 8.1 %collective-permute-start.14 = (bf16[320,128]{1,0:T(8,128)(2,1)S(1)}, bf16[320,128]{1,0:T(8,128)(2,1)S(1)}, u32[]{:S(2)}, u32[]{:S(2)}) collective-permute-start(bf16[320,128]{1,0:T(8,128)(2,1)S(1)} %get-tuple-element.52), channel_id=1, source_target_pairs={{0,8},{1,9},{2,10},{3,11},{4,12},{5,13},{6,14},{7,15},{8,0},{9,1},... | collective-permute-start | bytes 245768 | tf_op jit(solution)/shard_map/ppermute | solution.py:374
  63.9 6.9 %collective-permute-start.15 = (bf16[320,128]{1,0:T(8,128)(2,1)S(1)}, bf16[320,128]{1,0:T(8,128)(2,1)S(1)}, u32[]{:S(2)}, u32[]{:S(2)}) collective-permute-start(bf16[320,128]{1,0:T(8,128)(2,1)S(1)} %get-tuple-element.52), channel_id=1, source_target_pairs={{0,4},{1,5},{2,6},{3,7},{4,0},{5,1},{6,2},{7,3},{8,12},{9,13},{10,... | collective-permute-start | bytes 245768 | tf_op jit(solution)/shard_map/ppermute | solution.py:374
  65.9 6.3 %collective-permute-start.16 = (bf16[320,128]{1,0:T(8,128)(2,1)S(1)}, bf16[320,128]{1,0:T(8,128)(2,1)S(1)}, u32[]{:S(2)}, u32[]{:S(2)}) collective-permute-start(bf16[320,128]{1,0:T(8,128)(2,1)S(1)} %get-tuple-element.52), channel_id=1, source_target_pairs={{0,12},{1,13},{2,14},{3,15},{4,8},{5,9},{6,10},{7,11},{8,4},{9,5},... | collective-permute-start | bytes 245768 | tf_op jit(solution)/shard_map/ppermute | solution.py:374
  67.1 6.7 %collective-permute-start.17 = (bf16[320,128]{1,0:T(8,128)(2,1)S(1)}, bf16[320,128]{1,0:T(8,128)(2,1)S(1)}, u32[]{:S(2)}, u32[]{:S(2)}) collective-permute-start(bf16[320,128]{1,0:T(8,128)(2,1)S(1)} %get-tuple-element.52), channel_id=1, source_target_pairs={{0,2},{1,3},{2,0},{3,1},{4,6},{5,7},{6,4},{7,5},{8,10},{9,11},{10,... | collective-permute-start | bytes 245768 | tf_op jit(solution)/shard_map/ppermute | solution.py:374
  72.3 6.3 %collective-permute-start.18 = (bf16[960,128]{1,0:T(8,128)(2,1)S(1)}, bf16[960,128]{1,0:T(8,128)(2,1)S(1)}, u32[]{:S(2)}, u32[]{:S(2)}) collective-permute-start(bf16[960,128]{1,0:T(8,128)(2,1)S(1)} %pad_maximum_fusion), channel_id=1, source_target_pairs={{0,2},{1,3},{2,0},{3,1},{4,6},{5,7},{6,4},{7,5},{8,10},{9,11},{10,... | collective-permute-start | bytes 737288 | tf_op jit(solution)/shard_map/ppermute | solution.py:374
  73.9 4.6 %collective-permute-start.19 = (bf16[1600,128]{1,0:T(8,128)(2,1)S(1)}, bf16[1600,128]{1,0:T(8,128)(2,1)S(1)}, u32[]{:S(2)}, u32[]{:S(2)}) collective-permute-start(bf16[1600,128]{1,0:T(8,128)(2,1)S(1)} %constant_dynamic-update-slice_fusion.5.refs_0_), channel_id=1, source_target_pairs={{0,1},{1,0},{2,3},{3,2},{4,5},{5,4},{6,7},{7,6},{8,9},{9,8},{10,11... | collective-permute-start | bytes 1228808 | tf_op jit(solution)/shard_map/ppermute | solution.py:374
  91.9 8.1 %collective-permute-start.23 = (bf16[960,128]{1,0:T(8,128)(2,1)S(1)}, bf16[960,128]{1,0:T(8,128)(2,1)S(1)}, u32[]{:S(2)}, u32[]{:S(2)}) collective-permute-start(bf16[960,128]{1,0:T(8,128)(2,1)S(1)} %add_convert_fusion.1), channel_id=1, source_target_pairs={{0,2},{1,3},{2,0},{3,1},{4,6},{5,7},{6,4},{7,5},{8,10},{9,11},{10,... | collective-permute-start | bytes 737288 | tf_op jit(solution)/shard_map/ppermute | solution.py:374
  100.0 7.2 %collective-permute-start.24 = (bf16[320,128]{1,0:T(8,128)(2,1)S(1)}, bf16[320,128]{1,0:T(8,128)(2,1)S(1)}, u32[]{:S(2)}, u32[]{:S(2)}) collective-permute-start(bf16[320,128]{1,0:T(8,128)(2,1)S(1)} %get-tuple-element.56), channel_id=1, source_target_pairs={{0,12},{1,13},{2,14},{3,15},{4,8},{5,9},{6,10},{7,11},{8,4},{9,5},... | collective-permute-start | bytes 245768 | tf_op jit(solution)/shard_map/ppermute | solution.py:374
  101.8 8.2 %collective-permute-start.25 = (bf16[320,128]{1,0:T(8,128)(2,1)S(1)}, bf16[320,128]{1,0:T(8,128)(2,1)S(1)}, u32[]{:S(2)}, u32[]{:S(2)}) collective-permute-start(bf16[320,128]{1,0:T(8,128)(2,1)S(1)} %get-tuple-element.58), channel_id=1, source_target_pairs={{0,8},{1,9},{2,10},{3,11},{4,12},{5,13},{6,14},{7,15},{8,0},{9,1},... | collective-permute-start | bytes 245768 | tf_op jit(solution)/shard_map/ppermute | solution.py:374
  102.9 7.1 %collective-permute-start.26 = (bf16[320,128]{1,0:T(8,128)(2,1)S(1)}, bf16[320,128]{1,0:T(8,128)(2,1)S(1)}, u32[]{:S(2)}, u32[]{:S(2)}) collective-permute-start(bf16[320,128]{1,0:T(8,128)(2,1)S(1)} %get-tuple-element.57), channel_id=1, source_target_pairs={{0,4},{1,5},{2,6},{3,7},{4,0},{5,1},{6,2},{7,3},{8,12},{9,13},{10,... | collective-permute-start | bytes 245768 | tf_op jit(solution)/shard_map/ppermute | solution.py:374
  104.5 5.5 %collective-permute-start.27 = (bf16[320,128]{1,0:T(8,128)(2,1)S(1)}, bf16[320,128]{1,0:T(8,128)(2,1)S(1)}, u32[]{:S(2)}, u32[]{:S(2)}) collective-permute-start(bf16[320,128]{1,0:T(8,128)(2,1)S(1)} %slice.159), channel_id=1, source_target_pairs={{0,2},{1,3},{2,0},{3,1},{4,6},{5,7},{6,4},{7,5},{8,10},{9,11},{10,... | collective-permute-start | bytes 245768 | tf_op jit(solution)/shard_map/ppermute | solution.py:374
  110.2 7.1 %collective-permute-start.28 = (bf16[320,128]{1,0:T(8,128)(2,1)S(1)}, bf16[320,128]{1,0:T(8,128)(2,1)S(1)}, u32[]{:S(2)}, u32[]{:S(2)}) collective-permute-start(bf16[320,128]{1,0:T(8,128)(2,1)S(1)} %get-tuple-element.50), channel_id=1, source_target_pairs={{0,8},{1,9},{2,10},{3,11},{4,12},{5,13},{6,14},{7,15},{8,0},{9,1},... | collective-permute-start | bytes 245768 | tf_op jit(solution)/shard_map/ppermute | solution.py:374
  110.2 7.0 %collective-permute-start.29 = (bf16[320,128]{1,0:T(8,128)(2,1)S(1)}, bf16[320,128]{1,0:T(8,128)(2,1)S(1)}, u32[]{:S(2)}, u32[]{:S(2)}) collective-permute-start(bf16[320,128]{1,0:T(8,128)(2,1)S(1)} %get-tuple-element.50), channel_id=1, source_target_pairs={{0,4},{1,5},{2,6},{3,7},{4,0},{5,1},{6,2},{7,3},{8,12},{9,13},{10,... | collective-permute-start | bytes 245768 | tf_op jit(solution)/shard_map/ppermute | solution.py:374
  112.4 6.3 %collective-permute-start.30 = (bf16[320,128]{1,0:T(8,128)(2,1)S(1)}, bf16[320,128]{1,0:T(8,128)(2,1)S(1)}, u32[]{:S(2)}, u32[]{:S(2)}) collective-permute-start(bf16[320,128]{1,0:T(8,128)(2,1)S(1)} %get-tuple-element.50), channel_id=1, source_target_pairs={{0,12},{1,13},{2,14},{3,15},{4,8},{5,9},{6,10},{7,11},{8,4},{9,5},... | collective-permute-start | bytes 245768 | tf_op jit(solution)/shard_map/ppermute | solution.py:374
  114.6 5.4 %collective-permute-start.31 = (bf16[320,128]{1,0:T(8,128)(2,1)S(1)}, bf16[320,128]{1,0:T(8,128)(2,1)S(1)}, u32[]{:S(2)}, u32[]{:S(2)}) collective-permute-start(bf16[320,128]{1,0:T(8,128)(2,1)S(1)} %get-tuple-element.50), channel_id=1, source_target_pairs={{0,2},{1,3},{2,0},{3,1},{4,6},{5,7},{6,4},{7,5},{8,10},{9,11},{10,... | collective-permute-start | bytes 245768 | tf_op jit(solution)/shard_map/ppermute | solution.py:374
  118.8 6.3 %collective-permute-start.32 = (bf16[960,128]{1,0:T(8,128)(2,1)S(1)}, bf16[960,128]{1,0:T(8,128)(2,1)S(1)}, u32[]{:S(2)}, u32[]{:S(2)}) collective-permute-start(bf16[960,128]{1,0:T(8,128)(2,1)S(1)} %pad_maximum_fusion.1), channel_id=1, source_target_pairs={{0,2},{1,3},{2,0},{3,1},{4,6},{5,7},{6,4},{7,5},{8,10},{9,11},{10,... | collective-permute-start | bytes 737288 | tf_op jit(solution)/shard_map/ppermute | solution.py:374
  120.1 5.0 %collective-permute-start.33 = (bf16[1600,128]{1,0:T(8,128)(2,1)S(1)}, bf16[1600,128]{1,0:T(8,128)(2,1)S(1)}, u32[]{:S(2)}, u32[]{:S(2)}) collective-permute-start(bf16[1600,128]{1,0:T(8,128)(2,1)S(1)} %constant_dynamic-update-slice_fusion.10.refs_0_), channel_id=1, source_target_pairs={{0,1},{1,0},{2,3},{3,2},{4,5},{5,4},{6,7},{7,6},{8,9},{9,8},{10,11... | collective-permute-start | bytes 1228808 | tf_op jit(solution)/shard_map/ppermute | solution.py:374
  140.1 9.2 %collective-permute-start.37 = (bf16[2048,128]{1,0:T(8,128)(2,1)S(1)}, bf16[2048,128]{1,0:T(8,128)(2,1)S(1)}, u32[]{:S(2)}, u32[]{:S(2)}) collective-permute-start(bf16[2048,128]{1,0:T(8,128)(2,1)S(1)} %add_convert_fusion), channel_id=1, source_target_pairs={{0,2},{1,5},{2,0},{3,7},{4,6},{5,1},{6,4},{7,3},{8,10},{9,13},{10,... | collective-permute-start | bytes 1572872 | tf_op jit(solution)/shard_map/ppermute | solution.py:374
  149.6 11.5 %collective-permute-start.38 = (bf16[512,128]{1,0:T(8,128)(2,1)S(1)}, bf16[512,128]{1,0:T(8,128)(2,1)S(1)}, u32[]{:S(2)}, u32[]{:S(2)}) collective-permute-start(bf16[512,128]{1,0:T(8,128)(2,1)S(1)} %get-tuple-element.53), channel_id=1, source_target_pairs={{0,8},{1,3},{2,10},{3,1},{4,12},{5,7},{6,14},{7,5},{8,0},{9,11},{1... | collective-permute-start | bytes 393224 | tf_op jit(solution)/shard_map/ppermute | solution.py:374
  152.1 9.0 %collective-permute-start.39 = (bf16[512,128]{1,0:T(8,128)(2,1)S(1)}, bf16[512,128]{1,0:T(8,128)(2,1)S(1)}, u32[]{:S(2)}, u32[]{:S(2)}) collective-permute-start(bf16[512,128]{1,0:T(8,128)(2,1)S(1)} %get-tuple-element.55), channel_id=1, source_target_pairs={{0,4},{1,9},{2,6},{3,11},{4,0},{5,13},{6,2},{7,15},{8,12},{9,1},{1... | collective-permute-start | bytes 393224 | tf_op jit(solution)/shard_map/ppermute | solution.py:374
  152.3 10.3 %collective-permute-start.40 = (bf16[512,128]{1,0:T(8,128)(2,1)S(1)}, bf16[512,128]{1,0:T(8,128)(2,1)S(1)}, u32[]{:S(2)}, u32[]{:S(2)}) collective-permute-start(bf16[512,128]{1,0:T(8,128)(2,1)S(1)} %get-tuple-element.54), channel_id=1, source_target_pairs={{0,12},{1,11},{2,14},{3,9},{4,8},{5,15},{6,10},{7,13},{8,4},{9,3},... | collective-permute-start | bytes 393224 | tf_op jit(solution)/shard_map/ppermute | solution.py:374
  (11 other events, 21.6 us)

commit v16 on v12

--- a/solution.py
+++ b/solution.py
@@ -18,7 +18,7 @@
 SPARE = SLOT_PAIRS + 2
 ROW_TILE = 16
 SUPPORT_PARTS = 2
-SUPPORT_STEP = 4
+SUPPORT_STEP = 8
 PIECE = 5
 MATRIX_UNIT = 256
 VMEM_MARGIN = 3 * 1024 * 1024

time: 166 us -> 166 us (level)
  no operation moved by 1% of the time
where the time goes in v16:
time: 166 us; the launch traced here: 165 us
  waiting for transfers between devices  59.4 us (36%)
  Pallas kernels  50.7 us (31%)
  starting transfers between devices  45.3 us (27%)
  local copies, waits for them, and re-layouts  6.4 us (4%)
  other arithmetic  2.29 us (1%)
    ppermute x41, waiting for transfers between devices, exchange(): lax.ppermute(value, 'rows', [(i, i ^ apart[i % 2]) for i in range(devices)])  59.4 us
    ppermute x41, starting transfers between devices, exchange(): lax.ppermute(value, 'rows', [(i, i ^ apart[i % 2]) for i in range(devices)])  45.3 us
    pallas_call x3, Pallas kernels, gradient_call(): pl.pallas_call(functools.partial(gradient_kernel, mode, shards, pairs, gr...  33.1 us
    pallas_call x2, Pallas kernels, collect_support(): pl.pallas_call(functools.partial(support_kernel, part * entries, groups),...  17.7 us
  transfers between devices with their start and end apart: 41, of which 21 were waited for; matrix products, arithmetic and copies ran while one was open for 3% of the time, Pallas kernels for 11%

profile of v16, /device:TPU:0, one launch (start us, length us, event | category | flops | bytes accessed | tf_op | source)
XLA Modules:
  0.0 164.5 jit_solution(2568452036097539117)
XLA Ops:
  1.6 4.1 %collective-permute-start = (bf16[512,128]{1,0:T(8,128)(2,1)S(1)}, bf16[512,128]{1,0:T(8,128)(2,1)S(1)}, u32[]{:S(2)}, u32[]{:S(2)}) collective-permute-start(bf16[512,128]{1,0:T(8,128)(2,1)S(1)} %reshape.71), channel_id=1, source_target_pairs={{0,8},{1,9},{2,10},{3,11},{4,12},{5,13},{6,14},{7,15},{8,0},{9,1},... | collective-permute-start | bytes 393224 | tf_op jit(solution)/shard_map/ppermute | solution.py:376
  5.7 1.6 collective-permute-start.1
  7.3 1.7 %collective-permute-start.3 = (bf16[512,128]{1,0:T(8,128)(2,1)S(1)}, bf16[512,128]{1,0:T(8,128)(2,1)S(1)}, u32[]{:S(2)}, u32[]{:S(2)}) collective-permute-start(bf16[512,128]{1,0:T(8,128)(2,1)S(1)} %reshape.71), channel_id=1, source_target_pairs={{0,2},{1,3},{2,0},{3,1},{4,6},{5,7},{6,4},{7,5},{8,10},{9,11},{10,... | collective-permute-start | bytes 393224 | tf_op jit(solution)/shard_map/ppermute | solution.py:376
  11.7 8.7 %collect_support.2.refs_0_ = bf16[520,512,128]{2,1,0:T(8,128)(2,1)} custom-call(s32[305]{0:T(512)S(1)} %concatenate.18.scalars, bf16[512,32768]{1,0:T(8,128)(2,1)} %dictionary.3), custom_call_target="tpu_custom_call" | custom-call | bytes 31457280 | tf_op jit(solution)/shard_map/collect_support/pallas_call | solution.py:130
  21.0 8.9 %collect_support.3.blocks = bf16[520,512,128]{2,1,0:T(8,128)(2,1)} custom-call(s32[305]{0:T(512)S(1)} %concatenate.18.scalars, bf16[512,32768]{1,0:T(8,128)(2,1)} %dictionary.3, bf16[520,512,128]{2,1,0:T(8,128)(2,1)} %collect_support.2.refs_0_), custom_call_target="tpu_custom_call", output_to_operand_aliasing={{}: (2, {})} | custom-call | bytes 31457280 | tf_op jit(solution)/shard_map/collect_support/pallas_call | solution.py:130
  30.5 1.5 copy.13
  32.4 10.8 %gradient.3 = (f32[2560,128]{1,0:T(8,128)S(1)}, bf16[1600,128]{1,0:T(8,128)(2,1)S(1)}, bf16[960,128]{1,0:T(8,128)(2,1)S(1)}, bf16[320,128]{1,0:T(8,128)(2,1)S(1)}, f32[320,128]{1,0:T(8,128)S(1)}) custom-call(s32[305]{0:T(512)S(1)} %concatenate.18.scalars, bf16[520,512,128]{2,1,0:T(8,128)(2,1)} %collect_support.3.blocks, ...), custom_call_target="tpu_custom_call" | custom-call | flops 5368709120 | bytes 10485760 | tf_op jit(solution)/shard_map/gradient/pallas_call | solution.py:353
  44.9 1.7 %collective-permute-start.9 = (bf16[960,128]{1,0:T(8,128)(2,1)S(1)}, bf16[960,128]{1,0:T(8,128)(2,1)S(1)}, u32[]{:S(2)}, u32[]{:S(2)}) collective-permute-start(bf16[960,128]{1,0:T(8,128)(2,1)S(1)} %add_convert_fusion.2), channel_id=1, source_target_pairs={{0,2},{1,3},{2,0},{3,1},{4,6},{5,7},{6,4},{7,5},{8,10},{9,11},{10,... | collective-permute-start | bytes 737288 | tf_op jit(solution)/shard_map/ppermute | solution.py:376
  46.6 6.5 %collective-permute-done.9 = bf16[960,128]{1,0:T(8,128)(2,1)S(1)} collective-permute-done((bf16[960,128]{1,0:T(8,128)(2,1)S(1)}, bf16[960,128]{1,0:T(8,128)(2,1)S(1)}, u32[]{:S(2)}, u32[]{:S(2)}) %collective-permute-start.9) | collective-permute-done | bytes 245792 | tf_op jit(solution)/shard_map/ppermute | solution.py:376
  53.2 1.7 %collective-permute-start.11 = (bf16[320,128]{1,0:T(8,128)(2,1)S(1)}, bf16[320,128]{1,0:T(8,128)(2,1)S(1)}, u32[]{:S(2)}, u32[]{:S(2)}) collective-permute-start(bf16[320,128]{1,0:T(8,128)(2,1)S(1)} %get-tuple-element.59), channel_id=1, source_target_pairs={{0,8},{1,9},{2,10},{3,11},{4,12},{5,13},{6,14},{7,15},{8,0},{9,1},... | collective-permute-start | bytes 245768 | tf_op jit(solution)/shard_map/ppermute | solution.py:376
  54.9 2.5 %collective-permute-start.12 = (bf16[320,128]{1,0:T(8,128)(2,1)S(1)}, bf16[320,128]{1,0:T(8,128)(2,1)S(1)}, u32[]{:S(2)}, u32[]{:S(2)}) collective-permute-start(bf16[320,128]{1,0:T(8,128)(2,1)S(1)} %get-tuple-element.61), channel_id=1, source_target_pairs={{0,4},{1,5},{2,6},{3,7},{4,0},{5,1},{6,2},{7,3},{8,12},{9,13},{10,... | collective-permute-start | bytes 245768 | tf_op jit(solution)/shard_map/ppermute | solution.py:376
  60.3 3.3 %collective-permute-done.13 = bf16[320,128]{1,0:T(8,128)(2,1)S(1)} collective-permute-done((bf16[320,128]{1,0:T(8,128)(2,1)S(1)}, bf16[320,128]{1,0:T(8,128)(2,1)S(1)}, u32[]{:S(2)}, u32[]{:S(2)}) %collective-permute-start.13) | collective-permute-done | bytes 81952 | tf_op jit(solution)/shard_map/ppermute | solution.py:376
  66.4 1.8 %collective-permute-start.16 = (bf16[320,128]{1,0:T(8,128)(2,1)S(1)}, bf16[320,128]{1,0:T(8,128)(2,1)S(1)}, u32[]{:S(2)}, u32[]{:S(2)}) collective-permute-start(bf16[320,128]{1,0:T(8,128)(2,1)S(1)} %get-tuple-element.52), channel_id=1, source_target_pairs={{0,12},{1,13},{2,14},{3,15},{4,8},{5,9},{6,10},{7,11},{8,4},{9,5},... | collective-permute-start | bytes 245768 | tf_op jit(solution)/shard_map/ppermute | solution.py:376
  71.0 1.6 collective-permute-done.16
  72.7 1.6 collective-permute-start.18
  74.4 4.5 %collective-permute-done.18.refs_1_ = bf16[960,128]{1,0:T(8,128)(2,1)S(1)} collective-permute-done((bf16[960,128]{1,0:T(8,128)(2,1)S(1)}, bf16[960,128]{1,0:T(8,128)(2,1)S(1)}, u32[]{:S(2)}, u32[]{:S(2)}) %collective-permute-start.18) | collective-permute-done | bytes 245792 | tf_op jit(solution)/shard_map/ppermute | solution.py:376
  79.0 1.5 collective-permute-done.20.refs_3_
  80.5 10.5 %gradient.4 = (f32[2560,128]{1,0:T(8,128)S(1)}, bf16[1600,128]{1,0:T(8,128)(2,1)S(1)}, bf16[960,128]{1,0:T(8,128)(2,1)S(1)}) custom-call(s32[305]{0:T(512)S(1)} %concatenate.18.scalars, bf16[520,512,128]{2,1,0:T(8,128)(2,1)} %collect_support.3.blocks, bf16[1600,128]{1,0:T(8,128)(2,1)S(1)} %constant_dynamic-update-slice_fusion.5.refs_0_, ...), custom_call_target="tpu_custom_call" | custom-call | flops 5368709120 | bytes 10485760 | tf_op jit(solution)/shard_map/gradient/pallas_call | solution.py:353
  92.6 1.6 collective-permute-start.23
  94.3 6.4 %collective-permute-done.23 = bf16[960,128]{1,0:T(8,128)(2,1)S(1)} collective-permute-done((bf16[960,128]{1,0:T(8,128)(2,1)S(1)}, bf16[960,128]{1,0:T(8,128)(2,1)S(1)}, u32[]{:S(2)}, u32[]{:S(2)}) %collective-permute-start.23) | collective-permute-done | bytes 245792 | tf_op jit(solution)/shard_map/ppermute | solution.py:376
  103.3 1.9 %collective-permute-start.27 = (bf16[320,128]{1,0:T(8,128)(2,1)S(1)}, bf16[320,128]{1,0:T(8,128)(2,1)S(1)}, u32[]{:S(2)}, u32[]{:S(2)}) collective-permute-start(bf16[320,128]{1,0:T(8,128)(2,1)S(1)} %get-tuple-element.57), channel_id=1, source_target_pairs={{0,12},{1,13},{2,14},{3,15},{4,8},{5,9},{6,10},{7,11},{8,4},{9,5},... | collective-permute-start | bytes 245768 | tf_op jit(solution)/shard_map/ppermute | solution.py:376
  106.7 3.0 %collective-permute-done.25 = bf16[320,128]{1,0:T(8,128)(2,1)S(1)} collective-permute-done((bf16[320,128]{1,0:T(8,128)(2,1)S(1)}, bf16[320,128]{1,0:T(8,128)(2,1)S(1)}, u32[]{:S(2)}, u32[]{:S(2)}) %collective-permute-start.25) | collective-permute-done | bytes 81952 | tf_op jit(solution)/shard_map/ppermute | solution.py:376
  110.0 2.0 %collective-permute-start.28 = (bf16[320,128]{1,0:T(8,128)(2,1)S(1)}, bf16[320,128]{1,0:T(8,128)(2,1)S(1)}, u32[]{:S(2)}, u32[]{:S(2)}) collective-permute-start(bf16[320,128]{1,0:T(8,128)(2,1)S(1)} %get-tuple-element.50), channel_id=1, source_target_pairs={{0,8},{1,9},{2,10},{3,11},{4,12},{5,13},{6,14},{7,15},{8,0},{9,1},... | collective-permute-start | bytes 245768 | tf_op jit(solution)/shard_map/ppermute | solution.py:376
  112.5 1.9 %collective-permute-start.30 = (bf16[320,128]{1,0:T(8,128)(2,1)S(1)}, bf16[320,128]{1,0:T(8,128)(2,1)S(1)}, u32[]{:S(2)}, u32[]{:S(2)}) collective-permute-start(bf16[320,128]{1,0:T(8,128)(2,1)S(1)} %get-tuple-element.50), channel_id=1, source_target_pairs={{0,12},{1,13},{2,14},{3,15},{4,8},{5,9},{6,10},{7,11},{8,4},{9,5},... | collective-permute-start | bytes 245768 | tf_op jit(solution)/shard_map/ppermute | solution.py:376
  115.9 2.0 %collective-permute-done.28 = bf16[320,128]{1,0:T(8,128)(2,1)S(1)} collective-permute-done((bf16[320,128]{1,0:T(8,128)(2,1)S(1)}, bf16[320,128]{1,0:T(8,128)(2,1)S(1)}, u32[]{:S(2)}, u32[]{:S(2)}) %collective-permute-start.28) | collective-permute-done | bytes 81952 | tf_op jit(solution)/shard_map/ppermute | solution.py:376
  120.5 4.9 %collective-permute-done.32.refs_1_ = bf16[960,128]{1,0:T(8,128)(2,1)S(1)} collective-permute-done((bf16[960,128]{1,0:T(8,128)(2,1)S(1)}, bf16[960,128]{1,0:T(8,128)(2,1)S(1)}, u32[]{:S(2)}, u32[]{:S(2)}) %collective-permute-start.32) | collective-permute-done | bytes 245792 | tf_op jit(solution)/shard_map/ppermute | solution.py:376
  125.4 1.5 collective-permute-done.34.refs_3_
  126.9 11.7 %gradient.5 = (f32[4096,128]{1,0:T(8,128)S(1)}, bf16[2048,128]{1,0:T(8,128)(2,1)S(1)}, bf16[2048,128]{1,0:T(8,128)(2,1)S(1)}, bf16[8,64,128]{2,1,0:T(8,128)(2,1)S(1)}, f32[64,128]{1,0:T(8,128)S(1)}) custom-call(s32[305]{0:T(512)S(1)} %concatenate.18.scalars, bf16[520,512,128]{2,1,0:T(8,128)(2,1)} %collect_support.3.blocks, ...), custom_call_target="tpu_custom_call" | custom-call | flops 5368709120 | bytes 10485760 | tf_op jit(solution)/shard_map/gradient/pallas_call | solution.py:353
  142.0 8.0 %collective-permute-done.37 = bf16[2048,128]{1,0:T(8,128)(2,1)S(1)} collective-permute-done((bf16[2048,128]{1,0:T(8,128)(2,1)S(1)}, bf16[2048,128]{1,0:T(8,128)(2,1)S(1)}, u32[]{:S(2)}, u32[]{:S(2)}) %collective-permute-start.37) | collective-permute-done | bytes 524320 | tf_op jit(solution)/shard_map/ppermute | solution.py:376
  150.2 2.0 %collective-permute-start.38 = (bf16[512,128]{1,0:T(8,128)(2,1)S(1)}, bf16[512,128]{1,0:T(8,128)(2,1)S(1)}, u32[]{:S(2)}, u32[]{:S(2)}) collective-permute-start(bf16[512,128]{1,0:T(8,128)(2,1)S(1)} %get-tuple-element.53), channel_id=1, source_target_pairs={{0,8},{1,3},{2,10},{3,1},{4,12},{5,7},{6,14},{7,5},{8,0},{9,11},{1... | collective-permute-start | bytes 393224 | tf_op jit(solution)/shard_map/ppermute | solution.py:376
  152.8 2.2 %collective-permute-start.40 = (bf16[512,128]{1,0:T(8,128)(2,1)S(1)}, bf16[512,128]{1,0:T(8,128)(2,1)S(1)}, u32[]{:S(2)}, u32[]{:S(2)}) collective-permute-start(bf16[512,128]{1,0:T(8,128)(2,1)S(1)} %get-tuple-element.54), channel_id=1, source_target_pairs={{0,12},{1,11},{2,14},{3,9},{4,8},{5,15},{6,10},{7,13},{8,4},{9,3},... | collective-permute-start | bytes 393224 | tf_op jit(solution)/shard_map/ppermute | solution.py:376
  155.0 8.2 %collective-permute-done.38 = bf16[512,128]{1,0:T(8,128)(2,1)S(1)} collective-permute-done((bf16[512,128]{1,0:T(8,128)(2,1)S(1)}, bf16[512,128]{1,0:T(8,128)(2,1)S(1)}, u32[]{:S(2)}, u32[]{:S(2)}) %collective-permute-start.38) | collective-permute-done | bytes 131104 | tf_op jit(solution)/shard_map/ppermute | solution.py:376
  (106 shorter events, 32.3 us)
Async XLA Ops:
  1.6 18.9 %collective-permute-start = (bf16[512,128]{1,0:T(8,128)(2,1)S(1)}, bf16[512,128]{1,0:T(8,128)(2,1)S(1)}, u32[]{:S(2)}, u32[]{:S(2)}) collective-permute-start(bf16[512,128]{1,0:T(8,128)(2,1)S(1)} %reshape.71), channel_id=1, source_target_pairs={{0,8},{1,9},{2,10},{3,11},{4,12},{5,13},{6,14},{7,15},{8,0},{9,1},... | collective-permute-start | bytes 393224 | tf_op jit(solution)/shard_map/ppermute | solution.py:376
  5.7 14.8 %collective-permute-start.1 = (bf16[512,128]{1,0:T(8,128)(2,1)S(1)}, bf16[512,128]{1,0:T(8,128)(2,1)S(1)}, u32[]{:S(2)}, u32[]{:S(2)}) collective-permute-start(bf16[512,128]{1,0:T(8,128)(2,1)S(1)} %reshape.71), channel_id=1, source_target_pairs={{0,4},{1,5},{2,6},{3,7},{4,0},{5,1},{6,2},{7,3},{8,12},{9,13},{10,... | collective-permute-start | bytes 393224 | tf_op jit(solution)/shard_map/ppermute | solution.py:376
  7.3 13.3 %collective-permute-start.2 = (bf16[512,128]{1,0:T(8,128)(2,1)S(1)}, bf16[512,128]{1,0:T(8,128)(2,1)S(1)}, u32[]{:S(2)}, u32[]{:S(2)}) collective-permute-start(bf16[512,128]{1,0:T(8,128)(2,1)S(1)} %reshape.71), channel_id=1, source_target_pairs={{0,12},{1,13},{2,14},{3,15},{4,8},{5,9},{6,10},{7,11},{8,4},{9,5},... | collective-permute-start | bytes 393224 | tf_op jit(solution)/shard_map/ppermute | solution.py:376
  7.3 13.3 %collective-permute-start.3 = (bf16[512,128]{1,0:T(8,128)(2,1)S(1)}, bf16[512,128]{1,0:T(8,128)(2,1)S(1)}, u32[]{:S(2)}, u32[]{:S(2)}) collective-permute-start(bf16[512,128]{1,0:T(8,128)(2,1)S(1)} %reshape.71), channel_id=1, source_target_pairs={{0,2},{1,3},{2,0},{3,1},{4,6},{5,7},{6,4},{7,5},{8,10},{9,11},{10,... | collective-permute-start | bytes 393224 | tf_op jit(solution)/shard_map/ppermute | solution.py:376
  20.7 9.9 %collective-permute-start.4 = (bf16[1536,128]{1,0:T(8,128)(2,1)S(1)}, bf16[1536,128]{1,0:T(8,128)(2,1)S(1)}, u32[]{:S(2)}, u32[]{:S(2)}) collective-permute-start(bf16[1536,128]{1,0:T(8,128)(2,1)S(1)} %slice.75), channel_id=1, source_target_pairs={{0,2},{1,3},{2,0},{3,1},{4,6},{5,7},{6,4},{7,5},{8,10},{9,11},{10,... | collective-permute-start | bytes 1179656 | tf_op jit(solution)/shard_map/ppermute | solution.py:376
  21.0 11.1 %collective-permute-start.5 = (bf16[2560,128]{1,0:T(8,128)(2,1)S(1)}, bf16[2560,128]{1,0:T(8,128)(2,1)S(1)}, u32[]{:S(2)}, u32[]{:S(2)}) collective-permute-start(bf16[2560,128]{1,0:T(8,128)(2,1)S(1)} %constant_dynamic-update-slice_fusion.refs_0_), channel_id=1, source_target_pairs={{0,1},{1,0},{2,3},{3,2},{4,5},{5,4},{6,7},{7,6},{8,9},{9,8},{10,11... | collective-permute-start | bytes 1966088 | tf_op jit(solution)/shard_map/ppermute | solution.py:376
  44.9 8.3 %collective-permute-start.9 = (bf16[960,128]{1,0:T(8,128)(2,1)S(1)}, bf16[960,128]{1,0:T(8,128)(2,1)S(1)}, u32[]{:S(2)}, u32[]{:S(2)}) collective-permute-start(bf16[960,128]{1,0:T(8,128)(2,1)S(1)} %add_convert_fusion.2), channel_id=1, source_target_pairs={{0,2},{1,3},{2,0},{3,1},{4,6},{5,7},{6,4},{7,5},{8,10},{9,11},{10,... | collective-permute-start | bytes 737288 | tf_op jit(solution)/shard_map/ppermute | solution.py:376
  53.2 7.1 %collective-permute-start.11 = (bf16[320,128]{1,0:T(8,128)(2,1)S(1)}, bf16[320,128]{1,0:T(8,128)(2,1)S(1)}, u32[]{:S(2)}, u32[]{:S(2)}) collective-permute-start(bf16[320,128]{1,0:T(8,128)(2,1)S(1)} %get-tuple-element.59), channel_id=1, source_target_pairs={{0,8},{1,9},{2,10},{3,11},{4,12},{5,13},{6,14},{7,15},{8,0},{9,1},... | collective-permute-start | bytes 245768 | tf_op jit(solution)/shard_map/ppermute | solution.py:376
  54.9 5.4 %collective-permute-start.12 = (bf16[320,128]{1,0:T(8,128)(2,1)S(1)}, bf16[320,128]{1,0:T(8,128)(2,1)S(1)}, u32[]{:S(2)}, u32[]{:S(2)}) collective-permute-start(bf16[320,128]{1,0:T(8,128)(2,1)S(1)} %get-tuple-element.61), channel_id=1, source_target_pairs={{0,4},{1,5},{2,6},{3,7},{4,0},{5,1},{6,2},{7,3},{8,12},{9,13},{10,... | collective-permute-start | bytes 245768 | tf_op jit(solution)/shard_map/ppermute | solution.py:376
  57.4 6.2 %collective-permute-start.13 = (bf16[320,128]{1,0:T(8,128)(2,1)S(1)}, bf16[320,128]{1,0:T(8,128)(2,1)S(1)}, u32[]{:S(2)}, u32[]{:S(2)}) collective-permute-start(bf16[320,128]{1,0:T(8,128)(2,1)S(1)} %get-tuple-element.60), channel_id=1, source_target_pairs={{0,12},{1,13},{2,14},{3,15},{4,8},{5,9},{6,10},{7,11},{8,4},{9,5},... | collective-permute-start | bytes 245768 | tf_op jit(solution)/shard_map/ppermute | solution.py:376
  57.7 6.0 %collective-permute-start.10 = (bf16[320,128]{1,0:T(8,128)(2,1)S(1)}, bf16[320,128]{1,0:T(8,128)(2,1)S(1)}, u32[]{:S(2)}, u32[]{:S(2)}) collective-permute-start(bf16[320,128]{1,0:T(8,128)(2,1)S(1)} %slice.160), channel_id=1, source_target_pairs={{0,2},{1,3},{2,0},{3,1},{4,6},{5,7},{6,4},{7,5},{8,10},{9,11},{10,... | collective-permute-start | bytes 245768 | tf_op jit(solution)/shard_map/ppermute | solution.py:376
  63.8 7.1 %collective-permute-start.14 = (bf16[320,128]{1,0:T(8,128)(2,1)S(1)}, bf16[320,128]{1,0:T(8,128)(2,1)S(1)}, u32[]{:S(2)}, u32[]{:S(2)}) collective-permute-start(bf16[320,128]{1,0:T(8,128)(2,1)S(1)} %get-tuple-element.52), channel_id=1, source_target_pairs={{0,8},{1,9},{2,10},{3,11},{4,12},{5,13},{6,14},{7,15},{8,0},{9,1},... | collective-permute-start | bytes 245768 | tf_op jit(solution)/shard_map/ppermute | solution.py:376
  65.2 5.9 %collective-permute-start.15 = (bf16[320,128]{1,0:T(8,128)(2,1)S(1)}, bf16[320,128]{1,0:T(8,128)(2,1)S(1)}, u32[]{:S(2)}, u32[]{:S(2)}) collective-permute-start(bf16[320,128]{1,0:T(8,128)(2,1)S(1)} %get-tuple-element.52), channel_id=1, source_target_pairs={{0,4},{1,5},{2,6},{3,7},{4,0},{5,1},{6,2},{7,3},{8,12},{9,13},{10,... | collective-permute-start | bytes 245768 | tf_op jit(solution)/shard_map/ppermute | solution.py:376
  66.4 6.2 %collective-permute-start.16 = (bf16[320,128]{1,0:T(8,128)(2,1)S(1)}, bf16[320,128]{1,0:T(8,128)(2,1)S(1)}, u32[]{:S(2)}, u32[]{:S(2)}) collective-permute-start(bf16[320,128]{1,0:T(8,128)(2,1)S(1)} %get-tuple-element.52), channel_id=1, source_target_pairs={{0,12},{1,13},{2,14},{3,15},{4,8},{5,9},{6,10},{7,11},{8,4},{9,5},... | collective-permute-start | bytes 245768 | tf_op jit(solution)/shard_map/ppermute | solution.py:376
  68.2 6.1 %collective-permute-start.17 = (bf16[320,128]{1,0:T(8,128)(2,1)S(1)}, bf16[320,128]{1,0:T(8,128)(2,1)S(1)}, u32[]{:S(2)}, u32[]{:S(2)}) collective-permute-start(bf16[320,128]{1,0:T(8,128)(2,1)S(1)} %get-tuple-element.52), channel_id=1, source_target_pairs={{0,2},{1,3},{2,0},{3,1},{4,6},{5,7},{6,4},{7,5},{8,10},{9,11},{10,... | collective-permute-start | bytes 245768 | tf_op jit(solution)/shard_map/ppermute | solution.py:376
  72.7 6.3 %collective-permute-start.18 = (bf16[960,128]{1,0:T(8,128)(2,1)S(1)}, bf16[960,128]{1,0:T(8,128)(2,1)S(1)}, u32[]{:S(2)}, u32[]{:S(2)}) collective-permute-start(bf16[960,128]{1,0:T(8,128)(2,1)S(1)} %pad_maximum_fusion), channel_id=1, source_target_pairs={{0,2},{1,3},{2,0},{3,1},{4,6},{5,7},{6,4},{7,5},{8,10},{9,11},{10,... | collective-permute-start | bytes 737288 | tf_op jit(solution)/shard_map/ppermute | solution.py:376
  74.3 4.6 %collective-permute-start.19 = (bf16[1600,128]{1,0:T(8,128)(2,1)S(1)}, bf16[1600,128]{1,0:T(8,128)(2,1)S(1)}, u32[]{:S(2)}, u32[]{:S(2)}) collective-permute-start(bf16[1600,128]{1,0:T(8,128)(2,1)S(1)} %constant_dynamic-update-slice_fusion.5.refs_0_), channel_id=1, source_target_pairs={{0,1},{1,0},{2,3},{3,2},{4,5},{5,4},{6,7},{7,6},{8,9},{9,8},{10,11... | collective-permute-start | bytes 1228808 | tf_op jit(solution)/shard_map/ppermute | solution.py:376
  92.6 8.1 %collective-permute-start.23 = (bf16[960,128]{1,0:T(8,128)(2,1)S(1)}, bf16[960,128]{1,0:T(8,128)(2,1)S(1)}, u32[]{:S(2)}, u32[]{:S(2)}) collective-permute-start(bf16[960,128]{1,0:T(8,128)(2,1)S(1)} %add_convert_fusion.1), channel_id=1, source_target_pairs={{0,2},{1,3},{2,0},{3,1},{4,6},{5,7},{6,4},{7,5},{8,10},{9,11},{10,... | collective-permute-start | bytes 737288 | tf_op jit(solution)/shard_map/ppermute | solution.py:376
  100.8 9.0 %collective-permute-start.25 = (bf16[320,128]{1,0:T(8,128)(2,1)S(1)}, bf16[320,128]{1,0:T(8,128)(2,1)S(1)}, u32[]{:S(2)}, u32[]{:S(2)}) collective-permute-start(bf16[320,128]{1,0:T(8,128)(2,1)S(1)} %get-tuple-element.56), channel_id=1, source_target_pairs={{0,8},{1,9},{2,10},{3,11},{4,12},{5,13},{6,14},{7,15},{8,0},{9,1},... | collective-permute-start | bytes 245768 | tf_op jit(solution)/shard_map/ppermute | solution.py:376
  102.2 7.5 %collective-permute-start.26 = (bf16[320,128]{1,0:T(8,128)(2,1)S(1)}, bf16[320,128]{1,0:T(8,128)(2,1)S(1)}, u32[]{:S(2)}, u32[]{:S(2)}) collective-permute-start(bf16[320,128]{1,0:T(8,128)(2,1)S(1)} %get-tuple-element.58), channel_id=1, source_target_pairs={{0,4},{1,5},{2,6},{3,7},{4,0},{5,1},{6,2},{7,3},{8,12},{9,13},{10,... | collective-permute-start | bytes 245768 | tf_op jit(solution)/shard_map/ppermute | solution.py:376
  103.3 6.4 %collective-permute-start.27 = (bf16[320,128]{1,0:T(8,128)(2,1)S(1)}, bf16[320,128]{1,0:T(8,128)(2,1)S(1)}, u32[]{:S(2)}, u32[]{:S(2)}) collective-permute-start(bf16[320,128]{1,0:T(8,128)(2,1)S(1)} %get-tuple-element.57), channel_id=1, source_target_pairs={{0,12},{1,13},{2,14},{3,15},{4,8},{5,9},{6,10},{7,11},{8,4},{9,5},... | collective-permute-start | bytes 245768 | tf_op jit(solution)/shard_map/ppermute | solution.py:376
  105.2 4.5 %collective-permute-start.24 = (bf16[320,128]{1,0:T(8,128)(2,1)S(1)}, bf16[320,128]{1,0:T(8,128)(2,1)S(1)}, u32[]{:S(2)}, u32[]{:S(2)}) collective-permute-start(bf16[320,128]{1,0:T(8,128)(2,1)S(1)} %slice.159), channel_id=1, source_target_pairs={{0,2},{1,3},{2,0},{3,1},{4,6},{5,7},{6,4},{7,5},{8,10},{9,11},{10,... | collective-permute-start | bytes 245768 | tf_op jit(solution)/shard_map/ppermute | solution.py:376
  110.0 7.9 %collective-permute-start.28 = (bf16[320,128]{1,0:T(8,128)(2,1)S(1)}, bf16[320,128]{1,0:T(8,128)(2,1)S(1)}, u32[]{:S(2)}, u32[]{:S(2)}) collective-permute-start(bf16[320,128]{1,0:T(8,128)(2,1)S(1)} %get-tuple-element.50), channel_id=1, source_target_pairs={{0,8},{1,9},{2,10},{3,11},{4,12},{5,13},{6,14},{7,15},{8,0},{9,1},... | collective-permute-start | bytes 245768 | tf_op jit(solution)/shard_map/ppermute | solution.py:376
  112.0 6.0 %collective-permute-start.29 = (bf16[320,128]{1,0:T(8,128)(2,1)S(1)}, bf16[320,128]{1,0:T(8,128)(2,1)S(1)}, u32[]{:S(2)}, u32[]{:S(2)}) collective-permute-start(bf16[320,128]{1,0:T(8,128)(2,1)S(1)} %get-tuple-element.50), channel_id=1, source_target_pairs={{0,4},{1,5},{2,6},{3,7},{4,0},{5,1},{6,2},{7,3},{8,12},{9,13},{10,... | collective-permute-start | bytes 245768 | tf_op jit(solution)/shard_map/ppermute | solution.py:376
  112.5 6.6 %collective-permute-start.30 = (bf16[320,128]{1,0:T(8,128)(2,1)S(1)}, bf16[320,128]{1,0:T(8,128)(2,1)S(1)}, u32[]{:S(2)}, u32[]{:S(2)}) collective-permute-start(bf16[320,128]{1,0:T(8,128)(2,1)S(1)} %get-tuple-element.50), channel_id=1, source_target_pairs={{0,12},{1,13},{2,14},{3,15},{4,8},{5,9},{6,10},{7,11},{8,4},{9,5},... | collective-permute-start | bytes 245768 | tf_op jit(solution)/shard_map/ppermute | solution.py:376
  114.4 6.0 %collective-permute-start.31 = (bf16[320,128]{1,0:T(8,128)(2,1)S(1)}, bf16[320,128]{1,0:T(8,128)(2,1)S(1)}, u32[]{:S(2)}, u32[]{:S(2)}) collective-permute-start(bf16[320,128]{1,0:T(8,128)(2,1)S(1)} %get-tuple-element.50), channel_id=1, source_target_pairs={{0,2},{1,3},{2,0},{3,1},{4,6},{5,7},{6,4},{7,5},{8,10},{9,11},{10,... | collective-permute-start | bytes 245768 | tf_op jit(solution)/shard_map/ppermute | solution.py:376
  119.1 6.3 %collective-permute-start.32 = (bf16[960,128]{1,0:T(8,128)(2,1)S(1)}, bf16[960,128]{1,0:T(8,128)(2,1)S(1)}, u32[]{:S(2)}, u32[]{:S(2)}) collective-permute-start(bf16[960,128]{1,0:T(8,128)(2,1)S(1)} %pad_maximum_fusion.1), channel_id=1, source_target_pairs={{0,2},{1,3},{2,0},{3,1},{4,6},{5,7},{6,4},{7,5},{8,10},{9,11},{10,... | collective-permute-start | bytes 737288 | tf_op jit(solution)/shard_map/ppermute | solution.py:376
  120.4 5.0 %collective-permute-start.33 = (bf16[1600,128]{1,0:T(8,128)(2,1)S(1)}, bf16[1600,128]{1,0:T(8,128)(2,1)S(1)}, u32[]{:S(2)}, u32[]{:S(2)}) collective-permute-start(bf16[1600,128]{1,0:T(8,128)(2,1)S(1)} %constant_dynamic-update-slice_fusion.10.refs_0_), channel_id=1, source_target_pairs={{0,1},{1,0},{2,3},{3,2},{4,5},{5,4},{6,7},{7,6},{8,9},{9,8},{10,11... | collective-permute-start | bytes 1228808 | tf_op jit(solution)/shard_map/ppermute | solution.py:376
  140.7 9.2 %collective-permute-start.37 = (bf16[2048,128]{1,0:T(8,128)(2,1)S(1)}, bf16[2048,128]{1,0:T(8,128)(2,1)S(1)}, u32[]{:S(2)}, u32[]{:S(2)}) collective-permute-start(bf16[2048,128]{1,0:T(8,128)(2,1)S(1)} %add_convert_fusion), channel_id=1, source_target_pairs={{0,2},{1,5},{2,0},{3,7},{4,6},{5,1},{6,4},{7,3},{8,10},{9,13},{10,... | collective-permute-start | bytes 1572872 | tf_op jit(solution)/shard_map/ppermute | solution.py:376
  150.2 12.9 %collective-permute-start.38 = (bf16[512,128]{1,0:T(8,128)(2,1)S(1)}, bf16[512,128]{1,0:T(8,128)(2,1)S(1)}, u32[]{:S(2)}, u32[]{:S(2)}) collective-permute-start(bf16[512,128]{1,0:T(8,128)(2,1)S(1)} %get-tuple-element.53), channel_id=1, source_target_pairs={{0,8},{1,3},{2,10},{3,1},{4,12},{5,7},{6,14},{7,5},{8,0},{9,11},{1... | collective-permute-start | bytes 393224 | tf_op jit(solution)/shard_map/ppermute | solution.py:376
  152.2 10.9 %collective-permute-start.39 = (bf16[512,128]{1,0:T(8,128)(2,1)S(1)}, bf16[512,128]{1,0:T(8,128)(2,1)S(1)}, u32[]{:S(2)}, u32[]{:S(2)}) collective-permute-start(bf16[512,128]{1,0:T(8,128)(2,1)S(1)} %get-tuple-element.55), channel_id=1, source_target_pairs={{0,4},{1,9},{2,6},{3,11},{4,0},{5,13},{6,2},{7,15},{8,12},{9,1},{1... | collective-permute-start | bytes 393224 | tf_op jit(solution)/shard_map/ppermute | solution.py:376
  152.8 10.4 %collective-permute-start.40 = (bf16[512,128]{1,0:T(8,128)(2,1)S(1)}, bf16[512,128]{1,0:T(8,128)(2,1)S(1)}, u32[]{:S(2)}, u32[]{:S(2)}) collective-permute-start(bf16[512,128]{1,0:T(8,128)(2,1)S(1)} %get-tuple-element.54), channel_id=1, source_target_pairs={{0,12},{1,11},{2,14},{3,9},{4,8},{5,15},{6,10},{7,13},{8,4},{9,3},... | collective-permute-start | bytes 393224 | tf_op jit(solution)/shard_map/ppermute | solution.py:376
  (10 other events, 21.0 us)
